TPU v7x, 256 devices: a whole 4x4x8 slice. The times are simulated.
256 devices in a mesh: layer: 8 (over x, core), gx: 8 (over z), gy: 4 (over y).
Axes of the slice: x: 4, y: 4, z: 8, core: 2. Of those that a mesh axis runs over, the one named last changes fastest.
Arguments:
- pressure: float32 [64, 512, 1024], P('layer', 'gx', 'gy'), may hold values from -6 to 6
- source: float32 [64, 512, 1024], P('layer', 'gx', 'gy'), may hold values from -6 to 6
- perm_x: float32 [64, 512, 1024], P('layer', 'gx', 'gy'), may hold values from 0.05 to 0.5
- perm_y: float32 [64, 512, 1024], P('layer', 'gx', 'gy'), may hold values from 0.05 to 0.5
- line_inverse: float32 [8, 8, 8, 512, 1024], P('layer', None, None, 'gx', 'gy'), may hold values from -0.98 to 1.2
- robin_below: float32 [8, 512, 1024], P('layer', 'gx', 'gy'), may hold values from -6 to 6
- tile_count: int32 [8, 32], P('layer', ('gx', 'gy')), may hold values from 1 to 48, 512 in all within a row
- perf_owner: int32 [8, 1536, 1], P('layer', ('gx', 'gy')), may hold values from 0 to 31; in each aligned block of 48 rows (0 to 47, 48 to 95, ..., all dimensions but the last counted through in order) at most 2 rows name the same one
- perf_well: int32 [8, 1536], P('layer', ('gx', 'gy')), may hold values from 0 to 7
- perf_column: int32 [8, 1536], P('layer', ('gx', 'gy')), may hold values from 0 to 16383
- perf_index: float32 [8, 1536, 8], P('layer', ('gx', 'gy')), may hold values from 0.2 to 2
- well_rate: float32 [8, 256], P('layer', ('gx', 'gy')), may hold values from -8 to 8
Outputs:
- pressure_out: float32 [64, 512, 1024], P('layer', 'gx', 'gy')
- perf_flow: float32 [8, 1536, 8], P('layer', ('gx', 'gy'))
Inputs may be any that keep to these rules, and one draw needn't show every extreme that they name: `tile_count`: live slots of a tile are its first ones; some tile of every group has all 48 live. `perf_owner`: among the 48 slots of one tile at most 2 name one owner.
All inputs are finite; a program needn't handle non-finite values.
Results may differ from a plain program's by a relative error of at most 0.00018.
Values sent between devices are 32-bit elements; how exact they have to be, the bound alone decides.
No kernel may reach another device: no remote copies, remote signals or barrier semaphores. Data moves between devices by JAX's collectives and lax.ppermute only.
A program may use at most 64 MiB of HBM per device.

v0:
```python
import jax
import jax.numpy as jnp
from jax import lax
from jax.sharding import PartitionSpec as P

ITERS = 2


HIGHEST_PRECISION = lax.Precision.HIGHEST


def extended(value, sides, width):
    for axis, dim in sides:
        size, length = (lax.axis_size(axis), value.shape[dim])
        up = [(i, (i + 1) % size) for i in range(size - 1)]
        down = [(j, i) for i, j in up]
        last = lax.slice_in_dim(value, length - width, length, axis=dim)
        initial = lax.slice_in_dim(value, 0, width, axis=dim)
        before = lax.ppermute(last, axis, up)
        after = lax.ppermute(initial, axis, down)
        value = jnp.concatenate([before, value, after], axis=dim)
    return value


def passed_along(value, axis, steps):
    count = lax.axis_size(axis)
    initial, last = (max(0, -steps), min(count, count - steps))
    return lax.ppermute(value, axis, [(source, source + steps) for source in range(initial, last)])


def neighbours(padded_field, rock_x, rock_y, perm_x, perm_y):
    east_term = 0.5 * (perm_x + rock_x[:, 2:, 1:-1]) * padded_field[:, 2:, 1:-1]
    west_term = 0.5 * (perm_x + rock_x[:, :-2, 1:-1]) * padded_field[:, :-2, 1:-1]
    north_term = 0.5 * (perm_y + rock_y[:, 1:-1, 2:]) * padded_field[:, 1:-1, 2:]
    south_term = 0.5 * (perm_y + rock_y[:, 1:-1, :-2]) * padded_field[:, 1:-1, :-2]
    return east_term + west_term + (north_term + south_term)


def shards(
    pressure,
    source,
    perm_x,
    perm_y,
    line_inverse,
    robin_below,
    tile_count,
    perf_owner,
    perf_well,
    perf_column,
    perf_index,
    well_rate,
):
    layer_depth, width_x, width_y = pressure.shape
    columns = width_x * width_y
    tile_total = lax.axis_size(("gx", "gy"))
    slot_total = perf_well.shape[1]
    wells_own = well_rate.shape[1]
    capacity = max(2, (slot_total + tile_total - 1) // tile_total)
    rock_pair = jnp.stack([perm_x, perm_y])
    padded_rock = extended(rock_pair, (("gx", 2), ("gy", 3)), 1)
    rock_x = padded_rock[0]
    rock_y = padded_rock[1]
    inverse = line_inverse[0]
    live_slot = jnp.arange(slot_total) < tile_count[0, 0]
    owner_of = perf_owner[0, :, 0]
    owner_hits = (
        (owner_of[:, None] == jnp.arange(tile_total)[None, :]) & live_slot[:, None]
    ).astype(jnp.int32)
    earlier = (jnp.arange(slot_total)[None, :] < jnp.arange(slot_total)[:, None]).astype(jnp.int32)
    before = jnp.dot(earlier, owner_hits)
    slot_rank = jnp.sum(before * owner_hits, axis=1)
    target = owner_of * capacity + slot_rank
    placing = (jnp.arange(tile_total * capacity)[:, None] == target[None, :]) & live_slot[None, :]
    place_float = placing.astype(jnp.float32)
    slot_ids = jnp.sum(placing.astype(jnp.int32) * (perf_well[0] + 1)[None, :], axis=1).reshape(
        tile_total, capacity
    )
    ids_in = lax.all_to_all(
        slot_ids, ("gx", "gy"), split_axis=0, concat_axis=0, tiled=True
    ).reshape(tile_total * capacity)
    member = (ids_in[None, :] == jnp.arange(wells_own)[:, None] + 1).astype(jnp.float32)
    filled = (ids_in > 0).astype(jnp.float32)
    column = perf_column[0]
    index_slots = perf_index[0]
    field_now = pressure
    lower_data = robin_below[0]
    slot_flow = jnp.zeros((slot_total, layer_depth), jnp.float32)
    a_down = inverse[layer_depth - 1, 0]
    g_last = inverse[layer_depth - 1, layer_depth - 1]
    g_first = inverse[0, 0]
    a_up = inverse[0, layer_depth - 1]
    for sweep_step in range(ITERS):
        padded_field = extended(field_now, (("gx", 1), ("gy", 2)), 1)
        lateral = neighbours(padded_field, rock_x, rock_y, perm_x, perm_y)
        flat_field = field_now.reshape(layer_depth, columns)
        at_slots = jnp.take(flat_field, column, axis=1).T
        stacked = jnp.concatenate([at_slots, index_slots], axis=1)
        outgoing = jnp.dot(place_float, stacked, precision=HIGHEST_PRECISION).reshape(
            tile_total, capacity, 2 * layer_depth
        )
        both_in = lax.all_to_all(
            outgoing, ("gx", "gy"), split_axis=0, concat_axis=0, tiled=True
        ).reshape(tile_total * capacity, 2 * layer_depth)
        received = both_in[:, :layer_depth]
        index_here = both_in[:, layer_depth:]
        index_sum = jnp.dot(member, jnp.sum(index_here, axis=1), precision=HIGHEST_PRECISION)
        weighted_sum = jnp.dot(
            member, jnp.sum(index_here * received, axis=1), precision=HIGHEST_PRECISION
        )
        bottom_hole = (well_rate[0] + weighted_sum) / (index_sum + 1.0)
        hole_slots = jnp.dot(bottom_hole, member, precision=HIGHEST_PRECISION)
        flow_out = index_here * (hole_slots[:, None] - received) * filled[:, None]
        returned = lax.all_to_all(
            flow_out.reshape(tile_total, capacity, layer_depth),
            ("gx", "gy"),
            split_axis=0,
            concat_axis=0,
            tiled=True,
        ).reshape(tile_total * capacity, layer_depth)
        well_slot_flow = jnp.dot(place_float.T, returned, precision=HIGHEST_PRECISION)
        well_term = (
            jnp.zeros((layer_depth, columns), jnp.float32)
            .at[:, column]
            .add(well_slot_flow.T)
            .reshape(layer_depth, width_x, width_y)
        )
        well_term, slot_flow = (well_term, well_slot_flow)
        rhs = source + lateral + well_term
        solved = jnp.einsum("ijxy,jxy->ixy", inverse, rhs, precision=HIGHEST_PRECISION)
        c_down = solved[layer_depth - 1] + g_last * lower_data - lower_data
        upper_trace = jnp.zeros_like(lower_data)
        for link_step in range(lax.axis_size("layer") - 1):
            upper_trace = passed_along(a_down * upper_trace + c_down, "layer", 1)
        c_up = solved[0] + g_first * upper_trace - upper_trace
        lower_trace = jnp.zeros_like(lower_data)
        for link_step in range(lax.axis_size("layer") - 1):
            lower_trace = passed_along(a_up * lower_trace + c_up, "layer", -1)
        lower_data = lower_trace
        field_now = (
            solved
            + inverse[:, 0] * upper_trace[None]
            + inverse[:, layer_depth - 1] * lower_trace[None]
        )
    return (field_now, slot_flow[None])


def solution(mesh):
    placed = (
        P("layer", "gx", "gy"),
        P("layer", "gx", "gy"),
        P("layer", "gx", "gy"),
        P("layer", "gx", "gy"),
        P("layer", None, None, "gx", "gy"),
        P("layer", "gx", "gy"),
        P("layer", ("gx", "gy")),
        P("layer", ("gx", "gy"), None),
        P("layer", ("gx", "gy")),
        P("layer", ("gx", "gy")),
        P("layer", ("gx", "gy"), None),
        P("layer", ("gx", "gy")),
    )
    return jax.shard_map(
        shards,
        mesh=mesh,
        in_specs=placed,
        out_specs=(P("layer", "gx", "gy"), P("layer", ("gx", "gy"), None)),
        check_vma=False,
    )
```

profile of v0, /device:TPU:1, one launch (start us, length us, event | category | flops | bytes accessed | tf_op | source)
XLA Modules:
  0.0 319.8 jit_solution(12960480875023234168)
XLA Ops:
  4.4 12.0 %all-to-all-start.1 = ((s32[32,1,2]{2,1,0:T(1,128)}), s32[32,1,2]{2,1,0:T(1,128)S(1)}, u32[]{:S(2)}, u32[]{:S(2)}) async-start(s32[32,1,2]{2,1,0:T(1,128)} %bitcast.21), calls=%async_computation.1 | async-start | bytes 32768 | tf_op jit(solution)/shard_map/all_to_all | solution.py:78
  17.8 3.1 collective-permute-start.5
  25.4 4.7 %collective-permute-start = (f32[2,8,1,256]{3,1,2,0:T(8,128)S(1)}, f32[2,8,1,256]{3,1,2,0:T(8,128)S(1)}, u32[]{:S(2)}, u32[]{:S(2)}) collective-permute-start(f32[2,8,1,256]{3,1,2,0:T(8,128)S(1)} %get-tuple-element.27), channel_id=1, source_target_pairs={{0,4},{4,8},{8,12},{12,16},{16,20},{20,24},{24,28},{1,5},{5,9},{9,... | collective-permute-start | bytes 49160 | tf_op jit(solution)/shard_map/ppermute | solution.py:19
  30.2 4.6 %copy.110 = f32[8,64,256]{0,2,1:T(8,128)} copy(f32[8,64,256]{2,1,0:T(8,128)S(1)} %copy-done.2) | data formatting | bytes 1048576 | tf_op args[0]
  34.9 4.0 %gather_fusion = f32[48,8]{1,0:T(8,128)S(1)} fusion(f32[8,16384]{0,1:T(8,128)} %bitcast.273, s32[1024]{0:T(1024)S(1)} %pad_clamp_fusion), kind=kCustom, calls=%fused_computation.clone | custom fusion | bytes 3264 | tf_op jit(solution)/shard_map/jit(_take)/gather | solution.py:96
  39.9 10.7 %all-to-all-start = ((f32[32,2,16]{2,1,0:T(2,128)}), f32[32,2,16]{2,1,0:T(2,128)S(1)}, u32[]{:S(2)}, u32[]{:S(2)}) async-start(f32[32,2,16]{2,1,0:T(2,128)} %bitcast.17), calls=%async_computation | async-start | bytes 65536 | tf_op jit(solution)/shard_map/all_to_all | solution.py:101
  51.9 7.4 %all-to-all-done = f32[32,2,16]{2,1,0:T(2,128)S(1)} async-done(((f32[32,2,16]{2,1,0:T(2,128)}), f32[32,2,16]{2,1,0:T(2,128)S(1)}, u32[]{:S(2)}, u32[]{:S(2)}) %all-to-all-start) | async-done | bytes 4128 | tf_op jit(solution)/shard_map/all_to_all | solution.py:101
  60.8 3.9 %all-to-all-start.2 = ((f32[32,2,8]{2,1,0:T(2,128)}), f32[32,2,8]{2,1,0:T(2,128)S(1)}, u32[]{:S(2)}, u32[]{:S(2)}) async-start(f32[32,2,8]{2,1,0:T(2,128)} %bitcast.28), calls=%async_computation.2 | async-start | bytes 65536 | tf_op jit(solution)/shard_map/all_to_all | solution.py:113
  72.4 4.6 %collective-permute-start.2 = (f32[2,8,66,1]{2,1,3,0:T(8,128)S(1)}, f32[2,8,66,1]{2,1,3,0:T(8,128)S(1)}, u32[]{:S(2)}, u32[]{:S(2)}) collective-permute-start(f32[2,8,66,1]{2,1,3,0:T(8,128)S(1)} %copy.96), channel_id=1, source_target_pairs={{0,1},{1,2},{2,3},{4,5},{5,6},{6,7},{8,9},{9,10},{10,11},{12,13},{... | collective-permute-start | bytes 12680 | tf_op jit(solution)/shard_map/ppermute | solution.py:19
  77.2 4.5 %scatter_custom_fusion = f32[8,16384]{0,1:T(8,128)} fusion(s32[48]{0:T(128)S(1)} %fusion.92, f32[48,8]{1,0:T(8,128)S(1)} %fusion.53, f32[]{:T(128)} %constant.16.clone.1), kind=kCustom, calls=%fused_computation.10 | custom fusion | flops 384 | bytes 524292 | tf_op jit(solution)/shard_map/scatter-add | solution.py:124
  81.8 5.9 %copy.115 = f32[8,64,256]{2,0,1:T(8,128)} copy(f32[8,64,256]{0,2,1:T(8,128)} %bitcast.243) | data formatting | bytes 1048576 | tf_op jit(solution)/shard_map/reshape | solution.py:125
  94.6 7.9 %collective-permute-start.8 = (f32[64,256]{1,0:T(8,128)S(1)}, f32[64,256]{1,0:T(8,128)S(1)}, u32[]{:S(2)}, u32[]{:S(2)}) collective-permute-start(f32[64,256]{1,0:T(8,128)S(1)} %get-tuple-element.19), channel_id=1, source_target_pairs={{0,32},{32,64},{64,96},{96,128},{128,160},{160,192},{192,224},{1,3... | collective-permute-start | bytes 196616 | tf_op jit(solution)/shard_map/ppermute | solution.py:28
  103.8 4.3 %collective-permute-start.9 = (f32[64,256]{1,0:T(8,128)S(1)}, f32[64,256]{1,0:T(8,128)S(1)}, u32[]{:S(2)}, u32[]{:S(2)}) collective-permute-start(f32[64,256]{1,0:T(8,128)S(1)} %multiply_add_fusion.23), channel_id=1, source_target_pairs={{0,32},{32,64},{64,96},{96,128},{128,160},{160,192},{192,224},{1,3... | collective-permute-start | bytes 196616 | tf_op jit(solution)/shard_map/ppermute | solution.py:28
  109.4 4.3 %collective-permute-start.10 = (f32[64,256]{1,0:T(8,128)S(1)}, f32[64,256]{1,0:T(8,128)S(1)}, u32[]{:S(2)}, u32[]{:S(2)}) collective-permute-start(f32[64,256]{1,0:T(8,128)S(1)} %multiply_add_fusion.22), channel_id=1, source_target_pairs={{0,32},{32,64},{64,96},{96,128},{128,160},{160,192},{192,224},{1,3... | collective-permute-start | bytes 196616 | tf_op jit(solution)/shard_map/ppermute | solution.py:28
  115.0 4.3 %collective-permute-start.11 = (f32[64,256]{1,0:T(8,128)S(1)}, f32[64,256]{1,0:T(8,128)S(1)}, u32[]{:S(2)}, u32[]{:S(2)}) collective-permute-start(f32[64,256]{1,0:T(8,128)S(1)} %multiply_add_fusion.21), channel_id=1, source_target_pairs={{0,32},{32,64},{64,96},{96,128},{128,160},{160,192},{192,224},{1,3... | collective-permute-start | bytes 196616 | tf_op jit(solution)/shard_map/ppermute | solution.py:28
  120.6 4.3 %collective-permute-start.12 = (f32[64,256]{1,0:T(8,128)S(1)}, f32[64,256]{1,0:T(8,128)S(1)}, u32[]{:S(2)}, u32[]{:S(2)}) collective-permute-start(f32[64,256]{1,0:T(8,128)S(1)} %multiply_add_fusion.20), channel_id=1, source_target_pairs={{0,32},{32,64},{64,96},{96,128},{128,160},{160,192},{192,224},{1,3... | collective-permute-start | bytes 196616 | tf_op jit(solution)/shard_map/ppermute | solution.py:28
  126.2 4.3 %collective-permute-start.13 = (f32[64,256]{1,0:T(8,128)S(1)}, f32[64,256]{1,0:T(8,128)S(1)}, u32[]{:S(2)}, u32[]{:S(2)}) collective-permute-start(f32[64,256]{1,0:T(8,128)S(1)} %multiply_add_fusion.19), channel_id=1, source_target_pairs={{0,32},{32,64},{64,96},{96,128},{128,160},{160,192},{192,224},{1,3... | collective-permute-start | bytes 196616 | tf_op jit(solution)/shard_map/ppermute | solution.py:28
  131.8 4.3 %collective-permute-start.14 = (f32[64,256]{1,0:T(8,128)S(1)}, f32[64,256]{1,0:T(8,128)S(1)}, u32[]{:S(2)}, u32[]{:S(2)}) collective-permute-start(f32[64,256]{1,0:T(8,128)S(1)} %multiply_add_fusion.18), channel_id=1, source_target_pairs={{0,32},{32,64},{64,96},{96,128},{128,160},{160,192},{192,224},{1,3... | collective-permute-start | bytes 196616 | tf_op jit(solution)/shard_map/ppermute | solution.py:28
  139.4 4.3 %collective-permute-done.15 = f32[64,256]{1,0:T(8,128)S(1)} collective-permute-done((f32[64,256]{1,0:T(8,128)S(1)}, f32[64,256]{1,0:T(8,128)S(1)}, u32[]{:S(2)}, u32[]{:S(2)}) %collective-permute-start.15) | collective-permute-done | bytes 65568 | tf_op jit(solution)/shard_map/ppermute | solution.py:28
  145.6 3.7 %collective-permute-done.16 = f32[64,256]{1,0:T(8,128)S(1)} collective-permute-done((f32[64,256]{1,0:T(8,128)S(1)}, f32[64,256]{1,0:T(8,128)S(1)}, u32[]{:S(2)}, u32[]{:S(2)}) %collective-permute-start.16) | collective-permute-done | bytes 65568 | tf_op jit(solution)/shard_map/ppermute | solution.py:28
  151.2 3.7 %collective-permute-done.17 = f32[64,256]{1,0:T(8,128)S(1)} collective-permute-done((f32[64,256]{1,0:T(8,128)S(1)}, f32[64,256]{1,0:T(8,128)S(1)}, u32[]{:S(2)}, u32[]{:S(2)}) %collective-permute-start.17) | collective-permute-done | bytes 65568 | tf_op jit(solution)/shard_map/ppermute | solution.py:28
  156.8 3.7 %collective-permute-done.18 = f32[64,256]{1,0:T(8,128)S(1)} collective-permute-done((f32[64,256]{1,0:T(8,128)S(1)}, f32[64,256]{1,0:T(8,128)S(1)}, u32[]{:S(2)}, u32[]{:S(2)}) %collective-permute-start.18) | collective-permute-done | bytes 65568 | tf_op jit(solution)/shard_map/ppermute | solution.py:28
  162.4 3.7 %collective-permute-done.19 = f32[64,256]{1,0:T(8,128)S(1)} collective-permute-done((f32[64,256]{1,0:T(8,128)S(1)}, f32[64,256]{1,0:T(8,128)S(1)}, u32[]{:S(2)}, u32[]{:S(2)}) %collective-permute-start.19) | collective-permute-done | bytes 65568 | tf_op jit(solution)/shard_map/ppermute | solution.py:28
  168.0 3.7 %collective-permute-done.20 = f32[64,256]{1,0:T(8,128)S(1)} collective-permute-done((f32[64,256]{1,0:T(8,128)S(1)}, f32[64,256]{1,0:T(8,128)S(1)}, u32[]{:S(2)}, u32[]{:S(2)}) %collective-permute-start.20) | collective-permute-done | bytes 65568 | tf_op jit(solution)/shard_map/ppermute | solution.py:28
  173.9 3.4 %collective-permute-done.21 = f32[64,256]{1,0:T(8,128)S(1)} collective-permute-done((f32[64,256]{1,0:T(8,128)S(1)}, f32[64,256]{1,0:T(8,128)S(1)}, u32[]{:S(2)}, u32[]{:S(2)}) %collective-permute-start.21) | collective-permute-done | bytes 65568 | tf_op jit(solution)/shard_map/ppermute | solution.py:28
  178.2 4.8 %copy.120 = f32[8,64,256]{0,2,1:T(8,128)} copy(f32[8,64,256]{2,0,1:T(8,128)S(1)} %fusion.39) | data formatting | bytes 1048576 | tf_op jit(solution)/shard_map/add | solution.py:140
  183.0 4.0 %gather_fusion.1 = f32[48,8]{1,0:T(8,128)S(1)} fusion(f32[8,16384]{0,1:T(8,128)} %bitcast.274, s32[1024]{0:T(1024)S(1)} %pad_clamp_fusion), kind=kCustom, calls=%fused_computation.1.clone | custom fusion | bytes 3264 | tf_op jit(solution)/shard_map/jit(_take)/gather | solution.py:96
  188.1 9.8 %all-to-all-start.3 = ((f32[32,2,16]{2,1,0:T(2,128)}), f32[32,2,16]{2,1,0:T(2,128)S(1)}, u32[]{:S(2)}, u32[]{:S(2)}) async-start(f32[32,2,16]{2,1,0:T(2,128)} %bitcast.46), calls=%async_computation.3 | async-start | bytes 65536 | tf_op jit(solution)/shard_map/all_to_all | solution.py:101
  199.2 4.0 %collective-permute-start.23 = (f32[8,1,256]{2,0,1:T(8,128)S(1)}, f32[8,1,256]{2,0,1:T(8,128)S(1)}, u32[]{:S(2)}, u32[]{:S(2)}) collective-permute-start(f32[8,1,256]{2,0,1:T(8,128)S(1)} %get-tuple-element.33), channel_id=1, source_target_pairs={{0,4},{4,8},{8,12},{12,16},{16,20},{20,24},{24,28},{1,5},{5,9},{9,... | collective-permute-start | bytes 24584 | tf_op jit(solution)/shard_map/ppermute | solution.py:19
  203.2 3.4 %all-to-all-done.3 = f32[32,2,16]{2,1,0:T(2,128)S(1)} async-done(((f32[32,2,16]{2,1,0:T(2,128)}), f32[32,2,16]{2,1,0:T(2,128)S(1)}, u32[]{:S(2)}, u32[]{:S(2)}) %all-to-all-start.3) | async-done | bytes 4128 | tf_op jit(solution)/shard_map/all_to_all | solution.py:101
  208.1 6.0 %all-to-all-start.4 = ((f32[32,2,8]{2,1,0:T(2,128)}), f32[32,2,8]{2,1,0:T(2,128)}, u32[]{:S(2)}, u32[]{:S(2)}) async-start(f32[32,2,8]{2,1,0:T(2,128)} %bitcast.54), calls=%async_computation.4 | async-start | bytes 65536 | tf_op jit(solution)/shard_map/all_to_all | solution.py:113
  219.4 3.3 %all-to-all-done.4 = f32[32,2,8]{2,1,0:T(2,128)} async-done(((f32[32,2,8]{2,1,0:T(2,128)}), f32[32,2,8]{2,1,0:T(2,128)}, u32[]{:S(2)}, u32[]{:S(2)}) %all-to-all-start.4) | async-done | bytes 2080 | tf_op jit(solution)/shard_map/all_to_all | solution.py:113
  224.3 4.8 %scatter_custom_fusion.1 = f32[8,16384]{0,1:T(8,128)} fusion(s32[48]{0:T(128)} %copy-done.19, f32[48,8]{1,0:T(8,128)} %copy.123, f32[]{:T(128)} %constant.16.clone.1), kind=kCustom, calls=%fused_computation.8 | custom fusion | flops 384 | bytes 524800 | tf_op jit(solution)/shard_map/scatter-add | solution.py:124
  229.1 5.9 %copy.124 = f32[8,64,256]{2,0,1:T(8,128)} copy(f32[8,64,256]{0,2,1:T(8,128)} %bitcast.242) | data formatting | bytes 1048576 | tf_op jit(solution)/shard_map/reshape | solution.py:125
  238.7 4.4 %collective-permute-start.26 = (f32[64,256]{1,0:T(8,128)S(1)}, f32[64,256]{1,0:T(8,128)S(1)}, u32[]{:S(2)}, u32[]{:S(2)}) collective-permute-start(f32[64,256]{1,0:T(8,128)S(1)} %get-tuple-element.15), channel_id=1, source_target_pairs={{0,32},{32,64},{64,96},{96,128},{128,160},{160,192},{192,224},{1,3... | collective-permute-start | bytes 196616 | tf_op jit(solution)/shard_map/ppermute | solution.py:28
  244.5 4.3 %collective-permute-start.27 = (f32[64,256]{1,0:T(8,128)S(1)}, f32[64,256]{1,0:T(8,128)S(1)}, u32[]{:S(2)}, u32[]{:S(2)}) collective-permute-start(f32[64,256]{1,0:T(8,128)S(1)} %multiply_add_fusion.11), channel_id=1, source_target_pairs={{0,32},{32,64},{64,96},{96,128},{128,160},{160,192},{192,224},{1,3... | collective-permute-start | bytes 196616 | tf_op jit(solution)/shard_map/ppermute | solution.py:28
  250.1 4.3 %collective-permute-start.28 = (f32[64,256]{1,0:T(8,128)S(1)}, f32[64,256]{1,0:T(8,128)S(1)}, u32[]{:S(2)}, u32[]{:S(2)}) collective-permute-start(f32[64,256]{1,0:T(8,128)S(1)} %multiply_add_fusion.10), channel_id=1, source_target_pairs={{0,32},{32,64},{64,96},{96,128},{128,160},{160,192},{192,224},{1,3... | collective-permute-start | bytes 196616 | tf_op jit(solution)/shard_map/ppermute | solution.py:28
  255.7 4.3 %collective-permute-start.29 = (f32[64,256]{1,0:T(8,128)S(1)}, f32[64,256]{1,0:T(8,128)S(1)}, u32[]{:S(2)}, u32[]{:S(2)}) collective-permute-start(f32[64,256]{1,0:T(8,128)S(1)} %multiply_add_fusion.9), channel_id=1, source_target_pairs={{0,32},{32,64},{64,96},{96,128},{128,160},{160,192},{192,224},{1,3... | collective-permute-start | bytes 196616 | tf_op jit(solution)/shard_map/ppermute | solution.py:28
  261.3 4.3 %collective-permute-start.30 = (f32[64,256]{1,0:T(8,128)S(1)}, f32[64,256]{1,0:T(8,128)S(1)}, u32[]{:S(2)}, u32[]{:S(2)}) collective-permute-start(f32[64,256]{1,0:T(8,128)S(1)} %multiply_add_fusion.8), channel_id=1, source_target_pairs={{0,32},{32,64},{64,96},{96,128},{128,160},{160,192},{192,224},{1,3... | collective-permute-start | bytes 196616 | tf_op jit(solution)/shard_map/ppermute | solution.py:28
  266.9 4.3 %collective-permute-start.31 = (f32[64,256]{1,0:T(8,128)S(1)}, f32[64,256]{1,0:T(8,128)S(1)}, u32[]{:S(2)}, u32[]{:S(2)}) collective-permute-start(f32[64,256]{1,0:T(8,128)S(1)} %multiply_add_fusion.7), channel_id=1, source_target_pairs={{0,32},{32,64},{64,96},{96,128},{128,160},{160,192},{192,224},{1,3... | collective-permute-start | bytes 196616 | tf_op jit(solution)/shard_map/ppermute | solution.py:28
  272.5 4.3 %collective-permute-start.32 = (f32[64,256]{1,0:T(8,128)S(1)}, f32[64,256]{1,0:T(8,128)S(1)}, u32[]{:S(2)}, u32[]{:S(2)}) collective-permute-start(f32[64,256]{1,0:T(8,128)S(1)} %multiply_add_fusion.6), channel_id=1, source_target_pairs={{0,32},{32,64},{64,96},{96,128},{128,160},{160,192},{192,224},{1,3... | collective-permute-start | bytes 196616 | tf_op jit(solution)/shard_map/ppermute | solution.py:28
  280.0 4.3 %collective-permute-done.33 = f32[64,256]{1,0:T(8,128)S(1)} collective-permute-done((f32[64,256]{1,0:T(8,128)S(1)}, f32[64,256]{1,0:T(8,128)S(1)}, u32[]{:S(2)}, u32[]{:S(2)}) %collective-permute-start.33) | collective-permute-done | bytes 65568 | tf_op jit(solution)/shard_map/ppermute | solution.py:28
  286.3 3.7 %collective-permute-done.34 = f32[64,256]{1,0:T(8,128)S(1)} collective-permute-done((f32[64,256]{1,0:T(8,128)S(1)}, f32[64,256]{1,0:T(8,128)S(1)}, u32[]{:S(2)}, u32[]{:S(2)}) %collective-permute-start.34) | collective-permute-done | bytes 65568 | tf_op jit(solution)/shard_map/ppermute | solution.py:28
  291.9 3.7 %collective-permute-done.35 = f32[64,256]{1,0:T(8,128)S(1)} collective-permute-done((f32[64,256]{1,0:T(8,128)S(1)}, f32[64,256]{1,0:T(8,128)S(1)}, u32[]{:S(2)}, u32[]{:S(2)}) %collective-permute-start.35) | collective-permute-done | bytes 65568 | tf_op jit(solution)/shard_map/ppermute | solution.py:28
  297.5 3.7 %collective-permute-done.36 = f32[64,256]{1,0:T(8,128)S(1)} collective-permute-done((f32[64,256]{1,0:T(8,128)S(1)}, f32[64,256]{1,0:T(8,128)S(1)}, u32[]{:S(2)}, u32[]{:S(2)}) %collective-permute-start.36) | collective-permute-done | bytes 65568 | tf_op jit(solution)/shard_map/ppermute | solution.py:28
  303.1 3.7 %collective-permute-done.37 = f32[64,256]{1,0:T(8,128)S(1)} collective-permute-done((f32[64,256]{1,0:T(8,128)S(1)}, f32[64,256]{1,0:T(8,128)S(1)}, u32[]{:S(2)}, u32[]{:S(2)}) %collective-permute-start.37) | collective-permute-done | bytes 65568 | tf_op jit(solution)/shard_map/ppermute | solution.py:28
  308.7 3.7 %collective-permute-done.38 = f32[64,256]{1,0:T(8,128)S(1)} collective-permute-done((f32[64,256]{1,0:T(8,128)S(1)}, f32[64,256]{1,0:T(8,128)S(1)}, u32[]{:S(2)}, u32[]{:S(2)}) %collective-permute-start.38) | collective-permute-done | bytes 65568 | tf_op jit(solution)/shard_map/ppermute | solution.py:28
  314.3 3.7 %collective-permute-done.39 = f32[64,256]{1,0:T(8,128)S(1)} collective-permute-done((f32[64,256]{1,0:T(8,128)S(1)}, f32[64,256]{1,0:T(8,128)S(1)}, u32[]{:S(2)}, u32[]{:S(2)}) %collective-permute-start.39) | collective-permute-done | bytes 65568 | tf_op jit(solution)/shard_map/ppermute | solution.py:28
  (187 shorter events, 90.5 us)
Async XLA Ops:
  1.4 75.6 %copy-start.10 = (pred[48]{0:T(512)(128)(4,1)}, pred[48]{0:T(512)(128)(4,1)S(1)}, u32[]{:S(2)}) copy-start(pred[48]{0:T(512)(128)(4,1)S(1)} %iota_compare_fusion.4) | copy-start | bytes 148
  2.9 74.1 %copy-start.12 = (s32[48]{0:T(128)}, s32[48]{0:T(128)S(1)}, u32[]{:S(2)}) copy-start(s32[48]{0:T(128)S(1)} %multiply_add_fusion.28) | copy-start | bytes 580
  4.4 35.5 %all-to-all-start.1 = ((s32[32,1,2]{2,1,0:T(1,128)}), s32[32,1,2]{2,1,0:T(1,128)S(1)}, u32[]{:S(2)}, u32[]{:S(2)}) async-start(s32[32,1,2]{2,1,0:T(1,128)} %bitcast.21), calls=%async_computation.1 | async-start | bytes 32768 | tf_op jit(solution)/shard_map/all_to_all | solution.py:78
  17.8 46.8 %collective-permute-start.5 = (f32[8,1,256]{2,0,1:T(8,128)S(1)}, f32[8,1,256]{2,0,1:T(8,128)S(1)}, u32[]{:S(2)}, u32[]{:S(2)}) collective-permute-start(f32[8,1,256]{2,0,1:T(8,128)S(1)} %get-tuple-element.36), channel_id=1, source_target_pairs={{0,4},{4,8},{8,12},{12,16},{16,20},{20,24},{24,28},{1,5},{5,9},{9,... | collective-permute-start | bytes 24584 | tf_op jit(solution)/shard_map/ppermute | solution.py:19
  21.0 44.0 %collective-permute-start.4 = (f32[8,1,256]{2,0,1:T(8,128)S(1)}, f32[8,1,256]{2,0,1:T(8,128)S(1)}, u32[]{:S(2)}, u32[]{:S(2)}) collective-permute-start(f32[8,1,256]{2,0,1:T(8,128)S(1)} %get-tuple-element.35), channel_id=1, source_target_pairs={{4,0},{8,4},{12,8},{16,12},{20,16},{24,20},{28,24},{5,1},{9,5},{13... | collective-permute-start | bytes 24584 | tf_op jit(solution)/shard_map/ppermute | solution.py:20
  24.1 46.1 %collective-permute-start.1 = (f32[2,8,1,256]{3,1,2,0:T(8,128)S(1)}, f32[2,8,1,256]{3,1,2,0:T(8,128)S(1)}, u32[]{:S(2)}, u32[]{:S(2)}) collective-permute-start(f32[2,8,1,256]{3,1,2,0:T(8,128)S(1)} %get-tuple-element.28), channel_id=1, source_target_pairs={{4,0},{8,4},{12,8},{16,12},{20,16},{24,20},{28,24},{5,1},{9,5},{13... | collective-permute-start | bytes 49160 | tf_op jit(solution)/shard_map/ppermute | solution.py:20
  25.4 44.8 %collective-permute-start = (f32[2,8,1,256]{3,1,2,0:T(8,128)S(1)}, f32[2,8,1,256]{3,1,2,0:T(8,128)S(1)}, u32[]{:S(2)}, u32[]{:S(2)}) collective-permute-start(f32[2,8,1,256]{3,1,2,0:T(8,128)S(1)} %get-tuple-element.27), channel_id=1, source_target_pairs={{0,4},{4,8},{8,12},{12,16},{16,20},{20,24},{24,28},{1,5},{5,9},{9,... | collective-permute-start | bytes 49160 | tf_op jit(solution)/shard_map/ppermute | solution.py:19
  34.8 42.4 %copy-start.19 = (s32[48]{0:T(128)}, s32[48]{0:T(128)S(1)}, u32[]{:S(2)}) copy-start(s32[48]{0:T(128)S(1)} %fusion.92) | copy-start | bytes 580
  39.9 19.4 %all-to-all-start = ((f32[32,2,16]{2,1,0:T(2,128)}), f32[32,2,16]{2,1,0:T(2,128)S(1)}, u32[]{:S(2)}, u32[]{:S(2)}) async-start(f32[32,2,16]{2,1,0:T(2,128)} %bitcast.17), calls=%async_computation | async-start | bytes 65536 | tf_op jit(solution)/shard_map/all_to_all | solution.py:101
  60.8 16.2 %all-to-all-start.2 = ((f32[32,2,8]{2,1,0:T(2,128)}), f32[32,2,8]{2,1,0:T(2,128)S(1)}, u32[]{:S(2)}, u32[]{:S(2)}) async-start(f32[32,2,8]{2,1,0:T(2,128)} %bitcast.28), calls=%async_computation.2 | async-start | bytes 65536 | tf_op jit(solution)/shard_map/all_to_all | solution.py:113
  65.8 25.1 %collective-permute-start.7 = (f32[8,66,1]{2,0,1:T(8,128)}, f32[8,66,1]{2,0,1:T(8,128)S(1)}, u32[]{:S(2)}, u32[]{:S(2)}) collective-permute-start(f32[8,66,1]{2,0,1:T(8,128)} %get-tuple-element.32), channel_id=1, source_target_pairs={{0,1},{1,2},{2,3},{4,5},{5,6},{6,7},{8,9},{9,10},{10,11},{12,13},{... | collective-permute-start | bytes 6344 | tf_op jit(solution)/shard_map/ppermute | solution.py:19
  68.9 22.1 %collective-permute-start.6 = (f32[8,66,1]{2,0,1:T(8,128)}, f32[8,66,1]{2,0,1:T(8,128)}, u32[]{:S(2)}, u32[]{:S(2)}) collective-permute-start(f32[8,66,1]{2,0,1:T(8,128)} %get-tuple-element.31), channel_id=1, source_target_pairs={{1,0},{2,1},{3,2},{5,4},{6,5},{7,6},{9,8},{10,9},{11,10},{13,12},{... | collective-permute-start | bytes 6344 | tf_op jit(solution)/shard_map/ppermute | solution.py:20
  70.8 16.9 %collective-permute-start.3 = (f32[2,8,66,1]{2,1,3,0:T(8,128)S(1)}, f32[2,8,66,1]{2,1,3,0:T(8,128)S(1)}, u32[]{:S(2)}, u32[]{:S(2)}) collective-permute-start(f32[2,8,66,1]{2,1,3,0:T(8,128)S(1)} %copy.97), channel_id=1, source_target_pairs={{1,0},{2,1},{3,2},{5,4},{6,5},{7,6},{9,8},{10,9},{11,10},{13,12},{... | collective-permute-start | bytes 12680 | tf_op jit(solution)/shard_map/ppermute | solution.py:20
  72.4 15.6 %collective-permute-start.2 = (f32[2,8,66,1]{2,1,3,0:T(8,128)S(1)}, f32[2,8,66,1]{2,1,3,0:T(8,128)S(1)}, u32[]{:S(2)}, u32[]{:S(2)}) collective-permute-start(f32[2,8,66,1]{2,1,3,0:T(8,128)S(1)} %copy.96), channel_id=1, source_target_pairs={{0,1},{1,2},{2,3},{4,5},{5,6},{6,7},{8,9},{9,10},{10,11},{12,13},{... | collective-permute-start | bytes 12680 | tf_op jit(solution)/shard_map/ppermute | solution.py:19
  94.6 9.2 %collective-permute-start.8 = (f32[64,256]{1,0:T(8,128)S(1)}, f32[64,256]{1,0:T(8,128)S(1)}, u32[]{:S(2)}, u32[]{:S(2)}) collective-permute-start(f32[64,256]{1,0:T(8,128)S(1)} %get-tuple-element.19), channel_id=1, source_target_pairs={{0,32},{32,64},{64,96},{96,128},{128,160},{160,192},{192,224},{1,3... | collective-permute-start | bytes 196616 | tf_op jit(solution)/shard_map/ppermute | solution.py:28
  103.8 5.6 %collective-permute-start.9 = (f32[64,256]{1,0:T(8,128)S(1)}, f32[64,256]{1,0:T(8,128)S(1)}, u32[]{:S(2)}, u32[]{:S(2)}) collective-permute-start(f32[64,256]{1,0:T(8,128)S(1)} %multiply_add_fusion.23), channel_id=1, source_target_pairs={{0,32},{32,64},{64,96},{96,128},{128,160},{160,192},{192,224},{1,3... | collective-permute-start | bytes 196616 | tf_op jit(solution)/shard_map/ppermute | solution.py:28
  109.4 5.6 %collective-permute-start.10 = (f32[64,256]{1,0:T(8,128)S(1)}, f32[64,256]{1,0:T(8,128)S(1)}, u32[]{:S(2)}, u32[]{:S(2)}) collective-permute-start(f32[64,256]{1,0:T(8,128)S(1)} %multiply_add_fusion.22), channel_id=1, source_target_pairs={{0,32},{32,64},{64,96},{96,128},{128,160},{160,192},{192,224},{1,3... | collective-permute-start | bytes 196616 | tf_op jit(solution)/shard_map/ppermute | solution.py:28
  115.0 5.6 %collective-permute-start.11 = (f32[64,256]{1,0:T(8,128)S(1)}, f32[64,256]{1,0:T(8,128)S(1)}, u32[]{:S(2)}, u32[]{:S(2)}) collective-permute-start(f32[64,256]{1,0:T(8,128)S(1)} %multiply_add_fusion.21), channel_id=1, source_target_pairs={{0,32},{32,64},{64,96},{96,128},{128,160},{160,192},{192,224},{1,3... | collective-permute-start | bytes 196616 | tf_op jit(solution)/shard_map/ppermute | solution.py:28
  120.6 5.6 %collective-permute-start.12 = (f32[64,256]{1,0:T(8,128)S(1)}, f32[64,256]{1,0:T(8,128)S(1)}, u32[]{:S(2)}, u32[]{:S(2)}) collective-permute-start(f32[64,256]{1,0:T(8,128)S(1)} %multiply_add_fusion.20), channel_id=1, source_target_pairs={{0,32},{32,64},{64,96},{96,128},{128,160},{160,192},{192,224},{1,3... | collective-permute-start | bytes 196616 | tf_op jit(solution)/shard_map/ppermute | solution.py:28
  126.2 5.6 %collective-permute-start.13 = (f32[64,256]{1,0:T(8,128)S(1)}, f32[64,256]{1,0:T(8,128)S(1)}, u32[]{:S(2)}, u32[]{:S(2)}) collective-permute-start(f32[64,256]{1,0:T(8,128)S(1)} %multiply_add_fusion.19), channel_id=1, source_target_pairs={{0,32},{32,64},{64,96},{96,128},{128,160},{160,192},{192,224},{1,3... | collective-permute-start | bytes 196616 | tf_op jit(solution)/shard_map/ppermute | solution.py:28
  131.8 5.6 %collective-permute-start.14 = (f32[64,256]{1,0:T(8,128)S(1)}, f32[64,256]{1,0:T(8,128)S(1)}, u32[]{:S(2)}, u32[]{:S(2)}) collective-permute-start(f32[64,256]{1,0:T(8,128)S(1)} %multiply_add_fusion.18), channel_id=1, source_target_pairs={{0,32},{32,64},{64,96},{96,128},{128,160},{160,192},{192,224},{1,3... | collective-permute-start | bytes 196616 | tf_op jit(solution)/shard_map/ppermute | solution.py:28
  137.5 6.2 %collective-permute-start.15 = (f32[64,256]{1,0:T(8,128)S(1)}, f32[64,256]{1,0:T(8,128)S(1)}, u32[]{:S(2)}, u32[]{:S(2)}) collective-permute-start(f32[64,256]{1,0:T(8,128)S(1)} %get-tuple-element.17), channel_id=1, source_target_pairs={{32,0},{64,32},{96,64},{128,96},{160,128},{192,160},{224,192},{33,... | collective-permute-start | bytes 196616 | tf_op jit(solution)/shard_map/ppermute | solution.py:28
  143.7 5.6 %collective-permute-start.16 = (f32[64,256]{1,0:T(8,128)S(1)}, f32[64,256]{1,0:T(8,128)S(1)}, u32[]{:S(2)}, u32[]{:S(2)}) collective-permute-start(f32[64,256]{1,0:T(8,128)S(1)} %multiply_add_fusion.17), channel_id=1, source_target_pairs={{32,0},{64,32},{96,64},{128,96},{160,128},{192,160},{224,192},{33,... | collective-permute-start | bytes 196616 | tf_op jit(solution)/shard_map/ppermute | solution.py:28
  149.3 5.6 %collective-permute-start.17 = (f32[64,256]{1,0:T(8,128)S(1)}, f32[64,256]{1,0:T(8,128)S(1)}, u32[]{:S(2)}, u32[]{:S(2)}) collective-permute-start(f32[64,256]{1,0:T(8,128)S(1)} %multiply_add_fusion.16), channel_id=1, source_target_pairs={{32,0},{64,32},{96,64},{128,96},{160,128},{192,160},{224,192},{33,... | collective-permute-start | bytes 196616 | tf_op jit(solution)/shard_map/ppermute | solution.py:28
  154.9 5.6 %collective-permute-start.18 = (f32[64,256]{1,0:T(8,128)S(1)}, f32[64,256]{1,0:T(8,128)S(1)}, u32[]{:S(2)}, u32[]{:S(2)}) collective-permute-start(f32[64,256]{1,0:T(8,128)S(1)} %multiply_add_fusion.15), channel_id=1, source_target_pairs={{32,0},{64,32},{96,64},{128,96},{160,128},{192,160},{224,192},{33,... | collective-permute-start | bytes 196616 | tf_op jit(solution)/shard_map/ppermute | solution.py:28
  160.5 5.6 %collective-permute-start.19 = (f32[64,256]{1,0:T(8,128)S(1)}, f32[64,256]{1,0:T(8,128)S(1)}, u32[]{:S(2)}, u32[]{:S(2)}) collective-permute-start(f32[64,256]{1,0:T(8,128)S(1)} %multiply_add_fusion.14), channel_id=1, source_target_pairs={{32,0},{64,32},{96,64},{128,96},{160,128},{192,160},{224,192},{33,... | collective-permute-start | bytes 196616 | tf_op jit(solution)/shard_map/ppermute | solution.py:28
  166.1 5.6 %collective-permute-start.20 = (f32[64,256]{1,0:T(8,128)S(1)}, f32[64,256]{1,0:T(8,128)S(1)}, u32[]{:S(2)}, u32[]{:S(2)}) collective-permute-start(f32[64,256]{1,0:T(8,128)S(1)} %multiply_add_fusion.13), channel_id=1, source_target_pairs={{32,0},{64,32},{96,64},{128,96},{160,128},{192,160},{224,192},{33,... | collective-permute-start | bytes 196616 | tf_op jit(solution)/shard_map/ppermute | solution.py:28
  171.7 5.6 %collective-permute-start.21 = (f32[64,256]{1,0:T(8,128)S(1)}, f32[64,256]{1,0:T(8,128)S(1)}, u32[]{:S(2)}, u32[]{:S(2)}) collective-permute-start(f32[64,256]{1,0:T(8,128)S(1)} %multiply_add_fusion.12), channel_id=1, source_target_pairs={{32,0},{64,32},{96,64},{128,96},{160,128},{192,160},{224,192},{33,... | collective-permute-start | bytes 196616 | tf_op jit(solution)/shard_map/ppermute | solution.py:28
  188.1 18.5 %all-to-all-start.3 = ((f32[32,2,16]{2,1,0:T(2,128)}), f32[32,2,16]{2,1,0:T(2,128)S(1)}, u32[]{:S(2)}, u32[]{:S(2)}) async-start(f32[32,2,16]{2,1,0:T(2,128)} %bitcast.46), calls=%async_computation.3 | async-start | bytes 65536 | tf_op jit(solution)/shard_map/all_to_all | solution.py:101
  197.9 16.2 %collective-permute-start.22 = (f32[8,1,256]{2,0,1:T(8,128)S(1)}, f32[8,1,256]{2,0,1:T(8,128)S(1)}, u32[]{:S(2)}, u32[]{:S(2)}) collective-permute-start(f32[8,1,256]{2,0,1:T(8,128)S(1)} %get-tuple-element.34), channel_id=1, source_target_pairs={{4,0},{8,4},{12,8},{16,12},{20,16},{24,20},{28,24},{5,1},{9,5},{13... | collective-permute-start | bytes 24584 | tf_op jit(solution)/shard_map/ppermute | solution.py:20
  199.2 14.9 %collective-permute-start.23 = (f32[8,1,256]{2,0,1:T(8,128)S(1)}, f32[8,1,256]{2,0,1:T(8,128)S(1)}, u32[]{:S(2)}, u32[]{:S(2)}) collective-permute-start(f32[8,1,256]{2,0,1:T(8,128)S(1)} %get-tuple-element.33), channel_id=1, source_target_pairs={{0,4},{4,8},{8,12},{12,16},{16,20},{20,24},{24,28},{1,5},{5,9},{9,... | collective-permute-start | bytes 24584 | tf_op jit(solution)/shard_map/ppermute | solution.py:19
  208.1 14.6 %all-to-all-start.4 = ((f32[32,2,8]{2,1,0:T(2,128)}), f32[32,2,8]{2,1,0:T(2,128)}, u32[]{:S(2)}, u32[]{:S(2)}) async-start(f32[32,2,8]{2,1,0:T(2,128)} %bitcast.54), calls=%async_computation.4 | async-start | bytes 65536 | tf_op jit(solution)/shard_map/all_to_all | solution.py:113
  215.0 20.0 %collective-permute-start.25 = (f32[8,66,1]{2,0,1:T(8,128)}, f32[8,66,1]{2,0,1:T(8,128)S(1)}, u32[]{:S(2)}, u32[]{:S(2)}) collective-permute-start(f32[8,66,1]{2,0,1:T(8,128)} %get-tuple-element.30), channel_id=1, source_target_pairs={{0,1},{1,2},{2,3},{4,5},{5,6},{6,7},{8,9},{9,10},{10,11},{12,13},{... | collective-permute-start | bytes 6344 | tf_op jit(solution)/shard_map/ppermute | solution.py:19
  218.1 16.9 %collective-permute-start.24 = (f32[8,66,1]{2,0,1:T(8,128)}, f32[8,66,1]{2,0,1:T(8,128)}, u32[]{:S(2)}, u32[]{:S(2)}) collective-permute-start(f32[8,66,1]{2,0,1:T(8,128)} %get-tuple-element.29), channel_id=1, source_target_pairs={{1,0},{2,1},{3,2},{5,4},{6,5},{7,6},{9,8},{10,9},{11,10},{13,12},{... | collective-permute-start | bytes 6344 | tf_op jit(solution)/shard_map/ppermute | solution.py:20
  238.7 5.7 %collective-permute-start.26 = (f32[64,256]{1,0:T(8,128)S(1)}, f32[64,256]{1,0:T(8,128)S(1)}, u32[]{:S(2)}, u32[]{:S(2)}) collective-permute-start(f32[64,256]{1,0:T(8,128)S(1)} %get-tuple-element.15), channel_id=1, source_target_pairs={{0,32},{32,64},{64,96},{96,128},{128,160},{160,192},{192,224},{1,3... | collective-permute-start | bytes 196616 | tf_op jit(solution)/shard_map/ppermute | solution.py:28
  244.5 5.6 %collective-permute-start.27 = (f32[64,256]{1,0:T(8,128)S(1)}, f32[64,256]{1,0:T(8,128)S(1)}, u32[]{:S(2)}, u32[]{:S(2)}) collective-permute-start(f32[64,256]{1,0:T(8,128)S(1)} %multiply_add_fusion.11), channel_id=1, source_target_pairs={{0,32},{32,64},{64,96},{96,128},{128,160},{160,192},{192,224},{1,3... | collective-permute-start | bytes 196616 | tf_op jit(solution)/shard_map/ppermute | solution.py:28
  250.1 5.6 %collective-permute-start.28 = (f32[64,256]{1,0:T(8,128)S(1)}, f32[64,256]{1,0:T(8,128)S(1)}, u32[]{:S(2)}, u32[]{:S(2)}) collective-permute-start(f32[64,256]{1,0:T(8,128)S(1)} %multiply_add_fusion.10), channel_id=1, source_target_pairs={{0,32},{32,64},{64,96},{96,128},{128,160},{160,192},{192,224},{1,3... | collective-permute-start | bytes 196616 | tf_op jit(solution)/shard_map/ppermute | solution.py:28
  255.7 5.6 %collective-permute-start.29 = (f32[64,256]{1,0:T(8,128)S(1)}, f32[64,256]{1,0:T(8,128)S(1)}, u32[]{:S(2)}, u32[]{:S(2)}) collective-permute-start(f32[64,256]{1,0:T(8,128)S(1)} %multiply_add_fusion.9), channel_id=1, source_target_pairs={{0,32},{32,64},{64,96},{96,128},{128,160},{160,192},{192,224},{1,3... | collective-permute-start | bytes 196616 | tf_op jit(solution)/shard_map/ppermute | solution.py:28
  261.3 5.6 %collective-permute-start.30 = (f32[64,256]{1,0:T(8,128)S(1)}, f32[64,256]{1,0:T(8,128)S(1)}, u32[]{:S(2)}, u32[]{:S(2)}) collective-permute-start(f32[64,256]{1,0:T(8,128)S(1)} %multiply_add_fusion.8), channel_id=1, source_target_pairs={{0,32},{32,64},{64,96},{96,128},{128,160},{160,192},{192,224},{1,3... | collective-permute-start | bytes 196616 | tf_op jit(solution)/shard_map/ppermute | solution.py:28
  266.9 5.6 %collective-permute-start.31 = (f32[64,256]{1,0:T(8,128)S(1)}, f32[64,256]{1,0:T(8,128)S(1)}, u32[]{:S(2)}, u32[]{:S(2)}) collective-permute-start(f32[64,256]{1,0:T(8,128)S(1)} %multiply_add_fusion.7), channel_id=1, source_target_pairs={{0,32},{32,64},{64,96},{96,128},{128,160},{160,192},{192,224},{1,3... | collective-permute-start | bytes 196616 | tf_op jit(solution)/shard_map/ppermute | solution.py:28
  272.5 5.6 %collective-permute-start.32 = (f32[64,256]{1,0:T(8,128)S(1)}, f32[64,256]{1,0:T(8,128)S(1)}, u32[]{:S(2)}, u32[]{:S(2)}) collective-permute-start(f32[64,256]{1,0:T(8,128)S(1)} %multiply_add_fusion.6), channel_id=1, source_target_pairs={{0,32},{32,64},{64,96},{96,128},{128,160},{160,192},{192,224},{1,3... | collective-permute-start | bytes 196616 | tf_op jit(solution)/shard_map/ppermute | solution.py:28
  278.1 6.2 %collective-permute-start.33 = (f32[64,256]{1,0:T(8,128)S(1)}, f32[64,256]{1,0:T(8,128)S(1)}, u32[]{:S(2)}, u32[]{:S(2)}) collective-permute-start(f32[64,256]{1,0:T(8,128)S(1)} %get-tuple-element.13), channel_id=1, source_target_pairs={{32,0},{64,32},{96,64},{128,96},{160,128},{192,160},{224,192},{33,... | collective-permute-start | bytes 196616 | tf_op jit(solution)/shard_map/ppermute | solution.py:28
  284.3 5.6 %collective-permute-start.34 = (f32[64,256]{1,0:T(8,128)S(1)}, f32[64,256]{1,0:T(8,128)S(1)}, u32[]{:S(2)}, u32[]{:S(2)}) collective-permute-start(f32[64,256]{1,0:T(8,128)S(1)} %multiply_add_fusion.5), channel_id=1, source_target_pairs={{32,0},{64,32},{96,64},{128,96},{160,128},{192,160},{224,192},{33,... | collective-permute-start | bytes 196616 | tf_op jit(solution)/shard_map/ppermute | solution.py:28
  289.9 5.6 %collective-permute-start.35 = (f32[64,256]{1,0:T(8,128)S(1)}, f32[64,256]{1,0:T(8,128)S(1)}, u32[]{:S(2)}, u32[]{:S(2)}) collective-permute-start(f32[64,256]{1,0:T(8,128)S(1)} %multiply_add_fusion.4), channel_id=1, source_target_pairs={{32,0},{64,32},{96,64},{128,96},{160,128},{192,160},{224,192},{33,... | collective-permute-start | bytes 196616 | tf_op jit(solution)/shard_map/ppermute | solution.py:28
  295.5 5.6 %collective-permute-start.36 = (f32[64,256]{1,0:T(8,128)S(1)}, f32[64,256]{1,0:T(8,128)S(1)}, u32[]{:S(2)}, u32[]{:S(2)}) collective-permute-start(f32[64,256]{1,0:T(8,128)S(1)} %multiply_add_fusion.3), channel_id=1, source_target_pairs={{32,0},{64,32},{96,64},{128,96},{160,128},{192,160},{224,192},{33,... | collective-permute-start | bytes 196616 | tf_op jit(solution)/shard_map/ppermute | solution.py:28
  301.1 5.6 %collective-permute-start.37 = (f32[64,256]{1,0:T(8,128)S(1)}, f32[64,256]{1,0:T(8,128)S(1)}, u32[]{:S(2)}, u32[]{:S(2)}) collective-permute-start(f32[64,256]{1,0:T(8,128)S(1)} %multiply_add_fusion.2), channel_id=1, source_target_pairs={{32,0},{64,32},{96,64},{128,96},{160,128},{192,160},{224,192},{33,... | collective-permute-start | bytes 196616 | tf_op jit(solution)/shard_map/ppermute | solution.py:28
  306.7 5.6 %collective-permute-start.38 = (f32[64,256]{1,0:T(8,128)S(1)}, f32[64,256]{1,0:T(8,128)S(1)}, u32[]{:S(2)}, u32[]{:S(2)}) collective-permute-start(f32[64,256]{1,0:T(8,128)S(1)} %multiply_add_fusion.1), channel_id=1, source_target_pairs={{32,0},{64,32},{96,64},{128,96},{160,128},{192,160},{224,192},{33,... | collective-permute-start | bytes 196616 | tf_op jit(solution)/shard_map/ppermute | solution.py:28
  312.3 5.6 %collective-permute-start.39 = (f32[64,256]{1,0:T(8,128)S(1)}, f32[64,256]{1,0:T(8,128)S(1)}, u32[]{:S(2)}, u32[]{:S(2)}) collective-permute-start(f32[64,256]{1,0:T(8,128)S(1)} %multiply_add_fusion), channel_id=1, source_target_pairs={{32,0},{64,32},{96,64},{128,96},{160,128},{192,160},{224,192},{33,... | collective-permute-start | bytes 196616 | tf_op jit(solution)/shard_map/ppermute | solution.py:28
  (19 other events, 227.6 us)
where the time goes:
time: 322 us; the launch traced here: 320 us
  starting transfers between devices  163 us (51%)
  waiting for transfers between devices  84.2 us (26%)
  local copies, waits for them, and re-layouts  40.7 us (13%)
  other arithmetic  24.2 us (8%)
  matrix products  5.03 us (2%)
    ppermute x28, starting transfers between devices, passed_along(): lax.ppermute(value, axis, [(source, source + steps) for source in range(i...  90.6 us
    ppermute x28, waiting for transfers between devices, passed_along(): lax.ppermute(value, axis, [(source, source + steps) for source in range(i...  70.1 us
    ppermute x6, starting transfers between devices, extended(): before = lax.ppermute(last, axis, up)  22.6 us
    all_to_all x2, starting transfers between devices, shards(): lax.all_to_all(outgoing, ('gx', 'gy'), split_axis=0, concat_axis=0, tiled...  20.5 us
    all_to_all x1, starting transfers between devices, shards(): lax.all_to_all(slot_ids, ('gx', 'gy'), split_axis=0, concat_axis=0, tiled...  12 us
    reshape x2, local copies, waits for them, and re-layouts, shards(): well_term = jnp.zeros((layer_depth, columns), jnp.float32).at[:, column]....  11.7 us
    all_to_all x2, waiting for transfers between devices, shards(): lax.all_to_all(outgoing, ('gx', 'gy'), split_axis=0, concat_axis=0, tiled...  10.8 us
    all_to_all x2, starting transfers between devices, shards(): lax.all_to_all(flow_out.reshape(tile_total, capacity, layer_depth), ('gx'...  9.82 us
  transfers between devices with their start and end apart: 45, of which 31 were waited for; matrix products, arithmetic and copies ran while one was open for 15% of the time, Pallas kernels for 0%

commit v1 on v0

v1 whole, which is shorter than its diff:
```python
import functools

import jax
import jax.numpy as jnp
from jax import lax
from jax.experimental import pallas as pl
from jax.experimental.pallas import tpu as pltpu
from jax.sharding import PartitionSpec as P

ITERS = 2
LZ = 8
CX = 64
CY = 256
SLOTS = 48
WELLS = 256
TILES = 32
GROUPS = 8
F32 = jnp.float32
VMEM = pl.BlockSpec(memory_space=pltpu.VMEM)
SMEM = pl.BlockSpec(memory_space=pltpu.SMEM)
ANY = pl.BlockSpec(memory_space=pl.ANY)


def shape(*dims):
    return jax.ShapeDtypeStruct(dims, F32)


def lane_ids(rows, lanes):
    return lax.broadcasted_iota(jnp.int32, (rows, lanes), 1)


def x_edges(ref, row, out, first):
    for l in range(LZ):
        out[first + l : first + l + 1, :] = ref[l * CX + row : l * CX + row + 1, :]


def y_edges(pieces):
    lanes = lane_ids(2 * CX, 128)
    packed = jnp.zeros((2 * CX, 128), F32)
    row = 0
    for ref, column in pieces:
        start = (column // 128) * 128
        for r in range(LZ // 2):
            block = ref[r * 2 * CX : (r + 1) * 2 * CX, start : start + 128]
            value = block[:, column - start : column - start + 1]
            packed = jnp.where(lanes == row, value, packed)
            row += 1
    return packed.T


def gather_slots(split_ref, column_ref):
    lanes = lane_ids(LZ, 128)
    found = jnp.zeros((LZ, 128), F32)
    for s in range(SLOTS):
        column = column_ref[0, s]
        x = column // CY
        y = column % CY
        half = y // 128
        lane = y % 128
        block = split_ref.at[half][pl.ds(x, LZ, stride=CX), :]
        value = jnp.sum(jnp.where(lanes == lane, block, 0.0), axis=1, keepdims=True)
        found = jnp.where(lanes == s, value, found)
    return found


def well_columns(rows):
    block = jnp.concatenate(rows + [jnp.zeros((8 - len(rows), 128), F32)], axis=0)
    turned = block.T
    return [turned[:, i : i + 1] for i in range(len(rows))]


def pad_lanes(value):
    return jnp.concatenate([value, jnp.zeros((value.shape[0], 128 - value.shape[1]), value.dtype)], axis=1)


def send_partials(out, values):
    for t in range(TILES):
        out[t] = values


def live_index(index_ref, count_ref):
    index = pad_lanes(index_ref[...])
    return jnp.where(lane_ids(LZ, 128) < count_ref[0, 0], index, 0.0)


def well_row(owner_ref, well_ref):
    return pad_lanes((owner_ref[...] * 8 + well_ref[...]).astype(F32))


def totals_by_well(column, well_column):
    ids = well_column[:SLOTS].astype(jnp.int32)
    halves = []
    for half in range(2):
        hit = ids == lane_ids(SLOTS, 128) + half * 128
        halves.append(jnp.sum(jnp.where(hit, column[:SLOTS], 0.0), axis=0, keepdims=True))
    return jnp.concatenate(halves, axis=0)


def own_rates(rate_ref):
    tile = lax.axis_index("gx") * 4 + lax.axis_index("gy")
    rate = rate_ref[...]
    tiled = jnp.concatenate([rate] * 16, axis=1)
    lanes = lane_ids(1, 128)
    halves = [jnp.where((lanes + half * 128) // 8 == tile, tiled, 0.0) for half in range(2)]
    return jnp.concatenate(halves, axis=0)


def open_kernel(
    field, kx_lo, kx_hi, ky, index, owner, well, rate, column, count, xlo, xhi, ylo, yhi, partials, at_slots, split
):
    for half in range(2):
        split[half] = field[:, half * 128 : half * 128 + 128]
    x_edges(field, 0, xlo, 0)
    x_edges(field, CX - 1, xhi, 0)
    for l in range(LZ):
        xlo[LZ + l : LZ + l + 1, :] = kx_lo[l, 0:1, :]
        xhi[LZ + l : LZ + l + 1, :] = kx_hi[l, 7:8, :]
    turned = y_edges([(field, 0), (ky, 0), (field, CY - 1), (ky, CY - 1)])
    ylo[...] = turned[0:8]
    yhi[...] = turned[8:16]
    at = gather_slots(split, column)
    at_slots[...] = at
    live = live_index(index, count)
    weighted = jnp.sum(live * at, axis=0, keepdims=True)
    total = jnp.sum(live, axis=0, keepdims=True)
    weighted_c, total_c, wells_c = well_columns([weighted, total, well_row(owner, well)])
    values = jnp.concatenate(
        [totals_by_well(weighted_c, wells_c) + own_rates(rate), totals_by_well(total_c, wells_c)], axis=0
    )
    send_partials(partials, values)


def solve_kernel(
    first,
    field,
    source,
    kx,
    ky,
    inverse,
    lower,
    from_xlo,
    from_xhi,
    from_ylo,
    from_yhi,
    kx_edges_lo,
    kx_edges_hi,
    ky_edges_lo,
    ky_edges_hi,
    partials,
    sums,
    index,
    owner,
    well,
    at_slots,
    column,
    count,
    solved,
    carried,
    sums_out,
    flow_out,
    rhs,
):
    gx, gy = lax.axis_index("gx"), lax.axis_index("gy")
    total = partials[0]
    for t in range(1, TILES):
        total = total + partials[t]
    if first:
        numerator, index_sum = total[0:2], total[2:4]
        sums_out[...] = index_sum
    else:
        numerator, index_sum = total[0:2], sums[...]
    bottom_hole = numerator / (index_sum + 1.0)
    (wells_c,) = well_columns([well_row(owner, well)])
    ids = wells_c[:SLOTS].astype(jnp.int32)
    held = jnp.zeros((SLOTS, 128), F32)
    for half in range(2):
        hit = ids == lane_ids(SLOTS, 128) + half * 128
        held = held + jnp.where(hit, bottom_hole[half : half + 1], 0.0)
    hole = jnp.sum(held, axis=1, keepdims=True)
    hole = jnp.broadcast_to(hole, (SLOTS, 128))
    hole = jnp.concatenate([hole, jnp.zeros((128 - SLOTS, 128), F32)], axis=0).T[0:1]
    flow = live_index(index, count) * (hole - at_slots[...])
    flow_out[...] = flow

    rows = lax.broadcasted_iota(jnp.int32, (CX, CY), 0)
    lanes = lane_ids(CX, CY)
    ylo_c = from_ylo[...].T
    yhi_c = from_yhi[...].T
    kylo_c = ky_edges_lo[...].T
    kyhi_c = ky_edges_hi[...].T
    k_row = 4 if first else 4

    def y_column(turned, base, l):
        s = (l % 2) * CX
        return turned[s : s + CX, base + l // 2 : base + l // 2 + 1]

    for l in range(LZ):
        span = slice(l * CX, (l + 1) * CX)
        f = field[span, :]
        k = kx[span, :]
        f_after = jnp.where(gx < 7, from_xhi[l : l + 1, :], 0.0)
        k_after = kx_edges_hi[LZ + l : LZ + l + 1, :]
        f_before = jnp.where(gx > 0, from_xlo[l : l + 1, :], 0.0)
        k_before = kx_edges_lo[LZ + l : LZ + l + 1, :]
        f_east = jnp.where(rows == CX - 1, f_after, pltpu.roll(f, CX - 1, 0))
        k_east = jnp.where(rows == CX - 1, k_after, pltpu.roll(k, CX - 1, 0))
        face = k + k_east
        west_first = (k[0:1, :] + k_before) * f_before
        lateral = face * f_east + jnp.where(rows == 0, west_first, pltpu.roll(face * f, 1, 0))
        k = ky[span, :]
        f_after = jnp.where(gy < 3, y_column(yhi_c, 0, l), 0.0)
        k_after = y_column(kyhi_c, k_row, l)
        f_before = jnp.where(gy > 0, y_column(ylo_c, 0, l), 0.0)
        k_before = y_column(kylo_c, k_row, l)
        f_north = jnp.where(lanes == CY - 1, f_after, pltpu.roll(f, CY - 1, 1))
        k_north = jnp.where(lanes == CY - 1, k_after, pltpu.roll(k, CY - 1, 1))
        face = k + k_north
        south_first = (k[:, 0:1] + k_before) * f_before
        lateral = lateral + face * f_north + jnp.where(lanes == 0, south_first, pltpu.roll(face * f, 1, 1))
        value = source[span, :] + 0.5 * lateral
        rhs[0, span, :] = value[:, :128]
        rhs[1, span, :] = value[:, 128:]

    lanes8 = lane_ids(LZ, 128)
    for s in range(SLOTS):
        place = column[0, s]
        x = place // CY
        y = place % CY
        half = y // 128
        lane = y % 128
        part = rhs.at[half]
        where = (pl.ds(x, LZ, stride=CX), slice(None))
        part[where] = part[where] + jnp.where(lanes8 == lane, flow[:, s : s + 1], 0.0)

    def block(b, carry):
        at = pl.multiple_of(b * 8, 8)
        right = [
            jnp.concatenate([rhs[half, pl.ds(j * CX + at, 8), :] for half in range(2)], axis=1) for j in range(LZ)
        ]
        here = pl.ds(at, 8)
        for i in range(LZ):
            total = inverse[i, 0, here, :] * right[0]
            for j in range(1, LZ):
                total = total + inverse[i, j, here, :] * right[j]
            solved[pl.ds(i * CX + at, 8), :] = total
            if i == 0:
                carried[1, here, :] = total
            if i == LZ - 1:
                low = lower[here, :]
                carried[0, here, :] = total + inverse[i, i, here, :] * low - low
        return carry

    lax.fori_loop(0, CX // 8, block, 0)


def sweep_kernel(last, *refs):
    cds, refs = refs[:8], refs[8:]
    fixed, refs = refs[:8], refs[8:]
    solved, first_column, last_column, *refs = refs
    if last:
        field, cd_all, fixed_all, sem = refs
    else:
        (index, owner, well, rate, column, count, field, lower, xlo, xhi, ylo, yhi, partials, at_slots, cd_all, fixed_all, sem, split) = refs
    me = lax.axis_index("layer")
    copies = []
    for n in range(8):
        distance, other = n % 4, n // 4
        core = me % 2
        core = jnp.where(other == 1, 1 - core, core)
        group = ((me // 2 + 4 - distance) % 4) * 2 + core
        copies.append(pltpu.make_async_copy(cds[n], cd_all.at[group], sem.at[0]))
        copies.append(pltpu.make_async_copy(fixed[n], fixed_all.at[group], sem.at[0]))
    for copy in copies:
        copy.start()
    for copy in copies:
        copy.wait()

    def block(b, carry):
        here = pl.ds(pl.multiple_of(b * 8, 8), 8)
        upper = jnp.zeros((8, CY), F32)
        uppers = [upper]
        for g in range(GROUPS - 1):
            upper = fixed_all[g, 0, here, :] * upper + cd_all[g, 0, here, :]
            uppers.append(upper)
        low = jnp.zeros((8, CY), F32)
        own_low, own_upper = low, uppers[0]
        for g in range(GROUPS - 1, 0, -1):
            own_upper = jnp.where(me == g, uppers[g], own_upper)
            step = cd_all[g, 1, here, :] + fixed_all[g, 2, here, :] * uppers[g] - uppers[g]
            low = fixed_all[g, 1, here, :] * low + step
            own_low = jnp.where(me == g - 1, low, own_low)
        for i in range(LZ):
            span = pl.ds(pl.multiple_of(i * CX + b * 8, 8), 8)
            value = (
                solved[span, :]
                + first_column[i, 0, here, :] * own_upper
                + last_column[i, 0, here, :] * own_low
            )
            field[span, :] = value
            if not last:
                split[0, span, :] = value[:, :128]
                split[1, span, :] = value[:, 128:]
        if not last:
            lower[here, :] = own_low
        return carry

    lax.fori_loop(0, CX // 8, block, 0)
    if last:
        return
    x_edges(field, 0, xlo, 0)
    x_edges(field, CX - 1, xhi, 0)
    turned = y_edges([(field, 0), (field, CY - 1)])
    ylo[...] = turned[0:8]
    yhi[...] = jnp.concatenate([turned[4:8], turned[0:4]], axis=0)
    at = gather_slots(split, column)
    at_slots[...] = at
    live = live_index(index, count)
    weighted = jnp.sum(live * at, axis=0, keepdims=True)
    weighted_c, wells_c = well_columns([weighted, well_row(owner, well)])
    send_partials(partials, totals_by_well(weighted_c, wells_c) + own_rates(rate))


def params():
    return pltpu.CompilerParams(vmem_limit_bytes=40 * 1024 * 1024)


def around(n, step):
    return [(i, (i + step) % n) for i in range(n)]


def from_sides(xlo, xhi, ylo, yhi):
    return (
        lax.ppermute(xhi, "gx", around(8, 1)),
        lax.ppermute(xlo, "gx", around(8, -1)),
        lax.ppermute(yhi, "gy", around(4, 1)),
        lax.ppermute(ylo, "gy", around(4, -1)),
    )


def all_groups(value):
    own = [value] + [lax.ppermute(value, "layer", around(8, 2 * d)) for d in range(1, 4)]
    swap = [(i, i ^ 1) for i in range(8)]
    return own + [lax.ppermute(v, "layer", swap) for v in own]


def shards(
    pressure,
    source,
    perm_x,
    perm_y,
    line_inverse,
    robin_below,
    tile_count,
    perf_owner,
    perf_well,
    perf_column,
    perf_index,
    well_rate,
):
    rows = LZ * CX
    field = pressure.reshape(rows, CY)
    source = source.reshape(rows, CY)
    kx = perm_x.reshape(rows, CY)
    ky = perm_y.reshape(rows, CY)
    inverse = line_inverse[0]
    lower = robin_below[0]
    index = perf_index[0].T
    owner = perf_owner[0].T
    well = perf_well
    column = perf_column
    count = tile_count

    fixed = all_groups(jnp.stack([inverse[LZ - 1, 0], inverse[0, LZ - 1], inverse[0, 0]]))

    edge_x = pl.BlockSpec((LZ, 8, CY), lambda n: (0, 0, 0))
    edge_x_hi = pl.BlockSpec((LZ, 8, CY), lambda n: (0, CX // 8 - 1, 0))
    *edges, partials, at_slots = pl.pallas_call(
        open_kernel,
        out_shape=(
            shape(16, CY),
            shape(16, CY),
            shape(8, 128),
            shape(8, 128),
            shape(TILES, 4, 128),
            shape(LZ, 128),
        ),
        grid=(1,),
        in_specs=[VMEM, edge_x, edge_x_hi] + [VMEM] * 5 + [SMEM] * 2,
        out_specs=(VMEM,) * 6,
        scratch_shapes=[pltpu.VMEM((2, rows, 128), F32)],
        compiler_params=params(),
        name="open_edges",
    )(field, perm_x, perm_x, ky, index, owner, well, well_rate, column, count)
    k_sides = None
    sums = jnp.zeros((2, 128), F32)
    for sweep_step in range(ITERS):
        first, last = sweep_step == 0, sweep_step == ITERS - 1
        sides = from_sides(*edges)
        if first:
            k_sides = sides
        spread = lax.all_to_all(partials, ("gx", "gy"), split_axis=0, concat_axis=0, tiled=True)
        solved, carried, new_sums, flow = pl.pallas_call(
            functools.partial(solve_kernel, first),
            out_shape=(shape(rows, CY), shape(2, CX, CY), shape(2, 128), shape(LZ, 128)),
            in_specs=[VMEM] * 20 + [SMEM] * 2,
            out_specs=(VMEM,) * 4,
            scratch_shapes=[pltpu.VMEM((2, rows, 128), F32)],
            compiler_params=params(),
            name="solve_lines",
        )(
            field,
            source,
            kx,
            ky,
            inverse,
            lower,
            *sides,
            *k_sides,
            spread,
            sums,
            index,
            owner,
            well,
            at_slots,
            column,
            count,
        )
        if first:
            sums = new_sums
        groups = all_groups(carried)
        column_first = pl.BlockSpec((LZ, 1, CX, CY), lambda n: (0, 0, 0, 0))
        column_last = pl.BlockSpec((LZ, 1, CX, CY), lambda n: (0, LZ - 1, 0, 0))
        specs = [ANY] * 16 + [VMEM, column_first, column_last]
        scratch = [
            pltpu.VMEM((GROUPS, 2, CX, CY), F32),
            pltpu.VMEM((GROUPS, 3, CX, CY), F32),
            pltpu.SemaphoreType.DMA((1,)),
        ]
        if last:
            (field,) = pl.pallas_call(
                functools.partial(sweep_kernel, True),
                out_shape=(shape(rows, CY),),
                grid=(1,),
                in_specs=specs,
                out_specs=(VMEM,),
                scratch_shapes=scratch,
                compiler_params=params(),
                name="sweep_last",
            )(*groups, *fixed, solved, inverse, inverse)
        else:
            field, lower, *edges, partials, at_slots = pl.pallas_call(
                functools.partial(sweep_kernel, False),
                out_shape=(
                    shape(rows, CY),
                    shape(CX, CY),
                    shape(8, CY),
                    shape(8, CY),
                    shape(8, 128),
                    shape(8, 128),
                    shape(TILES, 2, 128),
                    shape(LZ, 128),
                ),
                grid=(1,),
                in_specs=specs + [VMEM] * 4 + [SMEM] * 2,
                out_specs=(VMEM,) * 8,
                scratch_shapes=scratch + [pltpu.VMEM((2, rows, 128), F32)],
                compiler_params=params(),
                name="sweep_mid",
            )(*groups, *fixed, solved, inverse, inverse, index, owner, well, well_rate, column, count)
    return (field.reshape(LZ, CX, CY), flow[:, :SLOTS].T[None])


def solution(mesh):
    placed = (
        P("layer", "gx", "gy"),
        P("layer", "gx", "gy"),
        P("layer", "gx", "gy"),
        P("layer", "gx", "gy"),
        P("layer", None, None, "gx", "gy"),
        P("layer", "gx", "gy"),
        P("layer", ("gx", "gy")),
        P("layer", ("gx", "gy"), None),
        P("layer", ("gx", "gy")),
        P("layer", ("gx", "gy")),
        P("layer", ("gx", "gy"), None),
        P("layer", ("gx", "gy")),
    )
    return jax.shard_map(
        shards,
        mesh=mesh,
        in_specs=placed,
        out_specs=(P("layer", "gx", "gy"), P("layer", ("gx", "gy"), None)),
        check_vma=False,
    )
```

time: 322 us -> 114 us (0.35)
  starting transfers between devices: 163 us -> 59.4 us
  waiting for transfers between devices: 84.2 us -> 9.97 us
  other arithmetic: 24.2 us -> 0.02 us
  Pallas kernels: 0 us -> 20.6 us
  local copies, waits for them, and re-layouts: 40.7 us -> 21.8 us
  matrix products: 5.03 us -> 0 us
    ppermute x40 -> x29, starting transfers between devices: 121 us -> 39.9 us  [the longest x12 21.6 us: all_groups(): return own + [lax.ppermute(v, 'layer', swap) for v in own]]
    ppermute x40 -> x29, waiting for transfers between devices: 70.2 us -> 8.04 us  [the longest x9 2.61 us: all_groups(): lax.ppermute(value, 'layer', around(8, 2 * d))]
    all_to_all x5 -> x2, starting transfers between devices: 42.3 us -> 19.5 us  [shards(): lax.all_to_all(partials, ('gx', 'gy'), split_axis=0, concat_axis=0, tiled...]
    pallas_call x0 -> x5, Pallas kernels: none -> 20.6 us  [the longest x2 7.28 us: shards(): pl.pallas_call(functools.partial(solve_kernel, first), out_shape=(shape(r...]
    unnamed x51 -> x62, local copies, waits for them, and re-layouts: 7.82 us -> 20.3 us
    all_to_all x5 -> x2, waiting for transfers between devices: 14.1 us -> 1.93 us  [shards(): lax.all_to_all(partials, ('gx', 'gy'), split_axis=0, concat_axis=0, tiled...]
    reshape x2 -> x0, local copies, waits for them, and re-layouts: 11.7 us -> none  [shards(): well_term = jnp.zeros((layer_depth, columns), jnp.float32).at[:, column]....]
    scatter-add x2 -> x0, other arithmetic: 9.3 us -> none  [shards(): well_term = jnp.zeros((layer_depth, columns), jnp.float32).at[:, column]....]
  transfers between devices with their start and end apart: 45 -> 31, of which waited for: 31 -> 9; matrix products, arithmetic and copies ran while one was open for 15% -> 1% of each run, Pallas kernels for 0% -> 5%
where the time goes in v1:
time: 114 us
  starting transfers between devices  59.4 us (52%)
  local copies, waits for them, and re-layouts  21.8 us (19%)
  Pallas kernels  20.6 us (18%)
  waiting for transfers between devices  9.97 us (9%)
  between operations  1.69 us (1%)
    ppermute x12, starting transfers between devices, all_groups(): return own + [lax.ppermute(v, 'layer', swap) for v in own]  21.6 us
    unnamed x62, local copies, waits for them, and re-layouts  20.3 us
    all_to_all x2, starting transfers between devices, shards(): lax.all_to_all(partials, ('gx', 'gy'), split_axis=0, concat_axis=0, tiled...  19.5 us
    ppermute x9, starting transfers between devices, all_groups(): lax.ppermute(value, 'layer', around(8, 2 * d))  7.39 us
    pallas_call x2, Pallas kernels, shards(): pl.pallas_call(functools.partial(solve_kernel, first), out_shape=(shape(r...  7.28 us
    pallas_call x1, Pallas kernels, shards(): pl.pallas_call(functools.partial(sweep_kernel, False), out_shape=(shape(r...  6.19 us
    pallas_call x1, Pallas kernels, shards(): pl.pallas_call(functools.partial(sweep_kernel, True), out_shape=(shape(ro...  4.92 us
    ppermute x2, starting transfers between devices, from_sides(): lax.ppermute(ylo, 'gy', around(4, -1))  2.92 us
  transfers between devices with their start and end apart: 31, of which 9 were waited for; matrix products, arithmetic and copies ran while one was open for 1% of the time, Pallas kernels for 5%

profile of v1, /device:TPU:1, one launch (start us, length us, event | category | flops | bytes accessed | tf_op | source)
XLA Modules:
  0.0 113.5 jit_solution(9903395881069129259)
XLA Ops:
  0.6 0.9 slice_bitcast_fusion.2
  1.6 3.3 %collective-permute-start.14 = (f32[3,64,256]{2,1,0:T(8,128)S(1)}, f32[3,64,256]{2,1,0:T(8,128)S(1)}, u32[]{:S(2)}, u32[]{:S(2)}) collective-permute-start(f32[3,64,256]{2,1,0:T(8,128)S(1)} %pad_maximum_fusion.refs_8_), channel_id=1, source_target_pairs={{0,32},{32,0},{64,96},{96,64},{128,160},{160,128},{192,224},{224,1... | collective-permute-start | bytes 589832 | tf_op jit(solution)/shard_map/ppermute | solution.py:343
  4.9 0.8 collective-permute-start.13
  6.3 1.0 copy-done.4
  7.4 1.0 copy-done.7
  8.4 1.0 copy-done.12
  12.8 2.2 %open_edges.1 = (f32[16,256]{1,0:T(8,128)S(1)}, f32[16,256]{1,0:T(8,128)S(1)}, f32[8,128]{1,0:T(8,128)S(1)}, f32[8,128]{1,0:T(8,128)S(1)}, f32[32,4,128]{2,1,0:T(4,128)}, /*index=5*/f32[8,128]{1,0:T(8,128)S(1)}) custom-call(f32[512,256]{1,0:T(8,128)S(1)} %bitcast.35, f32[8,64,256]{2,1,0:T(8,128)S(1)} %copy-done.4, f32[8,64,256]{2,1,0:T(8,128)S(1)} %copy-done.4, ...), custom_call_target="tpu_custom_call" | custom-call | tf_op jit(solution)/shard_map/open_edges/pallas_call | solution.py:377
  15.0 11.2 %all-to-all-start = ((f32[32,4,128]{2,1,0:T(4,128)}), f32[32,4,128]{2,1,0:T(4,128)S(1)}, u32[]{:S(2)}, u32[]{:S(2)}) async-start(f32[32,4,128]{2,1,0:T(4,128)} %get-tuple-element.26), calls=%async_computation | async-start | bytes 131072 | tf_op jit(solution)/shard_map/all_to_all | solution.py:401
  26.8 1.2 %collective-permute-start.2 = (f32[8,128]{1,0:T(8,128)S(1)}, f32[8,128]{1,0:T(8,128)S(1)}, u32[]{:S(2)}, u32[]{:S(2)}) collective-permute-start(f32[8,128]{1,0:T(8,128)S(1)} %get-tuple-element.24), channel_id=1, source_target_pairs={{0,1},{1,2},{2,3},{3,0},{4,5},{5,6},{6,7},{7,4},{8,9},{9,10},{10,1... | collective-permute-start | bytes 12296 | tf_op jit(solution)/shard_map/ppermute | solution.py:335
  28.0 1.4 %collective-permute-start.3 = (f32[8,128]{1,0:T(8,128)S(1)}, f32[8,128]{1,0:T(8,128)S(1)}, u32[]{:S(2)}, u32[]{:S(2)}) collective-permute-start(f32[8,128]{1,0:T(8,128)S(1)} %get-tuple-element.25), channel_id=1, source_target_pairs={{0,3},{1,0},{2,1},{3,2},{4,7},{5,4},{6,5},{7,6},{8,11},{9,8},{10,9... | collective-permute-start | bytes 12296 | tf_op jit(solution)/shard_map/ppermute | solution.py:336
  29.5 1.0 collective-permute-done.2.from_ylo.ky_edges_lo
  30.5 1.5 %collective-permute-start = (f32[16,256]{1,0:T(8,128)S(1)}, f32[16,256]{1,0:T(8,128)S(1)}, u32[]{:S(2)}, u32[]{:S(2)}) collective-permute-start(f32[16,256]{1,0:T(8,128)S(1)} %get-tuple-element.22), channel_id=1, source_target_pairs={{0,4},{4,8},{8,12},{12,16},{16,20},{20,24},{24,28},{28,0},{1,5},{5... | collective-permute-start | bytes 49160 | tf_op jit(solution)/shard_map/ppermute | solution.py:333
  32.0 1.3 %collective-permute-start.1 = (f32[16,256]{1,0:T(8,128)S(1)}, f32[16,256]{1,0:T(8,128)S(1)}, u32[]{:S(2)}, u32[]{:S(2)}) collective-permute-start(f32[16,256]{1,0:T(8,128)S(1)} %get-tuple-element.23), channel_id=1, source_target_pairs={{0,28},{4,0},{8,4},{12,8},{16,12},{20,16},{24,20},{28,24},{1,29},{... | collective-permute-start | bytes 49160 | tf_op jit(solution)/shard_map/ppermute | solution.py:334
  33.3 1.4 %collective-permute-done.from_xlo.kx_edges_lo = f32[16,256]{1,0:T(8,128)S(1)} collective-permute-done((f32[16,256]{1,0:T(8,128)S(1)}, f32[16,256]{1,0:T(8,128)S(1)}, u32[]{:S(2)}, u32[]{:S(2)}) %collective-permute-start) | collective-permute-done | bytes 16416 | tf_op jit(solution)/shard_map/ppermute | solution.py:333
  34.7 0.7 collective-permute-start.11
  35.4 2.2 %copy-done = f32[1,8,8,64,256]{4,3,2,1,0:T(8,128)S(1)} copy-done((f32[1,8,8,64,256]{4,3,2,1,0:T(8,128)S(1)}, f32[1,8,8,64,256]{4,3,2,1,0:T(8,128)}, u32[]{:S(2)}) %copy-start) | copy-done | bytes 4194328
  37.6 1.0 copy-done.5
  38.7 1.0 copy-done.8
  39.7 1.0 copy-done.10
  40.7 1.0 copy-done.13
  41.8 0.8 copy-done.16
  45.3 3.6 %solve_lines.2 = (f32[512,256]{1,0:T(8,128)S(1)}, f32[2,64,256]{2,1,0:T(8,128)S(1)}, f32[2,128]{1,0:T(2,128)S(1)}, f32[8,128]{1,0:T(8,128)}) custom-call(f32[512,256]{1,0:T(8,128)S(1)} %bitcast.36, f32[512,256]{1,0:T(8,128)S(1)} %bitcast.33, f32[512,256]{1,0:T(8,128)S(1)} %bitcast.28, f32[512,256]{1,0:T(8,128)S(1)} %bitcast.31, ...), custom_call_target="tpu_custom_call" | custom-call | tf_op jit(solution)/shard_map/solve_lines/pallas_call | solution.py:402
  48.9 2.0 %collective-permute-start.6 = (f32[2,64,256]{2,1,0:T(8,128)S(1)}, f32[2,64,256]{2,1,0:T(8,128)S(1)}, u32[]{:S(2)}, u32[]{:S(2)}) collective-permute-start(f32[2,64,256]{2,1,0:T(8,128)S(1)} %get-tuple-element.28.refs_0_), channel_id=1, source_target_pairs={{0,192},{32,224},{64,0},{96,32},{128,64},{160,96},{192,128},{224,1... | collective-permute-start | bytes 393224 | tf_op jit(solution)/shard_map/ppermute | solution.py:341
  50.9 3.3 %collective-permute-start.7 = (f32[2,64,256]{2,1,0:T(8,128)S(1)}, f32[2,64,256]{2,1,0:T(8,128)S(1)}, u32[]{:S(2)}, u32[]{:S(2)}) collective-permute-start(f32[2,64,256]{2,1,0:T(8,128)S(1)} %get-tuple-element.28.refs_0_), channel_id=1, source_target_pairs={{0,32},{32,0},{64,96},{96,64},{128,160},{160,128},{192,224},{224,1... | collective-permute-start | bytes 393224 | tf_op jit(solution)/shard_map/ppermute | solution.py:343
  54.3 1.3 %collective-permute-start.5 = (f32[2,64,256]{2,1,0:T(8,128)S(1)}, f32[2,64,256]{2,1,0:T(8,128)S(1)}, u32[]{:S(2)}, u32[]{:S(2)}) collective-permute-start(f32[2,64,256]{2,1,0:T(8,128)S(1)} %get-tuple-element.28.refs_0_), channel_id=1, source_target_pairs={{0,128},{32,160},{64,192},{96,224},{128,0},{160,32},{192,64},{224,... | collective-permute-start | bytes 393224 | tf_op jit(solution)/shard_map/ppermute | solution.py:341
  55.5 4.1 %collective-permute-start.10 = (f32[2,64,256]{2,1,0:T(8,128)S(1)}, f32[2,64,256]{2,1,0:T(8,128)S(1)}, u32[]{:S(2)}, u32[]{:S(2)}) collective-permute-start(f32[2,64,256]{2,1,0:T(8,128)S(1)} %collective-permute-done.6.refs_3_), channel_id=1, source_target_pairs={{0,32},{32,0},{64,96},{96,64},{128,160},{160,128},{192,224},{224,1... | collective-permute-start | bytes 393224 | tf_op jit(solution)/shard_map/ppermute | solution.py:343
  60.1 0.7 collective-permute-done.5.refs_2_
  60.8 1.3 %collective-permute-start.15 = (f32[3,64,256]{2,1,0:T(8,128)S(1)}, f32[3,64,256]{2,1,0:T(8,128)S(1)}, u32[]{:S(2)}, u32[]{:S(2)}) collective-permute-start(f32[3,64,256]{2,1,0:T(8,128)S(1)} %collective-permute-done.11.refs_9_), channel_id=1, source_target_pairs={{0,32},{32,0},{64,96},{96,64},{128,160},{160,128},{192,224},{224,1... | collective-permute-start | bytes 589832 | tf_op jit(solution)/shard_map/ppermute | solution.py:343
  62.1 1.9 %collective-permute-done.4.refs_1_ = f32[2,64,256]{2,1,0:T(8,128)S(1)} collective-permute-done((f32[2,64,256]{2,1,0:T(8,128)S(1)}, f32[2,64,256]{2,1,0:T(8,128)S(1)}, u32[]{:S(2)}, u32[]{:S(2)}) %collective-permute-start.4) | collective-permute-done | bytes 131104 | tf_op jit(solution)/shard_map/ppermute | solution.py:341
  64.5 0.9 collective-permute-done.9.refs_6_
  66.0 6.2 %sweep_mid.1 = (f32[512,256]{1,0:T(8,128)S(1)}, f32[64,256]{1,0:T(8,128)S(1)}, f32[8,256]{1,0:T(8,128)S(1)}, f32[8,256]{1,0:T(8,128)S(1)}, f32[8,128]{1,0:T(8,12...) custom-call(f32[2,64,256]{2,1,0:T(8,128)S(1)} %get-tuple-element.28.refs_0_, ...), custom_call_target="tpu_custom_call" | custom-call | tf_op jit(solution)/shard_map/sweep_mid/pallas_call | solution.py:451
  72.2 0.8 copy-done.14
  73.0 8.3 %all-to-all-start.1 = ((f32[32,2,128]{2,1,0:T(2,128)}), f32[32,2,128]{2,1,0:T(2,128)S(1)}, u32[]{:S(2)}, u32[]{:S(2)}) async-start(f32[32,2,128]{2,1,0:T(2,128)} %get-tuple-element.36), calls=%async_computation.1 | async-start | bytes 65536 | tf_op jit(solution)/shard_map/all_to_all | solution.py:401
  81.2 1.3 %collective-permute-start.18 = (f32[8,256]{1,0:T(8,128)S(1)}, f32[8,256]{1,0:T(8,128)S(1)}, u32[]{:S(2)}, u32[]{:S(2)}) collective-permute-start(f32[8,256]{1,0:T(8,128)S(1)} %get-tuple-element.32), channel_id=1, source_target_pairs={{0,4},{4,8},{8,12},{12,16},{16,20},{20,24},{24,28},{28,0},{1,5},{5... | collective-permute-start | bytes 24584 | tf_op jit(solution)/shard_map/ppermute | solution.py:333
  82.5 1.5 %collective-permute-start.19 = (f32[8,256]{1,0:T(8,128)S(1)}, f32[8,256]{1,0:T(8,128)S(1)}, u32[]{:S(2)}, u32[]{:S(2)}) collective-permute-start(f32[8,256]{1,0:T(8,128)S(1)} %get-tuple-element.33), channel_id=1, source_target_pairs={{0,28},{4,0},{8,4},{12,8},{16,12},{20,16},{24,20},{28,24},{1,29},{... | collective-permute-start | bytes 24584 | tf_op jit(solution)/shard_map/ppermute | solution.py:334
  84.0 1.2 %collective-permute-start.20 = (f32[8,128]{1,0:T(8,128)S(1)}, f32[8,128]{1,0:T(8,128)S(1)}, u32[]{:S(2)}, u32[]{:S(2)}) collective-permute-start(f32[8,128]{1,0:T(8,128)S(1)} %get-tuple-element.34), channel_id=1, source_target_pairs={{0,1},{1,2},{2,3},{3,0},{4,5},{5,6},{6,7},{7,4},{8,9},{9,10},{10,1... | collective-permute-start | bytes 12296 | tf_op jit(solution)/shard_map/ppermute | solution.py:335
  85.2 1.5 %collective-permute-start.21 = (f32[8,128]{1,0:T(8,128)S(1)}, f32[8,128]{1,0:T(8,128)S(1)}, u32[]{:S(2)}, u32[]{:S(2)}) collective-permute-start(f32[8,128]{1,0:T(8,128)S(1)} %get-tuple-element.35), channel_id=1, source_target_pairs={{0,3},{1,0},{2,1},{3,2},{4,7},{5,4},{6,5},{7,6},{8,11},{9,8},{10,9... | collective-permute-start | bytes 12296 | tf_op jit(solution)/shard_map/ppermute | solution.py:336
  86.7 1.3 %collective-permute-done.20.from_ylo = f32[8,128]{1,0:T(8,128)S(1)} collective-permute-done((f32[8,128]{1,0:T(8,128)S(1)}, f32[8,128]{1,0:T(8,128)S(1)}, u32[]{:S(2)}, u32[]{:S(2)}) %collective-permute-start.20) | collective-permute-done | bytes 4128 | tf_op jit(solution)/shard_map/ppermute | solution.py:335
  88.0 1.9 %all-to-all-done.1.partials = f32[32,2,128]{2,1,0:T(2,128)S(1)} async-done(((f32[32,2,128]{2,1,0:T(2,128)}), f32[32,2,128]{2,1,0:T(2,128)S(1)}, u32[]{:S(2)}, u32[]{:S(2)}) %all-to-all-start.1) | async-done | bytes 32800 | tf_op jit(solution)/shard_map/all_to_all | solution.py:401
  90.0 2.2 %copy-done.2 = f32[1,8,8,64,256]{4,3,2,1,0:T(8,128)S(1)} copy-done((f32[1,8,8,64,256]{4,3,2,1,0:T(8,128)S(1)}, f32[1,8,8,64,256]{4,3,2,1,0:T(8,128)}, u32[]{:S(2)}) %copy-start.2) | copy-done | bytes 4194328
  92.2 1.0 copy-done.15
  93.2 3.6 %solve_lines.3 = (f32[512,256]{1,0:T(8,128)S(1)}, f32[2,64,256]{2,1,0:T(8,128)S(1)}, f32[2,128]{1,0:T(2,128)}, f32[8,128]{1,0:T(8,128)S(1)}) custom-call(f32[512,256]{1,0:T(8,128)S(1)} %copy-done.15, f32[512,256]{1,0:T(8,128)S(1)} %bitcast.34, f32[512,256]{1,0:T(8,128)S(1)} %bitcast.29, f32[512,256]{1,0:T(8,128)S(1)} %bitcast.32, ...), custom_call_target="tpu_custom_call" | custom-call | tf_op jit(solution)/shard_map/solve_lines/pallas_call | solution.py:402
  97.1 1.3 %collective-permute-start.23 = (f32[2,64,256]{2,1,0:T(8,128)S(1)}, f32[2,64,256]{2,1,0:T(8,128)S(1)}, u32[]{:S(2)}, u32[]{:S(2)}) collective-permute-start(f32[2,64,256]{2,1,0:T(8,128)S(1)} %get-tuple-element.39.refs_0_), channel_id=1, source_target_pairs={{0,128},{32,160},{64,192},{96,224},{128,0},{160,32},{192,64},{224,... | collective-permute-start | bytes 393224 | tf_op jit(solution)/shard_map/ppermute | solution.py:341
  99.0 2.4 %collective-permute-start.25 = (f32[2,64,256]{2,1,0:T(8,128)S(1)}, f32[2,64,256]{2,1,0:T(8,128)S(1)}, u32[]{:S(2)}, u32[]{:S(2)}) collective-permute-start(f32[2,64,256]{2,1,0:T(8,128)S(1)} %get-tuple-element.39.refs_0_), channel_id=1, source_target_pairs={{0,32},{32,0},{64,96},{96,64},{128,160},{160,128},{192,224},{224,1... | collective-permute-start | bytes 393224 | tf_op jit(solution)/shard_map/ppermute | solution.py:343
  101.4 2.8 %collective-permute-start.28 = (f32[2,64,256]{2,1,0:T(8,128)S(1)}, f32[2,64,256]{2,1,0:T(8,128)S(1)}, u32[]{:S(2)}, u32[]{:S(2)}) collective-permute-start(f32[2,64,256]{2,1,0:T(8,128)S(1)} %collective-permute-done.24.refs_3_), channel_id=1, source_target_pairs={{0,32},{32,0},{64,96},{96,64},{128,160},{160,128},{192,224},{224,1... | collective-permute-start | bytes 393224 | tf_op jit(solution)/shard_map/ppermute | solution.py:343
  104.2 2.2 %collective-permute-start.27 = (f32[2,64,256]{2,1,0:T(8,128)S(1)}, f32[2,64,256]{2,1,0:T(8,128)S(1)}, u32[]{:S(2)}, u32[]{:S(2)}) collective-permute-start(f32[2,64,256]{2,1,0:T(8,128)S(1)} %collective-permute-done.23.refs_2_), channel_id=1, source_target_pairs={{0,32},{32,0},{64,96},{96,64},{128,160},{160,128},{192,224},{224,1... | collective-permute-start | bytes 393224 | tf_op jit(solution)/shard_map/ppermute | solution.py:343
  106.4 1.1 collective-permute-start.26
  108.4 4.9 %sweep_last.1 = f32[512,256]{1,0:T(8,128)} custom-call(f32[2,64,256]{2,1,0:T(8,128)S(1)} %get-tuple-element.39.refs_0_, f32[2,64,256]{2,1,0:T(8,128)S(1)} %collective-permute-done.22.refs_1_, f32[2,64,256]{2,1,0:T(8,128)S(1)} %collective-permute-done.23.refs_2_, f32[2,64,256]{2,1,0:T(8,128)S(1)} %collective-permute-done.24.refs_3_, ...), custom_call_target="tpu_custom_call" | custom-call | tf_op jit(solution)/shard_map/sweep_last/pallas_call | solution.py:440
  (85 shorter events, 9.9 us)
Async XLA Ops:
  1.6 49.3 %collective-permute-start.14 = (f32[3,64,256]{2,1,0:T(8,128)S(1)}, f32[3,64,256]{2,1,0:T(8,128)S(1)}, u32[]{:S(2)}, u32[]{:S(2)}) collective-permute-start(f32[3,64,256]{2,1,0:T(8,128)S(1)} %pad_maximum_fusion.refs_8_), channel_id=1, source_target_pairs={{0,32},{32,0},{64,96},{96,64},{128,160},{160,128},{192,224},{224,1... | collective-permute-start | bytes 589832 | tf_op jit(solution)/shard_map/ppermute | solution.py:343
  4.9 49.3 %collective-permute-start.13 = (f32[3,64,256]{2,1,0:T(8,128)S(1)}, f32[3,64,256]{2,1,0:T(8,128)S(1)}, u32[]{:S(2)}, u32[]{:S(2)}) collective-permute-start(f32[3,64,256]{2,1,0:T(8,128)S(1)} %pad_maximum_fusion.refs_8_), channel_id=1, source_target_pairs={{0,192},{32,224},{64,0},{96,32},{128,64},{160,96},{192,128},{224,1... | collective-permute-start | bytes 589832 | tf_op jit(solution)/shard_map/ppermute | solution.py:341
  6.3 1.0 copy-start.4
  7.4 1.0 copy-start.7
  8.4 1.0 copy-start.12
  12.8 53.1 %copy-start.30 = (f32[1,8]{1,0:T(1,128)S(1)}, f32[1,8]{1,0:T(1,128)}, u32[]{:S(2)}) copy-start(f32[1,8]{1,0:T(1,128)} %refs_22_.1) | copy-start | bytes 100
  15.0 20.4 %all-to-all-start = ((f32[32,4,128]{2,1,0:T(4,128)}), f32[32,4,128]{2,1,0:T(4,128)S(1)}, u32[]{:S(2)}, u32[]{:S(2)}) async-start(f32[32,4,128]{2,1,0:T(4,128)} %get-tuple-element.26), calls=%async_computation | async-start | bytes 131072 | tf_op jit(solution)/shard_map/all_to_all | solution.py:401
  26.2 29.3 %collective-permute-start.12 = (f32[3,64,256]{2,1,0:T(8,128)S(1)}, f32[3,64,256]{2,1,0:T(8,128)S(1)}, u32[]{:S(2)}, u32[]{:S(2)}) collective-permute-start(f32[3,64,256]{2,1,0:T(8,128)S(1)} %pad_maximum_fusion.refs_8_), channel_id=1, source_target_pairs={{0,128},{32,160},{64,192},{96,224},{128,0},{160,32},{192,64},{224,... | collective-permute-start | bytes 589832 | tf_op jit(solution)/shard_map/ppermute | solution.py:341
  26.8 3.7 %collective-permute-start.2 = (f32[8,128]{1,0:T(8,128)S(1)}, f32[8,128]{1,0:T(8,128)S(1)}, u32[]{:S(2)}, u32[]{:S(2)}) collective-permute-start(f32[8,128]{1,0:T(8,128)S(1)} %get-tuple-element.24), channel_id=1, source_target_pairs={{0,1},{1,2},{2,3},{3,0},{4,5},{5,6},{6,7},{7,4},{8,9},{9,10},{10,1... | collective-permute-start | bytes 12296 | tf_op jit(solution)/shard_map/ppermute | solution.py:335
  28.0 4.0 %collective-permute-start.3 = (f32[8,128]{1,0:T(8,128)S(1)}, f32[8,128]{1,0:T(8,128)S(1)}, u32[]{:S(2)}, u32[]{:S(2)}) collective-permute-start(f32[8,128]{1,0:T(8,128)S(1)} %get-tuple-element.25), channel_id=1, source_target_pairs={{0,3},{1,0},{2,1},{3,2},{4,7},{5,4},{6,5},{7,6},{8,11},{9,8},{10,9... | collective-permute-start | bytes 12296 | tf_op jit(solution)/shard_map/ppermute | solution.py:336
  30.5 4.2 %collective-permute-start = (f32[16,256]{1,0:T(8,128)S(1)}, f32[16,256]{1,0:T(8,128)S(1)}, u32[]{:S(2)}, u32[]{:S(2)}) collective-permute-start(f32[16,256]{1,0:T(8,128)S(1)} %get-tuple-element.22), channel_id=1, source_target_pairs={{0,4},{4,8},{8,12},{12,16},{16,20},{20,24},{24,28},{28,0},{1,5},{5... | collective-permute-start | bytes 49160 | tf_op jit(solution)/shard_map/ppermute | solution.py:333
  32.0 3.4 %collective-permute-start.1 = (f32[16,256]{1,0:T(8,128)S(1)}, f32[16,256]{1,0:T(8,128)S(1)}, u32[]{:S(2)}, u32[]{:S(2)}) collective-permute-start(f32[16,256]{1,0:T(8,128)S(1)} %get-tuple-element.23), channel_id=1, source_target_pairs={{0,28},{4,0},{8,4},{12,8},{16,12},{20,16},{24,20},{28,24},{1,29},{... | collective-permute-start | bytes 49160 | tf_op jit(solution)/shard_map/ppermute | solution.py:334
  34.7 24.9 %collective-permute-start.11 = (f32[3,64,256]{2,1,0:T(8,128)S(1)}, f32[3,64,256]{2,1,0:T(8,128)S(1)}, u32[]{:S(2)}, u32[]{:S(2)}) collective-permute-start(f32[3,64,256]{2,1,0:T(8,128)S(1)} %pad_maximum_fusion.refs_8_), channel_id=1, source_target_pairs={{0,64},{32,96},{64,128},{96,160},{128,192},{160,224},{192,0},{224,... | collective-permute-start | bytes 589832 | tf_op jit(solution)/shard_map/ppermute | solution.py:341
  35.4 2.2 %copy-start = (f32[1,8,8,64,256]{4,3,2,1,0:T(8,128)S(1)}, f32[1,8,8,64,256]{4,3,2,1,0:T(8,128)}, u32[]{:S(2)}) copy-start(f32[1,8,8,64,256]{4,3,2,1,0:T(8,128)} %param.16) | copy-start | bytes 12582916
  37.6 1.0 copy-start.5
  38.7 1.0 copy-start.8
  45.3 20.6 %copy-start.1 = (f32[1,8,8,64,256]{4,3,2,1,0:T(8,128)S(1)}, f32[1,8,8,64,256]{4,3,2,1,0:T(8,128)}, u32[]{:S(2)}) copy-start(f32[1,8,8,64,256]{4,3,2,1,0:T(8,128)} %param.16) | copy-start | bytes 12582916
  48.9 6.6 %collective-permute-start.6 = (f32[2,64,256]{2,1,0:T(8,128)S(1)}, f32[2,64,256]{2,1,0:T(8,128)S(1)}, u32[]{:S(2)}, u32[]{:S(2)}) collective-permute-start(f32[2,64,256]{2,1,0:T(8,128)S(1)} %get-tuple-element.28.refs_0_), channel_id=1, source_target_pairs={{0,192},{32,224},{64,0},{96,32},{128,64},{160,96},{192,128},{224,1... | collective-permute-start | bytes 393224 | tf_op jit(solution)/shard_map/ppermute | solution.py:341
  50.9 8.7 %collective-permute-start.7 = (f32[2,64,256]{2,1,0:T(8,128)S(1)}, f32[2,64,256]{2,1,0:T(8,128)S(1)}, u32[]{:S(2)}, u32[]{:S(2)}) collective-permute-start(f32[2,64,256]{2,1,0:T(8,128)S(1)} %get-tuple-element.28.refs_0_), channel_id=1, source_target_pairs={{0,32},{32,0},{64,96},{96,64},{128,160},{160,128},{192,224},{224,1... | collective-permute-start | bytes 393224 | tf_op jit(solution)/shard_map/ppermute | solution.py:343
  54.3 6.6 %collective-permute-start.5 = (f32[2,64,256]{2,1,0:T(8,128)S(1)}, f32[2,64,256]{2,1,0:T(8,128)S(1)}, u32[]{:S(2)}, u32[]{:S(2)}) collective-permute-start(f32[2,64,256]{2,1,0:T(8,128)S(1)} %get-tuple-element.28.refs_0_), channel_id=1, source_target_pairs={{0,128},{32,160},{64,192},{96,224},{128,0},{160,32},{192,64},{224,... | collective-permute-start | bytes 393224 | tf_op jit(solution)/shard_map/ppermute | solution.py:341
  55.5 8.5 %collective-permute-start.4 = (f32[2,64,256]{2,1,0:T(8,128)S(1)}, f32[2,64,256]{2,1,0:T(8,128)S(1)}, u32[]{:S(2)}, u32[]{:S(2)}) collective-permute-start(f32[2,64,256]{2,1,0:T(8,128)S(1)} %get-tuple-element.28.refs_0_), channel_id=1, source_target_pairs={{0,64},{32,96},{64,128},{96,160},{128,192},{160,224},{192,0},{224,... | collective-permute-start | bytes 393224 | tf_op jit(solution)/shard_map/ppermute | solution.py:341
  55.5 9.0 %collective-permute-start.10 = (f32[2,64,256]{2,1,0:T(8,128)S(1)}, f32[2,64,256]{2,1,0:T(8,128)S(1)}, u32[]{:S(2)}, u32[]{:S(2)}) collective-permute-start(f32[2,64,256]{2,1,0:T(8,128)S(1)} %collective-permute-done.6.refs_3_), channel_id=1, source_target_pairs={{0,32},{32,0},{64,96},{96,64},{128,160},{160,128},{192,224},{224,1... | collective-permute-start | bytes 393224 | tf_op jit(solution)/shard_map/ppermute | solution.py:343
  59.6 6.3 %collective-permute-start.17 = (f32[3,64,256]{2,1,0:T(8,128)S(1)}, f32[3,64,256]{2,1,0:T(8,128)S(1)}, u32[]{:S(2)}, u32[]{:S(2)}) collective-permute-start(f32[3,64,256]{2,1,0:T(8,128)S(1)} %collective-permute-done.13.refs_11_), channel_id=1, source_target_pairs={{0,32},{32,0},{64,96},{96,64},{128,160},{160,128},{192,224},{224,1... | collective-permute-start | bytes 589832 | tf_op jit(solution)/shard_map/ppermute | solution.py:343
  59.6 6.3 %collective-permute-start.16 = (f32[3,64,256]{2,1,0:T(8,128)S(1)}, f32[3,64,256]{2,1,0:T(8,128)S(1)}, u32[]{:S(2)}, u32[]{:S(2)}) collective-permute-start(f32[3,64,256]{2,1,0:T(8,128)S(1)} %collective-permute-done.12.refs_10_), channel_id=1, source_target_pairs={{0,32},{32,0},{64,96},{96,64},{128,160},{160,128},{192,224},{224,1... | collective-permute-start | bytes 589832 | tf_op jit(solution)/shard_map/ppermute | solution.py:343
  60.8 5.0 %collective-permute-start.15 = (f32[3,64,256]{2,1,0:T(8,128)S(1)}, f32[3,64,256]{2,1,0:T(8,128)S(1)}, u32[]{:S(2)}, u32[]{:S(2)}) collective-permute-start(f32[3,64,256]{2,1,0:T(8,128)S(1)} %collective-permute-done.11.refs_9_), channel_id=1, source_target_pairs={{0,32},{32,0},{64,96},{96,64},{128,160},{160,128},{192,224},{224,1... | collective-permute-start | bytes 589832 | tf_op jit(solution)/shard_map/ppermute | solution.py:343
  64.0 1.5 %collective-permute-start.9 = (f32[2,64,256]{2,1,0:T(8,128)S(1)}, f32[2,64,256]{2,1,0:T(8,128)S(1)}, u32[]{:S(2)}, u32[]{:S(2)}) collective-permute-start(f32[2,64,256]{2,1,0:T(8,128)S(1)} %collective-permute-done.5.refs_2_), channel_id=1, source_target_pairs={{0,32},{32,0},{64,96},{96,64},{128,160},{160,128},{192,224},{224,1... | collective-permute-start | bytes 393224 | tf_op jit(solution)/shard_map/ppermute | solution.py:343
  64.5 1.3 %collective-permute-start.8 = (f32[2,64,256]{2,1,0:T(8,128)S(1)}, f32[2,64,256]{2,1,0:T(8,128)S(1)}, u32[]{:S(2)}, u32[]{:S(2)}) collective-permute-start(f32[2,64,256]{2,1,0:T(8,128)S(1)} %collective-permute-done.4.refs_1_), channel_id=1, source_target_pairs={{0,32},{32,0},{64,96},{96,64},{128,160},{160,128},{192,224},{224,1... | collective-permute-start | bytes 393224 | tf_op jit(solution)/shard_map/ppermute | solution.py:343
  65.9 24.1 %copy-start.6 = (f32[8,64,256]{2,1,0:T(8,128)S(1)}, f32[8,64,256]{2,1,0:T(8,128)}, u32[]{:S(2)}) copy-start(f32[8,64,256]{2,1,0:T(8,128)} %kx_hi.1) | copy-start | bytes 1572868
  65.9 24.1 %copy-start.9 = (f32[8,64,256]{2,1,0:T(8,128)S(1)}, f32[8,64,256]{2,1,0:T(8,128)}, u32[]{:S(2)}) copy-start(f32[8,64,256]{2,1,0:T(8,128)} %param.15) | copy-start | bytes 1572868
  65.9 24.0 %copy-start.11 = (f32[8,64,256]{2,1,0:T(8,128)S(1)}, f32[8,64,256]{2,1,0:T(8,128)}, u32[]{:S(2)}) copy-start(f32[8,64,256]{2,1,0:T(8,128)} %param.13) | copy-start | bytes 1572868
  65.9 24.0 %copy-start.19 = (f32[1,48,8]{1,2,0:T(8,128)S(1)}, f32[1,48,8]{1,2,0:T(8,128)}, u32[]{:S(2)}) copy-start(f32[1,48,8]{1,2,0:T(8,128)} %param.22) | copy-start | bytes 4612
  65.9 24.0 %copy-start.22 = (s32[1,48,1]{1,2,0:T(1,128)S(1)}, s32[1,48,1]{1,2,0:T(1,128)}, u32[]{:S(2)}) copy-start(s32[1,48,1]{1,2,0:T(1,128)} %param.19) | copy-start | bytes 580
  65.9 24.0 %copy-start.25 = (s32[1,48]{1,0:T(1,128)S(1)}, s32[1,48]{1,0:T(1,128)}, u32[]{:S(2)}) copy-start(s32[1,48]{1,0:T(1,128)} %well.5) | copy-start | bytes 580
  65.9 24.0 %copy-start.28 = (s32[1,48]{1,0:T(1,128)S(1)}, s32[1,48]{1,0:T(1,128)}, u32[]{:S(2)}) copy-start(s32[1,48]{1,0:T(1,128)} %column.5) | copy-start | bytes 580
  73.0 17.0 %all-to-all-start.1 = ((f32[32,2,128]{2,1,0:T(2,128)}), f32[32,2,128]{2,1,0:T(2,128)S(1)}, u32[]{:S(2)}, u32[]{:S(2)}) async-start(f32[32,2,128]{2,1,0:T(2,128)} %get-tuple-element.36), calls=%async_computation.1 | async-start | bytes 65536 | tf_op jit(solution)/shard_map/all_to_all | solution.py:401
  81.2 6.8 %collective-permute-start.18 = (f32[8,256]{1,0:T(8,128)S(1)}, f32[8,256]{1,0:T(8,128)S(1)}, u32[]{:S(2)}, u32[]{:S(2)}) collective-permute-start(f32[8,256]{1,0:T(8,128)S(1)} %get-tuple-element.32), channel_id=1, source_target_pairs={{0,4},{4,8},{8,12},{12,16},{16,20},{20,24},{24,28},{28,0},{1,5},{5... | collective-permute-start | bytes 24584 | tf_op jit(solution)/shard_map/ppermute | solution.py:333
  82.5 5.5 %collective-permute-start.19 = (f32[8,256]{1,0:T(8,128)S(1)}, f32[8,256]{1,0:T(8,128)S(1)}, u32[]{:S(2)}, u32[]{:S(2)}) collective-permute-start(f32[8,256]{1,0:T(8,128)S(1)} %get-tuple-element.33), channel_id=1, source_target_pairs={{0,28},{4,0},{8,4},{12,8},{16,12},{20,16},{24,20},{28,24},{1,29},{... | collective-permute-start | bytes 24584 | tf_op jit(solution)/shard_map/ppermute | solution.py:334
  84.0 4.0 %collective-permute-start.20 = (f32[8,128]{1,0:T(8,128)S(1)}, f32[8,128]{1,0:T(8,128)S(1)}, u32[]{:S(2)}, u32[]{:S(2)}) collective-permute-start(f32[8,128]{1,0:T(8,128)S(1)} %get-tuple-element.34), channel_id=1, source_target_pairs={{0,1},{1,2},{2,3},{3,0},{4,5},{5,6},{6,7},{7,4},{8,9},{9,10},{10,1... | collective-permute-start | bytes 12296 | tf_op jit(solution)/shard_map/ppermute | solution.py:335
  85.2 2.8 %collective-permute-start.21 = (f32[8,128]{1,0:T(8,128)S(1)}, f32[8,128]{1,0:T(8,128)S(1)}, u32[]{:S(2)}, u32[]{:S(2)}) collective-permute-start(f32[8,128]{1,0:T(8,128)S(1)} %get-tuple-element.35), channel_id=1, source_target_pairs={{0,3},{1,0},{2,1},{3,2},{4,7},{5,4},{6,5},{7,6},{8,11},{9,8},{10,9... | collective-permute-start | bytes 12296 | tf_op jit(solution)/shard_map/ppermute | solution.py:336
  90.0 2.2 %copy-start.2 = (f32[1,8,8,64,256]{4,3,2,1,0:T(8,128)S(1)}, f32[1,8,8,64,256]{4,3,2,1,0:T(8,128)}, u32[]{:S(2)}) copy-start(f32[1,8,8,64,256]{4,3,2,1,0:T(8,128)} %param.16) | copy-start | bytes 12582916
  93.2 15.2 %copy-start.3 = (f32[1,8,8,64,256]{4,3,2,1,0:T(8,128)S(1)}, f32[1,8,8,64,256]{4,3,2,1,0:T(8,128)}, u32[]{:S(2)}) copy-start(f32[1,8,8,64,256]{4,3,2,1,0:T(8,128)} %param.16) | copy-start | bytes 12582916
  96.9 4.5 %collective-permute-start.24 = (f32[2,64,256]{2,1,0:T(8,128)S(1)}, f32[2,64,256]{2,1,0:T(8,128)S(1)}, u32[]{:S(2)}, u32[]{:S(2)}) collective-permute-start(f32[2,64,256]{2,1,0:T(8,128)S(1)} %get-tuple-element.39.refs_0_), channel_id=1, source_target_pairs={{0,192},{32,224},{64,0},{96,32},{128,64},{160,96},{192,128},{224,1... | collective-permute-start | bytes 393224 | tf_op jit(solution)/shard_map/ppermute | solution.py:341
  97.1 7.0 %collective-permute-start.23 = (f32[2,64,256]{2,1,0:T(8,128)S(1)}, f32[2,64,256]{2,1,0:T(8,128)S(1)}, u32[]{:S(2)}, u32[]{:S(2)}) collective-permute-start(f32[2,64,256]{2,1,0:T(8,128)S(1)} %get-tuple-element.39.refs_0_), channel_id=1, source_target_pairs={{0,128},{32,160},{64,192},{96,224},{128,0},{160,32},{192,64},{224,... | collective-permute-start | bytes 393224 | tf_op jit(solution)/shard_map/ppermute | solution.py:341
  98.4 8.0 %collective-permute-start.22 = (f32[2,64,256]{2,1,0:T(8,128)S(1)}, f32[2,64,256]{2,1,0:T(8,128)S(1)}, u32[]{:S(2)}, u32[]{:S(2)}) collective-permute-start(f32[2,64,256]{2,1,0:T(8,128)S(1)} %get-tuple-element.39.refs_0_), channel_id=1, source_target_pairs={{0,64},{32,96},{64,128},{96,160},{128,192},{160,224},{192,0},{224,... | collective-permute-start | bytes 393224 | tf_op jit(solution)/shard_map/ppermute | solution.py:341
  99.0 9.1 %collective-permute-start.25 = (f32[2,64,256]{2,1,0:T(8,128)S(1)}, f32[2,64,256]{2,1,0:T(8,128)S(1)}, u32[]{:S(2)}, u32[]{:S(2)}) collective-permute-start(f32[2,64,256]{2,1,0:T(8,128)S(1)} %get-tuple-element.39.refs_0_), channel_id=1, source_target_pairs={{0,32},{32,0},{64,96},{96,64},{128,160},{160,128},{192,224},{224,1... | collective-permute-start | bytes 393224 | tf_op jit(solution)/shard_map/ppermute | solution.py:343
  101.4 6.7 %collective-permute-start.28 = (f32[2,64,256]{2,1,0:T(8,128)S(1)}, f32[2,64,256]{2,1,0:T(8,128)S(1)}, u32[]{:S(2)}, u32[]{:S(2)}) collective-permute-start(f32[2,64,256]{2,1,0:T(8,128)S(1)} %collective-permute-done.24.refs_3_), channel_id=1, source_target_pairs={{0,32},{32,0},{64,96},{96,64},{128,160},{160,128},{192,224},{224,1... | collective-permute-start | bytes 393224 | tf_op jit(solution)/shard_map/ppermute | solution.py:343
  104.2 3.9 %collective-permute-start.27 = (f32[2,64,256]{2,1,0:T(8,128)S(1)}, f32[2,64,256]{2,1,0:T(8,128)S(1)}, u32[]{:S(2)}, u32[]{:S(2)}) collective-permute-start(f32[2,64,256]{2,1,0:T(8,128)S(1)} %collective-permute-done.23.refs_2_), channel_id=1, source_target_pairs={{0,32},{32,0},{64,96},{96,64},{128,160},{160,128},{192,224},{224,1... | collective-permute-start | bytes 393224 | tf_op jit(solution)/shard_map/ppermute | solution.py:343
  106.4 2.1 %collective-permute-start.26 = (f32[2,64,256]{2,1,0:T(8,128)S(1)}, f32[2,64,256]{2,1,0:T(8,128)S(1)}, u32[]{:S(2)}, u32[]{:S(2)}) collective-permute-start(f32[2,64,256]{2,1,0:T(8,128)S(1)} %collective-permute-done.22.refs_1_), channel_id=1, source_target_pairs={{0,32},{32,0},{64,96},{96,64},{128,160},{160,128},{192,224},{224,1... | collective-permute-start | bytes 393224 | tf_op jit(solution)/shard_map/ppermute | solution.py:343
  (14 other events, 10.7 us)

commit v2 on v1

v2 whole, which is shorter than its diff:
```python
import functools

import jax
import jax.numpy as jnp
from jax import lax
from jax.experimental import pallas as pl
from jax.experimental.pallas import tpu as pltpu
from jax.sharding import PartitionSpec as P

ITERS = 2
EDGE_MIB = 60
WELLS_MIB = 8
LZ = 8
CX = 64
CY = 256
SLOTS = 48
WELLS = 256
TILES = 32
GROUPS = 8
F32 = jnp.float32
VMEM = pl.BlockSpec(memory_space=pltpu.VMEM)
SMEM = pl.BlockSpec(memory_space=pltpu.SMEM)
ANY = pl.BlockSpec(memory_space=pltpu.HBM)


def shape(*dims):
    return jax.ShapeDtypeStruct(dims, F32)


def lane_ids(rows, lanes):
    return lax.broadcasted_iota(jnp.int32, (rows, lanes), 1)


def x_edges(ref, row, out, first):
    for l in range(LZ):
        out[first + l : first + l + 1, :] = ref[l * CX + row : l * CX + row + 1, :]


def y_edges(pieces):
    lanes = lane_ids(2 * CX, 128)
    packed = jnp.zeros((2 * CX, 128), F32)
    row = 0
    for ref, column in pieces:
        start = (column // 128) * 128
        for r in range(LZ // 2):
            block = ref[r * 2 * CX : (r + 1) * 2 * CX, start : start + 128]
            value = block[:, column - start : column - start + 1]
            packed = jnp.where(lanes == row, value, packed)
            row += 1
    return packed.T


def gather_slots(split_ref, column_ref):
    lanes = lane_ids(LZ, 128)
    found = jnp.zeros((LZ, 128), F32)
    for s in range(SLOTS):
        column = column_ref[0, s]
        x = column // CY
        y = column % CY
        half = y // 128
        lane = y % 128
        block = split_ref.at[half][pl.ds(x, LZ, stride=CX), :]
        value = jnp.sum(jnp.where(lanes == lane, block, 0.0), axis=1, keepdims=True)
        found = jnp.where(lanes == s, value, found)
    return found


def well_columns(rows):
    block = jnp.concatenate(rows + [jnp.zeros((8 - len(rows), 128), F32)], axis=0)
    turned = block.T
    return [turned[:, i : i + 1] for i in range(len(rows))]


def pad_lanes(value):
    return jnp.concatenate([value, jnp.zeros((value.shape[0], 128 - value.shape[1]), value.dtype)], axis=1)


def send_partials(out, values):
    for t in range(TILES):
        out[t] = values


def live_index(index_ref, count_ref):
    index = pad_lanes(index_ref[...])
    return jnp.where(lane_ids(LZ, 128) < count_ref[0, 0], index, 0.0)


def well_row(owner_ref, well_ref):
    return pad_lanes((owner_ref[...] * 8 + well_ref[...]).astype(F32))


def totals_by_well(column, well_column):
    ids = well_column[:SLOTS].astype(jnp.int32)
    halves = []
    for half in range(2):
        hit = ids == lane_ids(SLOTS, 128) + half * 128
        halves.append(jnp.sum(jnp.where(hit, column[:SLOTS], 0.0), axis=0, keepdims=True))
    return jnp.concatenate(halves, axis=0)


def own_rates(rate_ref):
    tile = lax.axis_index("gx") * 4 + lax.axis_index("gy")
    rate = rate_ref[...]
    tiled = jnp.concatenate([rate] * 16, axis=1)
    lanes = lane_ids(1, 128)
    halves = [jnp.where((lanes + half * 128) // 8 == tile, tiled, 0.0) for half in range(2)]
    return jnp.concatenate(halves, axis=0)


def load(copies, sem):
    started = [pltpu.make_async_copy(source, target, sem.at[n]) for n, (source, target) in enumerate(copies)]
    for copy in started:
        copy.start()
    return started


def halves_of(split, span):
    return jnp.concatenate([split[0, span, :], split[1, span, :]], axis=1)


def edges_kernel(pressure, perm_x, perm_y, inverse, xlo, xhi, ylo, yhi, fixed, split, kx_lo, kx_hi, ky, sem):
    copies = load(
        [(pressure.at[:, half * 128 : half * 128 + 128], split.at[half]) for half in range(2)]
        + [(perm_x.at[:, 0:8], kx_lo), (perm_x.at[:, CX - 8 : CX], kx_hi), (perm_y, ky)]
        + [(inverse.at[LZ - 1, 0], fixed.at[0]), (inverse.at[0, LZ - 1], fixed.at[1]), (inverse.at[0, 0], fixed.at[2])],
        sem,
    )
    for copy in copies[:5]:
        copy.wait()
    split_x_edges(split, xlo, xhi)
    for l in range(LZ):
        xlo[LZ + l : LZ + l + 1, :] = kx_lo[l, 0:1, :]
        xhi[LZ + l : LZ + l + 1, :] = kx_hi[l, 7:8, :]
    turned = y_edges([(split.at[0], 0), (ky, 0), (split.at[1], 127), (ky, CY - 1)])
    ylo[...] = turned[0:8]
    yhi[...] = turned[8:16]
    for copy in copies[5:]:
        copy.wait()


def split_x_edges(split, xlo, xhi):
    for l in range(LZ):
        for half in range(2):
            lanes = slice(half * 128, half * 128 + 128)
            xlo[l : l + 1, lanes] = split[half, l * CX : l * CX + 1, :]
            xhi[l : l + 1, lanes] = split[half, l * CX + CX - 1 : l * CX + CX, :]


def wells_first_kernel(
    pressure,
    index,
    owner,
    well,
    rate,
    column,
    count,
    partials,
    at_slots,
    live_out,
    wells_out,
    split,
    index_v,
    owner_v,
    well_v,
    rate_v,
    column_s,
    count_s,
    sem,
):
    copies = load(
        [(pressure.at[:, half * 128 : half * 128 + 128], split.at[half]) for half in range(2)]
        + [
            (column, column_s),
            (count, count_s),
            (index, index_v),
            (owner, owner_v),
            (well, well_v),
            (rate, rate_v),
        ],
        sem,
    )
    for copy in copies:
        copy.wait()
    at = gather_slots(split, column_s)
    at_slots[...] = at
    live = live_index(index_v, count_s)
    live_out[...] = live
    weighted = jnp.sum(live * at, axis=0, keepdims=True)
    total = jnp.sum(live, axis=0, keepdims=True)
    wells = well_row(owner_v, well_v)
    wells_out[...] = wells
    weighted_c, total_c, wells_c = well_columns([weighted, total, wells])
    values = jnp.concatenate(
        [totals_by_well(weighted_c, wells_c) + own_rates(rate_v), totals_by_well(total_c, wells_c)], axis=0
    )
    send_partials(partials, values)


def wells_next_kernel(split, live, wells, rate, column, partials, at_slots, rate_v, column_s, sem):
    copies = load([(column, column_s), (rate, rate_v)], sem)
    for copy in copies:
        copy.wait()
    at = gather_slots(split, column_s)
    at_slots[...] = at
    weighted = jnp.sum(live[...] * at, axis=0, keepdims=True)
    weighted_c, wells_c = well_columns([weighted, wells[...]])
    send_partials(partials, totals_by_well(weighted_c, wells_c) + own_rates(rate_v))


def solve_kernel(first, *refs):
    if first:
        (split, source, kx, ky, inverse, lower, from_xlo, from_xhi, from_ylo, from_yhi, partials, *refs) = refs
        kx_lo, kx_hi, ky_lo, ky_hi = from_xlo, from_xhi, from_ylo, from_yhi
        (live, wells, at_slots, column, solved, carried, sums_out, rhs, column_s, sem) = refs
    else:
        (split, source, kx, ky, inverse, lower, from_xlo, from_xhi, from_ylo, from_yhi, partials, *refs) = refs
        (kx_lo, kx_hi, ky_lo, ky_hi, sums, *refs) = refs
        (live, wells, at_slots, column, solved, carried, flow_out, rhs, column_s, sem) = refs
    copies = load([(column, column_s)], sem)
    gx, gy = lax.axis_index("gx"), lax.axis_index("gy")
    total = partials[0]
    for t in range(1, TILES):
        total = total + partials[t]
    if first:
        numerator, index_sum = total[0:2], total[2:4]
        sums_out[...] = index_sum
    else:
        numerator, index_sum = total, sums[...]
    bottom_hole = numerator / (index_sum + 1.0)
    (wells_c,) = well_columns([wells[...]])
    ids = wells_c[:SLOTS].astype(jnp.int32)
    held = jnp.zeros((SLOTS, 128), F32)
    for half in range(2):
        hit = ids == lane_ids(SLOTS, 128) + half * 128
        held = held + jnp.where(hit, bottom_hole[half : half + 1], 0.0)
    hole = jnp.sum(held, axis=1, keepdims=True)
    hole = jnp.broadcast_to(hole, (SLOTS, 128))
    hole = jnp.concatenate([hole, jnp.zeros((128 - SLOTS, 128), F32)], axis=0).T[0:1]
    flow = live[...] * (hole - at_slots[...])
    if not first:
        flow_out[...] = flow[:, :SLOTS]

    rows = lax.broadcasted_iota(jnp.int32, (CX, CY), 0)
    lanes = lane_ids(CX, CY)
    ylo_c = from_ylo[...].T
    yhi_c = from_yhi[...].T
    kylo_c = ky_lo[...].T
    kyhi_c = ky_hi[...].T

    def y_column(turned, base, l):
        s = (l % 2) * CX
        return turned[s : s + CX, base + l // 2 : base + l // 2 + 1]

    for l in range(LZ):
        span = slice(l * CX, (l + 1) * CX)
        f = halves_of(split, span)
        k = kx[span, :]
        f_after = jnp.where(gx < 7, from_xhi[l : l + 1, :], 0.0)
        k_after = kx_hi[LZ + l : LZ + l + 1, :]
        f_before = jnp.where(gx > 0, from_xlo[l : l + 1, :], 0.0)
        k_before = kx_lo[LZ + l : LZ + l + 1, :]
        f_east = jnp.where(rows == CX - 1, f_after, pltpu.roll(f, CX - 1, 0))
        k_east = jnp.where(rows == CX - 1, k_after, pltpu.roll(k, CX - 1, 0))
        face = k + k_east
        west_first = (k[0:1, :] + k_before) * f_before
        lateral = face * f_east + jnp.where(rows == 0, west_first, pltpu.roll(face * f, 1, 0))
        k = ky[span, :]
        f_after = jnp.where(gy < 3, y_column(yhi_c, 0, l), 0.0)
        k_after = y_column(kyhi_c, 4, l)
        f_before = jnp.where(gy > 0, y_column(ylo_c, 0, l), 0.0)
        k_before = y_column(kylo_c, 4, l)
        f_north = jnp.where(lanes == CY - 1, f_after, pltpu.roll(f, CY - 1, 1))
        k_north = jnp.where(lanes == CY - 1, k_after, pltpu.roll(k, CY - 1, 1))
        face = k + k_north
        south_first = (k[:, 0:1] + k_before) * f_before
        lateral = lateral + face * f_north + jnp.where(lanes == 0, south_first, pltpu.roll(face * f, 1, 1))
        value = source[span, :] + 0.5 * lateral
        rhs[0, span, :] = value[:, :128]
        rhs[1, span, :] = value[:, 128:]

    for copy in copies:
        copy.wait()
    lanes8 = lane_ids(LZ, 128)
    for s in range(SLOTS):
        place = column_s[0, s]
        x = place // CY
        y = place % CY
        half = y // 128
        lane = y % 128
        part = rhs.at[half]
        where = (pl.ds(x, LZ, stride=CX), slice(None))
        part[where] = part[where] + jnp.where(lanes8 == lane, flow[:, s : s + 1], 0.0)

    def block(b, carry):
        at = pl.multiple_of(b * 8, 8)
        right = [halves_of(rhs, pl.ds(j * CX + at, 8)) for j in range(LZ)]
        here = pl.ds(at, 8)
        for i in range(LZ):
            total = inverse[i, 0, here, :] * right[0]
            for j in range(1, LZ):
                total = total + inverse[i, j, here, :] * right[j]
            solved[pl.ds(i * CX + at, 8), :] = total
            if i == 0:
                carried[1, here, :] = total
            if i == LZ - 1:
                low = lower[here, :]
                carried[0, here, :] = total + inverse[i, i, here, :] * low - low
        return carry

    lax.fori_loop(0, CX // 8, block, 0)


def sweep_kernel(last, *refs):
    cds, fixed, refs = refs[:8], refs[8:16], refs[16:]
    if last:
        solved, inverse, field = refs
    else:
        solved, inverse, split, lower, xlo, xhi, ylo, yhi = refs
    me = lax.axis_index("layer")

    def position(own):
        def of(planes, g):
            distance = (own // 2 - g // 2) % 4
            return planes[distance + 4 * ((own ^ g) & 1)]

        def block(b, carry):
            here = pl.ds(pl.multiple_of(b * 8, 8), 8)
            upper = jnp.zeros((8, CY), F32)
            uppers = [upper]
            for g in range(GROUPS - 1):
                upper = of(fixed, g)[0, here, :] * upper + of(cds, g)[0, here, :]
                uppers.append(upper)
            low = jnp.zeros((8, CY), F32)
            for g in range(GROUPS - 1, own, -1):
                step = of(cds, g)[1, here, :] + of(fixed, g)[2, here, :] * uppers[g] - uppers[g]
                low = of(fixed, g)[1, here, :] * low + step
            for i in range(LZ):
                span = pl.ds(pl.multiple_of(i * CX + b * 8, 8), 8)
                value = solved[span, :] + inverse[i, 0, here, :] * uppers[own] + inverse[i, LZ - 1, here, :] * low
                if last:
                    field[span, :] = value
                else:
                    split[0, span, :] = value[:, :128]
                    split[1, span, :] = value[:, 128:]
            if not last:
                lower[here, :] = low
            return carry

        @pl.when(me == own)
        def _():
            lax.fori_loop(0, CX // 8, block, 0)

    for own in range(GROUPS):
        position(own)
    if last:
        return
    split_x_edges(split, xlo, xhi)
    turned = y_edges([(split.at[0], 0), (split.at[1], 127)])
    ylo[...] = turned[0:8]
    yhi[...] = jnp.concatenate([turned[4:8], turned[0:4]], axis=0)


def params(mib=8):
    return pltpu.CompilerParams(vmem_limit_bytes=mib * 1024 * 1024)


def around(n, step):
    return [(i, (i + step) % n) for i in range(n)]


def from_sides(xlo, xhi, ylo, yhi):
    return (
        lax.ppermute(xhi, "gx", around(8, 1)),
        lax.ppermute(xlo, "gx", around(8, -1)),
        lax.ppermute(yhi, "gy", around(4, 1)),
        lax.ppermute(ylo, "gy", around(4, -1)),
    )


def all_groups(value):
    own = [value] + [lax.ppermute(value, "layer", around(8, 2 * d)) for d in range(1, 4)]
    swap = [(i, i ^ 1) for i in range(8)]
    return own + [lax.ppermute(v, "layer", swap) for v in own]


def shards(
    pressure,
    source,
    perm_x,
    perm_y,
    line_inverse,
    robin_below,
    tile_count,
    perf_owner,
    perf_well,
    perf_column,
    perf_index,
    well_rate,
):
    rows = LZ * CX
    pressure = pressure.reshape(rows, CY)
    source = source.reshape(rows, CY)
    inverse = line_inverse[0]
    lower = robin_below[0]
    owner = perf_owner[0].T
    index = perf_index[0].T

    kx = perm_x.reshape(rows, CY)
    ky = perm_y.reshape(rows, CY)
    *edges, fixed = pl.pallas_call(
        edges_kernel,
        out_shape=(shape(16, CY), shape(16, CY), shape(8, 128), shape(8, 128), shape(3, CX, CY)),
        in_specs=[ANY] * 4,
        out_specs=(VMEM,) * 5,
        scratch_shapes=[
            pltpu.VMEM((2, rows, 128), F32),
            pltpu.VMEM((LZ, 8, CY), F32),
            pltpu.VMEM((LZ, 8, CY), F32),
            pltpu.VMEM((rows, CY), F32),
            pltpu.SemaphoreType.DMA((8,)),
        ],
        compiler_params=params(EDGE_MIB),
        name="first_edges",
    )(pressure, perm_x, ky, inverse)
    k_sides = sides = from_sides(*edges)
    fixed = all_groups(fixed)
    partials, at_slots, live, wells, field = pl.pallas_call(
        wells_first_kernel,
        out_shape=(
            shape(TILES, 4, 128),
            shape(LZ, 128),
            shape(LZ, 128),
            shape(1, 128),
            shape(2, rows, 128),
        ),
        in_specs=[ANY] * 7,
        out_specs=(VMEM,) * 5,
        scratch_shapes=[
            pltpu.VMEM((LZ, SLOTS), F32),
            pltpu.VMEM((1, SLOTS), jnp.int32),
            pltpu.VMEM((1, SLOTS), jnp.int32),
            pltpu.VMEM((1, 8), F32),
            pltpu.SMEM((1, SLOTS), jnp.int32),
            pltpu.SMEM((1, 1), jnp.int32),
            pltpu.SemaphoreType.DMA((8,)),
        ],
        compiler_params=params(WELLS_MIB),
        name="first_wells",
    )(pressure, index, owner, perf_well, well_rate, perf_column, tile_count)
    sums = None
    for sweep_step in range(ITERS):
        first, last = sweep_step == 0, sweep_step == ITERS - 1
        tied = lax.optimization_barrier((partials, *sides))
        partials, sides = tied[0], tied[1:]
        if first:
            k_sides = sides
        spread = lax.all_to_all(partials, ("gx", "gy"), split_axis=0, concat_axis=0, tiled=True)
        extra = () if first else (*k_sides, sums)
        solved, carried, small = pl.pallas_call(
            functools.partial(solve_kernel, first),
            out_shape=(shape(rows, CY), shape(2, CX, CY), shape(2, 128) if first else shape(LZ, SLOTS)),
            in_specs=[VMEM] * (14 + len(extra)) + [ANY],
            out_specs=(VMEM,) * 3,
            scratch_shapes=[
                pltpu.VMEM((2, rows, 128), F32),
                pltpu.SMEM((1, SLOTS), jnp.int32),
                pltpu.SemaphoreType.DMA((1,)),
            ],
            compiler_params=params(),
            name="solve_lines",
        )(field, source, kx, ky, inverse, lower, *sides, spread, *extra, live, wells, at_slots, perf_column)
        groups = all_groups(carried)
        if last:
            flow = small
            (field,) = pl.pallas_call(
                functools.partial(sweep_kernel, True),
                out_shape=(shape(rows, CY),),
                in_specs=[VMEM] * 18,
                out_specs=(VMEM,),
                compiler_params=params(),
                name="sweep_last",
            )(*groups, *fixed, solved, inverse)
            break
        sums = small
        field, lower, *edges = pl.pallas_call(
            functools.partial(sweep_kernel, False),
            out_shape=(
                shape(2, rows, 128),
                shape(CX, CY),
                shape(8, CY),
                shape(8, CY),
                shape(8, 128),
                shape(8, 128),
            ),
            in_specs=[VMEM] * 18,
            out_specs=(VMEM,) * 6,
            compiler_params=params(),
            name="sweep_mid",
        )(*groups, *fixed, solved, inverse)
        sides = from_sides(*edges)
        partials, at_slots = pl.pallas_call(
            wells_next_kernel,
            out_shape=(shape(TILES, 2, 128), shape(LZ, 128)),
            in_specs=[VMEM] * 3 + [ANY] * 2,
            out_specs=(VMEM,) * 2,
            scratch_shapes=[
                pltpu.VMEM((1, 8), F32),
                pltpu.SMEM((1, SLOTS), jnp.int32),
                pltpu.SemaphoreType.DMA((2,)),
            ],
            compiler_params=params(),
            name="next_wells",
        )(field, live, wells, well_rate, perf_column)
    return (field.reshape(LZ, CX, CY), flow.T[None])


def solution(mesh):
    placed = (
        P("layer", "gx", "gy"),
        P("layer", "gx", "gy"),
        P("layer", "gx", "gy"),
        P("layer", "gx", "gy"),
        P("layer", None, None, "gx", "gy"),
        P("layer", "gx", "gy"),
        P("layer", ("gx", "gy")),
        P("layer", ("gx", "gy"), None),
        P("layer", ("gx", "gy")),
        P("layer", ("gx", "gy")),
        P("layer", ("gx", "gy"), None),
        P("layer", ("gx", "gy")),
    )
    return jax.shard_map(
        shards,
        mesh=mesh,
        in_specs=placed,
        out_specs=(P("layer", "gx", "gy"), P("layer", ("gx", "gy"), None)),
        check_vma=False,
    )
```

time: 114 us -> 103 us (0.904)
  blocking collectives: 0 us -> 29.8 us
  local copies, waits for them, and re-layouts: 21.8 us -> 2.24 us
  starting transfers between devices: 59.4 us -> 45.6 us
  Pallas kernels: 20.6 us -> 13.9 us
    all_to_all x0 -> x2, blocking collectives: none -> 29.8 us  [shards(): lax.all_to_all(partials, ('gx', 'gy'), split_axis=0, concat_axis=0, tiled...]
    all_to_all x2 -> x0, starting transfers between devices: 19.5 us -> none  [shards(): lax.all_to_all(partials, ('gx', 'gy'), split_axis=0, concat_axis=0, tiled...]
    unnamed x62 -> x26, local copies, waits for them, and re-layouts: 20.3 us -> 2.24 us
    pallas_call x1, Pallas kernels: 4.92 us -> 1.18 us  [shards(): pl.pallas_call(functools.partial(sweep_kernel, True), out_shape=(shape(ro...]
    ppermute x2, starting transfers between devices: 2.76 us -> 6.04 us  [from_sides(): lax.ppermute(xlo, 'gx', around(8, -1))]
    ppermute x12, starting transfers between devices: 21.6 us -> 24.6 us  [all_groups(): return own + [lax.ppermute(v, 'layer', swap) for v in own]]
    pallas_call x2 -> x4, Pallas kernels: 8.42 us -> 6.03 us  [the longest x1 2.54 us: shards(): pl.pallas_call(edges_kernel, out_shape=(shape(16, CY), shape(16, CY), sha...]
    all_to_all x2 -> x0, waiting for transfers between devices: 1.93 us -> none  [shards(): lax.all_to_all(partials, ('gx', 'gy'), split_axis=0, concat_axis=0, tiled...]
  transfers between devices with their start and end apart: 31 -> 29, of which waited for: 9 -> 8; matrix products, arithmetic and copies ran while one was open for 1% -> 0% of each run, Pallas kernels for 5% -> 6%
where the time goes in v2:
time: 103 us; the launch traced here: 102 us
  starting transfers between devices  45.6 us (44%)
  blocking collectives  29.8 us (29%)
  Pallas kernels  13.9 us (13%)
  waiting for transfers between devices  9.19 us (9%)
  local copies, waits for them, and re-layouts  2.24 us (2%)
  between operations  1.56 us (2%)
    all_to_all x2, blocking collectives, shards(): lax.all_to_all(partials, ('gx', 'gy'), split_axis=0, concat_axis=0, tiled...  29.8 us
    ppermute x12, starting transfers between devices, all_groups(): return own + [lax.ppermute(v, 'layer', swap) for v in own]  24.6 us
    ppermute x9, starting transfers between devices, all_groups(): lax.ppermute(value, 'layer', around(8, 2 * d))  7.29 us
    pallas_call x2, Pallas kernels, shards(): pl.pallas_call(functools.partial(solve_kernel, first), out_shape=(shape(r...  6.73 us
    ppermute x2, starting transfers between devices, from_sides(): lax.ppermute(xlo, 'gx', around(8, -1))  6.04 us
    ppermute x2, starting transfers between devices, from_sides(): lax.ppermute(ylo, 'gy', around(4, -1))  3.9 us
    ppermute x9, waiting for transfers between devices, all_groups(): lax.ppermute(value, 'layer', around(8, 2 * d))  3.02 us
    ppermute x2, waiting for transfers between devices, from_sides(): lax.ppermute(yhi, 'gy', around(4, 1))  2.65 us
  transfers between devices with their start and end apart: 29, of which 8 were waited for; matrix products, arithmetic and copies ran while one was open for 0% of the time, Pallas kernels for 6%

profile of v2, /device:TPU:1, one launch (start us, length us, event | category | flops | bytes accessed | tf_op | source)
XLA Modules:
  0.0 102.4 jit_solution(12203955344215742681)
XLA Ops:
  0.7 2.5 %first_edges.1 = (f32[16,256]{1,0:T(8,128)}, f32[16,256]{1,0:T(8,128)}, f32[8,128]{1,0:T(8,128)}, f32[8,128]{1,0:T(8,128)}, f32[3,64,256]{2,1,0:T(8,128)}) custom-call(f32[512,256]{1,0:T(8,128)} %bitcast.26, f32[8,64,256]{2,1,0:T(8,128)} %perm_x.1, f32[512,256]{1,0:T(8,128)} %bitcast.21, f32[8,8,64,256]{3,2,1,0:T(8,128)} %bitcast.14), custom_call_target="tpu_custom_call" | custom-call | tf_op jit(solution)/shard_map/first_edges/pallas_call | solution.py:410
  3.3 0.0 copy-start.6
  3.3 3.3 %collective-permute-start.14 = (f32[3,64,256]{2,1,0:T(8,128)}, f32[3,64,256]{2,1,0:T(8,128)S(1)}, u32[]{:S(2)}, u32[]{:S(2)}) collective-permute-start(f32[3,64,256]{2,1,0:T(8,128)} %get-tuple-element.51.refs_8_), channel_id=1, source_target_pairs={{0,32},{32,0},{64,96},{96,64},{128,160},{160,128},{192,224},{224,1... | collective-permute-start | bytes 589832 | tf_op jit(solution)/shard_map/ppermute | solution.py:383
  6.6 0.8 collective-permute-start.13
  7.4 1.6 %collective-permute-start = (f32[16,256]{1,0:T(8,128)}, f32[16,256]{1,0:T(8,128)S(1)}, u32[]{:S(2)}, u32[]{:S(2)}) collective-permute-start(f32[16,256]{1,0:T(8,128)} %get-tuple-element.38), channel_id=1, source_target_pairs={{0,4},{4,8},{8,12},{12,16},{16,20},{20,24},{24,28},{28,0},{1,5},{5... | collective-permute-start | bytes 49160 | tf_op jit(solution)/shard_map/ppermute | solution.py:373
  9.0 3.9 %collective-permute-start.1 = (f32[16,256]{1,0:T(8,128)}, f32[16,256]{1,0:T(8,128)S(1)}, u32[]{:S(2)}, u32[]{:S(2)}) collective-permute-start(f32[16,256]{1,0:T(8,128)} %get-tuple-element.39), channel_id=1, source_target_pairs={{0,28},{4,0},{8,4},{12,8},{16,12},{20,16},{24,20},{28,24},{1,29},{... | collective-permute-start | bytes 49160 | tf_op jit(solution)/shard_map/ppermute | solution.py:374
  13.0 1.3 %collective-permute-start.2 = (f32[8,128]{1,0:T(8,128)}, f32[8,128]{1,0:T(8,128)S(1)}, u32[]{:S(2)}, u32[]{:S(2)}) collective-permute-start(f32[8,128]{1,0:T(8,128)} %get-tuple-element.40), channel_id=1, source_target_pairs={{0,1},{1,2},{2,3},{3,0},{4,5},{5,6},{6,7},{7,4},{8,9},{9,10},{10,1... | collective-permute-start | bytes 12296 | tf_op jit(solution)/shard_map/ppermute | solution.py:375
  14.3 2.6 %collective-permute-done.2.refs_8_.refs_13_ = f32[8,128]{1,0:T(8,128)S(1)} collective-permute-done((f32[8,128]{1,0:T(8,128)}, f32[8,128]{1,0:T(8,128)S(1)}, u32[]{:S(2)}, u32[]{:S(2)}) %collective-permute-start.2) | collective-permute-done | bytes 4128 | tf_op jit(solution)/shard_map/ppermute | solution.py:375
  16.9 1.5 %collective-permute-start.3 = (f32[8,128]{1,0:T(8,128)}, f32[8,128]{1,0:T(8,128)S(1)}, u32[]{:S(2)}, u32[]{:S(2)}) collective-permute-start(f32[8,128]{1,0:T(8,128)} %get-tuple-element.41), channel_id=1, source_target_pairs={{0,3},{1,0},{2,1},{3,2},{4,7},{5,4},{6,5},{7,6},{8,11},{9,8},{10,9... | collective-permute-start | bytes 12296 | tf_op jit(solution)/shard_map/ppermute | solution.py:376
  18.4 1.2 %collective-permute-done.3.refs_9_.refs_14_ = f32[8,128]{1,0:T(8,128)S(1)} collective-permute-done((f32[8,128]{1,0:T(8,128)}, f32[8,128]{1,0:T(8,128)S(1)}, u32[]{:S(2)}, u32[]{:S(2)}) %collective-permute-start.3) | collective-permute-done | bytes 4128 | tf_op jit(solution)/shard_map/ppermute | solution.py:376
  19.6 0.5 collective-permute-start.12
  20.1 0.6 collective-permute-start.11
  21.4 1.5 %first_wells.1 = (f32[32,4,128]{2,1,0:T(4,128)S(1)}, f32[8,128]{1,0:T(8,128)S(1)}, f32[8,128]{1,0:T(8,128)S(1)}, f32[1,128]{1,0:T(1,128)S(1)}, f32[2,512,128]{2,1,0:T(8,128)S(1)}) custom-call(f32[512,256]{1,0:T(8,128)S(1)} %bitcast.27, f32[8,48]{1,0:T(8,128)S(1)} %bitcast.29, s32[1,48]{1,0:T(1,128)S(1)} %bitcast.30, s32[1,48]{1,0:T(1,128)S(1)} %copy-done.12, ...), custom_call_target="tpu_custom_call" | custom-call | tf_op jit(solution)/shard_map/first_wells/pallas_call | solution.py:427
  22.9 17.0 %all_to_all.10.refs_10_ = f32[32,4,128]{2,1,0:T(4,128)S(1)} all-to-all(f32[32,4,128]{2,1,0:T(4,128)S(1)} %get-tuple-element.46), channel_id=1, replica_groups=mesh['layer'=8,'gx'=8,'gy'=4] {'gx','gy'}, dimensions={0} | all-to-all | bytes 131072 | tf_op jit(solution)/shard_map/all_to_all | solution.py:457
  39.9 0.0 copy-start
  39.9 2.2 %copy-done = f32[1,8,8,64,256]{4,3,2,1,0:T(8,128)S(1)} copy-done((f32[1,8,8,64,256]{4,3,2,1,0:T(8,128)S(1)}, f32[1,8,8,64,256]{4,3,2,1,0:T(8,128)}, u32[]{:S(2)}) %copy-start) | copy-done | bytes 4194328
  42.1 3.1 %solve_lines.2 = (f32[512,256]{1,0:T(8,128)S(1)}, f32[2,64,256]{2,1,0:T(8,128)S(1)}, f32[2,128]{1,0:T(2,128)S(1)}) custom-call(f32[2,512,128]{2,1,0:T(8,128)S(1)} %get-tuple-element.36.refs_0_, f32[512,256]{1,0:T(8,128)S(1)} %bitcast.24, f32[512,256]{1,0:T(8,128)S(1)} %bitcast.19, f32[512,256]{1,0:T(8,128)S(1)} %bitcast.22, f32[8,8,64,256]{3,2,1,0:T(8,128)S(1)} %bitcast.15, ...), custom_call_target="tpu_custom_call" | custom-call | tf_op jit(solution)/shard_map/solve_lines/pallas_call | solution.py:459
  45.2 5.0 %collective-permute-start.7 = (f32[2,64,256]{2,1,0:T(8,128)S(1)}, f32[2,64,256]{2,1,0:T(8,128)S(1)}, u32[]{:S(2)}, u32[]{:S(2)}) collective-permute-start(f32[2,64,256]{2,1,0:T(8,128)S(1)} %get-tuple-element.50.refs_0_), channel_id=1, source_target_pairs={{0,32},{32,0},{64,96},{96,64},{128,160},{160,128},{192,224},{224,1... | collective-permute-start | bytes 393224 | tf_op jit(solution)/shard_map/ppermute | solution.py:383
  50.2 2.1 %collective-permute-start.6 = (f32[2,64,256]{2,1,0:T(8,128)S(1)}, f32[2,64,256]{2,1,0:T(8,128)S(1)}, u32[]{:S(2)}, u32[]{:S(2)}) collective-permute-start(f32[2,64,256]{2,1,0:T(8,128)S(1)} %get-tuple-element.50.refs_0_), channel_id=1, source_target_pairs={{0,192},{32,224},{64,0},{96,32},{128,64},{160,96},{192,128},{224,1... | collective-permute-start | bytes 393224 | tf_op jit(solution)/shard_map/ppermute | solution.py:381
  52.3 0.4 collective-permute-start.17
  52.7 1.2 %collective-permute-start.5 = (f32[2,64,256]{2,1,0:T(8,128)S(1)}, f32[2,64,256]{2,1,0:T(8,128)S(1)}, u32[]{:S(2)}, u32[]{:S(2)}) collective-permute-start(f32[2,64,256]{2,1,0:T(8,128)S(1)} %get-tuple-element.50.refs_0_), channel_id=1, source_target_pairs={{0,128},{32,160},{64,192},{96,224},{128,0},{160,32},{192,64},{224,... | collective-permute-start | bytes 393224 | tf_op jit(solution)/shard_map/ppermute | solution.py:381
  53.9 0.5 collective-permute-start.16
  54.5 1.0 collective-permute-done.6.refs_3_
  55.4 3.4 %collective-permute-start.15 = (f32[3,64,256]{2,1,0:T(8,128)S(1)}, f32[3,64,256]{2,1,0:T(8,128)S(1)}, u32[]{:S(2)}, u32[]{:S(2)}) collective-permute-start(f32[3,64,256]{2,1,0:T(8,128)S(1)} %collective-permute-done.11.refs_9_), channel_id=1, source_target_pairs={{0,32},{32,0},{64,96},{96,64},{128,160},{160,128},{192,224},{224,1... | collective-permute-start | bytes 589832 | tf_op jit(solution)/shard_map/ppermute | solution.py:383
  58.9 0.3 collective-permute-done.5.refs_2_
  59.1 1.5 %collective-permute-start.10 = (f32[2,64,256]{2,1,0:T(8,128)S(1)}, f32[2,64,256]{2,1,0:T(8,128)S(1)}, u32[]{:S(2)}, u32[]{:S(2)}) collective-permute-start(f32[2,64,256]{2,1,0:T(8,128)S(1)} %collective-permute-done.6.refs_3_), channel_id=1, source_target_pairs={{0,32},{32,0},{64,96},{96,64},{128,160},{160,128},{192,224},{224,1... | collective-permute-start | bytes 393224 | tf_op jit(solution)/shard_map/ppermute | solution.py:383
  60.7 1.8 %collective-permute-done.4.refs_1_ = f32[2,64,256]{2,1,0:T(8,128)S(1)} collective-permute-done((f32[2,64,256]{2,1,0:T(8,128)S(1)}, f32[2,64,256]{2,1,0:T(8,128)S(1)}, u32[]{:S(2)}, u32[]{:S(2)}) %collective-permute-start.4) | collective-permute-done | bytes 131104 | tf_op jit(solution)/shard_map/ppermute | solution.py:381
  62.4 0.5 collective-permute-start.9
  62.9 0.0 collective-permute-start.8
  63.0 0.9 collective-permute-done.9.refs_6_
  63.9 0.4 collective-permute-done.8.refs_5_
  64.3 0.6 sweep_mid.1
  64.9 0.6 collective-permute-start.18
  65.5 2.1 %collective-permute-start.19 = (f32[8,256]{1,0:T(8,128)S(1)}, f32[8,256]{1,0:T(8,128)S(1)}, u32[]{:S(2)}, u32[]{:S(2)}) collective-permute-start(f32[8,256]{1,0:T(8,128)S(1)} %get-tuple-element.57), channel_id=1, source_target_pairs={{0,28},{4,0},{8,4},{12,8},{16,12},{20,16},{24,20},{28,24},{1,29},{... | collective-permute-start | bytes 24584 | tf_op jit(solution)/shard_map/ppermute | solution.py:374
  67.6 0.2 collective-permute-start.20
  67.8 2.4 %collective-permute-start.21 = (f32[8,128]{1,0:T(8,128)S(1)}, f32[8,128]{1,0:T(8,128)S(1)}, u32[]{:S(2)}, u32[]{:S(2)}) collective-permute-start(f32[8,128]{1,0:T(8,128)S(1)} %get-tuple-element.59), channel_id=1, source_target_pairs={{0,3},{1,0},{2,1},{3,2},{4,7},{5,4},{6,5},{7,6},{8,11},{9,8},{10,9... | collective-permute-start | bytes 12296 | tf_op jit(solution)/shard_map/ppermute | solution.py:376
  70.3 1.4 %next_wells.1 = (f32[32,2,128]{2,1,0:T(2,128)S(1)}, f32[8,128]{1,0:T(8,128)S(1)}) custom-call(f32[2,512,128]{2,1,0:T(8,128)S(1)} %get-tuple-element.53.split.refs_0_, f32[8,128]{1,0:T(8,128)S(1)} %get-tuple-element.47.refs_11_.live.refs_16_, f32[1,128]{1,0:T(1,128)S(1)} %get-tuple-element.48.refs_12_.wells.refs_17_, f32[1,8]{1,0:T(1,128)S(1)} %copy-done.10, ...), custom_call_target="tpu_custom_call" | custom-call | tf_op jit(solution)/shard_map/next_wells/pallas_call | solution.py:501
  71.7 12.8 %all_to_all.11.refs_10_ = f32[32,2,128]{2,1,0:T(2,128)S(1)} all-to-all(f32[32,2,128]{2,1,0:T(2,128)S(1)} %get-tuple-element.64), channel_id=1, replica_groups=mesh['layer'=8,'gx'=8,'gy'=4] {'gx','gy'}, dimensions={0} | all-to-all | bytes 65536 | tf_op jit(solution)/shard_map/all_to_all | solution.py:457
  84.6 3.6 %solve_lines.3 = (f32[512,256]{1,0:T(8,128)S(1)}, f32[2,64,256]{2,1,0:T(8,128)S(1)}, f32[8,48]{1,0:T(8,128)}) custom-call(f32[2,512,128]{2,1,0:T(8,128)S(1)} %get-tuple-element.53.split.refs_0_, f32[512,256]{1,0:T(8,128)S(1)} %bitcast.25, f32[512,256]{1,0:T(8,128)S(1)} %bitcast.20, f32[512,256]{1,0:T(8,128)S(1)} %bitcast.23, f32[8,8,64,256]{3,2,1,0:T(8,128)S(1)} %bitcast.17, ...), custom_call_target="tpu_custom_call" | custom-call | tf_op jit(solution)/shard_map/solve_lines/pallas_call | solution.py:459
  88.2 0.2 collective-permute-start.24
  88.4 1.4 %collective-permute-start.23 = (f32[2,64,256]{2,1,0:T(8,128)S(1)}, f32[2,64,256]{2,1,0:T(8,128)S(1)}, u32[]{:S(2)}, u32[]{:S(2)}) collective-permute-start(f32[2,64,256]{2,1,0:T(8,128)S(1)} %get-tuple-element.67.refs_0_), channel_id=1, source_target_pairs={{0,128},{32,160},{64,192},{96,224},{128,0},{160,32},{192,64},{224,... | collective-permute-start | bytes 393224 | tf_op jit(solution)/shard_map/ppermute | solution.py:381
  89.8 0.5 collective-permute-start.22
  90.3 4.5 %collective-permute-start.25 = (f32[2,64,256]{2,1,0:T(8,128)S(1)}, f32[2,64,256]{2,1,0:T(8,128)S(1)}, u32[]{:S(2)}, u32[]{:S(2)}) collective-permute-start(f32[2,64,256]{2,1,0:T(8,128)S(1)} %get-tuple-element.67.refs_0_), channel_id=1, source_target_pairs={{0,32},{32,0},{64,96},{96,64},{128,160},{160,128},{192,224},{224,1... | collective-permute-start | bytes 393224 | tf_op jit(solution)/shard_map/ppermute | solution.py:383
  94.7 2.1 %collective-permute-start.28 = (f32[2,64,256]{2,1,0:T(8,128)S(1)}, f32[2,64,256]{2,1,0:T(8,128)S(1)}, u32[]{:S(2)}, u32[]{:S(2)}) collective-permute-start(f32[2,64,256]{2,1,0:T(8,128)S(1)} %collective-permute-done.24.refs_3_), channel_id=1, source_target_pairs={{0,32},{32,0},{64,96},{96,64},{128,160},{160,128},{192,224},{224,1... | collective-permute-start | bytes 393224 | tf_op jit(solution)/shard_map/ppermute | solution.py:383
  96.9 1.9 %collective-permute-start.27 = (f32[2,64,256]{2,1,0:T(8,128)S(1)}, f32[2,64,256]{2,1,0:T(8,128)S(1)}, u32[]{:S(2)}, u32[]{:S(2)}) collective-permute-start(f32[2,64,256]{2,1,0:T(8,128)S(1)} %collective-permute-done.23.refs_2_), channel_id=1, source_target_pairs={{0,32},{32,0},{64,96},{96,64},{128,160},{160,128},{192,224},{224,1... | collective-permute-start | bytes 393224 | tf_op jit(solution)/shard_map/ppermute | solution.py:383
  98.8 1.4 %collective-permute-start.26 = (f32[2,64,256]{2,1,0:T(8,128)S(1)}, f32[2,64,256]{2,1,0:T(8,128)S(1)}, u32[]{:S(2)}, u32[]{:S(2)}) collective-permute-start(f32[2,64,256]{2,1,0:T(8,128)S(1)} %collective-permute-done.22.refs_1_), channel_id=1, source_target_pairs={{0,32},{32,0},{64,96},{96,64},{128,160},{160,128},{192,224},{224,1... | collective-permute-start | bytes 393224 | tf_op jit(solution)/shard_map/ppermute | solution.py:383
  100.2 1.0 collective-permute-done.26.refs_5_
  101.2 1.2 %sweep_last.1 = f32[512,256]{1,0:T(8,128)} custom-call(f32[2,64,256]{2,1,0:T(8,128)S(1)} %get-tuple-element.67.refs_0_, f32[2,64,256]{2,1,0:T(8,128)S(1)} %collective-permute-done.22.refs_1_, f32[2,64,256]{2,1,0:T(8,128)S(1)} %collective-permute-done.23.refs_2_, f32[2,64,256]{2,1,0:T(8,128)S(1)} %collective-permute-done.24.refs_3_, ...), custom_call_target="tpu_custom_call" | custom-call | tf_op jit(solution)/shard_map/sweep_last/pallas_call | solution.py:475
  (45 shorter events, 0.1 us)
Async XLA Ops:
  0.6 39.3 %copy-start.2 = (f32[8,64,256]{2,1,0:T(8,128)S(1)}, f32[8,64,256]{2,1,0:T(8,128)}, u32[]{:S(2)}) copy-start(f32[8,64,256]{2,1,0:T(8,128)} %perm_x.1) | copy-start | bytes 1572868
  0.6 39.3 %copy-start.3 = (f32[8,64,256]{2,1,0:T(8,128)S(1)}, f32[8,64,256]{2,1,0:T(8,128)}, u32[]{:S(2)}) copy-start(f32[8,64,256]{2,1,0:T(8,128)} %param.15) | copy-start | bytes 1572868
  0.7 20.7 %copy-start.5 = (f32[8,64,256]{2,1,0:T(8,128)S(1)}, f32[8,64,256]{2,1,0:T(8,128)}, u32[]{:S(2)}) copy-start(f32[8,64,256]{2,1,0:T(8,128)} %param.12) | copy-start | bytes 1572868
  0.7 20.7 %copy-start.8 = (s32[1,48]{1,0:T(1,128)S(1)}, s32[1,48]{1,0:T(1,128)}, u32[]{:S(2)}) copy-start(s32[1,48]{1,0:T(1,128)} %refs_19_.1) | copy-start | bytes 580
  0.7 20.7 %copy-start.10 = (f32[1,8]{1,0:T(1,128)S(1)}, f32[1,8]{1,0:T(1,128)}, u32[]{:S(2)}) copy-start(f32[1,8]{1,0:T(1,128)} %rate.3) | copy-start | bytes 100
  0.7 20.7 %copy-start.9 = (f32[1,48,8]{1,2,0:T(8,128)S(1)}, f32[1,48,8]{1,2,0:T(8,128)}, u32[]{:S(2)}) copy-start(f32[1,48,8]{1,2,0:T(8,128)} %param.22) | copy-start | bytes 4612
  0.7 20.7 %copy-start.12 = (s32[1,48]{1,0:T(1,128)S(1)}, s32[1,48]{1,0:T(1,128)}, u32[]{:S(2)}) copy-start(s32[1,48]{1,0:T(1,128)} %well.1) | copy-start | bytes 580
  0.7 20.7 %copy-start.11 = (s32[1,48,1]{1,2,0:T(1,128)S(1)}, s32[1,48,1]{1,2,0:T(1,128)}, u32[]{:S(2)}) copy-start(s32[1,48,1]{1,2,0:T(1,128)} %param.19) | copy-start | bytes 580
  0.7 39.2 %copy-start.7 = (f32[1,64,256]{2,1,0:T(8,128)S(1)}, f32[1,64,256]{2,1,0:T(8,128)}, u32[]{:S(2)}) copy-start(f32[1,64,256]{2,1,0:T(8,128)} %param.17) | copy-start | bytes 196612
  0.7 39.2 %copy-start.4 = (f32[8,64,256]{2,1,0:T(8,128)S(1)}, f32[8,64,256]{2,1,0:T(8,128)}, u32[]{:S(2)}) copy-start(f32[8,64,256]{2,1,0:T(8,128)} %param.13) | copy-start | bytes 1572868
  3.3 61.0 %copy-start.6 = (f32[3,64,256]{2,1,0:T(8,128)S(1)}, f32[3,64,256]{2,1,0:T(8,128)}, u32[]{:S(2)}) copy-start(f32[3,64,256]{2,1,0:T(8,128)} %get-tuple-element.51.refs_8_) | copy-start | bytes 589828
  3.3 46.9 %collective-permute-start.14 = (f32[3,64,256]{2,1,0:T(8,128)}, f32[3,64,256]{2,1,0:T(8,128)S(1)}, u32[]{:S(2)}, u32[]{:S(2)}) collective-permute-start(f32[3,64,256]{2,1,0:T(8,128)} %get-tuple-element.51.refs_8_), channel_id=1, source_target_pairs={{0,32},{32,0},{64,96},{96,64},{128,160},{160,128},{192,224},{224,1... | collective-permute-start | bytes 589832 | tf_op jit(solution)/shard_map/ppermute | solution.py:383
  6.6 45.7 %collective-permute-start.13 = (f32[3,64,256]{2,1,0:T(8,128)}, f32[3,64,256]{2,1,0:T(8,128)S(1)}, u32[]{:S(2)}, u32[]{:S(2)}) collective-permute-start(f32[3,64,256]{2,1,0:T(8,128)} %get-tuple-element.51.refs_8_), channel_id=1, source_target_pairs={{0,192},{32,224},{64,0},{96,32},{128,64},{160,96},{192,128},{224,1... | collective-permute-start | bytes 589832 | tf_op jit(solution)/shard_map/ppermute | solution.py:381
  7.4 12.7 %collective-permute-start = (f32[16,256]{1,0:T(8,128)}, f32[16,256]{1,0:T(8,128)S(1)}, u32[]{:S(2)}, u32[]{:S(2)}) collective-permute-start(f32[16,256]{1,0:T(8,128)} %get-tuple-element.38), channel_id=1, source_target_pairs={{0,4},{4,8},{8,12},{12,16},{16,20},{20,24},{24,28},{28,0},{1,5},{5... | collective-permute-start | bytes 49160 | tf_op jit(solution)/shard_map/ppermute | solution.py:373
  9.0 13.9 %collective-permute-start.1 = (f32[16,256]{1,0:T(8,128)}, f32[16,256]{1,0:T(8,128)S(1)}, u32[]{:S(2)}, u32[]{:S(2)}) collective-permute-start(f32[16,256]{1,0:T(8,128)} %get-tuple-element.39), channel_id=1, source_target_pairs={{0,28},{4,0},{8,4},{12,8},{16,12},{20,16},{24,20},{28,24},{1,29},{... | collective-permute-start | bytes 49160 | tf_op jit(solution)/shard_map/ppermute | solution.py:374
  13.0 3.9 %collective-permute-start.2 = (f32[8,128]{1,0:T(8,128)}, f32[8,128]{1,0:T(8,128)S(1)}, u32[]{:S(2)}, u32[]{:S(2)}) collective-permute-start(f32[8,128]{1,0:T(8,128)} %get-tuple-element.40), channel_id=1, source_target_pairs={{0,1},{1,2},{2,3},{3,0},{4,5},{5,6},{6,7},{7,4},{8,9},{9,10},{10,1... | collective-permute-start | bytes 12296 | tf_op jit(solution)/shard_map/ppermute | solution.py:375
  16.9 2.7 %collective-permute-start.3 = (f32[8,128]{1,0:T(8,128)}, f32[8,128]{1,0:T(8,128)S(1)}, u32[]{:S(2)}, u32[]{:S(2)}) collective-permute-start(f32[8,128]{1,0:T(8,128)} %get-tuple-element.41), channel_id=1, source_target_pairs={{0,3},{1,0},{2,1},{3,2},{4,7},{5,4},{6,5},{7,6},{8,11},{9,8},{10,9... | collective-permute-start | bytes 12296 | tf_op jit(solution)/shard_map/ppermute | solution.py:376
  19.6 33.1 %collective-permute-start.12 = (f32[3,64,256]{2,1,0:T(8,128)}, f32[3,64,256]{2,1,0:T(8,128)S(1)}, u32[]{:S(2)}, u32[]{:S(2)}) collective-permute-start(f32[3,64,256]{2,1,0:T(8,128)} %get-tuple-element.51.refs_8_), channel_id=1, source_target_pairs={{0,128},{32,160},{64,192},{96,224},{128,0},{160,32},{192,64},{224,... | collective-permute-start | bytes 589832 | tf_op jit(solution)/shard_map/ppermute | solution.py:381
  20.1 33.8 %collective-permute-start.11 = (f32[3,64,256]{2,1,0:T(8,128)}, f32[3,64,256]{2,1,0:T(8,128)S(1)}, u32[]{:S(2)}, u32[]{:S(2)}) collective-permute-start(f32[3,64,256]{2,1,0:T(8,128)} %get-tuple-element.51.refs_8_), channel_id=1, source_target_pairs={{0,64},{32,96},{64,128},{96,160},{128,192},{160,224},{192,0},{224,... | collective-permute-start | bytes 589832 | tf_op jit(solution)/shard_map/ppermute | solution.py:381
  39.9 2.2 %copy-start = (f32[1,8,8,64,256]{4,3,2,1,0:T(8,128)S(1)}, f32[1,8,8,64,256]{4,3,2,1,0:T(8,128)}, u32[]{:S(2)}) copy-start(f32[1,8,8,64,256]{4,3,2,1,0:T(8,128)} %param.16) | copy-start | bytes 12582916
  42.1 22.2 %copy-start.1 = (f32[1,8,8,64,256]{4,3,2,1,0:T(8,128)S(1)}, f32[1,8,8,64,256]{4,3,2,1,0:T(8,128)}, u32[]{:S(2)}) copy-start(f32[1,8,8,64,256]{4,3,2,1,0:T(8,128)} %param.16) | copy-start | bytes 12582916
  45.2 8.7 %collective-permute-start.7 = (f32[2,64,256]{2,1,0:T(8,128)S(1)}, f32[2,64,256]{2,1,0:T(8,128)S(1)}, u32[]{:S(2)}, u32[]{:S(2)}) collective-permute-start(f32[2,64,256]{2,1,0:T(8,128)S(1)} %get-tuple-element.50.refs_0_), channel_id=1, source_target_pairs={{0,32},{32,0},{64,96},{96,64},{128,160},{160,128},{192,224},{224,1... | collective-permute-start | bytes 393224 | tf_op jit(solution)/shard_map/ppermute | solution.py:383
  50.2 5.2 %collective-permute-start.6 = (f32[2,64,256]{2,1,0:T(8,128)S(1)}, f32[2,64,256]{2,1,0:T(8,128)S(1)}, u32[]{:S(2)}, u32[]{:S(2)}) collective-permute-start(f32[2,64,256]{2,1,0:T(8,128)S(1)} %get-tuple-element.50.refs_0_), channel_id=1, source_target_pairs={{0,192},{32,224},{64,0},{96,32},{128,64},{160,96},{192,128},{224,1... | collective-permute-start | bytes 393224 | tf_op jit(solution)/shard_map/ppermute | solution.py:381
  52.3 10.6 %collective-permute-start.17 = (f32[3,64,256]{2,1,0:T(8,128)S(1)}, f32[3,64,256]{2,1,0:T(8,128)S(1)}, u32[]{:S(2)}, u32[]{:S(2)}) collective-permute-start(f32[3,64,256]{2,1,0:T(8,128)S(1)} %collective-permute-done.13.refs_11_), channel_id=1, source_target_pairs={{0,32},{32,0},{64,96},{96,64},{128,160},{160,128},{192,224},{224,1... | collective-permute-start | bytes 589832 | tf_op jit(solution)/shard_map/ppermute | solution.py:383
  52.7 6.5 %collective-permute-start.5 = (f32[2,64,256]{2,1,0:T(8,128)S(1)}, f32[2,64,256]{2,1,0:T(8,128)S(1)}, u32[]{:S(2)}, u32[]{:S(2)}) collective-permute-start(f32[2,64,256]{2,1,0:T(8,128)S(1)} %get-tuple-element.50.refs_0_), channel_id=1, source_target_pairs={{0,128},{32,160},{64,192},{96,224},{128,0},{160,32},{192,64},{224,... | collective-permute-start | bytes 393224 | tf_op jit(solution)/shard_map/ppermute | solution.py:381
  53.9 8.5 %collective-permute-start.4 = (f32[2,64,256]{2,1,0:T(8,128)S(1)}, f32[2,64,256]{2,1,0:T(8,128)S(1)}, u32[]{:S(2)}, u32[]{:S(2)}) collective-permute-start(f32[2,64,256]{2,1,0:T(8,128)S(1)} %get-tuple-element.50.refs_0_), channel_id=1, source_target_pairs={{0,64},{32,96},{64,128},{96,160},{128,192},{160,224},{192,0},{224,... | collective-permute-start | bytes 393224 | tf_op jit(solution)/shard_map/ppermute | solution.py:381
  53.9 9.0 %collective-permute-start.16 = (f32[3,64,256]{2,1,0:T(8,128)S(1)}, f32[3,64,256]{2,1,0:T(8,128)S(1)}, u32[]{:S(2)}, u32[]{:S(2)}) collective-permute-start(f32[3,64,256]{2,1,0:T(8,128)S(1)} %collective-permute-done.12.refs_10_), channel_id=1, source_target_pairs={{0,32},{32,0},{64,96},{96,64},{128,160},{160,128},{192,224},{224,1... | collective-permute-start | bytes 589832 | tf_op jit(solution)/shard_map/ppermute | solution.py:383
  55.4 7.5 %collective-permute-start.15 = (f32[3,64,256]{2,1,0:T(8,128)S(1)}, f32[3,64,256]{2,1,0:T(8,128)S(1)}, u32[]{:S(2)}, u32[]{:S(2)}) collective-permute-start(f32[3,64,256]{2,1,0:T(8,128)S(1)} %collective-permute-done.11.refs_9_), channel_id=1, source_target_pairs={{0,32},{32,0},{64,96},{96,64},{128,160},{160,128},{192,224},{224,1... | collective-permute-start | bytes 589832 | tf_op jit(solution)/shard_map/ppermute | solution.py:383
  59.1 3.8 %collective-permute-start.10 = (f32[2,64,256]{2,1,0:T(8,128)S(1)}, f32[2,64,256]{2,1,0:T(8,128)S(1)}, u32[]{:S(2)}, u32[]{:S(2)}) collective-permute-start(f32[2,64,256]{2,1,0:T(8,128)S(1)} %collective-permute-done.6.refs_3_), channel_id=1, source_target_pairs={{0,32},{32,0},{64,96},{96,64},{128,160},{160,128},{192,224},{224,1... | collective-permute-start | bytes 393224 | tf_op jit(solution)/shard_map/ppermute | solution.py:383
  62.4 1.5 %collective-permute-start.9 = (f32[2,64,256]{2,1,0:T(8,128)S(1)}, f32[2,64,256]{2,1,0:T(8,128)S(1)}, u32[]{:S(2)}, u32[]{:S(2)}) collective-permute-start(f32[2,64,256]{2,1,0:T(8,128)S(1)} %collective-permute-done.5.refs_2_), channel_id=1, source_target_pairs={{0,32},{32,0},{64,96},{96,64},{128,160},{160,128},{192,224},{224,1... | collective-permute-start | bytes 393224 | tf_op jit(solution)/shard_map/ppermute | solution.py:383
  62.9 1.3 %collective-permute-start.8 = (f32[2,64,256]{2,1,0:T(8,128)S(1)}, f32[2,64,256]{2,1,0:T(8,128)S(1)}, u32[]{:S(2)}, u32[]{:S(2)}) collective-permute-start(f32[2,64,256]{2,1,0:T(8,128)S(1)} %collective-permute-done.4.refs_1_), channel_id=1, source_target_pairs={{0,32},{32,0},{64,96},{96,64},{128,160},{160,128},{192,224},{224,1... | collective-permute-start | bytes 393224 | tf_op jit(solution)/shard_map/ppermute | solution.py:383
  64.9 6.8 %collective-permute-start.18 = (f32[8,256]{1,0:T(8,128)S(1)}, f32[8,256]{1,0:T(8,128)S(1)}, u32[]{:S(2)}, u32[]{:S(2)}) collective-permute-start(f32[8,256]{1,0:T(8,128)S(1)} %get-tuple-element.56), channel_id=1, source_target_pairs={{0,4},{4,8},{8,12},{12,16},{16,20},{20,24},{24,28},{28,0},{1,5},{5... | collective-permute-start | bytes 24584 | tf_op jit(solution)/shard_map/ppermute | solution.py:373
  65.5 6.2 %collective-permute-start.19 = (f32[8,256]{1,0:T(8,128)S(1)}, f32[8,256]{1,0:T(8,128)S(1)}, u32[]{:S(2)}, u32[]{:S(2)}) collective-permute-start(f32[8,256]{1,0:T(8,128)S(1)} %get-tuple-element.57), channel_id=1, source_target_pairs={{0,28},{4,0},{8,4},{12,8},{16,12},{20,16},{24,20},{28,24},{1,29},{... | collective-permute-start | bytes 24584 | tf_op jit(solution)/shard_map/ppermute | solution.py:374
  67.6 4.1 %collective-permute-start.20 = (f32[8,128]{1,0:T(8,128)S(1)}, f32[8,128]{1,0:T(8,128)S(1)}, u32[]{:S(2)}, u32[]{:S(2)}) collective-permute-start(f32[8,128]{1,0:T(8,128)S(1)} %get-tuple-element.58), channel_id=1, source_target_pairs={{0,1},{1,2},{2,3},{3,0},{4,5},{5,6},{6,7},{7,4},{8,9},{9,10},{10,1... | collective-permute-start | bytes 12296 | tf_op jit(solution)/shard_map/ppermute | solution.py:375
  67.8 3.9 %collective-permute-start.21 = (f32[8,128]{1,0:T(8,128)S(1)}, f32[8,128]{1,0:T(8,128)S(1)}, u32[]{:S(2)}, u32[]{:S(2)}) collective-permute-start(f32[8,128]{1,0:T(8,128)S(1)} %get-tuple-element.59), channel_id=1, source_target_pairs={{0,3},{1,0},{2,1},{3,2},{4,7},{5,4},{6,5},{7,6},{8,11},{9,8},{10,9... | collective-permute-start | bytes 12296 | tf_op jit(solution)/shard_map/ppermute | solution.py:376
  88.2 6.5 %collective-permute-start.24 = (f32[2,64,256]{2,1,0:T(8,128)S(1)}, f32[2,64,256]{2,1,0:T(8,128)S(1)}, u32[]{:S(2)}, u32[]{:S(2)}) collective-permute-start(f32[2,64,256]{2,1,0:T(8,128)S(1)} %get-tuple-element.67.refs_0_), channel_id=1, source_target_pairs={{0,192},{32,224},{64,0},{96,32},{128,64},{160,96},{192,128},{224,1... | collective-permute-start | bytes 393224 | tf_op jit(solution)/shard_map/ppermute | solution.py:381
  88.4 8.5 %collective-permute-start.23 = (f32[2,64,256]{2,1,0:T(8,128)S(1)}, f32[2,64,256]{2,1,0:T(8,128)S(1)}, u32[]{:S(2)}, u32[]{:S(2)}) collective-permute-start(f32[2,64,256]{2,1,0:T(8,128)S(1)} %get-tuple-element.67.refs_0_), channel_id=1, source_target_pairs={{0,128},{32,160},{64,192},{96,224},{128,0},{160,32},{192,64},{224,... | collective-permute-start | bytes 393224 | tf_op jit(solution)/shard_map/ppermute | solution.py:381
  89.8 9.0 %collective-permute-start.22 = (f32[2,64,256]{2,1,0:T(8,128)S(1)}, f32[2,64,256]{2,1,0:T(8,128)S(1)}, u32[]{:S(2)}, u32[]{:S(2)}) collective-permute-start(f32[2,64,256]{2,1,0:T(8,128)S(1)} %get-tuple-element.67.refs_0_), channel_id=1, source_target_pairs={{0,64},{32,96},{64,128},{96,160},{128,192},{160,224},{192,0},{224,... | collective-permute-start | bytes 393224 | tf_op jit(solution)/shard_map/ppermute | solution.py:381
  90.3 9.9 %collective-permute-start.25 = (f32[2,64,256]{2,1,0:T(8,128)S(1)}, f32[2,64,256]{2,1,0:T(8,128)S(1)}, u32[]{:S(2)}, u32[]{:S(2)}) collective-permute-start(f32[2,64,256]{2,1,0:T(8,128)S(1)} %get-tuple-element.67.refs_0_), channel_id=1, source_target_pairs={{0,32},{32,0},{64,96},{96,64},{128,160},{160,128},{192,224},{224,1... | collective-permute-start | bytes 393224 | tf_op jit(solution)/shard_map/ppermute | solution.py:383
  94.7 5.5 %collective-permute-start.28 = (f32[2,64,256]{2,1,0:T(8,128)S(1)}, f32[2,64,256]{2,1,0:T(8,128)S(1)}, u32[]{:S(2)}, u32[]{:S(2)}) collective-permute-start(f32[2,64,256]{2,1,0:T(8,128)S(1)} %collective-permute-done.24.refs_3_), channel_id=1, source_target_pairs={{0,32},{32,0},{64,96},{96,64},{128,160},{160,128},{192,224},{224,1... | collective-permute-start | bytes 393224 | tf_op jit(solution)/shard_map/ppermute | solution.py:383
  96.9 3.3 %collective-permute-start.27 = (f32[2,64,256]{2,1,0:T(8,128)S(1)}, f32[2,64,256]{2,1,0:T(8,128)S(1)}, u32[]{:S(2)}, u32[]{:S(2)}) collective-permute-start(f32[2,64,256]{2,1,0:T(8,128)S(1)} %collective-permute-done.23.refs_2_), channel_id=1, source_target_pairs={{0,32},{32,0},{64,96},{96,64},{128,160},{160,128},{192,224},{224,1... | collective-permute-start | bytes 393224 | tf_op jit(solution)/shard_map/ppermute | solution.py:383
  98.8 2.4 %collective-permute-start.26 = (f32[2,64,256]{2,1,0:T(8,128)S(1)}, f32[2,64,256]{2,1,0:T(8,128)S(1)}, u32[]{:S(2)}, u32[]{:S(2)}) collective-permute-start(f32[2,64,256]{2,1,0:T(8,128)S(1)} %collective-permute-done.22.refs_1_), channel_id=1, source_target_pairs={{0,32},{32,0},{64,96},{96,64},{128,160},{160,128},{192,224},{224,1... | collective-permute-start | bytes 393224 | tf_op jit(solution)/shard_map/ppermute | solution.py:383

commit v3 on v2

--- a/solution.py
+++ b/solution.py
@@ -8,7 +8,7 @@
 from jax.sharding import PartitionSpec as P
 
 ITERS = 2
-EDGE_MIB = 60
+EDGE_MIB = 54
 WELLS_MIB = 8
 LZ = 8
 CX = 64
@@ -75,9 +75,51 @@
     return jnp.concatenate([value, jnp.zeros((value.shape[0], 128 - value.shape[1]), value.dtype)], axis=1)
 
 
-def send_partials(out, values):
+def own_tile():
+    return lax.axis_index("gx") * 4 + lax.axis_index("gy")
+
+
+def tile_at(step):
+    return lax.rem(own_tile() + step + TILES, TILES)
+
+
+def send_wells(out, wells):
+    count = out.shape[0] // TILES
     for t in range(TILES):
-        out[t] = values
+        out[t * count] = wells
+
+
+def send_y(out, lower_edge, upper_edge):
+    count, rows, _ = out.shape
+    count = count // TILES
+    for step, edge in ((1, upper_edge), (-1, lower_edge)):
+        first = tile_at(step) * count + 1
+        for n in range(edge.shape[0] // rows):
+            out[first + n] = edge[n * rows : (n + 1) * rows]
+
+
+def send_x(out, split):
+    count = out.shape[0] // TILES
+    for step, row in ((4, CX - 1), (-4, 0)):
+        first = tile_at(step) * count + 1
+        for l in range(LZ):
+            for half in range(2):
+                out[first + l, half : half + 1, :] = split[half, l * CX + row : l * CX + row + 1, :]
+
+
+def from_y(spread, blocks):
+    count = spread.shape[0] // TILES
+    result = []
+    for step in (-1, 1):
+        first = tile_at(step) * count + 1
+        result.append(jnp.concatenate([spread[first + n] for n in range(blocks)], axis=0))
+    return result
+
+
+def from_x(spread, step, l):
+    count = spread.shape[0] // TILES
+    block = spread[tile_at(step) * count + 1 + l]
+    return jnp.concatenate([block[0:1], block[1:2]], axis=1)
 
 
 def live_index(index_ref, count_ref):
@@ -99,7 +141,7 @@
 
 
 def own_rates(rate_ref):
-    tile = lax.axis_index("gx") * 4 + lax.axis_index("gy")
+    tile = own_tile()
     rate = rate_ref[...]
     tiled = jnp.concatenate([rate] * 16, axis=1)
     lanes = lane_ids(1, 128)
@@ -118,7 +160,7 @@
     return jnp.concatenate([split[0, span, :], split[1, span, :]], axis=1)
 
 
-def edges_kernel(pressure, perm_x, perm_y, inverse, xlo, xhi, ylo, yhi, fixed, split, kx_lo, kx_hi, ky, sem):
+def edges_kernel(pressure, perm_x, perm_y, inverse, xlo, xhi, y_edge, fixed, split, kx_lo, kx_hi, ky, sem):
     copies = load(
         [(pressure.at[:, half * 128 : half * 128 + 128], split.at[half]) for half in range(2)]
         + [(perm_x.at[:, 0:8], kx_lo), (perm_x.at[:, CX - 8 : CX], kx_hi), (perm_y, ky)]
@@ -131,9 +173,7 @@
     for l in range(LZ):
         xlo[LZ + l : LZ + l + 1, :] = kx_lo[l, 0:1, :]
         xhi[LZ + l : LZ + l + 1, :] = kx_hi[l, 7:8, :]
-    turned = y_edges([(split.at[0], 0), (ky, 0), (split.at[1], 127), (ky, CY - 1)])
-    ylo[...] = turned[0:8]
-    yhi[...] = turned[8:16]
+    y_edge[...] = y_edges([(split.at[0], 0), (ky, 0), (split.at[1], 127), (ky, CY - 1)])[0:16]
     for copy in copies[5:]:
         copy.wait()
 
@@ -147,6 +187,7 @@
 
 
 def wells_first_kernel(
+    y_edge,
     pressure,
     index,
     owner,
@@ -193,7 +234,8 @@
     values = jnp.concatenate(
         [totals_by_well(weighted_c, wells_c) + own_rates(rate_v), totals_by_well(total_c, wells_c)], axis=0
     )
-    send_partials(partials, values)
+    send_wells(partials, values)
+    send_y(partials, y_edge[0:8], y_edge[8:16])
 
 
 def wells_next_kernel(split, live, wells, rate, column, partials, at_slots, rate_v, column_s, sem):
@@ -204,23 +246,24 @@
     at_slots[...] = at
     weighted = jnp.sum(live[...] * at, axis=0, keepdims=True)
     weighted_c, wells_c = well_columns([weighted, wells[...]])
-    send_partials(partials, totals_by_well(weighted_c, wells_c) + own_rates(rate_v))
+    send_wells(partials, totals_by_well(weighted_c, wells_c) + own_rates(rate_v))
+    turned = y_edges([(split.at[0], 0), (split.at[1], 127)])
+    send_y(partials, turned[0:4], turned[4:8])
+    send_x(partials, split)
 
 
 def solve_kernel(first, *refs):
+    (split, source, kx, ky, inverse, lower, kx_lo, kx_hi, partials, *refs) = refs
     if first:
-        (split, source, kx, ky, inverse, lower, from_xlo, from_xhi, from_ylo, from_yhi, partials, *refs) = refs
-        kx_lo, kx_hi, ky_lo, ky_hi = from_xlo, from_xhi, from_ylo, from_yhi
-        (live, wells, at_slots, column, solved, carried, sums_out, rhs, column_s, sem) = refs
+        (live, wells, at_slots, column, solved, carried, sums_out, kylo_out, kyhi_out, rhs, column_s, sem) = refs
     else:
-        (split, source, kx, ky, inverse, lower, from_xlo, from_xhi, from_ylo, from_yhi, partials, *refs) = refs
-        (kx_lo, kx_hi, ky_lo, ky_hi, sums, *refs) = refs
+        (ky_lo, ky_hi, sums, *refs) = refs
         (live, wells, at_slots, column, solved, carried, flow_out, rhs, column_s, sem) = refs
     copies = load([(column, column_s)], sem)
     gx, gy = lax.axis_index("gx"), lax.axis_index("gy")
     total = partials[0]
     for t in range(1, TILES):
-        total = total + partials[t]
+        total = total + partials[partials.shape[0] // TILES * t]
     if first:
         numerator, index_sum = total[0:2], total[2:4]
         sums_out[...] = index_sum
@@ -242,10 +285,18 @@
 
     rows = lax.broadcasted_iota(jnp.int32, (CX, CY), 0)
     lanes = lane_ids(CX, CY)
-    ylo_c = from_ylo[...].T
-    yhi_c = from_yhi[...].T
-    kylo_c = ky_lo[...].T
-    kyhi_c = ky_hi[...].T
+    from_ylo, from_yhi = from_y(partials, 2)
+    if first:
+        kylo_out[...] = from_ylo
+        kyhi_out[...] = from_yhi
+        ylo_c = kylo_c = from_ylo.T
+        yhi_c = kyhi_c = from_yhi.T
+    else:
+        spare = jnp.zeros((4, 128), F32)
+        ylo_c = jnp.concatenate([from_ylo, spare], axis=0).T
+        yhi_c = jnp.concatenate([from_yhi, spare], axis=0).T
+        kylo_c = ky_lo[...].T
+        kyhi_c = ky_hi[...].T
 
     def y_column(turned, base, l):
         s = (l % 2) * CX
@@ -255,9 +306,11 @@
         span = slice(l * CX, (l + 1) * CX)
         f = halves_of(split, span)
         k = kx[span, :]
-        f_after = jnp.where(gx < 7, from_xhi[l : l + 1, :], 0.0)
+        f_after = kx_hi[l : l + 1, :] if first else from_x(partials, 4, l)
+        f_after = jnp.where(gx < 7, f_after, 0.0)
         k_after = kx_hi[LZ + l : LZ + l + 1, :]
-        f_before = jnp.where(gx > 0, from_xlo[l : l + 1, :], 0.0)
+        f_before = kx_lo[l : l + 1, :] if first else from_x(partials, -4, l)
+        f_before = jnp.where(gx > 0, f_before, 0.0)
         k_before = kx_lo[LZ + l : LZ + l + 1, :]
         f_east = jnp.where(rows == CX - 1, f_after, pltpu.roll(f, CX - 1, 0))
         k_east = jnp.where(rows == CX - 1, k_after, pltpu.roll(k, CX - 1, 0))
@@ -315,7 +368,7 @@
     if last:
         solved, inverse, field = refs
     else:
-        solved, inverse, split, lower, xlo, xhi, ylo, yhi = refs
+        solved, inverse, split, lower = refs
     me = lax.axis_index("layer")
 
     def position(own):
@@ -352,12 +405,6 @@
 
     for own in range(GROUPS):
         position(own)
-    if last:
-        return
-    split_x_edges(split, xlo, xhi)
-    turned = y_edges([(split.at[0], 0), (split.at[1], 127)])
-    ylo[...] = turned[0:8]
-    yhi[...] = jnp.concatenate([turned[4:8], turned[0:4]], axis=0)
 
 
 def params(mib=8):
@@ -368,13 +415,8 @@
     return [(i, (i + step) % n) for i in range(n)]
 
 
-def from_sides(xlo, xhi, ylo, yhi):
-    return (
-        lax.ppermute(xhi, "gx", around(8, 1)),
-        lax.ppermute(xlo, "gx", around(8, -1)),
-        lax.ppermute(yhi, "gy", around(4, 1)),
-        lax.ppermute(ylo, "gy", around(4, -1)),
-    )
+def from_sides(xlo, xhi):
+    return (lax.ppermute(xhi, "gx", around(8, 1)), lax.ppermute(xlo, "gx", around(8, -1)))
 
 
 def all_groups(value):
@@ -407,11 +449,11 @@
 
     kx = perm_x.reshape(rows, CY)
     ky = perm_y.reshape(rows, CY)
-    *edges, fixed = pl.pallas_call(
+    *edges, y_edge, fixed = pl.pallas_call(
         edges_kernel,
-        out_shape=(shape(16, CY), shape(16, CY), shape(8, 128), shape(8, 128), shape(3, CX, CY)),
+        out_shape=(shape(16, CY), shape(16, CY), shape(16, 128), shape(3, CX, CY)),
         in_specs=[ANY] * 4,
-        out_specs=(VMEM,) * 5,
+        out_specs=(VMEM,) * 4,
         scratch_shapes=[
             pltpu.VMEM((2, rows, 128), F32),
             pltpu.VMEM((LZ, 8, CY), F32),
@@ -422,18 +464,18 @@
         compiler_params=params(EDGE_MIB),
         name="first_edges",
     )(pressure, perm_x, ky, inverse)
-    k_sides = sides = from_sides(*edges)
+    sides = from_sides(*edges)
     fixed = all_groups(fixed)
     partials, at_slots, live, wells, field = pl.pallas_call(
         wells_first_kernel,
         out_shape=(
-            shape(TILES, 4, 128),
+            shape(3 * TILES, 4, 128),
             shape(LZ, 128),
             shape(LZ, 128),
             shape(1, 128),
             shape(2, rows, 128),
         ),
-        in_specs=[ANY] * 7,
+        in_specs=[VMEM] + [ANY] * 7,
         out_specs=(VMEM,) * 5,
         scratch_shapes=[
             pltpu.VMEM((LZ, SLOTS), F32),
@@ -446,21 +488,20 @@
         ],
         compiler_params=params(WELLS_MIB),
         name="first_wells",
-    )(pressure, index, owner, perf_well, well_rate, perf_column, tile_count)
+    )(y_edge, pressure, index, owner, perf_well, well_rate, perf_column, tile_count)
     sums = None
     for sweep_step in range(ITERS):
         first, last = sweep_step == 0, sweep_step == ITERS - 1
-        tied = lax.optimization_barrier((partials, *sides))
-        partials, sides = tied[0], tied[1:]
         if first:
-            k_sides = sides
+            partials, *sides = lax.optimization_barrier((partials, *sides))
         spread = lax.all_to_all(partials, ("gx", "gy"), split_axis=0, concat_axis=0, tiled=True)
-        extra = () if first else (*k_sides, sums)
-        solved, carried, small = pl.pallas_call(
+        extra = () if first else (*ky_sides, sums)
+        solved, carried, small, *ky_out = pl.pallas_call(
             functools.partial(solve_kernel, first),
-            out_shape=(shape(rows, CY), shape(2, CX, CY), shape(2, 128) if first else shape(LZ, SLOTS)),
-            in_specs=[VMEM] * (14 + len(extra)) + [ANY],
-            out_specs=(VMEM,) * 3,
+            out_shape=(shape(rows, CY), shape(2, CX, CY))
+            + ((shape(2, 128), shape(8, 128), shape(8, 128)) if first else (shape(LZ, SLOTS),)),
+            in_specs=[VMEM] * (12 + len(extra)) + [ANY],
+            out_specs=(VMEM,) * (5 if first else 3),
             scratch_shapes=[
                 pltpu.VMEM((2, rows, 128), F32),
                 pltpu.SMEM((1, SLOTS), jnp.int32),
@@ -481,26 +522,21 @@
                 name="sweep_last",
             )(*groups, *fixed, solved, inverse)
             break
-        sums = small
-        field, lower, *edges = pl.pallas_call(
+        sums, ky_sides = small, ky_out
+        field, lower = pl.pallas_call(
             functools.partial(sweep_kernel, False),
             out_shape=(
                 shape(2, rows, 128),
                 shape(CX, CY),
-                shape(8, CY),
-                shape(8, CY),
-                shape(8, 128),
-                shape(8, 128),
             ),
             in_specs=[VMEM] * 18,
-            out_specs=(VMEM,) * 6,
+            out_specs=(VMEM,) * 2,
             compiler_params=params(),
             name="sweep_mid",
         )(*groups, *fixed, solved, inverse)
-        sides = from_sides(*edges)
         partials, at_slots = pl.pallas_call(
             wells_next_kernel,
-            out_shape=(shape(TILES, 2, 128), shape(LZ, 128)),
+            out_shape=(shape(9 * TILES, 2, 128), shape(LZ, 128)),
             in_specs=[VMEM] * 3 + [ANY] * 2,
             out_specs=(VMEM,) * 2,
             scratch_shapes=[

time: 103 us -> 95.1 us (0.923)
  blocking collectives: 29.8 us -> 21.3 us
  waiting for transfers between devices: 9.19 us -> 5.98 us
  local copies, waits for them, and re-layouts: 2.24 us -> 4.75 us
  starting transfers between devices: 45.6 us -> 47.5 us
    all_to_all x2 -> x1, blocking collectives: 29.8 us -> 21.3 us  [shards(): lax.all_to_all(partials, ('gx', 'gy'), split_axis=0, concat_axis=0, tiled...]
    all_to_all x0 -> x1, starting transfers between devices: none -> 8.22 us  [shards(): lax.all_to_all(partials, ('gx', 'gy'), split_axis=0, concat_axis=0, tiled...]
    ppermute x4 -> x0, starting transfers between devices: 5.44 us -> none  [the longest x2 3.9 us: from_sides(): lax.ppermute(ylo, 'gy', around(4, -1))]
    ppermute x4 -> x0, waiting for transfers between devices: 3.85 us -> none  [the longest x2 2.65 us: from_sides(): lax.ppermute(yhi, 'gy', around(4, 1))]
    unnamed x26 -> x32, local copies, waits for them, and re-layouts: 2.24 us -> 4.75 us
    ppermute x2 -> x1, starting transfers between devices: 6.04 us -> 4.03 us  [from_sides(): lax.ppermute(xlo, 'gx', around(8, -1))]
    ppermute x2 -> x1, starting transfers between devices: 2.27 us -> 2.54 us  [from_sides(): lax.ppermute(xhi, 'gx', around(8, 1))]
  transfers between devices with their start and end apart: 29 -> 24, of which waited for: 8 -> 5; matrix products, arithmetic and copies ran while one was open for 0% -> 0% of each run, Pallas kernels for 6% -> 5%
where the time goes in v3:
time: 95.1 us; the launch traced here: 94.8 us
  starting transfers between devices  47.5 us (50%)
  blocking collectives  21.3 us (22%)
  Pallas kernels  13.7 us (14%)
  waiting for transfers between devices  5.98 us (6%)
  local copies, waits for them, and re-layouts  4.75 us (5%)
  between operations  1.56 us (2%)
    ppermute x12, starting transfers between devices, all_groups(): return own + [lax.ppermute(v, 'layer', swap) for v in own]  25 us
    all_to_all x1, blocking collectives, shards(): lax.all_to_all(partials, ('gx', 'gy'), split_axis=0, concat_axis=0, tiled...  21.3 us
    all_to_all x1, starting transfers between devices, shards(): lax.all_to_all(partials, ('gx', 'gy'), split_axis=0, concat_axis=0, tiled...  8.22 us
    ppermute x9, starting transfers between devices, all_groups(): lax.ppermute(value, 'layer', around(8, 2 * d))  7.72 us
    pallas_call x2, Pallas kernels, shards(): pl.pallas_call(functools.partial(solve_kernel, first), out_shape=(shape(r...  6.02 us
    unnamed x32, local copies, waits for them, and re-layouts  4.75 us
    ppermute x1, starting transfers between devices, from_sides(): lax.ppermute(xlo, 'gx', around(8, -1))  4.03 us
    ppermute x9, waiting for transfers between devices, all_groups(): lax.ppermute(value, 'layer', around(8, 2 * d))  4 us
  transfers between devices with their start and end apart: 24, of which 5 were waited for; matrix products, arithmetic and copies ran while one was open for 0% of the time, Pallas kernels for 5%

profile of v3, /device:TPU:1, one launch (start us, length us, event | category | flops | bytes accessed | tf_op | source)
XLA Modules:
  0.0 94.8 jit_solution(8034880827448264273)
XLA Ops:
  0.7 2.5 %first_edges.1 = (f32[16,256]{1,0:T(8,128)}, f32[16,256]{1,0:T(8,128)}, f32[16,128]{1,0:T(8,128)}, f32[3,64,256]{2,1,0:T(8,128)}) custom-call(f32[512,256]{1,0:T(8,128)} %bitcast.26, f32[8,64,256]{2,1,0:T(8,128)} %perm_x.1, f32[512,256]{1,0:T(8,128)} %bitcast.21, f32[8,8,64,256]{3,2,1,0:T(8,128)} %bitcast.14), custom_call_target="tpu_custom_call" | custom-call | tf_op jit(solution)/shard_map/first_edges/pallas_call | solution.py:452
  3.3 2.5 %collective-permute-start = (f32[16,256]{1,0:T(8,128)}, f32[16,256]{1,0:T(8,128)S(1)}, u32[]{:S(2)}, u32[]{:S(2)}) collective-permute-start(f32[16,256]{1,0:T(8,128)} %get-tuple-element.29), channel_id=1, source_target_pairs={{0,4},{4,8},{8,12},{12,16},{16,20},{20,24},{24,28},{28,0},{1,5},{5... | collective-permute-start | bytes 49160 | tf_op jit(solution)/shard_map/ppermute | solution.py:419
  5.8 4.0 %collective-permute-start.1 = (f32[16,256]{1,0:T(8,128)}, f32[16,256]{1,0:T(8,128)S(1)}, u32[]{:S(2)}, u32[]{:S(2)}) collective-permute-start(f32[16,256]{1,0:T(8,128)} %get-tuple-element.30), channel_id=1, source_target_pairs={{0,28},{4,0},{8,4},{12,8},{16,12},{20,16},{24,20},{28,24},{1,29},{... | collective-permute-start | bytes 49160 | tf_op jit(solution)/shard_map/ppermute | solution.py:419
  10.6 0.0 copy-start.10
  10.6 0.7 copy-done.10
  11.3 2.2 %first_wells.1 = (f32[96,4,128]{2,1,0:T(4,128)}, f32[8,128]{1,0:T(8,128)S(1)}, f32[8,128]{1,0:T(8,128)S(1)}, f32[1,128]{1,0:T(1,128)S(1)}, f32[2,512,128]{2,1,0:T(8,128)S(1)}) custom-call(f32[16,128]{1,0:T(8,128)S(1)} %copy-done.10, f32[512,256]{1,0:T(8,128)S(1)} %bitcast.27, f32[8,48]{1,0:T(8,128)S(1)} %bitcast.29, s32[1,48]{1,0:T(1,128)S(1)} %bitcast.30, ...), custom_call_target="tpu_custom_call" | custom-call | tf_op jit(solution)/shard_map/first_wells/pallas_call | solution.py:469
  13.4 0.0 copy-start.7
  13.5 0.8 copy-done.7
  14.3 8.2 %all-to-all-start = ((f32[96,4,128]{2,1,0:T(4,128)}), f32[96,4,128]{2,1,0:T(4,128)S(1)}, u32[]{:S(2)}, u32[]{:S(2)}) async-start(f32[96,4,128]{2,1,0:T(4,128)} %get-tuple-element.33), calls=%async_computation | async-start | bytes 393216 | tf_op jit(solution)/shard_map/all_to_all | solution.py:497
  22.5 2.6 %collective-permute-start.11 = (f32[3,64,256]{2,1,0:T(8,128)}, f32[3,64,256]{2,1,0:T(8,128)S(1)}, u32[]{:S(2)}, u32[]{:S(2)}) collective-permute-start(f32[3,64,256]{2,1,0:T(8,128)} %get-tuple-element.38.refs_8_), channel_id=1, source_target_pairs={{0,192},{32,224},{64,0},{96,32},{128,64},{160,96},{192,128},{224,1... | collective-permute-start | bytes 589832 | tf_op jit(solution)/shard_map/ppermute | solution.py:423
  25.0 0.5 collective-permute-start.10
  25.6 2.1 %collective-permute-start.12 = (f32[3,64,256]{2,1,0:T(8,128)}, f32[3,64,256]{2,1,0:T(8,128)S(1)}, u32[]{:S(2)}, u32[]{:S(2)}) collective-permute-start(f32[3,64,256]{2,1,0:T(8,128)} %get-tuple-element.38.refs_8_), channel_id=1, source_target_pairs={{0,32},{32,0},{64,96},{96,64},{128,160},{160,128},{192,224},{224,1... | collective-permute-start | bytes 589832 | tf_op jit(solution)/shard_map/ppermute | solution.py:425
  27.6 0.6 collective-permute-start.9
  28.2 1.7 %collective-permute-done.11.refs_11_ = f32[3,64,256]{2,1,0:T(8,128)S(1)} collective-permute-done((f32[3,64,256]{2,1,0:T(8,128)}, f32[3,64,256]{2,1,0:T(8,128)S(1)}, u32[]{:S(2)}, u32[]{:S(2)}) %collective-permute-start.11) | collective-permute-done | bytes 196640 | tf_op jit(solution)/shard_map/ppermute | solution.py:423
  29.9 4.8 %collective-permute-start.15 = (f32[3,64,256]{2,1,0:T(8,128)S(1)}, f32[3,64,256]{2,1,0:T(8,128)S(1)}, u32[]{:S(2)}, u32[]{:S(2)}) collective-permute-start(f32[3,64,256]{2,1,0:T(8,128)S(1)} %collective-permute-done.11.refs_11_), channel_id=1, source_target_pairs={{0,32},{32,0},{64,96},{96,64},{128,160},{160,128},{192,224},{224,1... | collective-permute-start | bytes 589832 | tf_op jit(solution)/shard_map/ppermute | solution.py:425
  34.7 0.0 collective-permute-done.10.refs_10_
  34.7 1.6 %collective-permute-start.14 = (f32[3,64,256]{2,1,0:T(8,128)S(1)}, f32[3,64,256]{2,1,0:T(8,128)S(1)}, u32[]{:S(2)}, u32[]{:S(2)}) collective-permute-start(f32[3,64,256]{2,1,0:T(8,128)S(1)} %collective-permute-done.10.refs_10_), channel_id=1, source_target_pairs={{0,32},{32,0},{64,96},{96,64},{128,160},{160,128},{192,224},{224,1... | collective-permute-start | bytes 589832 | tf_op jit(solution)/shard_map/ppermute | solution.py:425
  36.3 0.0 all-to-all-done.refs_8_
  36.3 0.0 copy-start
  36.3 2.2 %copy-done = f32[1,8,8,64,256]{4,3,2,1,0:T(8,128)S(1)} copy-done((f32[1,8,8,64,256]{4,3,2,1,0:T(8,128)S(1)}, f32[1,8,8,64,256]{4,3,2,1,0:T(8,128)}, u32[]{:S(2)}) %copy-start) | copy-done | bytes 4194328
  38.5 1.0 %copy-done.8 = f32[2,512,128]{2,1,0:T(8,128)S(1)} copy-done((f32[2,512,128]{2,1,0:T(8,128)S(1)}, f32[2,512,128]{2,1,0:T(8,128)}, u32[]{:S(2)}) %copy-start.8) | copy-done | bytes 524312
  39.6 2.7 %solve_lines.2 = (f32[512,256]{1,0:T(8,128)S(1)}, f32[2,64,256]{2,1,0:T(8,128)S(1)}, f32[2,128]{1,0:T(2,128)S(1)}, f32[8,128]{1,0:T(8,128)S(1)}, f32[8,128]{1,0:T(8,128)S(1)}) custom-call(f32[2,512,128]{2,1,0:T(8,128)S(1)} %copy-done.8, f32[512,256]{1,0:T(8,128)S(1)} %bitcast.24, f32[512,256]{1,0:T(8,128)S(1)} %bitcast.19, f32[512,256]{1,0:T(8,128)S(1)} %bitcast.22, ...), custom_call_target="tpu_custom_call" | custom-call | tf_op jit(solution)/shard_map/solve_lines/pallas_call | solution.py:499
  42.3 1.8 %collective-permute-start.4 = (f32[2,64,256]{2,1,0:T(8,128)S(1)}, f32[2,64,256]{2,1,0:T(8,128)S(1)}, u32[]{:S(2)}, u32[]{:S(2)}) collective-permute-start(f32[2,64,256]{2,1,0:T(8,128)S(1)} %get-tuple-element.37.refs_0_), channel_id=1, source_target_pairs={{0,192},{32,224},{64,0},{96,32},{128,64},{160,96},{192,128},{224,1... | collective-permute-start | bytes 393224 | tf_op jit(solution)/shard_map/ppermute | solution.py:423
  44.1 0.0 collective-permute-done.12.refs_12_
  44.1 0.2 collective-permute-start.3
  44.3 0.4 collective-permute-start.2
  44.8 1.1 %collective-permute-start.13 = (f32[3,64,256]{2,1,0:T(8,128)S(1)}, f32[3,64,256]{2,1,0:T(8,128)S(1)}, u32[]{:S(2)}, u32[]{:S(2)}) collective-permute-start(f32[3,64,256]{2,1,0:T(8,128)S(1)} %collective-permute-done.9.refs_9_), channel_id=1, source_target_pairs={{0,32},{32,0},{64,96},{96,64},{128,160},{160,128},{192,224},{224,1... | collective-permute-start | bytes 589832 | tf_op jit(solution)/shard_map/ppermute | solution.py:425
  45.9 0.3 collective-permute-start.5
  46.1 1.3 %collective-permute-done.4.refs_3_ = f32[2,64,256]{2,1,0:T(8,128)S(1)} collective-permute-done((f32[2,64,256]{2,1,0:T(8,128)S(1)}, f32[2,64,256]{2,1,0:T(8,128)S(1)}, u32[]{:S(2)}, u32[]{:S(2)}) %collective-permute-start.4) | collective-permute-done | bytes 131104 | tf_op jit(solution)/shard_map/ppermute | solution.py:423
  47.5 3.2 %collective-permute-start.8 = (f32[2,64,256]{2,1,0:T(8,128)S(1)}, f32[2,64,256]{2,1,0:T(8,128)S(1)}, u32[]{:S(2)}, u32[]{:S(2)}) collective-permute-start(f32[2,64,256]{2,1,0:T(8,128)S(1)} %collective-permute-done.4.refs_3_), channel_id=1, source_target_pairs={{0,32},{32,0},{64,96},{96,64},{128,160},{160,128},{192,224},{224,1... | collective-permute-start | bytes 393224 | tf_op jit(solution)/shard_map/ppermute | solution.py:425
  50.6 0.0 collective-permute-done.3.refs_2_
  50.6 2.1 %collective-permute-start.7 = (f32[2,64,256]{2,1,0:T(8,128)S(1)}, f32[2,64,256]{2,1,0:T(8,128)S(1)}, u32[]{:S(2)}, u32[]{:S(2)}) collective-permute-start(f32[2,64,256]{2,1,0:T(8,128)S(1)} %collective-permute-done.3.refs_2_), channel_id=1, source_target_pairs={{0,32},{32,0},{64,96},{96,64},{128,160},{160,128},{192,224},{224,1... | collective-permute-start | bytes 393224 | tf_op jit(solution)/shard_map/ppermute | solution.py:425
  52.8 1.0 %collective-permute-done.2.refs_1_ = f32[2,64,256]{2,1,0:T(8,128)S(1)} collective-permute-done((f32[2,64,256]{2,1,0:T(8,128)S(1)}, f32[2,64,256]{2,1,0:T(8,128)S(1)}, u32[]{:S(2)}, u32[]{:S(2)}) %collective-permute-start.2) | collective-permute-done | bytes 131104 | tf_op jit(solution)/shard_map/ppermute | solution.py:423
  53.7 0.5 collective-permute-start.6
  54.3 1.0 %collective-permute-done.6.refs_5_ = f32[2,64,256]{2,1,0:T(8,128)S(1)} collective-permute-done((f32[2,64,256]{2,1,0:T(8,128)S(1)}, f32[2,64,256]{2,1,0:T(8,128)S(1)}, u32[]{:S(2)}, u32[]{:S(2)}) %collective-permute-start.6) | collective-permute-done | bytes 131104 | tf_op jit(solution)/shard_map/ppermute | solution.py:425
  55.3 0.4 sweep_mid.1
  55.6 1.5 %next_wells.1 = (f32[288,2,128]{2,1,0:T(2,128)S(1)}, f32[8,128]{1,0:T(8,128)S(1)}) custom-call(f32[2,512,128]{2,1,0:T(8,128)S(1)} %get-tuple-element.40.split.refs_0_, f32[8,128]{1,0:T(8,128)S(1)} %get-tuple-element.34.refs_9_.live.refs_12_, f32[1,128]{1,0:T(1,128)S(1)} %get-tuple-element.35.refs_10_.wells.refs_13_, f32[1,8]{1,0:T(1,128)S(1)} %copy-done.13, ...), custom_call_target="tpu_custom_call" | custom-call | tf_op jit(solution)/shard_map/next_wells/pallas_call | solution.py:537
  57.1 21.3 %all_to_all.10.refs_8_ = f32[288,2,128]{2,1,0:T(2,128)S(1)} all-to-all(f32[288,2,128]{2,1,0:T(2,128)S(1)} %get-tuple-element.42), channel_id=1, replica_groups=mesh['layer'=8,'gx'=8,'gy'=4] {'gx','gy'}, dimensions={0} | all-to-all | bytes 589824 | tf_op jit(solution)/shard_map/all_to_all | solution.py:497
  78.4 3.3 %solve_lines.3 = (f32[512,256]{1,0:T(8,128)S(1)}, f32[2,64,256]{2,1,0:T(8,128)S(1)}, f32[8,48]{1,0:T(8,128)}) custom-call(f32[2,512,128]{2,1,0:T(8,128)S(1)} %get-tuple-element.40.split.refs_0_, f32[512,256]{1,0:T(8,128)S(1)} %bitcast.25, f32[512,256]{1,0:T(8,128)S(1)} %bitcast.20, f32[512,256]{1,0:T(8,128)S(1)} %bitcast.23, f32[8,8,64,256]{3,2,1,0:T(8,128)S(1)} %bitcast.17, ...), custom_call_target="tpu_custom_call" | custom-call | tf_op jit(solution)/shard_map/solve_lines/pallas_call | solution.py:499
  81.7 0.3 collective-permute-start.18
  82.0 0.3 collective-permute-start.17
  82.3 0.9 collective-permute-start.16
  83.2 2.9 %collective-permute-start.19 = (f32[2,64,256]{2,1,0:T(8,128)S(1)}, f32[2,64,256]{2,1,0:T(8,128)S(1)}, u32[]{:S(2)}, u32[]{:S(2)}) collective-permute-start(f32[2,64,256]{2,1,0:T(8,128)S(1)} %get-tuple-element.47.refs_0_), channel_id=1, source_target_pairs={{0,32},{32,0},{64,96},{96,64},{128,160},{160,128},{192,224},{224,1... | collective-permute-start | bytes 393224 | tf_op jit(solution)/shard_map/ppermute | solution.py:425
  86.1 3.0 %collective-permute-start.22 = (f32[2,64,256]{2,1,0:T(8,128)S(1)}, f32[2,64,256]{2,1,0:T(8,128)S(1)}, u32[]{:S(2)}, u32[]{:S(2)}) collective-permute-start(f32[2,64,256]{2,1,0:T(8,128)S(1)} %collective-permute-done.18.refs_3_), channel_id=1, source_target_pairs={{0,32},{32,0},{64,96},{96,64},{128,160},{160,128},{192,224},{224,1... | collective-permute-start | bytes 393224 | tf_op jit(solution)/shard_map/ppermute | solution.py:425
  89.1 2.3 %collective-permute-start.21 = (f32[2,64,256]{2,1,0:T(8,128)S(1)}, f32[2,64,256]{2,1,0:T(8,128)S(1)}, u32[]{:S(2)}, u32[]{:S(2)}) collective-permute-start(f32[2,64,256]{2,1,0:T(8,128)S(1)} %collective-permute-done.17.refs_2_), channel_id=1, source_target_pairs={{0,32},{32,0},{64,96},{96,64},{128,160},{160,128},{192,224},{224,1... | collective-permute-start | bytes 393224 | tf_op jit(solution)/shard_map/ppermute | solution.py:425
  91.4 1.3 %collective-permute-start.20 = (f32[2,64,256]{2,1,0:T(8,128)S(1)}, f32[2,64,256]{2,1,0:T(8,128)S(1)}, u32[]{:S(2)}, u32[]{:S(2)}) collective-permute-start(f32[2,64,256]{2,1,0:T(8,128)S(1)} %collective-permute-done.16.refs_1_), channel_id=1, source_target_pairs={{0,32},{32,0},{64,96},{96,64},{128,160},{160,128},{192,224},{224,1... | collective-permute-start | bytes 393224 | tf_op jit(solution)/shard_map/ppermute | solution.py:425
  92.7 1.0 %collective-permute-done.20.refs_5_ = f32[2,64,256]{2,1,0:T(8,128)S(1)} collective-permute-done((f32[2,64,256]{2,1,0:T(8,128)S(1)}, f32[2,64,256]{2,1,0:T(8,128)S(1)}, u32[]{:S(2)}, u32[]{:S(2)}) %collective-permute-start.20) | collective-permute-done | bytes 131104 | tf_op jit(solution)/shard_map/ppermute | solution.py:425
  93.7 1.2 %sweep_last.1 = f32[512,256]{1,0:T(8,128)} custom-call(f32[2,64,256]{2,1,0:T(8,128)S(1)} %get-tuple-element.47.refs_0_, f32[2,64,256]{2,1,0:T(8,128)S(1)} %collective-permute-done.16.refs_1_, f32[2,64,256]{2,1,0:T(8,128)S(1)} %collective-permute-done.17.refs_2_, f32[2,64,256]{2,1,0:T(8,128)S(1)} %collective-permute-done.18.refs_3_, ...), custom_call_target="tpu_custom_call" | custom-call | tf_op jit(solution)/shard_map/sweep_last/pallas_call | solution.py:516
  (40 shorter events, 0.1 us)
Async XLA Ops:
  0.6 35.7 %copy-start.2 = (f32[8,64,256]{2,1,0:T(8,128)S(1)}, f32[8,64,256]{2,1,0:T(8,128)}, u32[]{:S(2)}) copy-start(f32[8,64,256]{2,1,0:T(8,128)} %perm_x.1) | copy-start | bytes 1572868
  0.6 35.6 %copy-start.3 = (f32[8,64,256]{2,1,0:T(8,128)S(1)}, f32[8,64,256]{2,1,0:T(8,128)}, u32[]{:S(2)}) copy-start(f32[8,64,256]{2,1,0:T(8,128)} %param.15) | copy-start | bytes 1572868
  0.7 9.9 %copy-start.5 = (f32[8,64,256]{2,1,0:T(8,128)S(1)}, f32[8,64,256]{2,1,0:T(8,128)}, u32[]{:S(2)}) copy-start(f32[8,64,256]{2,1,0:T(8,128)} %param.12) | copy-start | bytes 1572868
  0.7 9.9 %copy-start.11 = (s32[1,48]{1,0:T(1,128)S(1)}, s32[1,48]{1,0:T(1,128)}, u32[]{:S(2)}) copy-start(s32[1,48]{1,0:T(1,128)} %refs_15_.1) | copy-start | bytes 580
  0.7 9.9 %copy-start.13 = (f32[1,8]{1,0:T(1,128)S(1)}, f32[1,8]{1,0:T(1,128)}, u32[]{:S(2)}) copy-start(f32[1,8]{1,0:T(1,128)} %rate.3) | copy-start | bytes 100
  0.7 9.9 %copy-start.12 = (f32[1,48,8]{1,2,0:T(8,128)S(1)}, f32[1,48,8]{1,2,0:T(8,128)}, u32[]{:S(2)}) copy-start(f32[1,48,8]{1,2,0:T(8,128)} %param.22) | copy-start | bytes 4612
  0.7 9.9 %copy-start.15 = (s32[1,48]{1,0:T(1,128)S(1)}, s32[1,48]{1,0:T(1,128)}, u32[]{:S(2)}) copy-start(s32[1,48]{1,0:T(1,128)} %well.1) | copy-start | bytes 580
  0.7 9.9 %copy-start.14 = (s32[1,48,1]{1,2,0:T(1,128)S(1)}, s32[1,48,1]{1,2,0:T(1,128)}, u32[]{:S(2)}) copy-start(s32[1,48,1]{1,2,0:T(1,128)} %param.19) | copy-start | bytes 580
  0.7 35.6 %copy-start.9 = (f32[1,64,256]{2,1,0:T(8,128)S(1)}, f32[1,64,256]{2,1,0:T(8,128)}, u32[]{:S(2)}) copy-start(f32[1,64,256]{2,1,0:T(8,128)} %param.17) | copy-start | bytes 196612
  0.7 35.6 %copy-start.4 = (f32[8,64,256]{2,1,0:T(8,128)S(1)}, f32[8,64,256]{2,1,0:T(8,128)}, u32[]{:S(2)}) copy-start(f32[8,64,256]{2,1,0:T(8,128)} %param.13) | copy-start | bytes 1572868
  3.3 52.0 %copy-start.6 = (f32[3,64,256]{2,1,0:T(8,128)S(1)}, f32[3,64,256]{2,1,0:T(8,128)}, u32[]{:S(2)}) copy-start(f32[3,64,256]{2,1,0:T(8,128)} %get-tuple-element.38.refs_8_) | copy-start | bytes 589828
  3.3 11.0 %collective-permute-start = (f32[16,256]{1,0:T(8,128)}, f32[16,256]{1,0:T(8,128)S(1)}, u32[]{:S(2)}, u32[]{:S(2)}) collective-permute-start(f32[16,256]{1,0:T(8,128)} %get-tuple-element.29), channel_id=1, source_target_pairs={{0,4},{4,8},{8,12},{12,16},{16,20},{20,24},{24,28},{28,0},{1,5},{5... | collective-permute-start | bytes 49160 | tf_op jit(solution)/shard_map/ppermute | solution.py:419
  5.8 8.4 %collective-permute-start.1 = (f32[16,256]{1,0:T(8,128)}, f32[16,256]{1,0:T(8,128)S(1)}, u32[]{:S(2)}, u32[]{:S(2)}) collective-permute-start(f32[16,256]{1,0:T(8,128)} %get-tuple-element.30), channel_id=1, source_target_pairs={{0,28},{4,0},{8,4},{12,8},{16,12},{20,16},{24,20},{28,24},{1,29},{... | collective-permute-start | bytes 49160 | tf_op jit(solution)/shard_map/ppermute | solution.py:419
  10.6 0.7 copy-start.10
  13.4 0.8 copy-start.7
  14.3 22.0 %all-to-all-start = ((f32[96,4,128]{2,1,0:T(4,128)}), f32[96,4,128]{2,1,0:T(4,128)S(1)}, u32[]{:S(2)}, u32[]{:S(2)}) async-start(f32[96,4,128]{2,1,0:T(4,128)} %get-tuple-element.33), calls=%async_computation | async-start | bytes 393216 | tf_op jit(solution)/shard_map/all_to_all | solution.py:497
  22.5 7.5 %collective-permute-start.11 = (f32[3,64,256]{2,1,0:T(8,128)}, f32[3,64,256]{2,1,0:T(8,128)S(1)}, u32[]{:S(2)}, u32[]{:S(2)}) collective-permute-start(f32[3,64,256]{2,1,0:T(8,128)} %get-tuple-element.38.refs_8_), channel_id=1, source_target_pairs={{0,192},{32,224},{64,0},{96,32},{128,64},{160,96},{192,128},{224,1... | collective-permute-start | bytes 589832 | tf_op jit(solution)/shard_map/ppermute | solution.py:423
  25.0 9.7 %collective-permute-start.10 = (f32[3,64,256]{2,1,0:T(8,128)}, f32[3,64,256]{2,1,0:T(8,128)S(1)}, u32[]{:S(2)}, u32[]{:S(2)}) collective-permute-start(f32[3,64,256]{2,1,0:T(8,128)} %get-tuple-element.38.refs_8_), channel_id=1, source_target_pairs={{0,128},{32,160},{64,192},{96,224},{128,0},{160,32},{192,64},{224,... | collective-permute-start | bytes 589832 | tf_op jit(solution)/shard_map/ppermute | solution.py:423
  25.6 18.5 %collective-permute-start.12 = (f32[3,64,256]{2,1,0:T(8,128)}, f32[3,64,256]{2,1,0:T(8,128)S(1)}, u32[]{:S(2)}, u32[]{:S(2)}) collective-permute-start(f32[3,64,256]{2,1,0:T(8,128)} %get-tuple-element.38.refs_8_), channel_id=1, source_target_pairs={{0,32},{32,0},{64,96},{96,64},{128,160},{160,128},{192,224},{224,1... | collective-permute-start | bytes 589832 | tf_op jit(solution)/shard_map/ppermute | solution.py:425
  27.6 16.7 %collective-permute-start.9 = (f32[3,64,256]{2,1,0:T(8,128)}, f32[3,64,256]{2,1,0:T(8,128)S(1)}, u32[]{:S(2)}, u32[]{:S(2)}) collective-permute-start(f32[3,64,256]{2,1,0:T(8,128)} %get-tuple-element.38.refs_8_), channel_id=1, source_target_pairs={{0,64},{32,96},{64,128},{96,160},{128,192},{160,224},{192,0},{224,... | collective-permute-start | bytes 589832 | tf_op jit(solution)/shard_map/ppermute | solution.py:423
  29.9 14.8 %collective-permute-start.15 = (f32[3,64,256]{2,1,0:T(8,128)S(1)}, f32[3,64,256]{2,1,0:T(8,128)S(1)}, u32[]{:S(2)}, u32[]{:S(2)}) collective-permute-start(f32[3,64,256]{2,1,0:T(8,128)S(1)} %collective-permute-done.11.refs_11_), channel_id=1, source_target_pairs={{0,32},{32,0},{64,96},{96,64},{128,160},{160,128},{192,224},{224,1... | collective-permute-start | bytes 589832 | tf_op jit(solution)/shard_map/ppermute | solution.py:425
  34.7 11.1 %collective-permute-start.14 = (f32[3,64,256]{2,1,0:T(8,128)S(1)}, f32[3,64,256]{2,1,0:T(8,128)S(1)}, u32[]{:S(2)}, u32[]{:S(2)}) collective-permute-start(f32[3,64,256]{2,1,0:T(8,128)S(1)} %collective-permute-done.10.refs_10_), channel_id=1, source_target_pairs={{0,32},{32,0},{64,96},{96,64},{128,160},{160,128},{192,224},{224,1... | collective-permute-start | bytes 589832 | tf_op jit(solution)/shard_map/ppermute | solution.py:425
  36.3 2.2 %copy-start = (f32[1,8,8,64,256]{4,3,2,1,0:T(8,128)S(1)}, f32[1,8,8,64,256]{4,3,2,1,0:T(8,128)}, u32[]{:S(2)}) copy-start(f32[1,8,8,64,256]{4,3,2,1,0:T(8,128)} %param.16) | copy-start | bytes 12582916
  38.5 1.0 %copy-start.8 = (f32[2,512,128]{2,1,0:T(8,128)S(1)}, f32[2,512,128]{2,1,0:T(8,128)}, u32[]{:S(2)}) copy-start(f32[2,512,128]{2,1,0:T(8,128)} %copy-done.7) | copy-start | bytes 1572868
  39.5 15.7 %copy-start.1 = (f32[1,8,8,64,256]{4,3,2,1,0:T(8,128)S(1)}, f32[1,8,8,64,256]{4,3,2,1,0:T(8,128)}, u32[]{:S(2)}) copy-start(f32[1,8,8,64,256]{4,3,2,1,0:T(8,128)} %param.16) | copy-start | bytes 12582916
  42.3 5.2 %collective-permute-start.4 = (f32[2,64,256]{2,1,0:T(8,128)S(1)}, f32[2,64,256]{2,1,0:T(8,128)S(1)}, u32[]{:S(2)}, u32[]{:S(2)}) collective-permute-start(f32[2,64,256]{2,1,0:T(8,128)S(1)} %get-tuple-element.37.refs_0_), channel_id=1, source_target_pairs={{0,192},{32,224},{64,0},{96,32},{128,64},{160,96},{192,128},{224,1... | collective-permute-start | bytes 393224 | tf_op jit(solution)/shard_map/ppermute | solution.py:423
  44.1 6.6 %collective-permute-start.3 = (f32[2,64,256]{2,1,0:T(8,128)S(1)}, f32[2,64,256]{2,1,0:T(8,128)S(1)}, u32[]{:S(2)}, u32[]{:S(2)}) collective-permute-start(f32[2,64,256]{2,1,0:T(8,128)S(1)} %get-tuple-element.37.refs_0_), channel_id=1, source_target_pairs={{0,128},{32,160},{64,192},{96,224},{128,0},{160,32},{192,64},{224,... | collective-permute-start | bytes 393224 | tf_op jit(solution)/shard_map/ppermute | solution.py:423
  44.3 9.4 %collective-permute-start.2 = (f32[2,64,256]{2,1,0:T(8,128)S(1)}, f32[2,64,256]{2,1,0:T(8,128)S(1)}, u32[]{:S(2)}, u32[]{:S(2)}) collective-permute-start(f32[2,64,256]{2,1,0:T(8,128)S(1)} %get-tuple-element.37.refs_0_), channel_id=1, source_target_pairs={{0,64},{32,96},{64,128},{96,160},{128,192},{160,224},{192,0},{224,... | collective-permute-start | bytes 393224 | tf_op jit(solution)/shard_map/ppermute | solution.py:423
  44.8 9.5 %collective-permute-start.13 = (f32[3,64,256]{2,1,0:T(8,128)S(1)}, f32[3,64,256]{2,1,0:T(8,128)S(1)}, u32[]{:S(2)}, u32[]{:S(2)}) collective-permute-start(f32[3,64,256]{2,1,0:T(8,128)S(1)} %collective-permute-done.9.refs_9_), channel_id=1, source_target_pairs={{0,32},{32,0},{64,96},{96,64},{128,160},{160,128},{192,224},{224,1... | collective-permute-start | bytes 589832 | tf_op jit(solution)/shard_map/ppermute | solution.py:425
  45.9 8.4 %collective-permute-start.5 = (f32[2,64,256]{2,1,0:T(8,128)S(1)}, f32[2,64,256]{2,1,0:T(8,128)S(1)}, u32[]{:S(2)}, u32[]{:S(2)}) collective-permute-start(f32[2,64,256]{2,1,0:T(8,128)S(1)} %get-tuple-element.37.refs_0_), channel_id=1, source_target_pairs={{0,32},{32,0},{64,96},{96,64},{128,160},{160,128},{192,224},{224,1... | collective-permute-start | bytes 393224 | tf_op jit(solution)/shard_map/ppermute | solution.py:425
  47.5 6.8 %collective-permute-start.8 = (f32[2,64,256]{2,1,0:T(8,128)S(1)}, f32[2,64,256]{2,1,0:T(8,128)S(1)}, u32[]{:S(2)}, u32[]{:S(2)}) collective-permute-start(f32[2,64,256]{2,1,0:T(8,128)S(1)} %collective-permute-done.4.refs_3_), channel_id=1, source_target_pairs={{0,32},{32,0},{64,96},{96,64},{128,160},{160,128},{192,224},{224,1... | collective-permute-start | bytes 393224 | tf_op jit(solution)/shard_map/ppermute | solution.py:425
  50.6 3.6 %collective-permute-start.7 = (f32[2,64,256]{2,1,0:T(8,128)S(1)}, f32[2,64,256]{2,1,0:T(8,128)S(1)}, u32[]{:S(2)}, u32[]{:S(2)}) collective-permute-start(f32[2,64,256]{2,1,0:T(8,128)S(1)} %collective-permute-done.3.refs_2_), channel_id=1, source_target_pairs={{0,32},{32,0},{64,96},{96,64},{128,160},{160,128},{192,224},{224,1... | collective-permute-start | bytes 393224 | tf_op jit(solution)/shard_map/ppermute | solution.py:425
  53.7 1.5 %collective-permute-start.6 = (f32[2,64,256]{2,1,0:T(8,128)S(1)}, f32[2,64,256]{2,1,0:T(8,128)S(1)}, u32[]{:S(2)}, u32[]{:S(2)}) collective-permute-start(f32[2,64,256]{2,1,0:T(8,128)S(1)} %collective-permute-done.2.refs_1_), channel_id=1, source_target_pairs={{0,32},{32,0},{64,96},{96,64},{128,160},{160,128},{192,224},{224,1... | collective-permute-start | bytes 393224 | tf_op jit(solution)/shard_map/ppermute | solution.py:425
  81.7 4.4 %collective-permute-start.18 = (f32[2,64,256]{2,1,0:T(8,128)S(1)}, f32[2,64,256]{2,1,0:T(8,128)S(1)}, u32[]{:S(2)}, u32[]{:S(2)}) collective-permute-start(f32[2,64,256]{2,1,0:T(8,128)S(1)} %get-tuple-element.47.refs_0_), channel_id=1, source_target_pairs={{0,192},{32,224},{64,0},{96,32},{128,64},{160,96},{192,128},{224,1... | collective-permute-start | bytes 393224 | tf_op jit(solution)/shard_map/ppermute | solution.py:423
  82.0 7.1 %collective-permute-start.17 = (f32[2,64,256]{2,1,0:T(8,128)S(1)}, f32[2,64,256]{2,1,0:T(8,128)S(1)}, u32[]{:S(2)}, u32[]{:S(2)}) collective-permute-start(f32[2,64,256]{2,1,0:T(8,128)S(1)} %get-tuple-element.47.refs_0_), channel_id=1, source_target_pairs={{0,128},{32,160},{64,192},{96,224},{128,0},{160,32},{192,64},{224,... | collective-permute-start | bytes 393224 | tf_op jit(solution)/shard_map/ppermute | solution.py:423
  82.3 9.1 %collective-permute-start.16 = (f32[2,64,256]{2,1,0:T(8,128)S(1)}, f32[2,64,256]{2,1,0:T(8,128)S(1)}, u32[]{:S(2)}, u32[]{:S(2)}) collective-permute-start(f32[2,64,256]{2,1,0:T(8,128)S(1)} %get-tuple-element.47.refs_0_), channel_id=1, source_target_pairs={{0,64},{32,96},{64,128},{96,160},{128,192},{160,224},{192,0},{224,... | collective-permute-start | bytes 393224 | tf_op jit(solution)/shard_map/ppermute | solution.py:423
  83.2 9.4 %collective-permute-start.19 = (f32[2,64,256]{2,1,0:T(8,128)S(1)}, f32[2,64,256]{2,1,0:T(8,128)S(1)}, u32[]{:S(2)}, u32[]{:S(2)}) collective-permute-start(f32[2,64,256]{2,1,0:T(8,128)S(1)} %get-tuple-element.47.refs_0_), channel_id=1, source_target_pairs={{0,32},{32,0},{64,96},{96,64},{128,160},{160,128},{192,224},{224,1... | collective-permute-start | bytes 393224 | tf_op jit(solution)/shard_map/ppermute | solution.py:425
  86.1 6.6 %collective-permute-start.22 = (f32[2,64,256]{2,1,0:T(8,128)S(1)}, f32[2,64,256]{2,1,0:T(8,128)S(1)}, u32[]{:S(2)}, u32[]{:S(2)}) collective-permute-start(f32[2,64,256]{2,1,0:T(8,128)S(1)} %collective-permute-done.18.refs_3_), channel_id=1, source_target_pairs={{0,32},{32,0},{64,96},{96,64},{128,160},{160,128},{192,224},{224,1... | collective-permute-start | bytes 393224 | tf_op jit(solution)/shard_map/ppermute | solution.py:425
  89.1 3.6 %collective-permute-start.21 = (f32[2,64,256]{2,1,0:T(8,128)S(1)}, f32[2,64,256]{2,1,0:T(8,128)S(1)}, u32[]{:S(2)}, u32[]{:S(2)}) collective-permute-start(f32[2,64,256]{2,1,0:T(8,128)S(1)} %collective-permute-done.17.refs_2_), channel_id=1, source_target_pairs={{0,32},{32,0},{64,96},{96,64},{128,160},{160,128},{192,224},{224,1... | collective-permute-start | bytes 393224 | tf_op jit(solution)/shard_map/ppermute | solution.py:425
  91.4 2.3 %collective-permute-start.20 = (f32[2,64,256]{2,1,0:T(8,128)S(1)}, f32[2,64,256]{2,1,0:T(8,128)S(1)}, u32[]{:S(2)}, u32[]{:S(2)}) collective-permute-start(f32[2,64,256]{2,1,0:T(8,128)S(1)} %collective-permute-done.16.refs_1_), channel_id=1, source_target_pairs={{0,32},{32,0},{64,96},{96,64},{128,160},{160,128},{192,224},{224,1... | collective-permute-start | bytes 393224 | tf_op jit(solution)/shard_map/ppermute | solution.py:425

commit v4 on v3

--- a/solution.py
+++ b/solution.py
@@ -8,8 +8,9 @@
 from jax.sharding import PartitionSpec as P
 
 ITERS = 2
-EDGE_MIB = 54
-WELLS_MIB = 8
+EDGE_MIB = 53.0
+WELLS_MIB = 52.0
+SOLVE_MIB = 52.0
 LZ = 8
 CX = 64
 CY = 256
@@ -98,15 +99,6 @@
             out[first + n] = edge[n * rows : (n + 1) * rows]
 
 
-def send_x(out, split):
-    count = out.shape[0] // TILES
-    for step, row in ((4, CX - 1), (-4, 0)):
-        first = tile_at(step) * count + 1
-        for l in range(LZ):
-            for half in range(2):
-                out[first + l, half : half + 1, :] = split[half, l * CX + row : l * CX + row + 1, :]
-
-
 def from_y(spread, blocks):
     count = spread.shape[0] // TILES
     result = []
@@ -114,12 +106,6 @@
         first = tile_at(step) * count + 1
         result.append(jnp.concatenate([spread[first + n] for n in range(blocks)], axis=0))
     return result
-
-
-def from_x(spread, step, l):
-    count = spread.shape[0] // TILES
-    block = spread[tile_at(step) * count + 1 + l]
-    return jnp.concatenate([block[0:1], block[1:2]], axis=1)
 
 
 def live_index(index_ref, count_ref):
@@ -186,31 +172,14 @@
             xhi[l : l + 1, lanes] = split[half, l * CX + CX - 1 : l * CX + CX, :]
 
 
-def wells_first_kernel(
-    y_edge,
-    pressure,
-    index,
-    owner,
-    well,
-    rate,
-    column,
-    count,
-    partials,
-    at_slots,
-    live_out,
-    wells_out,
-    split,
-    index_v,
-    owner_v,
-    well_v,
-    rate_v,
-    column_s,
-    count_s,
-    sem,
-):
+def wells_first_kernel(*refs):
+    (y_edge, pressure, index, owner, well, rate, column, count, *refs) = refs
+    (partials, at_slots, live_out, wells_out, *refs) = refs
+    (split, y_edge_v, index_v, owner_v, well_v, rate_v, column_s, count_s, sem) = refs
     copies = load(
         [(pressure.at[:, half * 128 : half * 128 + 128], split.at[half]) for half in range(2)]
         + [
+            (y_edge, y_edge_v),
             (column, column_s),
             (count, count_s),
             (index, index_v),
@@ -235,48 +204,61 @@
         [totals_by_well(weighted_c, wells_c) + own_rates(rate_v), totals_by_well(total_c, wells_c)], axis=0
     )
     send_wells(partials, values)
-    send_y(partials, y_edge[0:8], y_edge[8:16])
-
-
-def wells_next_kernel(split, live, wells, rate, column, partials, at_slots, rate_v, column_s, sem):
-    copies = load([(column, column_s), (rate, rate_v)], sem)
+    send_y(partials, y_edge_v[0:8], y_edge_v[8:16])
+
+
+def wells_next_kernel(split, live, wells, rate, column, partials, at_slots, live_v, wells_v, rate_v, column_s, sem):
+    copies = load([(column, column_s), (rate, rate_v), (live, live_v), (wells, wells_v)], sem)
     for copy in copies:
         copy.wait()
     at = gather_slots(split, column_s)
     at_slots[...] = at
-    weighted = jnp.sum(live[...] * at, axis=0, keepdims=True)
-    weighted_c, wells_c = well_columns([weighted, wells[...]])
+    weighted = jnp.sum(live_v[...] * at, axis=0, keepdims=True)
+    weighted_c, wells_c = well_columns([weighted, wells_v[...]])
     send_wells(partials, totals_by_well(weighted_c, wells_c) + own_rates(rate_v))
     turned = y_edges([(split.at[0], 0), (split.at[1], 127)])
     send_y(partials, turned[0:4], turned[4:8])
-    send_x(partials, split)
-
-
-def solve_kernel(first, *refs):
-    (split, source, kx, ky, inverse, lower, kx_lo, kx_hi, partials, *refs) = refs
+
+
+def solve_kernel(first, inputs, *refs):
+    away, refs = refs[:inputs], refs[inputs:]
     if first:
-        (live, wells, at_slots, column, solved, carried, sums_out, kylo_out, kyhi_out, rhs, column_s, sem) = refs
+        (solved, carried, sums_out, kylo_out, kyhi_out, rims, *refs) = refs
     else:
-        (ky_lo, ky_hi, sums, *refs) = refs
-        (live, wells, at_slots, column, solved, carried, flow_out, rhs, column_s, sem) = refs
-    copies = load([(column, column_s)], sem)
+        (solved, carried, flow_out, *refs) = refs
+    held, (rhs, column_s, sem) = refs[:inputs], refs[inputs:]
+    (column, partials, live, wells, at_slots, *small, field, kx, ky, source, lower, inverse) = held
+    held = dict(zip(range(inputs), held))
+    wanted = [(away[0], column_s)] + [(away[n], held[n]) for n in range(1, inputs - 6)]
+    if first:
+        wanted += [(away[inputs - 6].at[:, half * 128 : half * 128 + 128], field.at[half]) for half in range(2)]
+    else:
+        wanted += [(away[inputs - 6].at[half], field.at[half]) for half in range(2)]
+    wanted += [(away[n], held[n]) for n in range(inputs - 5, inputs)]
+    copies = load(wanted, sem)
+    for copy in copies[: inputs - 6]:
+        copy.wait()
     gx, gy = lax.axis_index("gx"), lax.axis_index("gy")
+    block = partials.shape[0] // TILES
     total = partials[0]
     for t in range(1, TILES):
-        total = total + partials[partials.shape[0] // TILES * t]
+        total = total + partials[block * t]
     if first:
+        x_lo, x_hi = small
+        kx_lo, kx_hi = x_lo, x_hi
         numerator, index_sum = total[0:2], total[2:4]
         sums_out[...] = index_sum
     else:
+        x_lo, x_hi, kx_lo, kx_hi, ky_lo, ky_hi, sums = small
         numerator, index_sum = total, sums[...]
     bottom_hole = numerator / (index_sum + 1.0)
     (wells_c,) = well_columns([wells[...]])
     ids = wells_c[:SLOTS].astype(jnp.int32)
-    held = jnp.zeros((SLOTS, 128), F32)
+    hole = jnp.zeros((SLOTS, 128), F32)
     for half in range(2):
         hit = ids == lane_ids(SLOTS, 128) + half * 128
-        held = held + jnp.where(hit, bottom_hole[half : half + 1], 0.0)
-    hole = jnp.sum(held, axis=1, keepdims=True)
+        hole = hole + jnp.where(hit, bottom_hole[half : half + 1], 0.0)
+    hole = jnp.sum(hole, axis=1, keepdims=True)
     hole = jnp.broadcast_to(hole, (SLOTS, 128))
     hole = jnp.concatenate([hole, jnp.zeros((128 - SLOTS, 128), F32)], axis=0).T[0:1]
     flow = live[...] * (hole - at_slots[...])
@@ -302,15 +284,15 @@
         s = (l % 2) * CX
         return turned[s : s + CX, base + l // 2 : base + l // 2 + 1]
 
+    for copy in copies[inputs - 6 : inputs - 1]:
+        copy.wait()
     for l in range(LZ):
         span = slice(l * CX, (l + 1) * CX)
-        f = halves_of(split, span)
+        f = halves_of(field, span)
         k = kx[span, :]
-        f_after = kx_hi[l : l + 1, :] if first else from_x(partials, 4, l)
-        f_after = jnp.where(gx < 7, f_after, 0.0)
+        f_after = jnp.where(gx < 7, x_hi[l : l + 1, :], 0.0)
         k_after = kx_hi[LZ + l : LZ + l + 1, :]
-        f_before = kx_lo[l : l + 1, :] if first else from_x(partials, -4, l)
-        f_before = jnp.where(gx > 0, f_before, 0.0)
+        f_before = jnp.where(gx > 0, x_lo[l : l + 1, :], 0.0)
         k_before = kx_lo[LZ + l : LZ + l + 1, :]
         f_east = jnp.where(rows == CX - 1, f_after, pltpu.roll(f, CX - 1, 0))
         k_east = jnp.where(rows == CX - 1, k_after, pltpu.roll(k, CX - 1, 0))
@@ -331,8 +313,6 @@
         rhs[0, span, :] = value[:, :128]
         rhs[1, span, :] = value[:, 128:]
 
-    for copy in copies:
-        copy.wait()
     lanes8 = lane_ids(LZ, 128)
     for s in range(SLOTS):
         place = column_s[0, s]
@@ -344,11 +324,17 @@
         where = (pl.ds(x, LZ, stride=CX), slice(None))
         part[where] = part[where] + jnp.where(lanes8 == lane, flow[:, s : s + 1], 0.0)
 
-    def block(b, carry):
+    for copy in copies[inputs - 1 :]:
+        copy.wait()
+
+    def solve_block(b, carry):
         at = pl.multiple_of(b * 8, 8)
         right = [halves_of(rhs, pl.ds(j * CX + at, 8)) for j in range(LZ)]
         here = pl.ds(at, 8)
         for i in range(LZ):
+            if first:
+                rims[0, i, here, :] = inverse[i, 0, here, :]
+                rims[1, i, here, :] = inverse[i, LZ - 1, here, :]
             total = inverse[i, 0, here, :] * right[0]
             for j in range(1, LZ):
                 total = total + inverse[i, j, here, :] * right[j]
@@ -360,36 +346,70 @@
                 carried[0, here, :] = total + inverse[i, i, here, :] * low - low
         return carry
 
-    lax.fori_loop(0, CX // 8, block, 0)
+    lax.fori_loop(0, CX // 8, solve_block, 0)
+
+
+def by_core(body):
+    core = lax.axis_index("layer") % 2
+    for own in range(2):
+        pl.when(core == own)(functools.partial(body, own))
+
+
+def pair_fixed_kernel(mine, other, out):
+    def body(own):
+        top, low = (mine, other) if own == 0 else (other, mine)
+        out[0] = low[0] * top[0]
+        out[1] = top[1] * low[1]
+        out[2] = top[2] + top[1] * (low[2] - 1.0) * top[0]
+
+    by_core(body)
+
+
+def pair_kernel(mine, other, fixed_mine, fixed_other, out):
+    def body(own):
+        top, low = (mine, other) if own == 0 else (other, mine)
+        fixed_top, fixed_low = (fixed_mine, fixed_other) if own == 0 else (fixed_other, fixed_mine)
+        out[0] = fixed_low[0] * top[0] + low[0]
+        out[1] = top[1] + fixed_top[1] * (low[1] + fixed_low[2] * top[0] - top[0])
+
+    by_core(body)
 
 
 def sweep_kernel(last, *refs):
-    cds, fixed, refs = refs[:8], refs[8:16], refs[16:]
+    cds, fixed, refs = refs[:4], refs[4:8], refs[8:]
+    cd_mine, cd_other, fixed_mine, fixed_other, solved, rims, *refs = refs
     if last:
-        solved, inverse, field = refs
+        (field,) = refs
     else:
-        solved, inverse, split, lower = refs
+        split, lower, xlo, xhi = refs
     me = lax.axis_index("layer")
 
     def position(own):
-        def of(planes, g):
-            distance = (own // 2 - g // 2) % 4
-            return planes[distance + 4 * ((own ^ g) & 1)]
+        chip = own // 2
 
         def block(b, carry):
             here = pl.ds(pl.multiple_of(b * 8, 8), 8)
             upper = jnp.zeros((8, CY), F32)
             uppers = [upper]
-            for g in range(GROUPS - 1):
-                upper = of(fixed, g)[0, here, :] * upper + of(cds, g)[0, here, :]
+            for c in range(3):
+                d = (chip - c) % 4
+                upper = fixed[d][0, here, :] * upper + cds[d][0, here, :]
                 uppers.append(upper)
             low = jnp.zeros((8, CY), F32)
-            for g in range(GROUPS - 1, own, -1):
-                step = of(cds, g)[1, here, :] + of(fixed, g)[2, here, :] * uppers[g] - uppers[g]
-                low = of(fixed, g)[1, here, :] * low + step
+            for c in range(3, chip, -1):
+                d = (chip - c) % 4
+                step = cds[d][1, here, :] + fixed[d][2, here, :] * uppers[c] - uppers[c]
+                low = fixed[d][1, here, :] * low + step
+            upper = uppers[chip]
+            if own % 2 == 0:
+                below = fixed_mine[0, here, :] * upper + cd_mine[0, here, :]
+                step = cd_other[1, here, :] + fixed_other[2, here, :] * below - below
+                low = fixed_other[1, here, :] * low + step
+            else:
+                upper = fixed_other[0, here, :] * upper + cd_other[0, here, :]
             for i in range(LZ):
                 span = pl.ds(pl.multiple_of(i * CX + b * 8, 8), 8)
-                value = solved[span, :] + inverse[i, 0, here, :] * uppers[own] + inverse[i, LZ - 1, here, :] * low
+                value = solved[span, :] + rims[0, i, here, :] * upper + rims[1, i, here, :] * low
                 if last:
                     field[span, :] = value
                 else:
@@ -405,10 +425,12 @@
 
     for own in range(GROUPS):
         position(own)
-
-
-def params(mib=8):
-    return pltpu.CompilerParams(vmem_limit_bytes=mib * 1024 * 1024)
+    if not last:
+        split_x_edges(split, xlo, xhi)
+
+
+def params(mib=8.0):
+    return pltpu.CompilerParams(vmem_limit_bytes=int(mib * 1024) * 1024)
 
 
 def around(n, step):
@@ -419,10 +441,23 @@
     return (lax.ppermute(xhi, "gx", around(8, 1)), lax.ppermute(xlo, "gx", around(8, -1)))
 
 
-def all_groups(value):
-    own = [value] + [lax.ppermute(value, "layer", around(8, 2 * d)) for d in range(1, 4)]
-    swap = [(i, i ^ 1) for i in range(8)]
-    return own + [lax.ppermute(v, "layer", swap) for v in own]
+def swapped(value):
+    return lax.ppermute(value, "layer", [(i, i ^ 1) for i in range(GROUPS)])
+
+
+def all_chips(value):
+    return [value] + [lax.ppermute(value, "layer", around(GROUPS, 2 * d)) for d in range(1, 4)]
+
+
+def whole(kernel, name, out_shape, *operands):
+    return pl.pallas_call(
+        kernel,
+        out_shape=out_shape,
+        in_specs=[VMEM] * len(operands),
+        out_specs=jax.tree.map(lambda _: VMEM, out_shape),
+        compiler_params=params(),
+        name=name,
+    )(*operands)
 
 
 def shards(
@@ -465,84 +500,85 @@
         name="first_edges",
     )(pressure, perm_x, ky, inverse)
     sides = from_sides(*edges)
-    fixed = all_groups(fixed)
-    partials, at_slots, live, wells, field = pl.pallas_call(
+    fixed_other = swapped(fixed)
+    fixed_pair = whole(pair_fixed_kernel, "pair_fixed", shape(3, CX, CY), fixed, fixed_other)
+    fixed_chips = all_chips(fixed_pair)
+    partials, at_slots, live, wells = pl.pallas_call(
         wells_first_kernel,
-        out_shape=(
-            shape(3 * TILES, 4, 128),
-            shape(LZ, 128),
-            shape(LZ, 128),
-            shape(1, 128),
-            shape(2, rows, 128),
-        ),
-        in_specs=[VMEM] + [ANY] * 7,
-        out_specs=(VMEM,) * 5,
+        out_shape=(shape(3 * TILES, 4, 128), shape(LZ, 128), shape(LZ, 128), shape(1, 128)),
+        in_specs=[ANY] * 8,
+        out_specs=(VMEM,) * 4,
         scratch_shapes=[
+            pltpu.VMEM((2, rows, 128), F32),
+            pltpu.VMEM((16, 128), F32),
             pltpu.VMEM((LZ, SLOTS), F32),
             pltpu.VMEM((1, SLOTS), jnp.int32),
             pltpu.VMEM((1, SLOTS), jnp.int32),
             pltpu.VMEM((1, 8), F32),
             pltpu.SMEM((1, SLOTS), jnp.int32),
             pltpu.SMEM((1, 1), jnp.int32),
-            pltpu.SemaphoreType.DMA((8,)),
+            pltpu.SemaphoreType.DMA((9,)),
         ],
         compiler_params=params(WELLS_MIB),
         name="first_wells",
     )(y_edge, pressure, index, owner, perf_well, well_rate, perf_column, tile_count)
-    sums = None
+    field = pressure
+    k_sides = sides
+    ky_sides = sums = None
     for sweep_step in range(ITERS):
         first, last = sweep_step == 0, sweep_step == ITERS - 1
         if first:
-            partials, *sides = lax.optimization_barrier((partials, *sides))
+            partials, fixed_pair = lax.optimization_barrier((partials, fixed_pair))
         spread = lax.all_to_all(partials, ("gx", "gy"), split_axis=0, concat_axis=0, tiled=True)
-        extra = () if first else (*ky_sides, sums)
-        solved, carried, small, *ky_out = pl.pallas_call(
-            functools.partial(solve_kernel, first),
+        if first:
+            spread, *fixed_chips = lax.optimization_barrier((spread, *fixed_chips))
+        small = sides if first else (*sides, *k_sides, *ky_sides, sums)
+        operands = (perf_column, spread, live, wells, at_slots, *small, field, kx, ky, source, lower, inverse)
+        held = [pltpu.VMEM(value.shape, value.dtype) for value in operands]
+        held[len(operands) - 6] = pltpu.VMEM((2, rows, 128), F32)
+        solved, carried, *small = pl.pallas_call(
+            functools.partial(solve_kernel, first, len(operands)),
             out_shape=(shape(rows, CY), shape(2, CX, CY))
-            + ((shape(2, 128), shape(8, 128), shape(8, 128)) if first else (shape(LZ, SLOTS),)),
-            in_specs=[VMEM] * (12 + len(extra)) + [ANY],
-            out_specs=(VMEM,) * (5 if first else 3),
-            scratch_shapes=[
+            + ((shape(2, 128), shape(8, 128), shape(8, 128), shape(2, LZ, CX, CY)) if first else (shape(LZ, SLOTS),)),
+            in_specs=[ANY] * len(operands),
+            out_specs=(VMEM,) * (6 if first else 3),
+            scratch_shapes=held
+            + [
                 pltpu.VMEM((2, rows, 128), F32),
                 pltpu.SMEM((1, SLOTS), jnp.int32),
-                pltpu.SemaphoreType.DMA((1,)),
+                pltpu.SemaphoreType.DMA((len(operands) + 1,)),
             ],
-            compiler_params=params(),
+            compiler_params=params(SOLVE_MIB),
             name="solve_lines",
-        )(field, source, kx, ky, inverse, lower, *sides, spread, *extra, live, wells, at_slots, perf_column)
-        groups = all_groups(carried)
+        )(*operands)
+        if first:
+            *small, rims = small
+        other = swapped(carried)
+        chips = all_chips(whole(pair_kernel, "pair", shape(2, CX, CY), carried, other, fixed, fixed_other))
+        planes = (*chips, *fixed_chips, carried, other, fixed, fixed_other, solved, rims)
         if last:
-            flow = small
-            (field,) = pl.pallas_call(
-                functools.partial(sweep_kernel, True),
-                out_shape=(shape(rows, CY),),
-                in_specs=[VMEM] * 18,
-                out_specs=(VMEM,),
-                compiler_params=params(),
-                name="sweep_last",
-            )(*groups, *fixed, solved, inverse)
+            (field,) = whole(functools.partial(sweep_kernel, True), "sweep_last", (shape(rows, CY),), *planes)
+            (flow,) = small
             break
-        sums, ky_sides = small, ky_out
-        field, lower = pl.pallas_call(
+        sums, *ky_sides = small
+        field, lower, *edges = whole(
             functools.partial(sweep_kernel, False),
-            out_shape=(
-                shape(2, rows, 128),
-                shape(CX, CY),
-            ),
-            in_specs=[VMEM] * 18,
-            out_specs=(VMEM,) * 2,
-            compiler_params=params(),
-            name="sweep_mid",
-        )(*groups, *fixed, solved, inverse)
+            "sweep_mid",
+            (shape(2, rows, 128), shape(CX, CY), shape(8, CY), shape(8, CY)),
+            *planes,
+        )
+        sides = from_sides(*edges)
         partials, at_slots = pl.pallas_call(
             wells_next_kernel,
-            out_shape=(shape(9 * TILES, 2, 128), shape(LZ, 128)),
-            in_specs=[VMEM] * 3 + [ANY] * 2,
+            out_shape=(shape(3 * TILES, 2, 128), shape(LZ, 128)),
+            in_specs=[VMEM] + [ANY] * 4,
             out_specs=(VMEM,) * 2,
             scratch_shapes=[
+                pltpu.VMEM((LZ, 128), F32),
+                pltpu.VMEM((1, 128), F32),
                 pltpu.VMEM((1, 8), F32),
                 pltpu.SMEM((1, SLOTS), jnp.int32),
-                pltpu.SemaphoreType.DMA((2,)),
+                pltpu.SemaphoreType.DMA((4,)),
             ],
             compiler_params=params(),
             name="next_wells",

time: 95.1 us -> 92.2 us (0.970)
  waiting for transfers between devices: 5.98 us -> 34.4 us
  blocking collectives: 21.3 us -> 0 us
  starting transfers between devices: 47.5 us -> 36.9 us
  Pallas kernels: 13.7 us -> 16.8 us
  local copies, waits for them, and re-layouts: 4.75 us -> 2.35 us
    ppermute x21 -> x12, waiting for transfers between devices: 5.97 us -> 28.1 us  [the longest x9 26.1 us: all_chips(): lax.ppermute(value, 'layer', around(GROUPS, 2 * d))]
    all_to_all x1 -> x0, blocking collectives: 21.3 us -> none  [shards(): lax.all_to_all(partials, ('gx', 'gy'), split_axis=0, concat_axis=0, tiled...]
    ppermute x21 -> x12, starting transfers between devices: 32.7 us -> 12.7 us  [the longest x9 6.77 us: all_chips(): lax.ppermute(value, 'layer', around(GROUPS, 2 * d))]
    all_to_all x1 -> x2, starting transfers between devices: 8.22 us -> 18.7 us  [shards(): lax.all_to_all(partials, ('gx', 'gy'), split_axis=0, concat_axis=0, tiled...]
    all_to_all x1 -> x2, waiting for transfers between devices: 0.01 us -> 5.04 us  [shards(): lax.all_to_all(partials, ('gx', 'gy'), split_axis=0, concat_axis=0, tiled...]
    pallas_call x5 -> x8, Pallas kernels: 9.03 us -> 12.9 us  [the longest x2 9.36 us: shards(): pl.pallas_call(functools.partial(solve_kernel, first, len(operands)), out...]
    unnamed x32 -> x22, local copies, waits for them, and re-layouts: 4.75 us -> 2.35 us
    ppermute x1 -> x2, waiting for transfers between devices: 0.01 us -> 1.29 us  [from_sides(): lax.ppermute(xhi, 'gx', around(8, 1))]
  transfers between devices with their start and end apart: 24 -> 18, of which waited for: 5 -> 12; matrix products, arithmetic and copies ran while one was open for 0% -> 0% of each run, Pallas kernels for 5% -> 2%
where the time goes in v4:
time: 92.2 us; the launch traced here: 91.9 us
  starting transfers between devices  36.9 us (40%)
  waiting for transfers between devices  34.4 us (37%)
  Pallas kernels  16.8 us (18%)
  local copies, waits for them, and re-layouts  2.35 us (3%)
  between operations  1.51 us (2%)
    ppermute x9, waiting for transfers between devices, all_chips(): lax.ppermute(value, 'layer', around(GROUPS, 2 * d))  26.1 us
    all_to_all x2, starting transfers between devices, shards(): lax.all_to_all(partials, ('gx', 'gy'), split_axis=0, concat_axis=0, tiled...  18.7 us
    pallas_call x2, Pallas kernels, shards(): pl.pallas_call(functools.partial(solve_kernel, first, len(operands)), out...  9.36 us
    ppermute x9, starting transfers between devices, all_chips(): lax.ppermute(value, 'layer', around(GROUPS, 2 * d))  6.77 us
    ppermute x3, starting transfers between devices, swapped(): return lax.ppermute(value, 'layer', [(i, i ^ 1) for i in range(GROUPS)])  5.94 us
    all_to_all x2, waiting for transfers between devices, shards(): lax.all_to_all(partials, ('gx', 'gy'), split_axis=0, concat_axis=0, tiled...  5.04 us
    ppermute x2, starting transfers between devices, from_sides(): lax.ppermute(xlo, 'gx', around(8, -1))  2.89 us
    ppermute x2, starting transfers between devices, from_sides(): lax.ppermute(xhi, 'gx', around(8, 1))  2.54 us
  transfers between devices with their start and end apart: 18, of which 12 were waited for; matrix products, arithmetic and copies ran while one was open for 0% of the time, Pallas kernels for 2%

profile of v4, /device:TPU:1, one launch (start us, length us, event | category | flops | bytes accessed | tf_op | source)
XLA Modules:
  0.0 91.9 jit_solution(6081202733001998674)
XLA Ops:
  0.6 0.0 copy-start
  0.6 0.0 copy-start.1
  0.7 1.1 %copy-done.1 = f32[8,64,256]{2,1,0:T(8,128)S(1)} copy-done((f32[8,64,256]{2,1,0:T(8,128)S(1)}, f32[8,64,256]{2,1,0:T(8,128)}, u32[]{:S(2)}) %copy-start.1) | copy-done | bytes 524312
  1.8 1.7 %first_edges.1 = (f32[16,256]{1,0:T(8,128)S(1)}, f32[16,256]{1,0:T(8,128)S(1)}, f32[16,128]{1,0:T(8,128)S(1)}, f32[3,64,256]{2,1,0:T(8,128)S(1)}) custom-call(f32[512,256]{1,0:T(8,128)S(1)} %bitcast.16, f32[8,64,256]{2,1,0:T(8,128)} %perm_x.1, f32[512,256]{1,0:T(8,128)} %bitcast.25, f32[8,8,64,256]{3,2,1,0:T(8,128)} %bitcast.22), custom_call_target="tpu_custom_call" | custom-call | tf_op jit(solution)/shard_map/first_edges/pallas_call | solution.py:487
  3.5 3.3 %collective-permute-start = (f32[3,64,256]{2,1,0:T(8,128)S(1)}, f32[3,64,256]{2,1,0:T(8,128)S(1)}, u32[]{:S(2)}, u32[]{:S(2)}) collective-permute-start(f32[3,64,256]{2,1,0:T(8,128)S(1)} %get-tuple-element.33.mine.fixed_mine.refs_10_), channel_id=1, source_target_pairs={{0,32},{32,0},{64,96},{96,64},{128,160},{160,128},{192,224},{224,1... | collective-permute-start | bytes 589832 | tf_op jit(solution)/shard_map/ppermute | solution.py:445
  7.5 2.2 %first_wells.1 = (f32[96,4,128]{2,1,0:T(4,128)}, f32[8,128]{1,0:T(8,128)S(1)}, f32[8,128]{1,0:T(8,128)S(1)}, f32[1,128]{1,0:T(1,128)S(1)}) custom-call(f32[16,128]{1,0:T(8,128)S(1)} %get-tuple-element.31.refs_0_, f32[512,256]{1,0:T(8,128)S(1)} %bitcast.17, f32[8,48]{1,0:T(8,128)S(1)} %bitcast.20, s32[1,48]{1,0:T(1,128)S(1)} %bitcast.21, ...), custom_call_target="tpu_custom_call" | custom-call | tf_op jit(solution)/shard_map/first_wells/pallas_call | solution.py:506
  9.7 0.0 collective-permute-done.other.fixed_other.refs_11_
  9.8 9.5 %all-to-all-start = ((f32[96,4,128]{2,1,0:T(4,128)}), f32[96,4,128]{2,1,0:T(4,128)S(1)}, u32[]{:S(2)}, u32[]{:S(2)}) async-start(f32[96,4,128]{2,1,0:T(4,128)} %get-tuple-element.34), calls=%async_computation | async-start | bytes 393216 | tf_op jit(solution)/shard_map/all_to_all | solution.py:532
  19.3 2.6 %collective-permute-start.3 = (f32[3,64,256]{2,1,0:T(8,128)S(1)}, f32[3,64,256]{2,1,0:T(8,128)S(1)}, u32[]{:S(2)}, u32[]{:S(2)}) collective-permute-start(f32[3,64,256]{2,1,0:T(8,128)S(1)} %pair_fixed.1.refs_4_), channel_id=1, source_target_pairs={{0,192},{32,224},{64,0},{96,32},{128,64},{160,96},{192,128},{224,1... | collective-permute-start | bytes 589832 | tf_op jit(solution)/shard_map/ppermute | solution.py:449
  21.8 0.5 collective-permute-start.2
  22.4 0.6 collective-permute-start.1
  23.0 1.2 %collective-permute-start.4 = (f32[16,256]{1,0:T(8,128)S(1)}, f32[16,256]{1,0:T(8,128)S(1)}, u32[]{:S(2)}, u32[]{:S(2)}) collective-permute-start(f32[16,256]{1,0:T(8,128)S(1)} %get-tuple-element.39), channel_id=1, source_target_pairs={{0,4},{4,8},{8,12},{12,16},{16,20},{20,24},{24,28},{28,0},{1,5},{5... | collective-permute-start | bytes 49160 | tf_op jit(solution)/shard_map/ppermute | solution.py:441
  24.2 1.4 %collective-permute-start.5 = (f32[16,256]{1,0:T(8,128)S(1)}, f32[16,256]{1,0:T(8,128)S(1)}, u32[]{:S(2)}, u32[]{:S(2)}) collective-permute-start(f32[16,256]{1,0:T(8,128)S(1)} %get-tuple-element.40), channel_id=1, source_target_pairs={{0,28},{4,0},{8,4},{12,8},{16,12},{20,16},{24,20},{28,24},{1,29},{... | collective-permute-start | bytes 49160 | tf_op jit(solution)/shard_map/ppermute | solution.py:441
  25.6 4.3 %collective-permute-done.3.refs_7_ = f32[3,64,256]{2,1,0:T(8,128)S(1)} collective-permute-done((f32[3,64,256]{2,1,0:T(8,128)S(1)}, f32[3,64,256]{2,1,0:T(8,128)S(1)}, u32[]{:S(2)}, u32[]{:S(2)}) %collective-permute-start.3) | collective-permute-done | bytes 196640 | tf_op jit(solution)/shard_map/ppermute | solution.py:449
  29.9 0.0 collective-permute-done.2.refs_6_
  29.9 4.5 %collective-permute-done.1.refs_5_ = f32[3,64,256]{2,1,0:T(8,128)S(1)} collective-permute-done((f32[3,64,256]{2,1,0:T(8,128)S(1)}, f32[3,64,256]{2,1,0:T(8,128)S(1)}, u32[]{:S(2)}, u32[]{:S(2)}) %collective-permute-start.1) | collective-permute-done | bytes 196640 | tf_op jit(solution)/shard_map/ppermute | solution.py:449
  34.4 0.0 all-to-all-done.refs_1_
  34.4 0.0 collective-permute-done.4.refs_5_.refs_7_
  34.4 0.0 collective-permute-done.5.refs_6_.refs_8_
  34.4 0.0 copy-done
  34.4 5.0 %solve_lines.2 = (f32[512,256]{1,0:T(8,128)S(1)}, f32[2,64,256]{2,1,0:T(8,128)S(1)}, f32[2,128]{1,0:T(2,128)S(1)}, f32[8,128]{1,0:T(8,128)S(1)}, f32[8,128]{1,0:T(8,128)S(1)}, /*index=5*/f32[2,8,64,256]{3,2,1,0:T(8,128)}) custom-call(s32[1,48]{1,0:T(1,128)S(1)} %copy-done.6, f32[96,4,128]{2,1,0:T(4,128)S(1)} %all-to-all-done.refs_1_, ...), custom_call_target="tpu_custom_call" | custom-call | tf_op jit(solution)/shard_map/solve_lines/pallas_call | solution.py:539
  39.4 0.6 collective-permute-start.6
  40.0 1.0 %collective-permute-done.6.other.refs_9_ = f32[2,64,256]{2,1,0:T(8,128)S(1)} collective-permute-done((f32[2,64,256]{2,1,0:T(8,128)S(1)}, f32[2,64,256]{2,1,0:T(8,128)S(1)}, u32[]{:S(2)}, u32[]{:S(2)}) %collective-permute-start.6) | collective-permute-done | bytes 131104 | tf_op jit(solution)/shard_map/ppermute | solution.py:445
  41.0 0.4 collective-permute-start.9
  41.4 0.5 collective-permute-start.8
  41.9 0.6 collective-permute-start.7
  42.5 3.2 %collective-permute-done.9.refs_3_ = f32[2,64,256]{2,1,0:T(8,128)S(1)} collective-permute-done((f32[2,64,256]{2,1,0:T(8,128)S(1)}, f32[2,64,256]{2,1,0:T(8,128)S(1)}, u32[]{:S(2)}, u32[]{:S(2)}) %collective-permute-start.9) | collective-permute-done | bytes 131104 | tf_op jit(solution)/shard_map/ppermute | solution.py:449
  45.8 1.5 %collective-permute-done.8.refs_2_ = f32[2,64,256]{2,1,0:T(8,128)S(1)} collective-permute-done((f32[2,64,256]{2,1,0:T(8,128)S(1)}, f32[2,64,256]{2,1,0:T(8,128)S(1)}, u32[]{:S(2)}, u32[]{:S(2)}) %collective-permute-start.8) | collective-permute-done | bytes 131104 | tf_op jit(solution)/shard_map/ppermute | solution.py:449
  47.3 3.8 %collective-permute-done.7.refs_1_ = f32[2,64,256]{2,1,0:T(8,128)S(1)} collective-permute-done((f32[2,64,256]{2,1,0:T(8,128)S(1)}, f32[2,64,256]{2,1,0:T(8,128)S(1)}, u32[]{:S(2)}, u32[]{:S(2)}) %collective-permute-start.7) | collective-permute-done | bytes 131104 | tf_op jit(solution)/shard_map/ppermute | solution.py:449
  51.1 1.2 %copy-done.3 = f32[2,8,64,256]{3,2,1,0:T(8,128)S(1)} copy-done((f32[2,8,64,256]{3,2,1,0:T(8,128)S(1)}, f32[2,8,64,256]{3,2,1,0:T(8,128)}, u32[]{:S(2)}) %copy-start.3) | copy-done | bytes 1048600
  52.4 0.3 sweep_mid.1
  52.6 2.1 %next_wells.1 = (f32[96,2,128]{2,1,0:T(2,128)}, f32[8,128]{1,0:T(8,128)S(1)}) custom-call(f32[2,512,128]{2,1,0:T(8,128)S(1)} %get-tuple-element.48.split.refs_12_, f32[8,128]{1,0:T(8,128)S(1)} %get-tuple-element.36.refs_2_.live, f32[1,128]{1,0:T(1,128)S(1)} %get-tuple-element.37.refs_3_.wells, f32[1,8]{1,0:T(1,128)S(1)} %copy-done.8, s32[1,48]{1,0:T(1,128)S(1)} %copy-done.6), custom_call_target="tpu_custom_call" | custom-call | tf_op jit(solution)/shard_map/next_wells/pallas_call | solution.py:571
  54.8 9.2 %all-to-all-start.1 = ((f32[96,2,128]{2,1,0:T(2,128)}), f32[96,2,128]{2,1,0:T(2,128)S(1)}, u32[]{:S(2)}, u32[]{:S(2)}) async-start(f32[96,2,128]{2,1,0:T(2,128)} %get-tuple-element.49), calls=%async_computation.1 | async-start | bytes 196608 | tf_op jit(solution)/shard_map/all_to_all | solution.py:532
  64.0 1.3 %collective-permute-start.10 = (f32[8,256]{1,0:T(8,128)S(1)}, f32[8,256]{1,0:T(8,128)S(1)}, u32[]{:S(2)}, u32[]{:S(2)}) collective-permute-start(f32[8,256]{1,0:T(8,128)S(1)} %get-tuple-element.51), channel_id=1, source_target_pairs={{0,4},{4,8},{8,12},{12,16},{16,20},{20,24},{24,28},{28,0},{1,5},{5... | collective-permute-start | bytes 24584 | tf_op jit(solution)/shard_map/ppermute | solution.py:441
  65.3 1.4 %collective-permute-start.11 = (f32[8,256]{1,0:T(8,128)S(1)}, f32[8,256]{1,0:T(8,128)S(1)}, u32[]{:S(2)}, u32[]{:S(2)}) collective-permute-start(f32[8,256]{1,0:T(8,128)S(1)} %get-tuple-element.52), channel_id=1, source_target_pairs={{0,28},{4,0},{8,4},{12,8},{16,12},{20,16},{24,20},{28,24},{1,29},{... | collective-permute-start | bytes 24584 | tf_op jit(solution)/shard_map/ppermute | solution.py:441
  66.8 1.3 %collective-permute-done.10.refs_5_ = f32[8,256]{1,0:T(8,128)S(1)} collective-permute-done((f32[8,256]{1,0:T(8,128)S(1)}, f32[8,256]{1,0:T(8,128)S(1)}, u32[]{:S(2)}, u32[]{:S(2)}) %collective-permute-start.10) | collective-permute-done | bytes 8224 | tf_op jit(solution)/shard_map/ppermute | solution.py:441
  68.1 0.0 collective-permute-done.11.refs_6_
  68.1 5.0 %all-to-all-done.1.refs_1_ = f32[96,2,128]{2,1,0:T(2,128)S(1)} async-done(((f32[96,2,128]{2,1,0:T(2,128)}), f32[96,2,128]{2,1,0:T(2,128)S(1)}, u32[]{:S(2)}, u32[]{:S(2)}) %all-to-all-start.1) | async-done | bytes 98336 | tf_op jit(solution)/shard_map/all_to_all | solution.py:532
  73.1 4.4 %solve_lines.3 = (f32[512,256]{1,0:T(8,128)S(1)}, f32[2,64,256]{2,1,0:T(8,128)S(1)}, f32[8,48]{1,0:T(8,128)}) custom-call(s32[1,48]{1,0:T(1,128)S(1)} %copy-done.6, f32[96,2,128]{2,1,0:T(2,128)S(1)} %all-to-all-done.1.refs_1_, f32[8,128]{1,0:T(8,128)S(1)} %get-tuple-element.36.refs_2_.live, f32[1,128]{1,0:T(1,128)S(1)} %get-tuple-element.37.refs_3_.wells, ...), custom_call_target="tpu_custom_call" | custom-call | tf_op jit(solution)/shard_map/solve_lines/pallas_call | solution.py:539
  77.5 2.0 %collective-permute-start.12 = (f32[2,64,256]{2,1,0:T(8,128)S(1)}, f32[2,64,256]{2,1,0:T(8,128)S(1)}, u32[]{:S(2)}, u32[]{:S(2)}) collective-permute-start(f32[2,64,256]{2,1,0:T(8,128)S(1)} %get-tuple-element.57.mine.refs_8_), channel_id=1, source_target_pairs={{0,32},{32,0},{64,96},{96,64},{128,160},{160,128},{192,224},{224,1... | collective-permute-start | bytes 393224 | tf_op jit(solution)/shard_map/ppermute | solution.py:445
  79.5 1.0 %collective-permute-done.12.other.refs_9_ = f32[2,64,256]{2,1,0:T(8,128)S(1)} collective-permute-done((f32[2,64,256]{2,1,0:T(8,128)S(1)}, f32[2,64,256]{2,1,0:T(8,128)S(1)}, u32[]{:S(2)}, u32[]{:S(2)}) %collective-permute-start.12) | collective-permute-done | bytes 131104 | tf_op jit(solution)/shard_map/ppermute | solution.py:445
  80.5 0.6 collective-permute-start.15
  81.1 0.2 collective-permute-start.14
  81.3 0.8 collective-permute-start.13
  82.1 3.2 %collective-permute-done.15.refs_3_ = f32[2,64,256]{2,1,0:T(8,128)S(1)} collective-permute-done((f32[2,64,256]{2,1,0:T(8,128)S(1)}, f32[2,64,256]{2,1,0:T(8,128)S(1)}, u32[]{:S(2)}, u32[]{:S(2)}) %collective-permute-start.15) | collective-permute-done | bytes 131104 | tf_op jit(solution)/shard_map/ppermute | solution.py:449
  85.3 1.7 %collective-permute-done.14.refs_2_ = f32[2,64,256]{2,1,0:T(8,128)S(1)} collective-permute-done((f32[2,64,256]{2,1,0:T(8,128)S(1)}, f32[2,64,256]{2,1,0:T(8,128)S(1)}, u32[]{:S(2)}, u32[]{:S(2)}) %collective-permute-start.14) | collective-permute-done | bytes 131104 | tf_op jit(solution)/shard_map/ppermute | solution.py:449
  87.0 3.8 %collective-permute-done.13.refs_1_ = f32[2,64,256]{2,1,0:T(8,128)S(1)} collective-permute-done((f32[2,64,256]{2,1,0:T(8,128)S(1)}, f32[2,64,256]{2,1,0:T(8,128)S(1)}, u32[]{:S(2)}, u32[]{:S(2)}) %collective-permute-start.13) | collective-permute-done | bytes 131104 | tf_op jit(solution)/shard_map/ppermute | solution.py:449
  90.9 1.0 %sweep_last.1 = f32[512,256]{1,0:T(8,128)} custom-call(f32[2,64,256]{2,1,0:T(8,128)S(1)} %pair.3.refs_0_, f32[2,64,256]{2,1,0:T(8,128)S(1)} %collective-permute-done.13.refs_1_, f32[2,64,256]{2,1,0:T(8,128)S(1)} %collective-permute-done.14.refs_2_, f32[2,64,256]{2,1,0:T(8,128)S(1)} %collective-permute-done.15.refs_3_, f32[3,64,256]{2,1,0:T(8,128)S(1)} %pair_fixed.1.refs_4_, ...), custom_call_target="tpu_custom_call" | custom-call | tf_op jit(solution)/shard_map/sweep_last/pallas_call | solution.py:453
  (20 shorter events, 0.1 us)
Async XLA Ops:
  0.6 33.8 %copy-start = (f32[8,64,256]{2,1,0:T(8,128)S(1)}, f32[8,64,256]{2,1,0:T(8,128)}, u32[]{:S(2)}) copy-start(f32[8,64,256]{2,1,0:T(8,128)} %perm_x.1) | copy-start | bytes 1572868
  0.6 1.1 %copy-start.1 = (f32[8,64,256]{2,1,0:T(8,128)S(1)}, f32[8,64,256]{2,1,0:T(8,128)}, u32[]{:S(2)}) copy-start(f32[8,64,256]{2,1,0:T(8,128)} %param.12) | copy-start | bytes 1572868
  1.7 5.7 %copy-start.6 = (s32[1,48]{1,0:T(1,128)S(1)}, s32[1,48]{1,0:T(1,128)}, u32[]{:S(2)}) copy-start(s32[1,48]{1,0:T(1,128)} %refs_0_.3) | copy-start | bytes 580
  1.7 5.7 %copy-start.7 = (f32[1,48,8]{1,2,0:T(8,128)S(1)}, f32[1,48,8]{1,2,0:T(8,128)}, u32[]{:S(2)}) copy-start(f32[1,48,8]{1,2,0:T(8,128)} %param.22) | copy-start | bytes 4612
  1.7 5.7 %copy-start.8 = (f32[1,8]{1,0:T(1,128)S(1)}, f32[1,8]{1,0:T(1,128)}, u32[]{:S(2)}) copy-start(f32[1,8]{1,0:T(1,128)} %rate.1) | copy-start | bytes 100
  1.7 5.8 %copy-start.9 = (s32[1,48,1]{1,2,0:T(1,128)S(1)}, s32[1,48,1]{1,2,0:T(1,128)}, u32[]{:S(2)}) copy-start(s32[1,48,1]{1,2,0:T(1,128)} %param.19) | copy-start | bytes 580
  1.8 5.8 %copy-start.10 = (s32[1,48]{1,0:T(1,128)S(1)}, s32[1,48]{1,0:T(1,128)}, u32[]{:S(2)}) copy-start(s32[1,48]{1,0:T(1,128)} %refs_4_.1) | copy-start | bytes 580
  1.8 32.6 %copy-start.2 = (f32[8,64,256]{2,1,0:T(8,128)S(1)}, f32[8,64,256]{2,1,0:T(8,128)}, u32[]{:S(2)}) copy-start(f32[8,64,256]{2,1,0:T(8,128)} %param.12) | copy-start | bytes 1572868
  1.8 32.6 %copy-start.5 = (f32[1,64,256]{2,1,0:T(8,128)S(1)}, f32[1,64,256]{2,1,0:T(8,128)}, u32[]{:S(2)}) copy-start(f32[1,64,256]{2,1,0:T(8,128)} %param.17) | copy-start | bytes 196612
  3.5 6.2 %collective-permute-start = (f32[3,64,256]{2,1,0:T(8,128)S(1)}, f32[3,64,256]{2,1,0:T(8,128)S(1)}, u32[]{:S(2)}, u32[]{:S(2)}) collective-permute-start(f32[3,64,256]{2,1,0:T(8,128)S(1)} %get-tuple-element.33.mine.fixed_mine.refs_10_), channel_id=1, source_target_pairs={{0,32},{32,0},{64,96},{96,64},{128,160},{160,128},{192,224},{224,1... | collective-permute-start | bytes 589832 | tf_op jit(solution)/shard_map/ppermute | solution.py:445
  9.8 24.6 %all-to-all-start = ((f32[96,4,128]{2,1,0:T(4,128)}), f32[96,4,128]{2,1,0:T(4,128)S(1)}, u32[]{:S(2)}, u32[]{:S(2)}) async-start(f32[96,4,128]{2,1,0:T(4,128)} %get-tuple-element.34), calls=%async_computation | async-start | bytes 393216 | tf_op jit(solution)/shard_map/all_to_all | solution.py:532
  19.3 10.6 %collective-permute-start.3 = (f32[3,64,256]{2,1,0:T(8,128)S(1)}, f32[3,64,256]{2,1,0:T(8,128)S(1)}, u32[]{:S(2)}, u32[]{:S(2)}) collective-permute-start(f32[3,64,256]{2,1,0:T(8,128)S(1)} %pair_fixed.1.refs_4_), channel_id=1, source_target_pairs={{0,192},{32,224},{64,0},{96,32},{128,64},{160,96},{192,128},{224,1... | collective-permute-start | bytes 589832 | tf_op jit(solution)/shard_map/ppermute | solution.py:449
  21.8 8.1 %collective-permute-start.2 = (f32[3,64,256]{2,1,0:T(8,128)S(1)}, f32[3,64,256]{2,1,0:T(8,128)S(1)}, u32[]{:S(2)}, u32[]{:S(2)}) collective-permute-start(f32[3,64,256]{2,1,0:T(8,128)S(1)} %pair_fixed.1.refs_4_), channel_id=1, source_target_pairs={{0,128},{32,160},{64,192},{96,224},{128,0},{160,32},{192,64},{224,... | collective-permute-start | bytes 589832 | tf_op jit(solution)/shard_map/ppermute | solution.py:449
  22.4 12.0 %collective-permute-start.1 = (f32[3,64,256]{2,1,0:T(8,128)S(1)}, f32[3,64,256]{2,1,0:T(8,128)S(1)}, u32[]{:S(2)}, u32[]{:S(2)}) collective-permute-start(f32[3,64,256]{2,1,0:T(8,128)S(1)} %pair_fixed.1.refs_4_), channel_id=1, source_target_pairs={{0,64},{32,96},{64,128},{96,160},{128,192},{160,224},{192,0},{224,... | collective-permute-start | bytes 589832 | tf_op jit(solution)/shard_map/ppermute | solution.py:449
  23.0 11.4 %collective-permute-start.4 = (f32[16,256]{1,0:T(8,128)S(1)}, f32[16,256]{1,0:T(8,128)S(1)}, u32[]{:S(2)}, u32[]{:S(2)}) collective-permute-start(f32[16,256]{1,0:T(8,128)S(1)} %get-tuple-element.39), channel_id=1, source_target_pairs={{0,4},{4,8},{8,12},{12,16},{16,20},{20,24},{24,28},{28,0},{1,5},{5... | collective-permute-start | bytes 49160 | tf_op jit(solution)/shard_map/ppermute | solution.py:441
  24.2 10.2 %collective-permute-start.5 = (f32[16,256]{1,0:T(8,128)S(1)}, f32[16,256]{1,0:T(8,128)S(1)}, u32[]{:S(2)}, u32[]{:S(2)}) collective-permute-start(f32[16,256]{1,0:T(8,128)S(1)} %get-tuple-element.40), channel_id=1, source_target_pairs={{0,28},{4,0},{8,4},{12,8},{16,12},{20,16},{24,20},{28,24},{1,29},{... | collective-permute-start | bytes 49160 | tf_op jit(solution)/shard_map/ppermute | solution.py:441
  39.4 1.6 %collective-permute-start.6 = (f32[2,64,256]{2,1,0:T(8,128)S(1)}, f32[2,64,256]{2,1,0:T(8,128)S(1)}, u32[]{:S(2)}, u32[]{:S(2)}) collective-permute-start(f32[2,64,256]{2,1,0:T(8,128)S(1)} %get-tuple-element.41.mine.refs_8_), channel_id=1, source_target_pairs={{0,32},{32,0},{64,96},{96,64},{128,160},{160,128},{192,224},{224,1... | collective-permute-start | bytes 393224 | tf_op jit(solution)/shard_map/ppermute | solution.py:445
  41.0 4.8 %collective-permute-start.9 = (f32[2,64,256]{2,1,0:T(8,128)S(1)}, f32[2,64,256]{2,1,0:T(8,128)S(1)}, u32[]{:S(2)}, u32[]{:S(2)}) collective-permute-start(f32[2,64,256]{2,1,0:T(8,128)S(1)} %pair.2.refs_0_), channel_id=1, source_target_pairs={{0,192},{32,224},{64,0},{96,32},{128,64},{160,96},{192,128},{224,1... | collective-permute-start | bytes 393224 | tf_op jit(solution)/shard_map/ppermute | solution.py:449
  41.4 5.9 %collective-permute-start.8 = (f32[2,64,256]{2,1,0:T(8,128)S(1)}, f32[2,64,256]{2,1,0:T(8,128)S(1)}, u32[]{:S(2)}, u32[]{:S(2)}) collective-permute-start(f32[2,64,256]{2,1,0:T(8,128)S(1)} %pair.2.refs_0_), channel_id=1, source_target_pairs={{0,128},{32,160},{64,192},{96,224},{128,0},{160,32},{192,64},{224,... | collective-permute-start | bytes 393224 | tf_op jit(solution)/shard_map/ppermute | solution.py:449
  41.9 9.2 %collective-permute-start.7 = (f32[2,64,256]{2,1,0:T(8,128)S(1)}, f32[2,64,256]{2,1,0:T(8,128)S(1)}, u32[]{:S(2)}, u32[]{:S(2)}) collective-permute-start(f32[2,64,256]{2,1,0:T(8,128)S(1)} %pair.2.refs_0_), channel_id=1, source_target_pairs={{0,64},{32,96},{64,128},{96,160},{128,192},{160,224},{192,0},{224,... | collective-permute-start | bytes 393224 | tf_op jit(solution)/shard_map/ppermute | solution.py:449
  51.1 1.2 %copy-start.3 = (f32[2,8,64,256]{3,2,1,0:T(8,128)S(1)}, f32[2,8,64,256]{3,2,1,0:T(8,128)}, u32[]{:S(2)}) copy-start(f32[2,8,64,256]{3,2,1,0:T(8,128)} %get-tuple-element.47.refs_13_) | copy-start | bytes 3145732
  52.6 38.2 %copy-start.4 = (f32[2,8,64,256]{3,2,1,0:T(8,128)S(1)}, f32[2,8,64,256]{3,2,1,0:T(8,128)}, u32[]{:S(2)}) copy-start(f32[2,8,64,256]{3,2,1,0:T(8,128)} %get-tuple-element.47.refs_13_) | copy-start | bytes 3145732
  54.8 18.3 %all-to-all-start.1 = ((f32[96,2,128]{2,1,0:T(2,128)}), f32[96,2,128]{2,1,0:T(2,128)S(1)}, u32[]{:S(2)}, u32[]{:S(2)}) async-start(f32[96,2,128]{2,1,0:T(2,128)} %get-tuple-element.49), calls=%async_computation.1 | async-start | bytes 196608 | tf_op jit(solution)/shard_map/all_to_all | solution.py:532
  64.0 4.0 %collective-permute-start.10 = (f32[8,256]{1,0:T(8,128)S(1)}, f32[8,256]{1,0:T(8,128)S(1)}, u32[]{:S(2)}, u32[]{:S(2)}) collective-permute-start(f32[8,256]{1,0:T(8,128)S(1)} %get-tuple-element.51), channel_id=1, source_target_pairs={{0,4},{4,8},{8,12},{12,16},{16,20},{20,24},{24,28},{28,0},{1,5},{5... | collective-permute-start | bytes 24584 | tf_op jit(solution)/shard_map/ppermute | solution.py:441
  65.3 2.7 %collective-permute-start.11 = (f32[8,256]{1,0:T(8,128)S(1)}, f32[8,256]{1,0:T(8,128)S(1)}, u32[]{:S(2)}, u32[]{:S(2)}) collective-permute-start(f32[8,256]{1,0:T(8,128)S(1)} %get-tuple-element.52), channel_id=1, source_target_pairs={{0,28},{4,0},{8,4},{12,8},{16,12},{20,16},{24,20},{28,24},{1,29},{... | collective-permute-start | bytes 24584 | tf_op jit(solution)/shard_map/ppermute | solution.py:441
  77.5 3.0 %collective-permute-start.12 = (f32[2,64,256]{2,1,0:T(8,128)S(1)}, f32[2,64,256]{2,1,0:T(8,128)S(1)}, u32[]{:S(2)}, u32[]{:S(2)}) collective-permute-start(f32[2,64,256]{2,1,0:T(8,128)S(1)} %get-tuple-element.57.mine.refs_8_), channel_id=1, source_target_pairs={{0,32},{32,0},{64,96},{96,64},{128,160},{160,128},{192,224},{224,1... | collective-permute-start | bytes 393224 | tf_op jit(solution)/shard_map/ppermute | solution.py:445
  80.5 4.8 %collective-permute-start.15 = (f32[2,64,256]{2,1,0:T(8,128)S(1)}, f32[2,64,256]{2,1,0:T(8,128)S(1)}, u32[]{:S(2)}, u32[]{:S(2)}) collective-permute-start(f32[2,64,256]{2,1,0:T(8,128)S(1)} %pair.3.refs_0_), channel_id=1, source_target_pairs={{0,192},{32,224},{64,0},{96,32},{128,64},{160,96},{192,128},{224,1... | collective-permute-start | bytes 393224 | tf_op jit(solution)/shard_map/ppermute | solution.py:449
  81.1 5.9 %collective-permute-start.14 = (f32[2,64,256]{2,1,0:T(8,128)S(1)}, f32[2,64,256]{2,1,0:T(8,128)S(1)}, u32[]{:S(2)}, u32[]{:S(2)}) collective-permute-start(f32[2,64,256]{2,1,0:T(8,128)S(1)} %pair.3.refs_0_), channel_id=1, source_target_pairs={{0,128},{32,160},{64,192},{96,224},{128,0},{160,32},{192,64},{224,... | collective-permute-start | bytes 393224 | tf_op jit(solution)/shard_map/ppermute | solution.py:449
  81.3 9.5 %collective-permute-start.13 = (f32[2,64,256]{2,1,0:T(8,128)S(1)}, f32[2,64,256]{2,1,0:T(8,128)S(1)}, u32[]{:S(2)}, u32[]{:S(2)}) collective-permute-start(f32[2,64,256]{2,1,0:T(8,128)S(1)} %pair.3.refs_0_), channel_id=1, source_target_pairs={{0,64},{32,96},{64,128},{96,160},{128,192},{160,224},{192,0},{224,... | collective-permute-start | bytes 393224 | tf_op jit(solution)/shard_map/ppermute | solution.py:449

commit v5 on v4

--- a/solution.py
+++ b/solution.py
@@ -14,6 +14,7 @@
 LZ = 8
 CX = 64
 CY = 256
+HALF = CX // 2
 SLOTS = 48
 WELLS = 256
 TILES = 32
@@ -146,11 +147,20 @@
     return jnp.concatenate([split[0, span, :], split[1, span, :]], axis=1)
 
 
-def edges_kernel(pressure, perm_x, perm_y, inverse, xlo, xhi, y_edge, fixed, split, kx_lo, kx_hi, ky, sem):
+def rows_of(side):
+    core = lax.rem(lax.axis_index("layer") + side, 2)
+    return pl.ds(pl.multiple_of(core * HALF, HALF), HALF)
+
+
+def edges_kernel(pressure, perm_x, perm_y, inverse, xlo, xhi, y_edge, fixed, fixed_give, split, kx_lo, kx_hi, ky, sem):
     copies = load(
         [(pressure.at[:, half * 128 : half * 128 + 128], split.at[half]) for half in range(2)]
         + [(perm_x.at[:, 0:8], kx_lo), (perm_x.at[:, CX - 8 : CX], kx_hi), (perm_y, ky)]
-        + [(inverse.at[LZ - 1, 0], fixed.at[0]), (inverse.at[0, LZ - 1], fixed.at[1]), (inverse.at[0, 0], fixed.at[2])],
+        + [
+            (inverse.at[i, j, rows_of(side)], target.at[n])
+            for n, (i, j) in enumerate(((LZ - 1, 0), (0, LZ - 1), (0, 0)))
+            for side, target in ((0, fixed), (1, fixed_give))
+        ],
         sem,
     )
     for copy in copies[:5]:
@@ -223,10 +233,10 @@
 def solve_kernel(first, inputs, *refs):
     away, refs = refs[:inputs], refs[inputs:]
     if first:
-        (solved, carried, sums_out, kylo_out, kyhi_out, rims, *refs) = refs
+        (solved, keep, give, sums_out, kylo_out, kyhi_out, rims, *refs) = refs
     else:
-        (solved, carried, flow_out, *refs) = refs
-    held, (rhs, column_s, sem) = refs[:inputs], refs[inputs:]
+        (solved, keep, give, flow_out, *refs) = refs
+    held, (rhs, carried, column_s, sem) = refs[:inputs], refs[inputs:]
     (column, partials, live, wells, at_slots, *small, field, kx, ky, source, lower, inverse) = held
     held = dict(zip(range(inputs), held))
     wanted = [(away[0], column_s)] + [(away[n], held[n]) for n in range(1, inputs - 6)]
@@ -347,6 +357,8 @@
         return carry
 
     lax.fori_loop(0, CX // 8, solve_block, 0)
+    for side, out in ((0, keep), (1, give)):
+        out[...] = carried[:, rows_of(side), :]
 
 
 def by_core(body):
@@ -375,56 +387,74 @@
     by_core(body)
 
 
-def sweep_kernel(last, *refs):
+def chain_kernel(*refs):
     cds, fixed, refs = refs[:4], refs[4:8], refs[8:]
-    cd_mine, cd_other, fixed_mine, fixed_other, solved, rims, *refs = refs
-    if last:
-        (field,) = refs
-    else:
-        split, lower, xlo, xhi = refs
+    cd_mine, cd_other, fixed_mine, fixed_other, mine, give = refs
     me = lax.axis_index("layer")
 
     def position(own):
-        chip = own // 2
+        chip, even = own // 2, own % 2 == 0
+        cd_top, cd_low = (cd_mine, cd_other) if even else (cd_other, cd_mine)
+        fixed_top, fixed_low = (fixed_mine, fixed_other) if even else (fixed_other, fixed_mine)
+        out_top, out_low = (mine, give) if even else (give, mine)
 
         def block(b, carry):
             here = pl.ds(pl.multiple_of(b * 8, 8), 8)
-            upper = jnp.zeros((8, CY), F32)
-            uppers = [upper]
+            uppers = [jnp.zeros((8, CY), F32)]
             for c in range(3):
                 d = (chip - c) % 4
-                upper = fixed[d][0, here, :] * upper + cds[d][0, here, :]
-                uppers.append(upper)
+                uppers.append(fixed[d][0, here, :] * uppers[-1] + cds[d][0, here, :])
             low = jnp.zeros((8, CY), F32)
             for c in range(3, chip, -1):
                 d = (chip - c) % 4
                 step = cds[d][1, here, :] + fixed[d][2, here, :] * uppers[c] - uppers[c]
                 low = fixed[d][1, here, :] * low + step
             upper = uppers[chip]
-            if own % 2 == 0:
-                below = fixed_mine[0, here, :] * upper + cd_mine[0, here, :]
-                step = cd_other[1, here, :] + fixed_other[2, here, :] * below - below
-                low = fixed_other[1, here, :] * low + step
-            else:
-                upper = fixed_other[0, here, :] * upper + cd_other[0, here, :]
-            for i in range(LZ):
-                span = pl.ds(pl.multiple_of(i * CX + b * 8, 8), 8)
-                value = solved[span, :] + rims[0, i, here, :] * upper + rims[1, i, here, :] * low
-                if last:
-                    field[span, :] = value
-                else:
-                    split[0, span, :] = value[:, :128]
-                    split[1, span, :] = value[:, 128:]
-            if not last:
-                lower[here, :] = low
+            below = fixed_top[0, here, :] * upper + cd_top[0, here, :]
+            step = cd_low[1, here, :] + fixed_low[2, here, :] * below - below
+            out_top[0, here, :] = upper
+            out_top[1, here, :] = fixed_low[1, here, :] * low + step
+            out_low[0, here, :] = below
+            out_low[1, here, :] = low
             return carry
 
         @pl.when(me == own)
         def _():
-            lax.fori_loop(0, CX // 8, block, 0)
+            lax.fori_loop(0, HALF // 8, block, 0)
 
     for own in range(GROUPS):
         position(own)
+
+
+def sweep_kernel(last, mine, other, solved, rims, *refs):
+    if last:
+        (field,) = refs
+    else:
+        split, lower, xlo, xhi = refs
+
+    def body(own):
+        for side in range(2):
+            ends = mine if side == own else other
+
+            def block(b, carry):
+                there = pl.ds(pl.multiple_of(b * 8, 8), 8)
+                here = pl.ds(pl.multiple_of(side * HALF + b * 8, 8), 8)
+                upper, low = ends[0, there, :], ends[1, there, :]
+                for i in range(LZ):
+                    span = pl.ds(pl.multiple_of(i * CX + side * HALF + b * 8, 8), 8)
+                    value = solved[span, :] + rims[0, i, here, :] * upper + rims[1, i, here, :] * low
+                    if last:
+                        field[span, :] = value
+                    else:
+                        split[0, span, :] = value[:, :128]
+                        split[1, span, :] = value[:, 128:]
+                if not last:
+                    lower[here, :] = low
+                return carry
+
+            lax.fori_loop(0, HALF // 8, block, 0)
+
+    by_core(body)
     if not last:
         split_x_edges(split, xlo, xhi)
 
@@ -484,24 +514,24 @@
 
     kx = perm_x.reshape(rows, CY)
     ky = perm_y.reshape(rows, CY)
-    *edges, y_edge, fixed = pl.pallas_call(
+    *edges, y_edge, fixed, fixed_give = pl.pallas_call(
         edges_kernel,
-        out_shape=(shape(16, CY), shape(16, CY), shape(16, 128), shape(3, CX, CY)),
+        out_shape=(shape(16, CY), shape(16, CY), shape(16, 128), shape(3, HALF, CY), shape(3, HALF, CY)),
         in_specs=[ANY] * 4,
-        out_specs=(VMEM,) * 4,
+        out_specs=(VMEM,) * 5,
         scratch_shapes=[
             pltpu.VMEM((2, rows, 128), F32),
             pltpu.VMEM((LZ, 8, CY), F32),
             pltpu.VMEM((LZ, 8, CY), F32),
             pltpu.VMEM((rows, CY), F32),
-            pltpu.SemaphoreType.DMA((8,)),
+            pltpu.SemaphoreType.DMA((11,)),
         ],
         compiler_params=params(EDGE_MIB),
         name="first_edges",
     )(pressure, perm_x, ky, inverse)
     sides = from_sides(*edges)
-    fixed_other = swapped(fixed)
-    fixed_pair = whole(pair_fixed_kernel, "pair_fixed", shape(3, CX, CY), fixed, fixed_other)
+    fixed_other = swapped(fixed_give)
+    fixed_pair = whole(pair_fixed_kernel, "pair_fixed", shape(3, HALF, CY), fixed, fixed_other)
     fixed_chips = all_chips(fixed_pair)
     partials, at_slots, live, wells = pl.pallas_call(
         wells_first_kernel,
@@ -536,15 +566,16 @@
         operands = (perf_column, spread, live, wells, at_slots, *small, field, kx, ky, source, lower, inverse)
         held = [pltpu.VMEM(value.shape, value.dtype) for value in operands]
         held[len(operands) - 6] = pltpu.VMEM((2, rows, 128), F32)
-        solved, carried, *small = pl.pallas_call(
+        solved, carried, give, *small = pl.pallas_call(
             functools.partial(solve_kernel, first, len(operands)),
-            out_shape=(shape(rows, CY), shape(2, CX, CY))
+            out_shape=(shape(rows, CY), shape(2, HALF, CY), shape(2, HALF, CY))
             + ((shape(2, 128), shape(8, 128), shape(8, 128), shape(2, LZ, CX, CY)) if first else (shape(LZ, SLOTS),)),
             in_specs=[ANY] * len(operands),
-            out_specs=(VMEM,) * (6 if first else 3),
+            out_specs=(VMEM,) * (7 if first else 4),
             scratch_shapes=held
             + [
                 pltpu.VMEM((2, rows, 128), F32),
+                pltpu.VMEM((2, CX, CY), F32),
                 pltpu.SMEM((1, SLOTS), jnp.int32),
                 pltpu.SemaphoreType.DMA((len(operands) + 1,)),
             ],
@@ -553,9 +584,15 @@
         )(*operands)
         if first:
             *small, rims = small
-        other = swapped(carried)
-        chips = all_chips(whole(pair_kernel, "pair", shape(2, CX, CY), carried, other, fixed, fixed_other))
-        planes = (*chips, *fixed_chips, carried, other, fixed, fixed_other, solved, rims)
+        other = swapped(give)
+        chips = all_chips(whole(pair_kernel, "pair", shape(2, HALF, CY), carried, other, fixed, fixed_other))
+        ends, ends_give = whole(
+            chain_kernel,
+            "chain",
+            (shape(2, HALF, CY),) * 2,
+            *(*chips, *fixed_chips, carried, other, fixed, fixed_other),
+        )
+        planes = (ends, swapped(ends_give), solved, rims)
         if last:
             (field,) = whole(functools.partial(sweep_kernel, True), "sweep_last", (shape(rows, CY),), *planes)
             (flow,) = small

time: 92.2 us -> 86.4 us (0.937)
  waiting for transfers between devices: 34.4 us -> 23.5 us
  starting transfers between devices: 36.9 us -> 41.6 us
    ppermute x9, waiting for transfers between devices: 26.1 us -> 13.5 us  [all_chips(): lax.ppermute(value, 'layer', around(GROUPS, 2 * d))]
    ppermute x3 -> x5, starting transfers between devices: 5.94 us -> 10.1 us  [swapped(): return lax.ppermute(value, 'layer', [(i, i ^ 1) for i in range(GROUPS)])]
    ppermute x9, starting transfers between devices: 6.77 us -> 9.65 us  [all_chips(): lax.ppermute(value, 'layer', around(GROUPS, 2 * d))]
    all_to_all x2, starting transfers between devices: 18.7 us -> 16.4 us  [shards(): lax.all_to_all(partials, ('gx', 'gy'), split_axis=0, concat_axis=0, tiled...]
    ppermute x3 -> x5, waiting for transfers between devices: 1.98 us -> 3.61 us  [swapped(): return lax.ppermute(value, 'layer', [(i, i ^ 1) for i in range(GROUPS)])]
  transfers between devices with their start and end apart: 18 -> 20, of which waited for: 12 -> 15; matrix products, arithmetic and copies ran while one was open for 0% -> 0% of each run, Pallas kernels for 2% -> 3%
where the time goes in v5:
time: 86.4 us; the launch traced here: 86 us
  starting transfers between devices  41.6 us (48%)
  waiting for transfers between devices  23.5 us (27%)
  Pallas kernels  17.1 us (20%)
  local copies, waits for them, and re-layouts  2.35 us (3%)
  between operations  1.52 us (2%)
    all_to_all x2, starting transfers between devices, shards(): lax.all_to_all(partials, ('gx', 'gy'), split_axis=0, concat_axis=0, tiled...  16.4 us
    ppermute x9, waiting for transfers between devices, all_chips(): lax.ppermute(value, 'layer', around(GROUPS, 2 * d))  13.5 us
    ppermute x5, starting transfers between devices, swapped(): return lax.ppermute(value, 'layer', [(i, i ^ 1) for i in range(GROUPS)])  10.1 us
    ppermute x9, starting transfers between devices, all_chips(): lax.ppermute(value, 'layer', around(GROUPS, 2 * d))  9.65 us
    pallas_call x2, Pallas kernels, shards(): pl.pallas_call(functools.partial(solve_kernel, first, len(operands)), out...  9.44 us
    all_to_all x2, waiting for transfers between devices, shards(): lax.all_to_all(partials, ('gx', 'gy'), split_axis=0, concat_axis=0, tiled...  4.91 us
    ppermute x5, waiting for transfers between devices, swapped(): return lax.ppermute(value, 'layer', [(i, i ^ 1) for i in range(GROUPS)])  3.61 us
    ppermute x2, starting transfers between devices, from_sides(): lax.ppermute(xlo, 'gx', around(8, -1))  2.89 us
  transfers between devices with their start and end apart: 20, of which 15 were waited for; matrix products, arithmetic and copies ran while one was open for 0% of the time, Pallas kernels for 3%

profile of v5, /device:TPU:1, one launch (start us, length us, event | category | flops | bytes accessed | tf_op | source)
XLA Modules:
  0.0 86.0 jit_solution(8554662957042777015)
XLA Ops:
  0.7 1.1 %copy-done.1 = f32[8,64,256]{2,1,0:T(8,128)S(1)} copy-done((f32[8,64,256]{2,1,0:T(8,128)S(1)}, f32[8,64,256]{2,1,0:T(8,128)}, u32[]{:S(2)}) %copy-start.1) | copy-done | bytes 524312
  1.8 1.8 %first_edges.1 = (f32[16,256]{1,0:T(8,128)S(1)}, f32[16,256]{1,0:T(8,128)S(1)}, f32[16,128]{1,0:T(8,128)S(1)}, f32[3,32,256]{2,1,0:T(8,128)S(1)}, f32[3,32,256]{2,1,0:T(8,128)S(1)}) custom-call(f32[512,256]{1,0:T(8,128)S(1)} %bitcast.16, f32[8,64,256]{2,1,0:T(8,128)} %perm_x.1, f32[512,256]{1,0:T(8,128)} %bitcast.25, f32[8,8,64,256]{3,2,1,0:T(8,128)} %bitcast.22), custom_call_target="tpu_custom_call" | custom-call | tf_op jit(solution)/shard_map/first_edges/pallas_call | solution.py:517
  3.5 3.3 %collective-permute-start = (f32[3,32,256]{2,1,0:T(8,128)S(1)}, f32[3,32,256]{2,1,0:T(8,128)S(1)}, u32[]{:S(2)}, u32[]{:S(2)}) collective-permute-start(f32[3,32,256]{2,1,0:T(8,128)S(1)} %get-tuple-element.41), channel_id=1, source_target_pairs={{0,32},{32,0},{64,96},{96,64},{128,160},{160,128},{192,224},{224,1... | collective-permute-start | bytes 294920 | tf_op jit(solution)/shard_map/ppermute | solution.py:475
  7.6 2.2 %first_wells.1 = (f32[96,4,128]{2,1,0:T(4,128)}, f32[8,128]{1,0:T(8,128)S(1)}, f32[8,128]{1,0:T(8,128)S(1)}, f32[1,128]{1,0:T(1,128)S(1)}) custom-call(f32[16,128]{1,0:T(8,128)S(1)} %get-tuple-element.38.refs_0_, f32[512,256]{1,0:T(8,128)S(1)} %bitcast.17, f32[8,48]{1,0:T(8,128)S(1)} %bitcast.20, s32[1,48]{1,0:T(1,128)S(1)} %bitcast.21, ...), custom_call_target="tpu_custom_call" | custom-call | tf_op jit(solution)/shard_map/first_wells/pallas_call | solution.py:536
  9.8 0.0 collective-permute-done.other.fixed_other.refs_11_
  9.8 9.5 %all-to-all-start = ((f32[96,4,128]{2,1,0:T(4,128)}), f32[96,4,128]{2,1,0:T(4,128)S(1)}, u32[]{:S(2)}, u32[]{:S(2)}) async-start(f32[96,4,128]{2,1,0:T(4,128)} %get-tuple-element.42), calls=%async_computation | async-start | bytes 393216 | tf_op jit(solution)/shard_map/all_to_all | solution.py:562
  19.3 2.6 %collective-permute-start.3 = (f32[3,32,256]{2,1,0:T(8,128)S(1)}, f32[3,32,256]{2,1,0:T(8,128)S(1)}, u32[]{:S(2)}, u32[]{:S(2)}) collective-permute-start(f32[3,32,256]{2,1,0:T(8,128)S(1)} %pair_fixed.1.refs_4_), channel_id=1, source_target_pairs={{0,192},{32,224},{64,0},{96,32},{128,64},{160,96},{192,128},{224,1... | collective-permute-start | bytes 294920 | tf_op jit(solution)/shard_map/ppermute | solution.py:479
  21.9 0.5 collective-permute-start.2
  22.4 0.6 collective-permute-start.1
  23.0 1.2 %collective-permute-start.4 = (f32[16,256]{1,0:T(8,128)S(1)}, f32[16,256]{1,0:T(8,128)S(1)}, u32[]{:S(2)}, u32[]{:S(2)}) collective-permute-start(f32[16,256]{1,0:T(8,128)S(1)} %get-tuple-element.47), channel_id=1, source_target_pairs={{0,4},{4,8},{8,12},{12,16},{16,20},{20,24},{24,28},{28,0},{1,5},{5... | collective-permute-start | bytes 49160 | tf_op jit(solution)/shard_map/ppermute | solution.py:471
  24.2 1.4 %collective-permute-start.5 = (f32[16,256]{1,0:T(8,128)S(1)}, f32[16,256]{1,0:T(8,128)S(1)}, u32[]{:S(2)}, u32[]{:S(2)}) collective-permute-start(f32[16,256]{1,0:T(8,128)S(1)} %get-tuple-element.48), channel_id=1, source_target_pairs={{0,28},{4,0},{8,4},{12,8},{16,12},{20,16},{24,20},{28,24},{1,29},{... | collective-permute-start | bytes 49160 | tf_op jit(solution)/shard_map/ppermute | solution.py:471
  25.7 0.1 collective-permute-done.3.refs_7_
  25.7 1.4 %collective-permute-done.2.refs_6_ = f32[3,32,256]{2,1,0:T(8,128)S(1)} collective-permute-done((f32[3,32,256]{2,1,0:T(8,128)S(1)}, f32[3,32,256]{2,1,0:T(8,128)S(1)}, u32[]{:S(2)}, u32[]{:S(2)}) %collective-permute-start.2) | collective-permute-done | bytes 98336 | tf_op jit(solution)/shard_map/ppermute | solution.py:479
  27.2 2.9 %collective-permute-done.1.refs_5_ = f32[3,32,256]{2,1,0:T(8,128)S(1)} collective-permute-done((f32[3,32,256]{2,1,0:T(8,128)S(1)}, f32[3,32,256]{2,1,0:T(8,128)S(1)}, u32[]{:S(2)}, u32[]{:S(2)}) %collective-permute-start.1) | collective-permute-done | bytes 98336 | tf_op jit(solution)/shard_map/ppermute | solution.py:479
  30.1 0.0 all-to-all-done.refs_1_
  30.1 5.0 %solve_lines.2 = (f32[512,256]{1,0:T(8,128)S(1)}, f32[2,32,256]{2,1,0:T(8,128)S(1)}, f32[2,32,256]{2,1,0:T(8,128)S(1)}, f32[2,128]{1,0:T(2,128)S(1)}, f32[8,128]...) custom-call(s32[1,48]{1,0:T(1,128)S(1)} %copy-done.6, f32[96,4,128]{2,1,0:T(4,128)S(1)} %all-to-all-done.refs_1_, ...), custom_call_target="tpu_custom_call" | custom-call | tf_op jit(solution)/shard_map/solve_lines/pallas_call | solution.py:569
  35.1 2.0 %collective-permute-start.6 = (f32[2,32,256]{2,1,0:T(8,128)S(1)}, f32[2,32,256]{2,1,0:T(8,128)S(1)}, u32[]{:S(2)}, u32[]{:S(2)}) collective-permute-start(f32[2,32,256]{2,1,0:T(8,128)S(1)} %get-tuple-element.50), channel_id=1, source_target_pairs={{0,32},{32,0},{64,96},{96,64},{128,160},{160,128},{192,224},{224,1... | collective-permute-start | bytes 196616 | tf_op jit(solution)/shard_map/ppermute | solution.py:475
  37.2 0.9 %collective-permute-done.6.other.refs_9_ = f32[2,32,256]{2,1,0:T(8,128)S(1)} collective-permute-done((f32[2,32,256]{2,1,0:T(8,128)S(1)}, f32[2,32,256]{2,1,0:T(8,128)S(1)}, u32[]{:S(2)}, u32[]{:S(2)}) %collective-permute-start.6) | collective-permute-done | bytes 65568 | tf_op jit(solution)/shard_map/ppermute | solution.py:475
  38.1 2.6 %collective-permute-start.9 = (f32[2,32,256]{2,1,0:T(8,128)S(1)}, f32[2,32,256]{2,1,0:T(8,128)S(1)}, u32[]{:S(2)}, u32[]{:S(2)}) collective-permute-start(f32[2,32,256]{2,1,0:T(8,128)S(1)} %pair.2.refs_0_), channel_id=1, source_target_pairs={{0,192},{32,224},{64,0},{96,32},{128,64},{160,96},{192,128},{224,1... | collective-permute-start | bytes 196616 | tf_op jit(solution)/shard_map/ppermute | solution.py:479
  40.6 0.8 collective-permute-start.8
  41.4 0.8 collective-permute-start.7
  42.1 3.1 %collective-permute-done.8.refs_2_ = f32[2,32,256]{2,1,0:T(8,128)S(1)} collective-permute-done((f32[2,32,256]{2,1,0:T(8,128)S(1)}, f32[2,32,256]{2,1,0:T(8,128)S(1)}, u32[]{:S(2)}, u32[]{:S(2)}) %collective-permute-start.8) | collective-permute-done | bytes 65568 | tf_op jit(solution)/shard_map/ppermute | solution.py:479
  45.3 1.5 %collective-permute-done.7.refs_1_ = f32[2,32,256]{2,1,0:T(8,128)S(1)} collective-permute-done((f32[2,32,256]{2,1,0:T(8,128)S(1)}, f32[2,32,256]{2,1,0:T(8,128)S(1)}, u32[]{:S(2)}, u32[]{:S(2)}) %collective-permute-start.7) | collective-permute-done | bytes 65568 | tf_op jit(solution)/shard_map/ppermute | solution.py:479
  46.8 0.1 chain.2
  46.9 1.3 %collective-permute-start.10 = (f32[2,32,256]{2,1,0:T(8,128)S(1)}, f32[2,32,256]{2,1,0:T(8,128)S(1)}, u32[]{:S(2)}, u32[]{:S(2)}) collective-permute-start(f32[2,32,256]{2,1,0:T(8,128)S(1)} %get-tuple-element.56), channel_id=1, source_target_pairs={{0,32},{32,0},{64,96},{96,64},{128,160},{160,128},{192,224},{224,1... | collective-permute-start | bytes 196616 | tf_op jit(solution)/shard_map/ppermute | solution.py:475
  48.2 0.9 %collective-permute-done.10.other = f32[2,32,256]{2,1,0:T(8,128)S(1)} collective-permute-done((f32[2,32,256]{2,1,0:T(8,128)S(1)}, f32[2,32,256]{2,1,0:T(8,128)S(1)}, u32[]{:S(2)}, u32[]{:S(2)}) %collective-permute-start.10) | collective-permute-done | bytes 65568 | tf_op jit(solution)/shard_map/ppermute | solution.py:475
  49.2 1.2 %copy-done.3 = f32[2,8,64,256]{3,2,1,0:T(8,128)S(1)} copy-done((f32[2,8,64,256]{3,2,1,0:T(8,128)S(1)}, f32[2,8,64,256]{3,2,1,0:T(8,128)}, u32[]{:S(2)}) %copy-start.3) | copy-done | bytes 1048600
  50.4 0.3 sweep_mid.1
  50.7 2.1 %next_wells.1 = (f32[96,2,128]{2,1,0:T(2,128)}, f32[8,128]{1,0:T(8,128)S(1)}) custom-call(f32[2,512,128]{2,1,0:T(8,128)S(1)} %get-tuple-element.59.split.refs_12_, f32[8,128]{1,0:T(8,128)S(1)} %get-tuple-element.44.refs_2_.live, f32[1,128]{1,0:T(1,128)S(1)} %get-tuple-element.45.refs_3_.wells, f32[1,8]{1,0:T(1,128)S(1)} %copy-done.8, s32[1,48]{1,0:T(1,128)S(1)} %copy-done.6), custom_call_target="tpu_custom_call" | custom-call | tf_op jit(solution)/shard_map/next_wells/pallas_call | solution.py:608
  52.9 6.9 %all-to-all-start.1 = ((f32[96,2,128]{2,1,0:T(2,128)}), f32[96,2,128]{2,1,0:T(2,128)S(1)}, u32[]{:S(2)}, u32[]{:S(2)}) async-start(f32[96,2,128]{2,1,0:T(2,128)} %get-tuple-element.60), calls=%async_computation.1 | async-start | bytes 196608 | tf_op jit(solution)/shard_map/all_to_all | solution.py:562
  59.8 1.3 %collective-permute-start.11 = (f32[8,256]{1,0:T(8,128)S(1)}, f32[8,256]{1,0:T(8,128)S(1)}, u32[]{:S(2)}, u32[]{:S(2)}) collective-permute-start(f32[8,256]{1,0:T(8,128)S(1)} %get-tuple-element.62), channel_id=1, source_target_pairs={{0,4},{4,8},{8,12},{12,16},{16,20},{20,24},{24,28},{28,0},{1,5},{5... | collective-permute-start | bytes 24584 | tf_op jit(solution)/shard_map/ppermute | solution.py:471
  61.1 1.4 %collective-permute-start.12 = (f32[8,256]{1,0:T(8,128)S(1)}, f32[8,256]{1,0:T(8,128)S(1)}, u32[]{:S(2)}, u32[]{:S(2)}) collective-permute-start(f32[8,256]{1,0:T(8,128)S(1)} %get-tuple-element.63), channel_id=1, source_target_pairs={{0,28},{4,0},{8,4},{12,8},{16,12},{20,16},{24,20},{28,24},{1,29},{... | collective-permute-start | bytes 24584 | tf_op jit(solution)/shard_map/ppermute | solution.py:471
  62.6 1.3 %collective-permute-done.11.refs_5_ = f32[8,256]{1,0:T(8,128)S(1)} collective-permute-done((f32[8,256]{1,0:T(8,128)S(1)}, f32[8,256]{1,0:T(8,128)S(1)}, u32[]{:S(2)}, u32[]{:S(2)}) %collective-permute-start.11) | collective-permute-done | bytes 8224 | tf_op jit(solution)/shard_map/ppermute | solution.py:471
  63.9 0.1 collective-permute-done.12.refs_6_
  64.0 4.9 %all-to-all-done.1.refs_1_ = f32[96,2,128]{2,1,0:T(2,128)S(1)} async-done(((f32[96,2,128]{2,1,0:T(2,128)}), f32[96,2,128]{2,1,0:T(2,128)S(1)}, u32[]{:S(2)}, u32[]{:S(2)}) %all-to-all-start.1) | async-done | bytes 98336 | tf_op jit(solution)/shard_map/all_to_all | solution.py:562
  68.9 4.4 %solve_lines.3 = (f32[512,256]{1,0:T(8,128)S(1)}, f32[2,32,256]{2,1,0:T(8,128)S(1)}, f32[2,32,256]{2,1,0:T(8,128)S(1)}, f32[8,48]{1,0:T(8,128)}) custom-call(s32[1,48]{1,0:T(1,128)S(1)} %copy-done.6, f32[96,2,128]{2,1,0:T(2,128)S(1)} %all-to-all-done.1.refs_1_, f32[8,128]{1,0:T(8,128)S(1)} %get-tuple-element.44.refs_2_.live, ...), custom_call_target="tpu_custom_call" | custom-call | tf_op jit(solution)/shard_map/solve_lines/pallas_call | solution.py:569
  73.3 1.9 %collective-permute-start.13 = (f32[2,32,256]{2,1,0:T(8,128)S(1)}, f32[2,32,256]{2,1,0:T(8,128)S(1)}, u32[]{:S(2)}, u32[]{:S(2)}) collective-permute-start(f32[2,32,256]{2,1,0:T(8,128)S(1)} %get-tuple-element.69), channel_id=1, source_target_pairs={{0,32},{32,0},{64,96},{96,64},{128,160},{160,128},{192,224},{224,1... | collective-permute-start | bytes 196616 | tf_op jit(solution)/shard_map/ppermute | solution.py:475
  75.3 0.9 %collective-permute-done.13.other.refs_9_ = f32[2,32,256]{2,1,0:T(8,128)S(1)} collective-permute-done((f32[2,32,256]{2,1,0:T(8,128)S(1)}, f32[2,32,256]{2,1,0:T(8,128)S(1)}, u32[]{:S(2)}, u32[]{:S(2)}) %collective-permute-start.13) | collective-permute-done | bytes 65568 | tf_op jit(solution)/shard_map/ppermute | solution.py:475
  76.2 0.1 collective-permute-start.16
  76.4 1.2 %collective-permute-start.15 = (f32[2,32,256]{2,1,0:T(8,128)S(1)}, f32[2,32,256]{2,1,0:T(8,128)S(1)}, u32[]{:S(2)}, u32[]{:S(2)}) collective-permute-start(f32[2,32,256]{2,1,0:T(8,128)S(1)} %pair.3.refs_0_), channel_id=1, source_target_pairs={{0,128},{32,160},{64,192},{96,224},{128,0},{160,32},{192,64},{224,... | collective-permute-start | bytes 196616 | tf_op jit(solution)/shard_map/ppermute | solution.py:479
  77.6 0.6 collective-permute-start.14
  78.1 1.3 %collective-permute-done.16.refs_3_ = f32[2,32,256]{2,1,0:T(8,128)S(1)} collective-permute-done((f32[2,32,256]{2,1,0:T(8,128)S(1)}, f32[2,32,256]{2,1,0:T(8,128)S(1)}, u32[]{:S(2)}, u32[]{:S(2)}) %collective-permute-start.16) | collective-permute-done | bytes 65568 | tf_op jit(solution)/shard_map/ppermute | solution.py:479
  79.4 1.6 %collective-permute-done.15.refs_2_ = f32[2,32,256]{2,1,0:T(8,128)S(1)} collective-permute-done((f32[2,32,256]{2,1,0:T(8,128)S(1)}, f32[2,32,256]{2,1,0:T(8,128)S(1)}, u32[]{:S(2)}, u32[]{:S(2)}) %collective-permute-start.15) | collective-permute-done | bytes 65568 | tf_op jit(solution)/shard_map/ppermute | solution.py:479
  81.0 1.6 %collective-permute-done.14.refs_1_ = f32[2,32,256]{2,1,0:T(8,128)S(1)} collective-permute-done((f32[2,32,256]{2,1,0:T(8,128)S(1)}, f32[2,32,256]{2,1,0:T(8,128)S(1)}, u32[]{:S(2)}, u32[]{:S(2)}) %collective-permute-start.14) | collective-permute-done | bytes 65568 | tf_op jit(solution)/shard_map/ppermute | solution.py:479
  82.6 0.1 chain.3
  82.7 1.5 %collective-permute-start.17 = (f32[2,32,256]{2,1,0:T(8,128)S(1)}, f32[2,32,256]{2,1,0:T(8,128)S(1)}, u32[]{:S(2)}, u32[]{:S(2)}) collective-permute-start(f32[2,32,256]{2,1,0:T(8,128)S(1)} %get-tuple-element.71), channel_id=1, source_target_pairs={{0,32},{32,0},{64,96},{96,64},{128,160},{160,128},{192,224},{224,1... | collective-permute-start | bytes 196616 | tf_op jit(solution)/shard_map/ppermute | solution.py:475
  84.2 0.9 %collective-permute-done.17.other = f32[2,32,256]{2,1,0:T(8,128)S(1)} collective-permute-done((f32[2,32,256]{2,1,0:T(8,128)S(1)}, f32[2,32,256]{2,1,0:T(8,128)S(1)}, u32[]{:S(2)}, u32[]{:S(2)}) %collective-permute-start.17) | collective-permute-done | bytes 65568 | tf_op jit(solution)/shard_map/ppermute | solution.py:475
  85.1 0.9 %sweep_last.1 = f32[512,256]{1,0:T(8,128)} custom-call(f32[2,32,256]{2,1,0:T(8,128)S(1)} %get-tuple-element.70.mine, f32[2,32,256]{2,1,0:T(8,128)S(1)} %collective-permute-done.17.other, f32[512,256]{1,0:T(8,128)S(1)} %get-tuple-element.72.solved, f32[2,8,64,256]{3,2,1,0:T(8,128)S(1)} %copy-done.4), custom_call_target="tpu_custom_call" | custom-call | tf_op jit(solution)/shard_map/sweep_last/pallas_call | solution.py:483
  (26 shorter events, 0.1 us)
Async XLA Ops:
  0.6 29.5 %copy-start = (f32[8,64,256]{2,1,0:T(8,128)S(1)}, f32[8,64,256]{2,1,0:T(8,128)}, u32[]{:S(2)}) copy-start(f32[8,64,256]{2,1,0:T(8,128)} %perm_x.1) | copy-start | bytes 1572868
  0.6 1.1 %copy-start.1 = (f32[8,64,256]{2,1,0:T(8,128)S(1)}, f32[8,64,256]{2,1,0:T(8,128)}, u32[]{:S(2)}) copy-start(f32[8,64,256]{2,1,0:T(8,128)} %param.12) | copy-start | bytes 1572868
  1.7 5.8 %copy-start.6 = (s32[1,48]{1,0:T(1,128)S(1)}, s32[1,48]{1,0:T(1,128)}, u32[]{:S(2)}) copy-start(s32[1,48]{1,0:T(1,128)} %refs_0_.3) | copy-start | bytes 580
  1.7 5.8 %copy-start.7 = (f32[1,48,8]{1,2,0:T(8,128)S(1)}, f32[1,48,8]{1,2,0:T(8,128)}, u32[]{:S(2)}) copy-start(f32[1,48,8]{1,2,0:T(8,128)} %param.22) | copy-start | bytes 4612
  1.7 5.8 %copy-start.8 = (f32[1,8]{1,0:T(1,128)S(1)}, f32[1,8]{1,0:T(1,128)}, u32[]{:S(2)}) copy-start(f32[1,8]{1,0:T(1,128)} %rate.1) | copy-start | bytes 100
  1.7 5.8 %copy-start.9 = (s32[1,48,1]{1,2,0:T(1,128)S(1)}, s32[1,48,1]{1,2,0:T(1,128)}, u32[]{:S(2)}) copy-start(s32[1,48,1]{1,2,0:T(1,128)} %param.19) | copy-start | bytes 580
  1.8 5.8 %copy-start.10 = (s32[1,48]{1,0:T(1,128)S(1)}, s32[1,48]{1,0:T(1,128)}, u32[]{:S(2)}) copy-start(s32[1,48]{1,0:T(1,128)} %refs_4_.1) | copy-start | bytes 580
  1.8 28.3 %copy-start.2 = (f32[8,64,256]{2,1,0:T(8,128)S(1)}, f32[8,64,256]{2,1,0:T(8,128)}, u32[]{:S(2)}) copy-start(f32[8,64,256]{2,1,0:T(8,128)} %param.12) | copy-start | bytes 1572868
  1.8 28.3 %copy-start.5 = (f32[1,64,256]{2,1,0:T(8,128)S(1)}, f32[1,64,256]{2,1,0:T(8,128)}, u32[]{:S(2)}) copy-start(f32[1,64,256]{2,1,0:T(8,128)} %param.17) | copy-start | bytes 196612
  3.5 6.2 %collective-permute-start = (f32[3,32,256]{2,1,0:T(8,128)S(1)}, f32[3,32,256]{2,1,0:T(8,128)S(1)}, u32[]{:S(2)}, u32[]{:S(2)}) collective-permute-start(f32[3,32,256]{2,1,0:T(8,128)S(1)} %get-tuple-element.41), channel_id=1, source_target_pairs={{0,32},{32,0},{64,96},{96,64},{128,160},{160,128},{192,224},{224,1... | collective-permute-start | bytes 294920 | tf_op jit(solution)/shard_map/ppermute | solution.py:475
  9.8 20.3 %all-to-all-start = ((f32[96,4,128]{2,1,0:T(4,128)}), f32[96,4,128]{2,1,0:T(4,128)S(1)}, u32[]{:S(2)}, u32[]{:S(2)}) async-start(f32[96,4,128]{2,1,0:T(4,128)} %get-tuple-element.42), calls=%async_computation | async-start | bytes 393216 | tf_op jit(solution)/shard_map/all_to_all | solution.py:562
  19.3 6.4 %collective-permute-start.3 = (f32[3,32,256]{2,1,0:T(8,128)S(1)}, f32[3,32,256]{2,1,0:T(8,128)S(1)}, u32[]{:S(2)}, u32[]{:S(2)}) collective-permute-start(f32[3,32,256]{2,1,0:T(8,128)S(1)} %pair_fixed.1.refs_4_), channel_id=1, source_target_pairs={{0,192},{32,224},{64,0},{96,32},{128,64},{160,96},{192,128},{224,1... | collective-permute-start | bytes 294920 | tf_op jit(solution)/shard_map/ppermute | solution.py:479
  21.9 5.3 %collective-permute-start.2 = (f32[3,32,256]{2,1,0:T(8,128)S(1)}, f32[3,32,256]{2,1,0:T(8,128)S(1)}, u32[]{:S(2)}, u32[]{:S(2)}) collective-permute-start(f32[3,32,256]{2,1,0:T(8,128)S(1)} %pair_fixed.1.refs_4_), channel_id=1, source_target_pairs={{0,128},{32,160},{64,192},{96,224},{128,0},{160,32},{192,64},{224,... | collective-permute-start | bytes 294920 | tf_op jit(solution)/shard_map/ppermute | solution.py:479
  22.4 7.7 %collective-permute-start.1 = (f32[3,32,256]{2,1,0:T(8,128)S(1)}, f32[3,32,256]{2,1,0:T(8,128)S(1)}, u32[]{:S(2)}, u32[]{:S(2)}) collective-permute-start(f32[3,32,256]{2,1,0:T(8,128)S(1)} %pair_fixed.1.refs_4_), channel_id=1, source_target_pairs={{0,64},{32,96},{64,128},{96,160},{128,192},{160,224},{192,0},{224,... | collective-permute-start | bytes 294920 | tf_op jit(solution)/shard_map/ppermute | solution.py:479
  23.0 7.1 %collective-permute-start.4 = (f32[16,256]{1,0:T(8,128)S(1)}, f32[16,256]{1,0:T(8,128)S(1)}, u32[]{:S(2)}, u32[]{:S(2)}) collective-permute-start(f32[16,256]{1,0:T(8,128)S(1)} %get-tuple-element.47), channel_id=1, source_target_pairs={{0,4},{4,8},{8,12},{12,16},{16,20},{20,24},{24,28},{28,0},{1,5},{5... | collective-permute-start | bytes 49160 | tf_op jit(solution)/shard_map/ppermute | solution.py:471
  24.2 5.9 %collective-permute-start.5 = (f32[16,256]{1,0:T(8,128)S(1)}, f32[16,256]{1,0:T(8,128)S(1)}, u32[]{:S(2)}, u32[]{:S(2)}) collective-permute-start(f32[16,256]{1,0:T(8,128)S(1)} %get-tuple-element.48), channel_id=1, source_target_pairs={{0,28},{4,0},{8,4},{12,8},{16,12},{20,16},{24,20},{28,24},{1,29},{... | collective-permute-start | bytes 49160 | tf_op jit(solution)/shard_map/ppermute | solution.py:471
  35.1 2.9 %collective-permute-start.6 = (f32[2,32,256]{2,1,0:T(8,128)S(1)}, f32[2,32,256]{2,1,0:T(8,128)S(1)}, u32[]{:S(2)}, u32[]{:S(2)}) collective-permute-start(f32[2,32,256]{2,1,0:T(8,128)S(1)} %get-tuple-element.50), channel_id=1, source_target_pairs={{0,32},{32,0},{64,96},{96,64},{128,160},{160,128},{192,224},{224,1... | collective-permute-start | bytes 196616 | tf_op jit(solution)/shard_map/ppermute | solution.py:475
  38.1 4.1 %collective-permute-start.9 = (f32[2,32,256]{2,1,0:T(8,128)S(1)}, f32[2,32,256]{2,1,0:T(8,128)S(1)}, u32[]{:S(2)}, u32[]{:S(2)}) collective-permute-start(f32[2,32,256]{2,1,0:T(8,128)S(1)} %pair.2.refs_0_), channel_id=1, source_target_pairs={{0,192},{32,224},{64,0},{96,32},{128,64},{160,96},{192,128},{224,1... | collective-permute-start | bytes 196616 | tf_op jit(solution)/shard_map/ppermute | solution.py:479
  40.6 4.6 %collective-permute-start.8 = (f32[2,32,256]{2,1,0:T(8,128)S(1)}, f32[2,32,256]{2,1,0:T(8,128)S(1)}, u32[]{:S(2)}, u32[]{:S(2)}) collective-permute-start(f32[2,32,256]{2,1,0:T(8,128)S(1)} %pair.2.refs_0_), channel_id=1, source_target_pairs={{0,128},{32,160},{64,192},{96,224},{128,0},{160,32},{192,64},{224,... | collective-permute-start | bytes 196616 | tf_op jit(solution)/shard_map/ppermute | solution.py:479
  41.4 5.4 %collective-permute-start.7 = (f32[2,32,256]{2,1,0:T(8,128)S(1)}, f32[2,32,256]{2,1,0:T(8,128)S(1)}, u32[]{:S(2)}, u32[]{:S(2)}) collective-permute-start(f32[2,32,256]{2,1,0:T(8,128)S(1)} %pair.2.refs_0_), channel_id=1, source_target_pairs={{0,64},{32,96},{64,128},{96,160},{128,192},{160,224},{192,0},{224,... | collective-permute-start | bytes 196616 | tf_op jit(solution)/shard_map/ppermute | solution.py:479
  46.9 2.2 %collective-permute-start.10 = (f32[2,32,256]{2,1,0:T(8,128)S(1)}, f32[2,32,256]{2,1,0:T(8,128)S(1)}, u32[]{:S(2)}, u32[]{:S(2)}) collective-permute-start(f32[2,32,256]{2,1,0:T(8,128)S(1)} %get-tuple-element.56), channel_id=1, source_target_pairs={{0,32},{32,0},{64,96},{96,64},{128,160},{160,128},{192,224},{224,1... | collective-permute-start | bytes 196616 | tf_op jit(solution)/shard_map/ppermute | solution.py:475
  49.2 1.2 %copy-start.3 = (f32[2,8,64,256]{3,2,1,0:T(8,128)S(1)}, f32[2,8,64,256]{3,2,1,0:T(8,128)}, u32[]{:S(2)}) copy-start(f32[2,8,64,256]{3,2,1,0:T(8,128)} %get-tuple-element.58.rims) | copy-start | bytes 3145732
  50.7 34.4 %copy-start.4 = (f32[2,8,64,256]{3,2,1,0:T(8,128)S(1)}, f32[2,8,64,256]{3,2,1,0:T(8,128)}, u32[]{:S(2)}) copy-start(f32[2,8,64,256]{3,2,1,0:T(8,128)} %get-tuple-element.58.rims) | copy-start | bytes 3145732
  52.9 16.0 %all-to-all-start.1 = ((f32[96,2,128]{2,1,0:T(2,128)}), f32[96,2,128]{2,1,0:T(2,128)S(1)}, u32[]{:S(2)}, u32[]{:S(2)}) async-start(f32[96,2,128]{2,1,0:T(2,128)} %get-tuple-element.60), calls=%async_computation.1 | async-start | bytes 196608 | tf_op jit(solution)/shard_map/all_to_all | solution.py:562
  59.8 4.0 %collective-permute-start.11 = (f32[8,256]{1,0:T(8,128)S(1)}, f32[8,256]{1,0:T(8,128)S(1)}, u32[]{:S(2)}, u32[]{:S(2)}) collective-permute-start(f32[8,256]{1,0:T(8,128)S(1)} %get-tuple-element.62), channel_id=1, source_target_pairs={{0,4},{4,8},{8,12},{12,16},{16,20},{20,24},{24,28},{28,0},{1,5},{5... | collective-permute-start | bytes 24584 | tf_op jit(solution)/shard_map/ppermute | solution.py:471
  61.1 2.9 %collective-permute-start.12 = (f32[8,256]{1,0:T(8,128)S(1)}, f32[8,256]{1,0:T(8,128)S(1)}, u32[]{:S(2)}, u32[]{:S(2)}) collective-permute-start(f32[8,256]{1,0:T(8,128)S(1)} %get-tuple-element.63), channel_id=1, source_target_pairs={{0,28},{4,0},{8,4},{12,8},{16,12},{20,16},{24,20},{28,24},{1,29},{... | collective-permute-start | bytes 24584 | tf_op jit(solution)/shard_map/ppermute | solution.py:471
  73.3 2.9 %collective-permute-start.13 = (f32[2,32,256]{2,1,0:T(8,128)S(1)}, f32[2,32,256]{2,1,0:T(8,128)S(1)}, u32[]{:S(2)}, u32[]{:S(2)}) collective-permute-start(f32[2,32,256]{2,1,0:T(8,128)S(1)} %get-tuple-element.69), channel_id=1, source_target_pairs={{0,32},{32,0},{64,96},{96,64},{128,160},{160,128},{192,224},{224,1... | collective-permute-start | bytes 196616 | tf_op jit(solution)/shard_map/ppermute | solution.py:475
  76.2 3.2 %collective-permute-start.16 = (f32[2,32,256]{2,1,0:T(8,128)S(1)}, f32[2,32,256]{2,1,0:T(8,128)S(1)}, u32[]{:S(2)}, u32[]{:S(2)}) collective-permute-start(f32[2,32,256]{2,1,0:T(8,128)S(1)} %pair.3.refs_0_), channel_id=1, source_target_pairs={{0,192},{32,224},{64,0},{96,32},{128,64},{160,96},{192,128},{224,1... | collective-permute-start | bytes 196616 | tf_op jit(solution)/shard_map/ppermute | solution.py:479
  76.4 4.7 %collective-permute-start.15 = (f32[2,32,256]{2,1,0:T(8,128)S(1)}, f32[2,32,256]{2,1,0:T(8,128)S(1)}, u32[]{:S(2)}, u32[]{:S(2)}) collective-permute-start(f32[2,32,256]{2,1,0:T(8,128)S(1)} %pair.3.refs_0_), channel_id=1, source_target_pairs={{0,128},{32,160},{64,192},{96,224},{128,0},{160,32},{192,64},{224,... | collective-permute-start | bytes 196616 | tf_op jit(solution)/shard_map/ppermute | solution.py:479
  77.6 5.0 %collective-permute-start.14 = (f32[2,32,256]{2,1,0:T(8,128)S(1)}, f32[2,32,256]{2,1,0:T(8,128)S(1)}, u32[]{:S(2)}, u32[]{:S(2)}) collective-permute-start(f32[2,32,256]{2,1,0:T(8,128)S(1)} %pair.3.refs_0_), channel_id=1, source_target_pairs={{0,64},{32,96},{64,128},{96,160},{128,192},{160,224},{192,0},{224,... | collective-permute-start | bytes 196616 | tf_op jit(solution)/shard_map/ppermute | solution.py:479
  82.7 2.4 %collective-permute-start.17 = (f32[2,32,256]{2,1,0:T(8,128)S(1)}, f32[2,32,256]{2,1,0:T(8,128)S(1)}, u32[]{:S(2)}, u32[]{:S(2)}) collective-permute-start(f32[2,32,256]{2,1,0:T(8,128)S(1)} %get-tuple-element.71), channel_id=1, source_target_pairs={{0,32},{32,0},{64,96},{96,64},{128,160},{160,128},{192,224},{224,1... | collective-permute-start | bytes 196616 | tf_op jit(solution)/shard_map/ppermute | solution.py:475

commit v6 on v5

--- a/solution.py
+++ b/solution.py
@@ -11,6 +11,7 @@
 EDGE_MIB = 53.0
 WELLS_MIB = 52.0
 SOLVE_MIB = 52.0
+LATERAL_MIB = 52.0
 LZ = 8
 CX = 64
 CY = 256
@@ -230,36 +231,59 @@
     send_y(partials, turned[0:4], turned[4:8])
 
 
+def lateral_kernel(first, field, kx, ky, source, rhs, field_v, kx_v, ky_v, source_v, sem):
+    if first:
+        wanted = [(field.at[:, half * 128 : half * 128 + 128], field_v.at[half]) for half in range(2)]
+    else:
+        wanted = [(field.at[half], field_v.at[half]) for half in range(2)]
+    for copy in load(wanted + [(kx, kx_v), (ky, ky_v), (source, source_v)], sem):
+        copy.wait()
+    rows = lax.broadcasted_iota(jnp.int32, (CX, CY), 0)
+    lanes = lane_ids(CX, CY)
+    for l in range(LZ):
+        span = slice(l * CX, (l + 1) * CX)
+        f = halves_of(field_v, span)
+        k = kx_v[span, :]
+        face = k + pltpu.roll(k, CX - 1, 0)
+        lateral = face * jnp.where(rows == CX - 1, 0.0, pltpu.roll(f, CX - 1, 0))
+        lateral = lateral + jnp.where(rows == 0, 0.0, pltpu.roll(face * f, 1, 0))
+        k = ky_v[span, :]
+        face = k + pltpu.roll(k, CY - 1, 1)
+        lateral = lateral + face * jnp.where(lanes == CY - 1, 0.0, pltpu.roll(f, CY - 1, 1))
+        lateral = lateral + jnp.where(lanes == 0, 0.0, pltpu.roll(face * f, 1, 1))
+        value = source_v[span, :] + 0.5 * lateral
+        rhs[0, span, :] = value[:, :128]
+        rhs[1, span, :] = value[:, 128:]
+
+
 def solve_kernel(first, inputs, *refs):
     away, refs = refs[:inputs], refs[inputs:]
     if first:
         (solved, keep, give, sums_out, kylo_out, kyhi_out, rims, *refs) = refs
     else:
         (solved, keep, give, flow_out, *refs) = refs
-    held, (rhs, carried, column_s, sem) = refs[:inputs], refs[inputs:]
-    (column, partials, live, wells, at_slots, *small, field, kx, ky, source, lower, inverse) = held
-    held = dict(zip(range(inputs), held))
-    wanted = [(away[0], column_s)] + [(away[n], held[n]) for n in range(1, inputs - 6)]
-    if first:
-        wanted += [(away[inputs - 6].at[:, half * 128 : half * 128 + 128], field.at[half]) for half in range(2)]
-    else:
-        wanted += [(away[inputs - 6].at[half], field.at[half]) for half in range(2)]
-    wanted += [(away[n], held[n]) for n in range(inputs - 5, inputs)]
-    copies = load(wanted, sem)
-    for copy in copies[: inputs - 6]:
+    held, (carried, column_s, sem) = refs[:inputs], refs[inputs:]
+    (column, partials, live, wells, at_slots, y_own, x_own_lo, x_own_hi, *small, rhs, lower, inverse) = held
+    copies = load([(away[0], column_s)] + [(away[n], held[n]) for n in range(1, inputs)], sem)
+    for copy in copies[: inputs - 3]:
         copy.wait()
     gx, gy = lax.axis_index("gx"), lax.axis_index("gy")
     block = partials.shape[0] // TILES
     total = partials[0]
     for t in range(1, TILES):
         total = total + partials[block * t]
+    from_ylo, from_yhi = from_y(partials, 2)
     if first:
         x_lo, x_hi = small
         kx_lo, kx_hi = x_lo, x_hi
+        ky_lo, ky_hi = from_ylo[4:8], from_yhi[4:8]
+        kylo_out[...] = from_ylo
+        kyhi_out[...] = from_yhi
         numerator, index_sum = total[0:2], total[2:4]
         sums_out[...] = index_sum
     else:
         x_lo, x_hi, kx_lo, kx_hi, ky_lo, ky_hi, sums = small
+        ky_lo, ky_hi = ky_lo[4:8], ky_hi[4:8]
         numerator, index_sum = total, sums[...]
     bottom_hole = numerator / (index_sum + 1.0)
     (wells_c,) = well_columns([wells[...]])
@@ -275,53 +299,31 @@
     if not first:
         flow_out[...] = flow[:, :SLOTS]
 
-    rows = lax.broadcasted_iota(jnp.int32, (CX, CY), 0)
-    lanes = lane_ids(CX, CY)
-    from_ylo, from_yhi = from_y(partials, 2)
-    if first:
-        kylo_out[...] = from_ylo
-        kyhi_out[...] = from_yhi
-        ylo_c = kylo_c = from_ylo.T
-        yhi_c = kyhi_c = from_yhi.T
-    else:
-        spare = jnp.zeros((4, 128), F32)
-        ylo_c = jnp.concatenate([from_ylo, spare], axis=0).T
-        yhi_c = jnp.concatenate([from_yhi, spare], axis=0).T
-        kylo_c = ky_lo[...].T
-        kyhi_c = ky_hi[...].T
-
-    def y_column(turned, base, l):
-        s = (l % 2) * CX
-        return turned[s : s + CX, base + l // 2 : base + l // 2 + 1]
-
-    for copy in copies[inputs - 6 : inputs - 1]:
-        copy.wait()
+    for copy in copies[inputs - 3 : inputs - 2]:
+        copy.wait()
+    add = jnp.concatenate(
+        [
+            jnp.where(gy > 0, 0.5 * (y_own[4:8] + ky_lo) * from_ylo[0:4], 0.0),
+            jnp.where(gy < 3, 0.5 * (y_own[12:16] + ky_hi) * from_yhi[0:4], 0.0),
+        ],
+        axis=0,
+    ).T
+    lanes = lane_ids(CX, 128)
     for l in range(LZ):
         span = slice(l * CX, (l + 1) * CX)
-        f = halves_of(field, span)
-        k = kx[span, :]
-        f_after = jnp.where(gx < 7, x_hi[l : l + 1, :], 0.0)
-        k_after = kx_hi[LZ + l : LZ + l + 1, :]
-        f_before = jnp.where(gx > 0, x_lo[l : l + 1, :], 0.0)
-        k_before = kx_lo[LZ + l : LZ + l + 1, :]
-        f_east = jnp.where(rows == CX - 1, f_after, pltpu.roll(f, CX - 1, 0))
-        k_east = jnp.where(rows == CX - 1, k_after, pltpu.roll(k, CX - 1, 0))
-        face = k + k_east
-        west_first = (k[0:1, :] + k_before) * f_before
-        lateral = face * f_east + jnp.where(rows == 0, west_first, pltpu.roll(face * f, 1, 0))
-        k = ky[span, :]
-        f_after = jnp.where(gy < 3, y_column(yhi_c, 0, l), 0.0)
-        k_after = y_column(kyhi_c, 4, l)
-        f_before = jnp.where(gy > 0, y_column(ylo_c, 0, l), 0.0)
-        k_before = y_column(kylo_c, 4, l)
-        f_north = jnp.where(lanes == CY - 1, f_after, pltpu.roll(f, CY - 1, 1))
-        k_north = jnp.where(lanes == CY - 1, k_after, pltpu.roll(k, CY - 1, 1))
-        face = k + k_north
-        south_first = (k[:, 0:1] + k_before) * f_before
-        lateral = lateral + face * f_north + jnp.where(lanes == 0, south_first, pltpu.roll(face * f, 1, 1))
-        value = source[span, :] + 0.5 * lateral
-        rhs[0, span, :] = value[:, :128]
-        rhs[1, span, :] = value[:, 128:]
+        part = slice((l % 2) * CX, (l % 2) * CX + CX)
+        for half, lane in ((0, 0), (1, 127)):
+            value = add[part, half * 4 + l // 2 : half * 4 + l // 2 + 1]
+            rhs[half, span, :] = rhs[half, span, :] + jnp.where(lanes == lane, value, 0.0)
+    sides = (
+        (0, jnp.where(gx > 0, 0.5 * (x_own_lo[LZ : 2 * LZ] + kx_lo[LZ : 2 * LZ]) * x_lo[0:LZ], 0.0)),
+        (CX - 1, jnp.where(gx < 7, 0.5 * (x_own_hi[LZ : 2 * LZ] + kx_hi[LZ : 2 * LZ]) * x_hi[0:LZ], 0.0)),
+    )
+    for row, value in sides:
+        for half in range(2):
+            part = rhs.at[half]
+            where = (pl.ds(row, LZ, stride=CX), slice(None))
+            part[where] = part[where] + value[:, half * 128 : half * 128 + 128]
 
     lanes8 = lane_ids(LZ, 128)
     for s in range(SLOTS):
@@ -334,7 +336,7 @@
         where = (pl.ds(x, LZ, stride=CX), slice(None))
         part[where] = part[where] + jnp.where(lanes8 == lane, flow[:, s : s + 1], 0.0)
 
-    for copy in copies[inputs - 1 :]:
+    for copy in copies[inputs - 2 :]:
         copy.wait()
 
     def solve_block(b, carry):
@@ -554,6 +556,7 @@
     )(y_edge, pressure, index, owner, perf_well, well_rate, perf_column, tile_count)
     field = pressure
     k_sides = sides
+    own_edges = (y_edge, *edges)
     ky_sides = sums = None
     for sweep_step in range(ITERS):
         first, last = sweep_step == 0, sweep_step == ITERS - 1
@@ -563,9 +566,22 @@
         if first:
             spread, *fixed_chips = lax.optimization_barrier((spread, *fixed_chips))
         small = sides if first else (*sides, *k_sides, *ky_sides, sums)
-        operands = (perf_column, spread, live, wells, at_slots, *small, field, kx, ky, source, lower, inverse)
+        rhs = pl.pallas_call(
+            functools.partial(lateral_kernel, first),
+            out_shape=shape(2, rows, 128),
+            in_specs=[ANY] * 4,
+            out_specs=VMEM,
+            scratch_shapes=[pltpu.VMEM((2, rows, 128), F32)]
+            + [pltpu.VMEM((rows, CY), F32)] * 3
+            + [pltpu.SemaphoreType.DMA((5,))],
+            compiler_params=params(LATERAL_MIB),
+            cost_estimate=pl.CostEstimate(
+                flops=17 * rows * CY, bytes_accessed=5 * 4 * rows * CY, transcendentals=0
+            ),
+            name="lateral",
+        )(field, kx, ky, source)
+        operands = (perf_column, spread, live, wells, at_slots, *own_edges, *small, rhs, lower, inverse)
         held = [pltpu.VMEM(value.shape, value.dtype) for value in operands]
-        held[len(operands) - 6] = pltpu.VMEM((2, rows, 128), F32)
         solved, carried, give, *small = pl.pallas_call(
             functools.partial(solve_kernel, first, len(operands)),
             out_shape=(shape(rows, CY), shape(2, HALF, CY), shape(2, HALF, CY))
@@ -574,10 +590,9 @@
             out_specs=(VMEM,) * (7 if first else 4),
             scratch_shapes=held
             + [
-                pltpu.VMEM((2, rows, 128), F32),
                 pltpu.VMEM((2, CX, CY), F32),
                 pltpu.SMEM((1, SLOTS), jnp.int32),
-                pltpu.SemaphoreType.DMA((len(operands) + 1,)),
+                pltpu.SemaphoreType.DMA((len(operands),)),
             ],
             compiler_params=params(SOLVE_MIB),
             name="solve_lines",

time: 86.4 us -> 85.1 us (0.985)
  waiting for transfers between devices: 23.5 us -> 19.6 us
  Pallas kernels: 17.1 us -> 19.8 us
    pallas_call x0 -> x2, Pallas kernels: none -> 4.08 us  [shards(): pl.pallas_call(functools.partial(lateral_kernel, first), out_shape=shape(...]
    ppermute x9, waiting for transfers between devices: 13.5 us -> 11.7 us  [all_chips(): lax.ppermute(value, 'layer', around(GROUPS, 2 * d))]
    pallas_call x2, Pallas kernels: 9.44 us -> 8.1 us  [shards(): pl.pallas_call(functools.partial(solve_kernel, first, len(operands)), out...]
    ppermute x2, waiting for transfers between devices: 1.29 us -> 0.01 us  [from_sides(): lax.ppermute(xhi, 'gx', around(8, 1))]
    ppermute x2, starting transfers between devices: 2.54 us -> 1.31 us  [from_sides(): lax.ppermute(xhi, 'gx', around(8, 1))]
    ppermute x2, starting transfers between devices: 2.89 us -> 3.96 us  [from_sides(): lax.ppermute(xlo, 'gx', around(8, -1))]
  transfers between devices with their start and end apart: 20 -> 20, of which waited for: 15 -> 12; matrix products, arithmetic and copies ran while one was open for 0% -> 0% of each run, Pallas kernels for 3% -> 7%
where the time goes in v6:
time: 85.1 us; the launch traced here: 84.7 us
  starting transfers between devices  41.3 us (49%)
  Pallas kernels  19.8 us (23%)
  waiting for transfers between devices  19.6 us (23%)
  local copies, waits for them, and re-layouts  2.35 us (3%)
  between operations  1.54 us (2%)
    all_to_all x2, starting transfers between devices, shards(): lax.all_to_all(partials, ('gx', 'gy'), split_axis=0, concat_axis=0, tiled...  16.4 us
    ppermute x9, waiting for transfers between devices, all_chips(): lax.ppermute(value, 'layer', around(GROUPS, 2 * d))  11.7 us
    ppermute x5, starting transfers between devices, swapped(): return lax.ppermute(value, 'layer', [(i, i ^ 1) for i in range(GROUPS)])  10.5 us
    ppermute x9, starting transfers between devices, all_chips(): lax.ppermute(value, 'layer', around(GROUPS, 2 * d))  9.17 us
    pallas_call x2, Pallas kernels, shards(): pl.pallas_call(functools.partial(solve_kernel, first, len(operands)), out...  8.1 us
    all_to_all x2, waiting for transfers between devices, shards(): lax.all_to_all(partials, ('gx', 'gy'), split_axis=0, concat_axis=0, tiled...  4.27 us
    pallas_call x2, Pallas kernels, shards(): pl.pallas_call(functools.partial(lateral_kernel, first), out_shape=shape(...  4.08 us
    ppermute x2, starting transfers between devices, from_sides(): lax.ppermute(xlo, 'gx', around(8, -1))  3.96 us
  transfers between devices with their start and end apart: 20, of which 12 were waited for; matrix products, arithmetic and copies ran while one was open for 0% of the time, Pallas kernels for 7%

profile of v6, /device:TPU:1, one launch (start us, length us, event | category | flops | bytes accessed | tf_op | source)
XLA Modules:
  0.0 84.7 jit_solution(8792449223733856002)
XLA Ops:
  0.7 1.1 %copy-done.1 = f32[8,64,256]{2,1,0:T(8,128)S(1)} copy-done((f32[8,64,256]{2,1,0:T(8,128)S(1)}, f32[8,64,256]{2,1,0:T(8,128)}, u32[]{:S(2)}) %copy-start.1) | copy-done | bytes 524312
  1.8 1.8 %first_edges.1 = (f32[16,256]{1,0:T(8,128)S(1)}, f32[16,256]{1,0:T(8,128)S(1)}, f32[16,128]{1,0:T(8,128)S(1)}, f32[3,32,256]{2,1,0:T(8,128)S(1)}, f32[3,32,256]{2,1,0:T(8,128)S(1)}) custom-call(f32[512,256]{1,0:T(8,128)S(1)} %bitcast.16, f32[8,64,256]{2,1,0:T(8,128)} %perm_x.1, f32[512,256]{1,0:T(8,128)} %bitcast.25, f32[8,8,64,256]{3,2,1,0:T(8,128)} %bitcast.22), custom_call_target="tpu_custom_call" | custom-call | tf_op jit(solution)/shard_map/first_edges/pallas_call | solution.py:519
  3.5 3.3 %collective-permute-start = (f32[3,32,256]{2,1,0:T(8,128)S(1)}, f32[3,32,256]{2,1,0:T(8,128)S(1)}, u32[]{:S(2)}, u32[]{:S(2)}) collective-permute-start(f32[3,32,256]{2,1,0:T(8,128)S(1)} %get-tuple-element.41), channel_id=1, source_target_pairs={{0,32},{32,0},{64,96},{96,64},{128,160},{160,128},{192,224},{224,1... | collective-permute-start | bytes 294920 | tf_op jit(solution)/shard_map/ppermute | solution.py:477
  7.6 2.2 %first_wells.1 = (f32[96,4,128]{2,1,0:T(4,128)}, f32[8,128]{1,0:T(8,128)S(1)}, f32[8,128]{1,0:T(8,128)S(1)}, f32[1,128]{1,0:T(1,128)S(1)}) custom-call(f32[16,128]{1,0:T(8,128)S(1)} %get-tuple-element.38.refs_0_.refs_5_, f32[512,256]{1,0:T(8,128)S(1)} %bitcast.17, f32[8,48]{1,0:T(8,128)S(1)} %bitcast.20, s32[1,48]{1,0:T(1,128)S(1)} %bitcast.21, ...), custom_call_target="tpu_custom_call" | custom-call | tf_op jit(solution)/shard_map/first_wells/pallas_call | solution.py:538
  9.8 0.0 collective-permute-done.other.fixed_other.refs_11_
  9.8 9.5 %all-to-all-start = ((f32[96,4,128]{2,1,0:T(4,128)}), f32[96,4,128]{2,1,0:T(4,128)S(1)}, u32[]{:S(2)}, u32[]{:S(2)}) async-start(f32[96,4,128]{2,1,0:T(4,128)} %get-tuple-element.42), calls=%async_computation | async-start | bytes 393216 | tf_op jit(solution)/shard_map/all_to_all | solution.py:565
  19.3 2.6 %collective-permute-start.3 = (f32[3,32,256]{2,1,0:T(8,128)S(1)}, f32[3,32,256]{2,1,0:T(8,128)S(1)}, u32[]{:S(2)}, u32[]{:S(2)}) collective-permute-start(f32[3,32,256]{2,1,0:T(8,128)S(1)} %pair_fixed.1.refs_4_), channel_id=1, source_target_pairs={{0,192},{32,224},{64,0},{96,32},{128,64},{160,96},{192,128},{224,1... | collective-permute-start | bytes 294920 | tf_op jit(solution)/shard_map/ppermute | solution.py:481
  21.9 0.5 collective-permute-start.2
  22.4 0.6 collective-permute-start.1
  23.0 2.5 %collective-permute-start.5 = (f32[16,256]{1,0:T(8,128)S(1)}, f32[16,256]{1,0:T(8,128)S(1)}, u32[]{:S(2)}, u32[]{:S(2)}) collective-permute-start(f32[16,256]{1,0:T(8,128)S(1)} %get-tuple-element.47.refs_6_), channel_id=1, source_target_pairs={{0,28},{4,0},{8,4},{12,8},{16,12},{20,16},{24,20},{28,24},{1,29},{... | collective-permute-start | bytes 49160 | tf_op jit(solution)/shard_map/ppermute | solution.py:473
  25.5 2.0 %lateral.2.refs_10_ = f32[2,512,128]{2,1,0:T(8,128)S(1)} custom-call(f32[512,256]{1,0:T(8,128)S(1)} %bitcast.18, f32[512,256]{1,0:T(8,128)S(1)} %bitcast.14, f32[512,256]{1,0:T(8,128)} %bitcast.26, f32[512,256]{1,0:T(8,128)} %bitcast.28), custom_call_target="tpu_custom_call" | custom-call | flops 2228224 | bytes 2621440 | tf_op jit(solution)/shard_map/lateral/pallas_call | solution.py:569
  27.6 2.5 %collective-permute-done.1.refs_5_ = f32[3,32,256]{2,1,0:T(8,128)S(1)} collective-permute-done((f32[3,32,256]{2,1,0:T(8,128)S(1)}, f32[3,32,256]{2,1,0:T(8,128)S(1)}, u32[]{:S(2)}, u32[]{:S(2)}) %collective-permute-start.1) | collective-permute-done | bytes 98336 | tf_op jit(solution)/shard_map/ppermute | solution.py:481
  30.1 0.0 all-to-all-done.refs_1_
  30.1 0.0 collective-permute-done.5.refs_9_.refs_11_
  30.1 0.0 collective-permute-done.4.refs_8_.refs_10_
  30.1 4.3 %solve_lines.2 = (f32[512,256]{1,0:T(8,128)S(1)}, f32[2,32,256]{2,1,0:T(8,128)S(1)}, f32[2,32,256]{2,1,0:T(8,128)S(1)}, f32[2,128]{1,0:T(2,128)S(1)}, f32[8,128]...) custom-call(s32[1,48]{1,0:T(1,128)S(1)} %copy-done.6, f32[96,4,128]{2,1,0:T(4,128)S(1)} %all-to-all-done.refs_1_, ...), custom_call_target="tpu_custom_call" | custom-call | tf_op jit(solution)/shard_map/solve_lines/pallas_call | solution.py:585
  34.4 2.1 %collective-permute-start.6 = (f32[2,32,256]{2,1,0:T(8,128)S(1)}, f32[2,32,256]{2,1,0:T(8,128)S(1)}, u32[]{:S(2)}, u32[]{:S(2)}) collective-permute-start(f32[2,32,256]{2,1,0:T(8,128)S(1)} %get-tuple-element.50), channel_id=1, source_target_pairs={{0,32},{32,0},{64,96},{96,64},{128,160},{160,128},{192,224},{224,1... | collective-permute-start | bytes 196616 | tf_op jit(solution)/shard_map/ppermute | solution.py:477
  36.6 0.9 %collective-permute-done.6.other.refs_9_ = f32[2,32,256]{2,1,0:T(8,128)S(1)} collective-permute-done((f32[2,32,256]{2,1,0:T(8,128)S(1)}, f32[2,32,256]{2,1,0:T(8,128)S(1)}, u32[]{:S(2)}, u32[]{:S(2)}) %collective-permute-start.6) | collective-permute-done | bytes 65568 | tf_op jit(solution)/shard_map/ppermute | solution.py:477
  37.5 2.5 %collective-permute-start.9 = (f32[2,32,256]{2,1,0:T(8,128)S(1)}, f32[2,32,256]{2,1,0:T(8,128)S(1)}, u32[]{:S(2)}, u32[]{:S(2)}) collective-permute-start(f32[2,32,256]{2,1,0:T(8,128)S(1)} %pair.2.refs_0_), channel_id=1, source_target_pairs={{0,192},{32,224},{64,0},{96,32},{128,64},{160,96},{192,128},{224,1... | collective-permute-start | bytes 196616 | tf_op jit(solution)/shard_map/ppermute | solution.py:481
  39.9 0.9 %collective-permute-start.8 = (f32[2,32,256]{2,1,0:T(8,128)S(1)}, f32[2,32,256]{2,1,0:T(8,128)S(1)}, u32[]{:S(2)}, u32[]{:S(2)}) collective-permute-start(f32[2,32,256]{2,1,0:T(8,128)S(1)} %pair.2.refs_0_), channel_id=1, source_target_pairs={{0,128},{32,160},{64,192},{96,224},{128,0},{160,32},{192,64},{224,... | collective-permute-start | bytes 196616 | tf_op jit(solution)/shard_map/ppermute | solution.py:481
  40.9 0.2 collective-permute-start.7
  41.1 0.2 collective-permute-done.9.refs_3_
  41.3 3.3 %collective-permute-done.8.refs_2_ = f32[2,32,256]{2,1,0:T(8,128)S(1)} collective-permute-done((f32[2,32,256]{2,1,0:T(8,128)S(1)}, f32[2,32,256]{2,1,0:T(8,128)S(1)}, u32[]{:S(2)}, u32[]{:S(2)}) %collective-permute-start.8) | collective-permute-done | bytes 65568 | tf_op jit(solution)/shard_map/ppermute | solution.py:481
  44.6 1.3 %collective-permute-done.7.refs_1_ = f32[2,32,256]{2,1,0:T(8,128)S(1)} collective-permute-done((f32[2,32,256]{2,1,0:T(8,128)S(1)}, f32[2,32,256]{2,1,0:T(8,128)S(1)}, u32[]{:S(2)}, u32[]{:S(2)}) %collective-permute-start.7) | collective-permute-done | bytes 65568 | tf_op jit(solution)/shard_map/ppermute | solution.py:481
  45.9 0.1 chain.2
  46.0 1.6 %collective-permute-start.10 = (f32[2,32,256]{2,1,0:T(8,128)S(1)}, f32[2,32,256]{2,1,0:T(8,128)S(1)}, u32[]{:S(2)}, u32[]{:S(2)}) collective-permute-start(f32[2,32,256]{2,1,0:T(8,128)S(1)} %get-tuple-element.56), channel_id=1, source_target_pairs={{0,32},{32,0},{64,96},{96,64},{128,160},{160,128},{192,224},{224,1... | collective-permute-start | bytes 196616 | tf_op jit(solution)/shard_map/ppermute | solution.py:477
  47.6 0.9 %collective-permute-done.10.other = f32[2,32,256]{2,1,0:T(8,128)S(1)} collective-permute-done((f32[2,32,256]{2,1,0:T(8,128)S(1)}, f32[2,32,256]{2,1,0:T(8,128)S(1)}, u32[]{:S(2)}, u32[]{:S(2)}) %collective-permute-start.10) | collective-permute-done | bytes 65568 | tf_op jit(solution)/shard_map/ppermute | solution.py:477
  48.5 1.2 %copy-done.3 = f32[2,8,64,256]{3,2,1,0:T(8,128)S(1)} copy-done((f32[2,8,64,256]{3,2,1,0:T(8,128)S(1)}, f32[2,8,64,256]{3,2,1,0:T(8,128)}, u32[]{:S(2)}) %copy-start.3) | copy-done | bytes 1048600
  49.7 0.3 sweep_mid.1
  50.0 2.1 %next_wells.1 = (f32[96,2,128]{2,1,0:T(2,128)}, f32[8,128]{1,0:T(8,128)S(1)}) custom-call(f32[2,512,128]{2,1,0:T(8,128)S(1)} %get-tuple-element.59.split.field, f32[8,128]{1,0:T(8,128)S(1)} %get-tuple-element.44.refs_2_.live, f32[1,128]{1,0:T(1,128)S(1)} %get-tuple-element.45.refs_3_.wells, f32[1,8]{1,0:T(1,128)S(1)} %copy-done.8, s32[1,48]{1,0:T(1,128)S(1)} %copy-done.6), custom_call_target="tpu_custom_call" | custom-call | tf_op jit(solution)/shard_map/next_wells/pallas_call | solution.py:623
  52.2 6.9 %all-to-all-start.1 = ((f32[96,2,128]{2,1,0:T(2,128)}), f32[96,2,128]{2,1,0:T(2,128)S(1)}, u32[]{:S(2)}, u32[]{:S(2)}) async-start(f32[96,2,128]{2,1,0:T(2,128)} %get-tuple-element.60), calls=%async_computation.1 | async-start | bytes 196608 | tf_op jit(solution)/shard_map/all_to_all | solution.py:565
  59.1 1.3 %collective-permute-start.11 = (f32[8,256]{1,0:T(8,128)S(1)}, f32[8,256]{1,0:T(8,128)S(1)}, u32[]{:S(2)}, u32[]{:S(2)}) collective-permute-start(f32[8,256]{1,0:T(8,128)S(1)} %get-tuple-element.62), channel_id=1, source_target_pairs={{0,4},{4,8},{8,12},{12,16},{16,20},{20,24},{24,28},{28,0},{1,5},{5... | collective-permute-start | bytes 24584 | tf_op jit(solution)/shard_map/ppermute | solution.py:473
  60.4 1.4 %collective-permute-start.12 = (f32[8,256]{1,0:T(8,128)S(1)}, f32[8,256]{1,0:T(8,128)S(1)}, u32[]{:S(2)}, u32[]{:S(2)}) collective-permute-start(f32[8,256]{1,0:T(8,128)S(1)} %get-tuple-element.63), channel_id=1, source_target_pairs={{0,28},{4,0},{8,4},{12,8},{16,12},{20,16},{24,20},{28,24},{1,29},{... | collective-permute-start | bytes 24584 | tf_op jit(solution)/shard_map/ppermute | solution.py:473
  61.9 2.0 %lateral.3.refs_15_ = f32[2,512,128]{2,1,0:T(8,128)S(1)} custom-call(f32[2,512,128]{2,1,0:T(8,128)S(1)} %get-tuple-element.59.split.field, f32[512,256]{1,0:T(8,128)S(1)} %bitcast.15, f32[512,256]{1,0:T(8,128)} %bitcast.27, f32[512,256]{1,0:T(8,128)} %bitcast.29), custom_call_target="tpu_custom_call" | custom-call | flops 2228224 | bytes 2621440 | tf_op jit(solution)/shard_map/lateral/pallas_call | solution.py:569
  63.9 4.3 %all-to-all-done.1.refs_1_ = f32[96,2,128]{2,1,0:T(2,128)S(1)} async-done(((f32[96,2,128]{2,1,0:T(2,128)}), f32[96,2,128]{2,1,0:T(2,128)S(1)}, u32[]{:S(2)}, u32[]{:S(2)}) %all-to-all-start.1) | async-done | bytes 98336 | tf_op jit(solution)/shard_map/all_to_all | solution.py:565
  68.2 3.8 %solve_lines.3 = (f32[512,256]{1,0:T(8,128)S(1)}, f32[2,32,256]{2,1,0:T(8,128)S(1)}, f32[2,32,256]{2,1,0:T(8,128)S(1)}, f32[8,48]{1,0:T(8,128)}) custom-call(s32[1,48]{1,0:T(1,128)S(1)} %copy-done.6, f32[96,2,128]{2,1,0:T(2,128)S(1)} %all-to-all-done.1.refs_1_, f32[8,128]{1,0:T(8,128)S(1)} %get-tuple-element.44.refs_2_.live, ...), custom_call_target="tpu_custom_call" | custom-call | tf_op jit(solution)/shard_map/solve_lines/pallas_call | solution.py:585
  72.0 2.0 %collective-permute-start.13 = (f32[2,32,256]{2,1,0:T(8,128)S(1)}, f32[2,32,256]{2,1,0:T(8,128)S(1)}, u32[]{:S(2)}, u32[]{:S(2)}) collective-permute-start(f32[2,32,256]{2,1,0:T(8,128)S(1)} %get-tuple-element.69), channel_id=1, source_target_pairs={{0,32},{32,0},{64,96},{96,64},{128,160},{160,128},{192,224},{224,1... | collective-permute-start | bytes 196616 | tf_op jit(solution)/shard_map/ppermute | solution.py:477
  73.9 0.9 %collective-permute-done.13.other.refs_9_ = f32[2,32,256]{2,1,0:T(8,128)S(1)} collective-permute-done((f32[2,32,256]{2,1,0:T(8,128)S(1)}, f32[2,32,256]{2,1,0:T(8,128)S(1)}, u32[]{:S(2)}, u32[]{:S(2)}) %collective-permute-start.13) | collective-permute-done | bytes 65568 | tf_op jit(solution)/shard_map/ppermute | solution.py:477
  74.8 0.2 collective-permute-start.16
  75.0 1.1 %collective-permute-start.15 = (f32[2,32,256]{2,1,0:T(8,128)S(1)}, f32[2,32,256]{2,1,0:T(8,128)S(1)}, u32[]{:S(2)}, u32[]{:S(2)}) collective-permute-start(f32[2,32,256]{2,1,0:T(8,128)S(1)} %pair.3.refs_0_), channel_id=1, source_target_pairs={{0,128},{32,160},{64,192},{96,224},{128,0},{160,32},{192,64},{224,... | collective-permute-start | bytes 196616 | tf_op jit(solution)/shard_map/ppermute | solution.py:481
  76.2 0.6 collective-permute-start.14
  76.7 1.3 %collective-permute-done.16.refs_3_ = f32[2,32,256]{2,1,0:T(8,128)S(1)} collective-permute-done((f32[2,32,256]{2,1,0:T(8,128)S(1)}, f32[2,32,256]{2,1,0:T(8,128)S(1)}, u32[]{:S(2)}, u32[]{:S(2)}) %collective-permute-start.16) | collective-permute-done | bytes 65568 | tf_op jit(solution)/shard_map/ppermute | solution.py:481
  78.0 1.6 %collective-permute-done.15.refs_2_ = f32[2,32,256]{2,1,0:T(8,128)S(1)} collective-permute-done((f32[2,32,256]{2,1,0:T(8,128)S(1)}, f32[2,32,256]{2,1,0:T(8,128)S(1)}, u32[]{:S(2)}, u32[]{:S(2)}) %collective-permute-start.15) | collective-permute-done | bytes 65568 | tf_op jit(solution)/shard_map/ppermute | solution.py:481
  79.7 1.6 %collective-permute-done.14.refs_1_ = f32[2,32,256]{2,1,0:T(8,128)S(1)} collective-permute-done((f32[2,32,256]{2,1,0:T(8,128)S(1)}, f32[2,32,256]{2,1,0:T(8,128)S(1)}, u32[]{:S(2)}, u32[]{:S(2)}) %collective-permute-start.14) | collective-permute-done | bytes 65568 | tf_op jit(solution)/shard_map/ppermute | solution.py:481
  81.2 0.1 chain.3
  81.3 1.5 %collective-permute-start.17 = (f32[2,32,256]{2,1,0:T(8,128)S(1)}, f32[2,32,256]{2,1,0:T(8,128)S(1)}, u32[]{:S(2)}, u32[]{:S(2)}) collective-permute-start(f32[2,32,256]{2,1,0:T(8,128)S(1)} %get-tuple-element.71), channel_id=1, source_target_pairs={{0,32},{32,0},{64,96},{96,64},{128,160},{160,128},{192,224},{224,1... | collective-permute-start | bytes 196616 | tf_op jit(solution)/shard_map/ppermute | solution.py:477
  82.8 0.9 %collective-permute-done.17.other = f32[2,32,256]{2,1,0:T(8,128)S(1)} collective-permute-done((f32[2,32,256]{2,1,0:T(8,128)S(1)}, f32[2,32,256]{2,1,0:T(8,128)S(1)}, u32[]{:S(2)}, u32[]{:S(2)}) %collective-permute-start.17) | collective-permute-done | bytes 65568 | tf_op jit(solution)/shard_map/ppermute | solution.py:477
  83.7 0.9 %sweep_last.1 = f32[512,256]{1,0:T(8,128)} custom-call(f32[2,32,256]{2,1,0:T(8,128)S(1)} %get-tuple-element.70.mine, f32[2,32,256]{2,1,0:T(8,128)S(1)} %collective-permute-done.17.other, f32[512,256]{1,0:T(8,128)S(1)} %get-tuple-element.72.solved, f32[2,8,64,256]{3,2,1,0:T(8,128)S(1)} %copy-done.4), custom_call_target="tpu_custom_call" | custom-call | tf_op jit(solution)/shard_map/sweep_last/pallas_call | solution.py:485
  (28 shorter events, 0.1 us)
Async XLA Ops:
  0.6 24.9 %copy-start = (f32[8,64,256]{2,1,0:T(8,128)S(1)}, f32[8,64,256]{2,1,0:T(8,128)}, u32[]{:S(2)}) copy-start(f32[8,64,256]{2,1,0:T(8,128)} %perm_x.1) | copy-start | bytes 1572868
  0.6 1.1 %copy-start.1 = (f32[8,64,256]{2,1,0:T(8,128)S(1)}, f32[8,64,256]{2,1,0:T(8,128)}, u32[]{:S(2)}) copy-start(f32[8,64,256]{2,1,0:T(8,128)} %param.12) | copy-start | bytes 1572868
  1.7 5.8 %copy-start.6 = (s32[1,48]{1,0:T(1,128)S(1)}, s32[1,48]{1,0:T(1,128)}, u32[]{:S(2)}) copy-start(s32[1,48]{1,0:T(1,128)} %refs_0_.3) | copy-start | bytes 580
  1.7 5.8 %copy-start.7 = (f32[1,48,8]{1,2,0:T(8,128)S(1)}, f32[1,48,8]{1,2,0:T(8,128)}, u32[]{:S(2)}) copy-start(f32[1,48,8]{1,2,0:T(8,128)} %param.22) | copy-start | bytes 4612
  1.7 5.8 %copy-start.8 = (f32[1,8]{1,0:T(1,128)S(1)}, f32[1,8]{1,0:T(1,128)}, u32[]{:S(2)}) copy-start(f32[1,8]{1,0:T(1,128)} %rate.1) | copy-start | bytes 100
  1.7 5.8 %copy-start.9 = (s32[1,48,1]{1,2,0:T(1,128)S(1)}, s32[1,48,1]{1,2,0:T(1,128)}, u32[]{:S(2)}) copy-start(s32[1,48,1]{1,2,0:T(1,128)} %param.19) | copy-start | bytes 580
  1.8 5.8 %copy-start.10 = (s32[1,48]{1,0:T(1,128)S(1)}, s32[1,48]{1,0:T(1,128)}, u32[]{:S(2)}) copy-start(s32[1,48]{1,0:T(1,128)} %refs_4_.1) | copy-start | bytes 580
  1.8 23.8 %copy-start.2 = (f32[8,64,256]{2,1,0:T(8,128)S(1)}, f32[8,64,256]{2,1,0:T(8,128)}, u32[]{:S(2)}) copy-start(f32[8,64,256]{2,1,0:T(8,128)} %param.12) | copy-start | bytes 1572868
  1.8 28.3 %copy-start.5 = (f32[1,64,256]{2,1,0:T(8,128)S(1)}, f32[1,64,256]{2,1,0:T(8,128)}, u32[]{:S(2)}) copy-start(f32[1,64,256]{2,1,0:T(8,128)} %param.17) | copy-start | bytes 196612
  3.5 6.2 %collective-permute-start = (f32[3,32,256]{2,1,0:T(8,128)S(1)}, f32[3,32,256]{2,1,0:T(8,128)S(1)}, u32[]{:S(2)}, u32[]{:S(2)}) collective-permute-start(f32[3,32,256]{2,1,0:T(8,128)S(1)} %get-tuple-element.41), channel_id=1, source_target_pairs={{0,32},{32,0},{64,96},{96,64},{128,160},{160,128},{192,224},{224,1... | collective-permute-start | bytes 294920 | tf_op jit(solution)/shard_map/ppermute | solution.py:477
  9.8 20.3 %all-to-all-start = ((f32[96,4,128]{2,1,0:T(4,128)}), f32[96,4,128]{2,1,0:T(4,128)S(1)}, u32[]{:S(2)}, u32[]{:S(2)}) async-start(f32[96,4,128]{2,1,0:T(4,128)} %get-tuple-element.42), calls=%async_computation | async-start | bytes 393216 | tf_op jit(solution)/shard_map/all_to_all | solution.py:565
  19.3 8.3 %collective-permute-start.3 = (f32[3,32,256]{2,1,0:T(8,128)S(1)}, f32[3,32,256]{2,1,0:T(8,128)S(1)}, u32[]{:S(2)}, u32[]{:S(2)}) collective-permute-start(f32[3,32,256]{2,1,0:T(8,128)S(1)} %pair_fixed.1.refs_4_), channel_id=1, source_target_pairs={{0,192},{32,224},{64,0},{96,32},{128,64},{160,96},{192,128},{224,1... | collective-permute-start | bytes 294920 | tf_op jit(solution)/shard_map/ppermute | solution.py:481
  21.9 5.7 %collective-permute-start.2 = (f32[3,32,256]{2,1,0:T(8,128)S(1)}, f32[3,32,256]{2,1,0:T(8,128)S(1)}, u32[]{:S(2)}, u32[]{:S(2)}) collective-permute-start(f32[3,32,256]{2,1,0:T(8,128)S(1)} %pair_fixed.1.refs_4_), channel_id=1, source_target_pairs={{0,128},{32,160},{64,192},{96,224},{128,0},{160,32},{192,64},{224,... | collective-permute-start | bytes 294920 | tf_op jit(solution)/shard_map/ppermute | solution.py:481
  22.4 7.7 %collective-permute-start.1 = (f32[3,32,256]{2,1,0:T(8,128)S(1)}, f32[3,32,256]{2,1,0:T(8,128)S(1)}, u32[]{:S(2)}, u32[]{:S(2)}) collective-permute-start(f32[3,32,256]{2,1,0:T(8,128)S(1)} %pair_fixed.1.refs_4_), channel_id=1, source_target_pairs={{0,64},{32,96},{64,128},{96,160},{128,192},{160,224},{192,0},{224,... | collective-permute-start | bytes 294920 | tf_op jit(solution)/shard_map/ppermute | solution.py:481
  23.0 7.1 %collective-permute-start.5 = (f32[16,256]{1,0:T(8,128)S(1)}, f32[16,256]{1,0:T(8,128)S(1)}, u32[]{:S(2)}, u32[]{:S(2)}) collective-permute-start(f32[16,256]{1,0:T(8,128)S(1)} %get-tuple-element.47.refs_6_), channel_id=1, source_target_pairs={{0,28},{4,0},{8,4},{12,8},{16,12},{20,16},{24,20},{28,24},{1,29},{... | collective-permute-start | bytes 49160 | tf_op jit(solution)/shard_map/ppermute | solution.py:473
  25.5 4.6 %collective-permute-start.4 = (f32[16,256]{1,0:T(8,128)S(1)}, f32[16,256]{1,0:T(8,128)S(1)}, u32[]{:S(2)}, u32[]{:S(2)}) collective-permute-start(f32[16,256]{1,0:T(8,128)S(1)} %get-tuple-element.48.refs_7_), channel_id=1, source_target_pairs={{0,4},{4,8},{8,12},{12,16},{16,20},{20,24},{24,28},{28,0},{1,5},{5... | collective-permute-start | bytes 49160 | tf_op jit(solution)/shard_map/ppermute | solution.py:473
  34.4 3.0 %collective-permute-start.6 = (f32[2,32,256]{2,1,0:T(8,128)S(1)}, f32[2,32,256]{2,1,0:T(8,128)S(1)}, u32[]{:S(2)}, u32[]{:S(2)}) collective-permute-start(f32[2,32,256]{2,1,0:T(8,128)S(1)} %get-tuple-element.50), channel_id=1, source_target_pairs={{0,32},{32,0},{64,96},{96,64},{128,160},{160,128},{192,224},{224,1... | collective-permute-start | bytes 196616 | tf_op jit(solution)/shard_map/ppermute | solution.py:477
  37.5 3.8 %collective-permute-start.9 = (f32[2,32,256]{2,1,0:T(8,128)S(1)}, f32[2,32,256]{2,1,0:T(8,128)S(1)}, u32[]{:S(2)}, u32[]{:S(2)}) collective-permute-start(f32[2,32,256]{2,1,0:T(8,128)S(1)} %pair.2.refs_0_), channel_id=1, source_target_pairs={{0,192},{32,224},{64,0},{96,32},{128,64},{160,96},{192,128},{224,1... | collective-permute-start | bytes 196616 | tf_op jit(solution)/shard_map/ppermute | solution.py:481
  39.9 4.6 %collective-permute-start.8 = (f32[2,32,256]{2,1,0:T(8,128)S(1)}, f32[2,32,256]{2,1,0:T(8,128)S(1)}, u32[]{:S(2)}, u32[]{:S(2)}) collective-permute-start(f32[2,32,256]{2,1,0:T(8,128)S(1)} %pair.2.refs_0_), channel_id=1, source_target_pairs={{0,128},{32,160},{64,192},{96,224},{128,0},{160,32},{192,64},{224,... | collective-permute-start | bytes 196616 | tf_op jit(solution)/shard_map/ppermute | solution.py:481
  40.9 5.0 %collective-permute-start.7 = (f32[2,32,256]{2,1,0:T(8,128)S(1)}, f32[2,32,256]{2,1,0:T(8,128)S(1)}, u32[]{:S(2)}, u32[]{:S(2)}) collective-permute-start(f32[2,32,256]{2,1,0:T(8,128)S(1)} %pair.2.refs_0_), channel_id=1, source_target_pairs={{0,64},{32,96},{64,128},{96,160},{128,192},{160,224},{192,0},{224,... | collective-permute-start | bytes 196616 | tf_op jit(solution)/shard_map/ppermute | solution.py:481
  46.0 2.5 %collective-permute-start.10 = (f32[2,32,256]{2,1,0:T(8,128)S(1)}, f32[2,32,256]{2,1,0:T(8,128)S(1)}, u32[]{:S(2)}, u32[]{:S(2)}) collective-permute-start(f32[2,32,256]{2,1,0:T(8,128)S(1)} %get-tuple-element.56), channel_id=1, source_target_pairs={{0,32},{32,0},{64,96},{96,64},{128,160},{160,128},{192,224},{224,1... | collective-permute-start | bytes 196616 | tf_op jit(solution)/shard_map/ppermute | solution.py:477
  48.5 1.2 %copy-start.3 = (f32[2,8,64,256]{3,2,1,0:T(8,128)S(1)}, f32[2,8,64,256]{3,2,1,0:T(8,128)}, u32[]{:S(2)}) copy-start(f32[2,8,64,256]{3,2,1,0:T(8,128)} %get-tuple-element.58.rims) | copy-start | bytes 3145732
  52.2 16.0 %all-to-all-start.1 = ((f32[96,2,128]{2,1,0:T(2,128)}), f32[96,2,128]{2,1,0:T(2,128)S(1)}, u32[]{:S(2)}, u32[]{:S(2)}) async-start(f32[96,2,128]{2,1,0:T(2,128)} %get-tuple-element.60), calls=%async_computation.1 | async-start | bytes 196608 | tf_op jit(solution)/shard_map/all_to_all | solution.py:565
  59.1 4.8 %collective-permute-start.11 = (f32[8,256]{1,0:T(8,128)S(1)}, f32[8,256]{1,0:T(8,128)S(1)}, u32[]{:S(2)}, u32[]{:S(2)}) collective-permute-start(f32[8,256]{1,0:T(8,128)S(1)} %get-tuple-element.62), channel_id=1, source_target_pairs={{0,4},{4,8},{8,12},{12,16},{16,20},{20,24},{24,28},{28,0},{1,5},{5... | collective-permute-start | bytes 24584 | tf_op jit(solution)/shard_map/ppermute | solution.py:473
  60.4 23.3 %copy-start.4 = (f32[2,8,64,256]{3,2,1,0:T(8,128)S(1)}, f32[2,8,64,256]{3,2,1,0:T(8,128)}, u32[]{:S(2)}) copy-start(f32[2,8,64,256]{3,2,1,0:T(8,128)} %get-tuple-element.58.rims) | copy-start | bytes 3145732
  60.4 3.5 %collective-permute-start.12 = (f32[8,256]{1,0:T(8,128)S(1)}, f32[8,256]{1,0:T(8,128)S(1)}, u32[]{:S(2)}, u32[]{:S(2)}) collective-permute-start(f32[8,256]{1,0:T(8,128)S(1)} %get-tuple-element.63), channel_id=1, source_target_pairs={{0,28},{4,0},{8,4},{12,8},{16,12},{20,16},{24,20},{28,24},{1,29},{... | collective-permute-start | bytes 24584 | tf_op jit(solution)/shard_map/ppermute | solution.py:473
  72.0 2.9 %collective-permute-start.13 = (f32[2,32,256]{2,1,0:T(8,128)S(1)}, f32[2,32,256]{2,1,0:T(8,128)S(1)}, u32[]{:S(2)}, u32[]{:S(2)}) collective-permute-start(f32[2,32,256]{2,1,0:T(8,128)S(1)} %get-tuple-element.69), channel_id=1, source_target_pairs={{0,32},{32,0},{64,96},{96,64},{128,160},{160,128},{192,224},{224,1... | collective-permute-start | bytes 196616 | tf_op jit(solution)/shard_map/ppermute | solution.py:477
  74.8 3.2 %collective-permute-start.16 = (f32[2,32,256]{2,1,0:T(8,128)S(1)}, f32[2,32,256]{2,1,0:T(8,128)S(1)}, u32[]{:S(2)}, u32[]{:S(2)}) collective-permute-start(f32[2,32,256]{2,1,0:T(8,128)S(1)} %pair.3.refs_0_), channel_id=1, source_target_pairs={{0,192},{32,224},{64,0},{96,32},{128,64},{160,96},{192,128},{224,1... | collective-permute-start | bytes 196616 | tf_op jit(solution)/shard_map/ppermute | solution.py:481
  75.0 4.6 %collective-permute-start.15 = (f32[2,32,256]{2,1,0:T(8,128)S(1)}, f32[2,32,256]{2,1,0:T(8,128)S(1)}, u32[]{:S(2)}, u32[]{:S(2)}) collective-permute-start(f32[2,32,256]{2,1,0:T(8,128)S(1)} %pair.3.refs_0_), channel_id=1, source_target_pairs={{0,128},{32,160},{64,192},{96,224},{128,0},{160,32},{192,64},{224,... | collective-permute-start | bytes 196616 | tf_op jit(solution)/shard_map/ppermute | solution.py:481
  76.2 5.0 %collective-permute-start.14 = (f32[2,32,256]{2,1,0:T(8,128)S(1)}, f32[2,32,256]{2,1,0:T(8,128)S(1)}, u32[]{:S(2)}, u32[]{:S(2)}) collective-permute-start(f32[2,32,256]{2,1,0:T(8,128)S(1)} %pair.3.refs_0_), channel_id=1, source_target_pairs={{0,64},{32,96},{64,128},{96,160},{128,192},{160,224},{192,0},{224,... | collective-permute-start | bytes 196616 | tf_op jit(solution)/shard_map/ppermute | solution.py:481
  81.3 2.4 %collective-permute-start.17 = (f32[2,32,256]{2,1,0:T(8,128)S(1)}, f32[2,32,256]{2,1,0:T(8,128)S(1)}, u32[]{:S(2)}, u32[]{:S(2)}) collective-permute-start(f32[2,32,256]{2,1,0:T(8,128)S(1)} %get-tuple-element.71), channel_id=1, source_target_pairs={{0,32},{32,0},{64,96},{96,64},{128,160},{160,128},{192,224},{224,1... | collective-permute-start | bytes 196616 | tf_op jit(solution)/shard_map/ppermute | solution.py:477

commit v7 on v6

--- a/solution.py
+++ b/solution.py
@@ -8,7 +8,7 @@
 from jax.sharding import PartitionSpec as P
 
 ITERS = 2
-EDGE_MIB = 53.0
+EDGE_MIB = 53.5
 WELLS_MIB = 52.0
 SOLVE_MIB = 52.0
 LATERAL_MIB = 52.0
@@ -20,6 +20,7 @@
 WELLS = 256
 TILES = 32
 GROUPS = 8
+PARTS = 4
 F32 = jnp.float32
 VMEM = pl.BlockSpec(memory_space=pltpu.VMEM)
 SMEM = pl.BlockSpec(memory_space=pltpu.SMEM)
@@ -220,6 +221,8 @@
 
 def wells_next_kernel(split, live, wells, rate, column, partials, at_slots, live_v, wells_v, rate_v, column_s, sem):
     copies = load([(column, column_s), (rate, rate_v), (live, live_v), (wells, wells_v)], sem)
+    turned = y_edges([(split.at[0], 0), (split.at[1], 127)])
+    send_y(partials, turned[0:4], turned[4:8])
     for copy in copies:
         copy.wait()
     at = gather_slots(split, column_s)
@@ -227,8 +230,6 @@
     weighted = jnp.sum(live_v[...] * at, axis=0, keepdims=True)
     weighted_c, wells_c = well_columns([weighted, wells_v[...]])
     send_wells(partials, totals_by_well(weighted_c, wells_c) + own_rates(rate_v))
-    turned = y_edges([(split.at[0], 0), (split.at[1], 127)])
-    send_y(partials, turned[0:4], turned[4:8])
 
 
 def lateral_kernel(first, field, kx, ky, source, rhs, field_v, kx_v, ky_v, source_v, sem):
@@ -264,7 +265,13 @@
         (solved, keep, give, flow_out, *refs) = refs
     held, (carried, column_s, sem) = refs[:inputs], refs[inputs:]
     (column, partials, live, wells, at_slots, y_own, x_own_lo, x_own_hi, *small, rhs, lower, inverse) = held
-    copies = load([(away[0], column_s)] + [(away[n], held[n]) for n in range(1, inputs)], sem)
+    parts = [slice(n * CX // PARTS, (n + 1) * CX // PARTS) for n in range(PARTS)]
+    copies = load(
+        [(away[0], column_s)]
+        + [(away[n], held[n]) for n in range(1, inputs - 1)]
+        + [(away[inputs - 1].at[:, :, part], inverse.at[:, :, part]) for part in parts],
+        sem,
+    )
     for copy in copies[: inputs - 3]:
         copy.wait()
     gx, gy = lax.axis_index("gx"), lax.axis_index("gy")
@@ -336,8 +343,7 @@
         where = (pl.ds(x, LZ, stride=CX), slice(None))
         part[where] = part[where] + jnp.where(lanes8 == lane, flow[:, s : s + 1], 0.0)
 
-    for copy in copies[inputs - 2 :]:
-        copy.wait()
+    copies[inputs - 2].wait()
 
     def solve_block(b, carry):
         at = pl.multiple_of(b * 8, 8)
@@ -358,7 +364,9 @@
                 carried[0, here, :] = total + inverse[i, i, here, :] * low - low
         return carry
 
-    lax.fori_loop(0, CX // 8, solve_block, 0)
+    for n in range(PARTS):
+        copies[inputs - 1 + n].wait()
+        lax.fori_loop(n * (CX // 8) // PARTS, (n + 1) * (CX // 8) // PARTS, solve_block, 0)
     for side, out in ((0, keep), (1, give)):
         out[...] = carried[:, rows_of(side), :]
 
@@ -592,7 +600,7 @@
             + [
                 pltpu.VMEM((2, CX, CY), F32),
                 pltpu.SMEM((1, SLOTS), jnp.int32),
-                pltpu.SemaphoreType.DMA((len(operands),)),
+                pltpu.SemaphoreType.DMA((len(operands) + PARTS - 1,)),
             ],
             compiler_params=params(SOLVE_MIB),
             name="solve_lines",

time: 85.1 us -> 83.2 us (0.978)
  local copies, waits for them, and re-layouts: 2.35 us -> 1.26 us
    unnamed x22 -> x20, local copies, waits for them, and re-layouts: 2.35 us -> 1.26 us
  transfers between devices with their start and end apart: 20 -> 20, of which waited for: 12 -> 12; matrix products, arithmetic and copies ran while one was open for 0% -> 0% of each run, Pallas kernels for 7% -> 8%
where the time goes in v7:
time: 83.2 us; the launch traced here: 82.9 us
  starting transfers between devices  41.3 us (50%)
  waiting for transfers between devices  19.6 us (24%)
  Pallas kernels  19.1 us (23%)
  between operations  1.56 us (2%)
  local copies, waits for them, and re-layouts  1.26 us (2%)
    all_to_all x2, starting transfers between devices, shards(): lax.all_to_all(partials, ('gx', 'gy'), split_axis=0, concat_axis=0, tiled...  16.4 us
    ppermute x9, waiting for transfers between devices, all_chips(): lax.ppermute(value, 'layer', around(GROUPS, 2 * d))  11.7 us
    ppermute x5, starting transfers between devices, swapped(): return lax.ppermute(value, 'layer', [(i, i ^ 1) for i in range(GROUPS)])  10.5 us
    ppermute x9, starting transfers between devices, all_chips(): lax.ppermute(value, 'layer', around(GROUPS, 2 * d))  9.17 us
    pallas_call x2, Pallas kernels, shards(): pl.pallas_call(functools.partial(solve_kernel, first, len(operands)), out...  7.41 us
    all_to_all x2, waiting for transfers between devices, shards(): lax.all_to_all(partials, ('gx', 'gy'), split_axis=0, concat_axis=0, tiled...  4.27 us
    pallas_call x2, Pallas kernels, shards(): pl.pallas_call(functools.partial(lateral_kernel, first), out_shape=shape(...  4.07 us
    ppermute x2, starting transfers between devices, from_sides(): lax.ppermute(xlo, 'gx', around(8, -1))  3.96 us
  transfers between devices with their start and end apart: 20, of which 12 were waited for; matrix products, arithmetic and copies ran while one was open for 0% of the time, Pallas kernels for 8%

profile of v7, /device:TPU:1, one launch (start us, length us, event | category | flops | bytes accessed | tf_op | source)
XLA Modules:
  0.0 82.9 jit_solution(708393097965095216)
XLA Ops:
  0.7 1.8 %first_edges.1 = (f32[16,256]{1,0:T(8,128)S(1)}, f32[16,256]{1,0:T(8,128)S(1)}, f32[16,128]{1,0:T(8,128)S(1)}, f32[3,32,256]{2,1,0:T(8,128)S(1)}, f32[3,32,256]{2,1,0:T(8,128)S(1)}) custom-call(f32[512,256]{1,0:T(8,128)} %bitcast.16, f32[8,64,256]{2,1,0:T(8,128)} %perm_x.1, f32[512,256]{1,0:T(8,128)} %bitcast.25, f32[8,8,64,256]{3,2,1,0:T(8,128)} %bitcast.22), custom_call_target="tpu_custom_call" | custom-call | tf_op jit(solution)/shard_map/first_edges/pallas_call | solution.py:527
  2.5 3.3 %collective-permute-start = (f32[3,32,256]{2,1,0:T(8,128)S(1)}, f32[3,32,256]{2,1,0:T(8,128)S(1)}, u32[]{:S(2)}, u32[]{:S(2)}) collective-permute-start(f32[3,32,256]{2,1,0:T(8,128)S(1)} %get-tuple-element.41), channel_id=1, source_target_pairs={{0,32},{32,0},{64,96},{96,64},{128,160},{160,128},{192,224},{224,1... | collective-permute-start | bytes 294920 | tf_op jit(solution)/shard_map/ppermute | solution.py:485
  6.6 2.2 %first_wells.1 = (f32[96,4,128]{2,1,0:T(4,128)}, f32[8,128]{1,0:T(8,128)S(1)}, f32[8,128]{1,0:T(8,128)S(1)}, f32[1,128]{1,0:T(1,128)S(1)}) custom-call(f32[16,128]{1,0:T(8,128)S(1)} %get-tuple-element.38.refs_0_.refs_5_, f32[512,256]{1,0:T(8,128)S(1)} %bitcast.17, f32[8,48]{1,0:T(8,128)S(1)} %bitcast.20, s32[1,48]{1,0:T(1,128)S(1)} %bitcast.21, ...), custom_call_target="tpu_custom_call" | custom-call | tf_op jit(solution)/shard_map/first_wells/pallas_call | solution.py:546
  8.8 9.5 %all-to-all-start = ((f32[96,4,128]{2,1,0:T(4,128)}), f32[96,4,128]{2,1,0:T(4,128)S(1)}, u32[]{:S(2)}, u32[]{:S(2)}) async-start(f32[96,4,128]{2,1,0:T(4,128)} %get-tuple-element.42), calls=%async_computation | async-start | bytes 393216 | tf_op jit(solution)/shard_map/all_to_all | solution.py:573
  18.3 2.6 %collective-permute-start.3 = (f32[3,32,256]{2,1,0:T(8,128)S(1)}, f32[3,32,256]{2,1,0:T(8,128)S(1)}, u32[]{:S(2)}, u32[]{:S(2)}) collective-permute-start(f32[3,32,256]{2,1,0:T(8,128)S(1)} %pair_fixed.1.refs_4_), channel_id=1, source_target_pairs={{0,192},{32,224},{64,0},{96,32},{128,64},{160,96},{192,128},{224,1... | collective-permute-start | bytes 294920 | tf_op jit(solution)/shard_map/ppermute | solution.py:489
  20.9 0.5 collective-permute-start.2
  21.4 0.6 collective-permute-start.1
  22.0 2.5 %collective-permute-start.5 = (f32[16,256]{1,0:T(8,128)S(1)}, f32[16,256]{1,0:T(8,128)S(1)}, u32[]{:S(2)}, u32[]{:S(2)}) collective-permute-start(f32[16,256]{1,0:T(8,128)S(1)} %get-tuple-element.47.refs_6_), channel_id=1, source_target_pairs={{0,28},{4,0},{8,4},{12,8},{16,12},{20,16},{24,20},{28,24},{1,29},{... | collective-permute-start | bytes 49160 | tf_op jit(solution)/shard_map/ppermute | solution.py:481
  24.5 0.0 collective-permute-start.4
  24.5 2.0 %lateral.2.refs_10_ = f32[2,512,128]{2,1,0:T(8,128)S(1)} custom-call(f32[512,256]{1,0:T(8,128)S(1)} %bitcast.18, f32[512,256]{1,0:T(8,128)S(1)} %bitcast.14, f32[512,256]{1,0:T(8,128)} %bitcast.26, f32[512,256]{1,0:T(8,128)} %bitcast.28), custom_call_target="tpu_custom_call" | custom-call | flops 2228224 | bytes 2621440 | tf_op jit(solution)/shard_map/lateral/pallas_call | solution.py:577
  26.6 0.0 collective-permute-done.2.refs_6_
  26.6 2.5 %collective-permute-done.1.refs_5_ = f32[3,32,256]{2,1,0:T(8,128)S(1)} collective-permute-done((f32[3,32,256]{2,1,0:T(8,128)S(1)}, f32[3,32,256]{2,1,0:T(8,128)S(1)}, u32[]{:S(2)}, u32[]{:S(2)}) %collective-permute-start.1) | collective-permute-done | bytes 98336 | tf_op jit(solution)/shard_map/ppermute | solution.py:489
  29.1 0.0 all-to-all-done.refs_1_
  29.1 0.0 collective-permute-done.5.refs_9_.refs_11_
  29.1 0.0 collective-permute-done.4.refs_8_.refs_10_
  29.1 4.0 %solve_lines.2 = (f32[512,256]{1,0:T(8,128)S(1)}, f32[2,32,256]{2,1,0:T(8,128)S(1)}, f32[2,32,256]{2,1,0:T(8,128)S(1)}, f32[2,128]{1,0:T(2,128)S(1)}, f32[8,128]...) custom-call(s32[1,48]{1,0:T(1,128)S(1)} %copy-done.5, f32[96,4,128]{2,1,0:T(4,128)S(1)} %all-to-all-done.refs_1_, ...), custom_call_target="tpu_custom_call" | custom-call | tf_op jit(solution)/shard_map/solve_lines/pallas_call | solution.py:593
  33.1 2.1 %collective-permute-start.6 = (f32[2,32,256]{2,1,0:T(8,128)S(1)}, f32[2,32,256]{2,1,0:T(8,128)S(1)}, u32[]{:S(2)}, u32[]{:S(2)}) collective-permute-start(f32[2,32,256]{2,1,0:T(8,128)S(1)} %get-tuple-element.50), channel_id=1, source_target_pairs={{0,32},{32,0},{64,96},{96,64},{128,160},{160,128},{192,224},{224,1... | collective-permute-start | bytes 196616 | tf_op jit(solution)/shard_map/ppermute | solution.py:485
  35.2 0.9 %collective-permute-done.6.other.refs_9_ = f32[2,32,256]{2,1,0:T(8,128)S(1)} collective-permute-done((f32[2,32,256]{2,1,0:T(8,128)S(1)}, f32[2,32,256]{2,1,0:T(8,128)S(1)}, u32[]{:S(2)}, u32[]{:S(2)}) %collective-permute-start.6) | collective-permute-done | bytes 65568 | tf_op jit(solution)/shard_map/ppermute | solution.py:485
  36.1 2.5 %collective-permute-start.9 = (f32[2,32,256]{2,1,0:T(8,128)S(1)}, f32[2,32,256]{2,1,0:T(8,128)S(1)}, u32[]{:S(2)}, u32[]{:S(2)}) collective-permute-start(f32[2,32,256]{2,1,0:T(8,128)S(1)} %pair.2.refs_0_), channel_id=1, source_target_pairs={{0,192},{32,224},{64,0},{96,32},{128,64},{160,96},{192,128},{224,1... | collective-permute-start | bytes 196616 | tf_op jit(solution)/shard_map/ppermute | solution.py:489
  38.6 0.9 %collective-permute-start.8 = (f32[2,32,256]{2,1,0:T(8,128)S(1)}, f32[2,32,256]{2,1,0:T(8,128)S(1)}, u32[]{:S(2)}, u32[]{:S(2)}) collective-permute-start(f32[2,32,256]{2,1,0:T(8,128)S(1)} %pair.2.refs_0_), channel_id=1, source_target_pairs={{0,128},{32,160},{64,192},{96,224},{128,0},{160,32},{192,64},{224,... | collective-permute-start | bytes 196616 | tf_op jit(solution)/shard_map/ppermute | solution.py:489
  39.5 0.2 collective-permute-start.7
  39.7 0.2 collective-permute-done.9.refs_3_
  39.9 3.3 %collective-permute-done.8.refs_2_ = f32[2,32,256]{2,1,0:T(8,128)S(1)} collective-permute-done((f32[2,32,256]{2,1,0:T(8,128)S(1)}, f32[2,32,256]{2,1,0:T(8,128)S(1)}, u32[]{:S(2)}, u32[]{:S(2)}) %collective-permute-start.8) | collective-permute-done | bytes 65568 | tf_op jit(solution)/shard_map/ppermute | solution.py:489
  43.2 1.3 %collective-permute-done.7.refs_1_ = f32[2,32,256]{2,1,0:T(8,128)S(1)} collective-permute-done((f32[2,32,256]{2,1,0:T(8,128)S(1)}, f32[2,32,256]{2,1,0:T(8,128)S(1)}, u32[]{:S(2)}, u32[]{:S(2)}) %collective-permute-start.7) | collective-permute-done | bytes 65568 | tf_op jit(solution)/shard_map/ppermute | solution.py:489
  44.5 0.1 chain.2
  44.6 1.6 %collective-permute-start.10 = (f32[2,32,256]{2,1,0:T(8,128)S(1)}, f32[2,32,256]{2,1,0:T(8,128)S(1)}, u32[]{:S(2)}, u32[]{:S(2)}) collective-permute-start(f32[2,32,256]{2,1,0:T(8,128)S(1)} %get-tuple-element.56), channel_id=1, source_target_pairs={{0,32},{32,0},{64,96},{96,64},{128,160},{160,128},{192,224},{224,1... | collective-permute-start | bytes 196616 | tf_op jit(solution)/shard_map/ppermute | solution.py:485
  46.2 0.9 %collective-permute-done.10.other = f32[2,32,256]{2,1,0:T(8,128)S(1)} collective-permute-done((f32[2,32,256]{2,1,0:T(8,128)S(1)}, f32[2,32,256]{2,1,0:T(8,128)S(1)}, u32[]{:S(2)}, u32[]{:S(2)}) %collective-permute-start.10) | collective-permute-done | bytes 65568 | tf_op jit(solution)/shard_map/ppermute | solution.py:485
  47.1 1.2 %copy-done.2 = f32[2,8,64,256]{3,2,1,0:T(8,128)S(1)} copy-done((f32[2,8,64,256]{3,2,1,0:T(8,128)S(1)}, f32[2,8,64,256]{3,2,1,0:T(8,128)}, u32[]{:S(2)}) %copy-start.2) | copy-done | bytes 1048600
  48.3 0.3 sweep_mid.1
  48.7 2.1 %next_wells.1 = (f32[96,2,128]{2,1,0:T(2,128)}, f32[8,128]{1,0:T(8,128)S(1)}) custom-call(f32[2,512,128]{2,1,0:T(8,128)S(1)} %get-tuple-element.59.split.field, f32[8,128]{1,0:T(8,128)S(1)} %get-tuple-element.44.refs_2_.live, f32[1,128]{1,0:T(1,128)S(1)} %get-tuple-element.45.refs_3_.wells, f32[1,8]{1,0:T(1,128)S(1)} %copy-done.7, s32[1,48]{1,0:T(1,128)S(1)} %copy-done.5), custom_call_target="tpu_custom_call" | custom-call | tf_op jit(solution)/shard_map/next_wells/pallas_call | solution.py:631
  50.7 6.9 %all-to-all-start.1 = ((f32[96,2,128]{2,1,0:T(2,128)}), f32[96,2,128]{2,1,0:T(2,128)S(1)}, u32[]{:S(2)}, u32[]{:S(2)}) async-start(f32[96,2,128]{2,1,0:T(2,128)} %get-tuple-element.60), calls=%async_computation.1 | async-start | bytes 196608 | tf_op jit(solution)/shard_map/all_to_all | solution.py:573
  57.7 1.3 %collective-permute-start.11 = (f32[8,256]{1,0:T(8,128)S(1)}, f32[8,256]{1,0:T(8,128)S(1)}, u32[]{:S(2)}, u32[]{:S(2)}) collective-permute-start(f32[8,256]{1,0:T(8,128)S(1)} %get-tuple-element.62), channel_id=1, source_target_pairs={{0,4},{4,8},{8,12},{12,16},{16,20},{20,24},{24,28},{28,0},{1,5},{5... | collective-permute-start | bytes 24584 | tf_op jit(solution)/shard_map/ppermute | solution.py:481
  59.0 1.4 %collective-permute-start.12 = (f32[8,256]{1,0:T(8,128)S(1)}, f32[8,256]{1,0:T(8,128)S(1)}, u32[]{:S(2)}, u32[]{:S(2)}) collective-permute-start(f32[8,256]{1,0:T(8,128)S(1)} %get-tuple-element.63), channel_id=1, source_target_pairs={{0,28},{4,0},{8,4},{12,8},{16,12},{20,16},{24,20},{28,24},{1,29},{... | collective-permute-start | bytes 24584 | tf_op jit(solution)/shard_map/ppermute | solution.py:481
  60.4 2.0 %lateral.3.refs_15_ = f32[2,512,128]{2,1,0:T(8,128)S(1)} custom-call(f32[2,512,128]{2,1,0:T(8,128)S(1)} %get-tuple-element.59.split.field, f32[512,256]{1,0:T(8,128)S(1)} %bitcast.15, f32[512,256]{1,0:T(8,128)} %bitcast.27, f32[512,256]{1,0:T(8,128)} %bitcast.29), custom_call_target="tpu_custom_call" | custom-call | flops 2228224 | bytes 2621440 | tf_op jit(solution)/shard_map/lateral/pallas_call | solution.py:577
  62.5 4.3 %all-to-all-done.1.refs_1_ = f32[96,2,128]{2,1,0:T(2,128)S(1)} async-done(((f32[96,2,128]{2,1,0:T(2,128)}), f32[96,2,128]{2,1,0:T(2,128)S(1)}, u32[]{:S(2)}, u32[]{:S(2)}) %all-to-all-start.1) | async-done | bytes 98336 | tf_op jit(solution)/shard_map/all_to_all | solution.py:573
  66.7 3.4 %solve_lines.3 = (f32[512,256]{1,0:T(8,128)S(1)}, f32[2,32,256]{2,1,0:T(8,128)S(1)}, f32[2,32,256]{2,1,0:T(8,128)S(1)}, f32[8,48]{1,0:T(8,128)}) custom-call(s32[1,48]{1,0:T(1,128)S(1)} %copy-done.5, f32[96,2,128]{2,1,0:T(2,128)S(1)} %all-to-all-done.1.refs_1_, f32[8,128]{1,0:T(8,128)S(1)} %get-tuple-element.44.refs_2_.live, ...), custom_call_target="tpu_custom_call" | custom-call | tf_op jit(solution)/shard_map/solve_lines/pallas_call | solution.py:593
  70.2 2.0 %collective-permute-start.13 = (f32[2,32,256]{2,1,0:T(8,128)S(1)}, f32[2,32,256]{2,1,0:T(8,128)S(1)}, u32[]{:S(2)}, u32[]{:S(2)}) collective-permute-start(f32[2,32,256]{2,1,0:T(8,128)S(1)} %get-tuple-element.69), channel_id=1, source_target_pairs={{0,32},{32,0},{64,96},{96,64},{128,160},{160,128},{192,224},{224,1... | collective-permute-start | bytes 196616 | tf_op jit(solution)/shard_map/ppermute | solution.py:485
  72.2 0.9 %collective-permute-done.13.other.refs_9_ = f32[2,32,256]{2,1,0:T(8,128)S(1)} collective-permute-done((f32[2,32,256]{2,1,0:T(8,128)S(1)}, f32[2,32,256]{2,1,0:T(8,128)S(1)}, u32[]{:S(2)}, u32[]{:S(2)}) %collective-permute-start.13) | collective-permute-done | bytes 65568 | tf_op jit(solution)/shard_map/ppermute | solution.py:485
  73.1 0.2 collective-permute-start.16
  73.3 1.1 %collective-permute-start.15 = (f32[2,32,256]{2,1,0:T(8,128)S(1)}, f32[2,32,256]{2,1,0:T(8,128)S(1)}, u32[]{:S(2)}, u32[]{:S(2)}) collective-permute-start(f32[2,32,256]{2,1,0:T(8,128)S(1)} %pair.3.refs_0_), channel_id=1, source_target_pairs={{0,128},{32,160},{64,192},{96,224},{128,0},{160,32},{192,64},{224,... | collective-permute-start | bytes 196616 | tf_op jit(solution)/shard_map/ppermute | solution.py:489
  74.4 0.6 collective-permute-start.14
  75.0 1.3 %collective-permute-done.16.refs_3_ = f32[2,32,256]{2,1,0:T(8,128)S(1)} collective-permute-done((f32[2,32,256]{2,1,0:T(8,128)S(1)}, f32[2,32,256]{2,1,0:T(8,128)S(1)}, u32[]{:S(2)}, u32[]{:S(2)}) %collective-permute-start.16) | collective-permute-done | bytes 65568 | tf_op jit(solution)/shard_map/ppermute | solution.py:489
  76.3 1.6 %collective-permute-done.15.refs_2_ = f32[2,32,256]{2,1,0:T(8,128)S(1)} collective-permute-done((f32[2,32,256]{2,1,0:T(8,128)S(1)}, f32[2,32,256]{2,1,0:T(8,128)S(1)}, u32[]{:S(2)}, u32[]{:S(2)}) %collective-permute-start.15) | collective-permute-done | bytes 65568 | tf_op jit(solution)/shard_map/ppermute | solution.py:489
  77.9 1.6 %collective-permute-done.14.refs_1_ = f32[2,32,256]{2,1,0:T(8,128)S(1)} collective-permute-done((f32[2,32,256]{2,1,0:T(8,128)S(1)}, f32[2,32,256]{2,1,0:T(8,128)S(1)}, u32[]{:S(2)}, u32[]{:S(2)}) %collective-permute-start.14) | collective-permute-done | bytes 65568 | tf_op jit(solution)/shard_map/ppermute | solution.py:489
  79.4 0.1 chain.3
  79.5 1.5 %collective-permute-start.17 = (f32[2,32,256]{2,1,0:T(8,128)S(1)}, f32[2,32,256]{2,1,0:T(8,128)S(1)}, u32[]{:S(2)}, u32[]{:S(2)}) collective-permute-start(f32[2,32,256]{2,1,0:T(8,128)S(1)} %get-tuple-element.71), channel_id=1, source_target_pairs={{0,32},{32,0},{64,96},{96,64},{128,160},{160,128},{192,224},{224,1... | collective-permute-start | bytes 196616 | tf_op jit(solution)/shard_map/ppermute | solution.py:485
  81.0 0.9 %collective-permute-done.17.other = f32[2,32,256]{2,1,0:T(8,128)S(1)} collective-permute-done((f32[2,32,256]{2,1,0:T(8,128)S(1)}, f32[2,32,256]{2,1,0:T(8,128)S(1)}, u32[]{:S(2)}, u32[]{:S(2)}) %collective-permute-start.17) | collective-permute-done | bytes 65568 | tf_op jit(solution)/shard_map/ppermute | solution.py:485
  81.9 0.9 %sweep_last.1 = f32[512,256]{1,0:T(8,128)} custom-call(f32[2,32,256]{2,1,0:T(8,128)S(1)} %get-tuple-element.70.mine, f32[2,32,256]{2,1,0:T(8,128)S(1)} %collective-permute-done.17.other, f32[512,256]{1,0:T(8,128)S(1)} %get-tuple-element.72.solved, f32[2,8,64,256]{3,2,1,0:T(8,128)S(1)} %copy-done.3), custom_call_target="tpu_custom_call" | custom-call | tf_op jit(solution)/shard_map/sweep_last/pallas_call | solution.py:493
  (26 shorter events, 0.1 us)
Async XLA Ops:
  0.6 23.9 %copy-start = (f32[8,64,256]{2,1,0:T(8,128)S(1)}, f32[8,64,256]{2,1,0:T(8,128)}, u32[]{:S(2)}) copy-start(f32[8,64,256]{2,1,0:T(8,128)} %perm_x.1) | copy-start | bytes 1572868
  0.6 5.9 %copy-start.1 = (f32[8,64,256]{2,1,0:T(8,128)S(1)}, f32[8,64,256]{2,1,0:T(8,128)}, u32[]{:S(2)}) copy-start(f32[8,64,256]{2,1,0:T(8,128)} %param.12) | copy-start | bytes 1572868
  0.7 5.9 %copy-start.5 = (s32[1,48]{1,0:T(1,128)S(1)}, s32[1,48]{1,0:T(1,128)}, u32[]{:S(2)}) copy-start(s32[1,48]{1,0:T(1,128)} %refs_0_.3) | copy-start | bytes 580
  0.7 5.9 %copy-start.7 = (f32[1,8]{1,0:T(1,128)S(1)}, f32[1,8]{1,0:T(1,128)}, u32[]{:S(2)}) copy-start(f32[1,8]{1,0:T(1,128)} %rate.1) | copy-start | bytes 100
  0.7 5.9 %copy-start.6 = (f32[1,48,8]{1,2,0:T(8,128)S(1)}, f32[1,48,8]{1,2,0:T(8,128)}, u32[]{:S(2)}) copy-start(f32[1,48,8]{1,2,0:T(8,128)} %param.22) | copy-start | bytes 4612
  0.7 5.9 %copy-start.9 = (s32[1,48]{1,0:T(1,128)S(1)}, s32[1,48]{1,0:T(1,128)}, u32[]{:S(2)}) copy-start(s32[1,48]{1,0:T(1,128)} %refs_4_.1) | copy-start | bytes 580
  0.7 5.9 %copy-start.8 = (s32[1,48,1]{1,2,0:T(1,128)S(1)}, s32[1,48,1]{1,2,0:T(1,128)}, u32[]{:S(2)}) copy-start(s32[1,48,1]{1,2,0:T(1,128)} %param.19) | copy-start | bytes 580
  0.7 28.4 %copy-start.4 = (f32[1,64,256]{2,1,0:T(8,128)S(1)}, f32[1,64,256]{2,1,0:T(8,128)}, u32[]{:S(2)}) copy-start(f32[1,64,256]{2,1,0:T(8,128)} %param.17) | copy-start | bytes 196612
  2.5 6.2 %collective-permute-start = (f32[3,32,256]{2,1,0:T(8,128)S(1)}, f32[3,32,256]{2,1,0:T(8,128)S(1)}, u32[]{:S(2)}, u32[]{:S(2)}) collective-permute-start(f32[3,32,256]{2,1,0:T(8,128)S(1)} %get-tuple-element.41), channel_id=1, source_target_pairs={{0,32},{32,0},{64,96},{96,64},{128,160},{160,128},{192,224},{224,1... | collective-permute-start | bytes 294920 | tf_op jit(solution)/shard_map/ppermute | solution.py:485
  8.8 20.3 %all-to-all-start = ((f32[96,4,128]{2,1,0:T(4,128)}), f32[96,4,128]{2,1,0:T(4,128)S(1)}, u32[]{:S(2)}, u32[]{:S(2)}) async-start(f32[96,4,128]{2,1,0:T(4,128)} %get-tuple-element.42), calls=%async_computation | async-start | bytes 393216 | tf_op jit(solution)/shard_map/all_to_all | solution.py:573
  18.3 8.2 %collective-permute-start.3 = (f32[3,32,256]{2,1,0:T(8,128)S(1)}, f32[3,32,256]{2,1,0:T(8,128)S(1)}, u32[]{:S(2)}, u32[]{:S(2)}) collective-permute-start(f32[3,32,256]{2,1,0:T(8,128)S(1)} %pair_fixed.1.refs_4_), channel_id=1, source_target_pairs={{0,192},{32,224},{64,0},{96,32},{128,64},{160,96},{192,128},{224,1... | collective-permute-start | bytes 294920 | tf_op jit(solution)/shard_map/ppermute | solution.py:489
  20.9 5.7 %collective-permute-start.2 = (f32[3,32,256]{2,1,0:T(8,128)S(1)}, f32[3,32,256]{2,1,0:T(8,128)S(1)}, u32[]{:S(2)}, u32[]{:S(2)}) collective-permute-start(f32[3,32,256]{2,1,0:T(8,128)S(1)} %pair_fixed.1.refs_4_), channel_id=1, source_target_pairs={{0,128},{32,160},{64,192},{96,224},{128,0},{160,32},{192,64},{224,... | collective-permute-start | bytes 294920 | tf_op jit(solution)/shard_map/ppermute | solution.py:489
  21.4 7.7 %collective-permute-start.1 = (f32[3,32,256]{2,1,0:T(8,128)S(1)}, f32[3,32,256]{2,1,0:T(8,128)S(1)}, u32[]{:S(2)}, u32[]{:S(2)}) collective-permute-start(f32[3,32,256]{2,1,0:T(8,128)S(1)} %pair_fixed.1.refs_4_), channel_id=1, source_target_pairs={{0,64},{32,96},{64,128},{96,160},{128,192},{160,224},{192,0},{224,... | collective-permute-start | bytes 294920 | tf_op jit(solution)/shard_map/ppermute | solution.py:489
  22.0 7.1 %collective-permute-start.5 = (f32[16,256]{1,0:T(8,128)S(1)}, f32[16,256]{1,0:T(8,128)S(1)}, u32[]{:S(2)}, u32[]{:S(2)}) collective-permute-start(f32[16,256]{1,0:T(8,128)S(1)} %get-tuple-element.47.refs_6_), channel_id=1, source_target_pairs={{0,28},{4,0},{8,4},{12,8},{16,12},{20,16},{24,20},{28,24},{1,29},{... | collective-permute-start | bytes 49160 | tf_op jit(solution)/shard_map/ppermute | solution.py:481
  24.5 4.6 %collective-permute-start.4 = (f32[16,256]{1,0:T(8,128)S(1)}, f32[16,256]{1,0:T(8,128)S(1)}, u32[]{:S(2)}, u32[]{:S(2)}) collective-permute-start(f32[16,256]{1,0:T(8,128)S(1)} %get-tuple-element.48.refs_7_), channel_id=1, source_target_pairs={{0,4},{4,8},{8,12},{12,16},{16,20},{20,24},{24,28},{28,0},{1,5},{5... | collective-permute-start | bytes 49160 | tf_op jit(solution)/shard_map/ppermute | solution.py:481
  33.1 3.0 %collective-permute-start.6 = (f32[2,32,256]{2,1,0:T(8,128)S(1)}, f32[2,32,256]{2,1,0:T(8,128)S(1)}, u32[]{:S(2)}, u32[]{:S(2)}) collective-permute-start(f32[2,32,256]{2,1,0:T(8,128)S(1)} %get-tuple-element.50), channel_id=1, source_target_pairs={{0,32},{32,0},{64,96},{96,64},{128,160},{160,128},{192,224},{224,1... | collective-permute-start | bytes 196616 | tf_op jit(solution)/shard_map/ppermute | solution.py:485
  36.1 3.8 %collective-permute-start.9 = (f32[2,32,256]{2,1,0:T(8,128)S(1)}, f32[2,32,256]{2,1,0:T(8,128)S(1)}, u32[]{:S(2)}, u32[]{:S(2)}) collective-permute-start(f32[2,32,256]{2,1,0:T(8,128)S(1)} %pair.2.refs_0_), channel_id=1, source_target_pairs={{0,192},{32,224},{64,0},{96,32},{128,64},{160,96},{192,128},{224,1... | collective-permute-start | bytes 196616 | tf_op jit(solution)/shard_map/ppermute | solution.py:489
  38.6 4.6 %collective-permute-start.8 = (f32[2,32,256]{2,1,0:T(8,128)S(1)}, f32[2,32,256]{2,1,0:T(8,128)S(1)}, u32[]{:S(2)}, u32[]{:S(2)}) collective-permute-start(f32[2,32,256]{2,1,0:T(8,128)S(1)} %pair.2.refs_0_), channel_id=1, source_target_pairs={{0,128},{32,160},{64,192},{96,224},{128,0},{160,32},{192,64},{224,... | collective-permute-start | bytes 196616 | tf_op jit(solution)/shard_map/ppermute | solution.py:489
  39.5 5.0 %collective-permute-start.7 = (f32[2,32,256]{2,1,0:T(8,128)S(1)}, f32[2,32,256]{2,1,0:T(8,128)S(1)}, u32[]{:S(2)}, u32[]{:S(2)}) collective-permute-start(f32[2,32,256]{2,1,0:T(8,128)S(1)} %pair.2.refs_0_), channel_id=1, source_target_pairs={{0,64},{32,96},{64,128},{96,160},{128,192},{160,224},{192,0},{224,... | collective-permute-start | bytes 196616 | tf_op jit(solution)/shard_map/ppermute | solution.py:489
  44.6 2.5 %collective-permute-start.10 = (f32[2,32,256]{2,1,0:T(8,128)S(1)}, f32[2,32,256]{2,1,0:T(8,128)S(1)}, u32[]{:S(2)}, u32[]{:S(2)}) collective-permute-start(f32[2,32,256]{2,1,0:T(8,128)S(1)} %get-tuple-element.56), channel_id=1, source_target_pairs={{0,32},{32,0},{64,96},{96,64},{128,160},{160,128},{192,224},{224,1... | collective-permute-start | bytes 196616 | tf_op jit(solution)/shard_map/ppermute | solution.py:485
  47.1 1.2 %copy-start.2 = (f32[2,8,64,256]{3,2,1,0:T(8,128)S(1)}, f32[2,8,64,256]{3,2,1,0:T(8,128)}, u32[]{:S(2)}) copy-start(f32[2,8,64,256]{3,2,1,0:T(8,128)} %get-tuple-element.58.rims) | copy-start | bytes 3145732
  50.7 16.0 %all-to-all-start.1 = ((f32[96,2,128]{2,1,0:T(2,128)}), f32[96,2,128]{2,1,0:T(2,128)S(1)}, u32[]{:S(2)}, u32[]{:S(2)}) async-start(f32[96,2,128]{2,1,0:T(2,128)} %get-tuple-element.60), calls=%async_computation.1 | async-start | bytes 196608 | tf_op jit(solution)/shard_map/all_to_all | solution.py:573
  57.7 4.8 %collective-permute-start.11 = (f32[8,256]{1,0:T(8,128)S(1)}, f32[8,256]{1,0:T(8,128)S(1)}, u32[]{:S(2)}, u32[]{:S(2)}) collective-permute-start(f32[8,256]{1,0:T(8,128)S(1)} %get-tuple-element.62), channel_id=1, source_target_pairs={{0,4},{4,8},{8,12},{12,16},{16,20},{20,24},{24,28},{28,0},{1,5},{5... | collective-permute-start | bytes 24584 | tf_op jit(solution)/shard_map/ppermute | solution.py:481
  59.0 23.0 %copy-start.3 = (f32[2,8,64,256]{3,2,1,0:T(8,128)S(1)}, f32[2,8,64,256]{3,2,1,0:T(8,128)}, u32[]{:S(2)}) copy-start(f32[2,8,64,256]{3,2,1,0:T(8,128)} %get-tuple-element.58.rims) | copy-start | bytes 3145732
  59.0 3.5 %collective-permute-start.12 = (f32[8,256]{1,0:T(8,128)S(1)}, f32[8,256]{1,0:T(8,128)S(1)}, u32[]{:S(2)}, u32[]{:S(2)}) collective-permute-start(f32[8,256]{1,0:T(8,128)S(1)} %get-tuple-element.63), channel_id=1, source_target_pairs={{0,28},{4,0},{8,4},{12,8},{16,12},{20,16},{24,20},{28,24},{1,29},{... | collective-permute-start | bytes 24584 | tf_op jit(solution)/shard_map/ppermute | solution.py:481
  70.2 2.9 %collective-permute-start.13 = (f32[2,32,256]{2,1,0:T(8,128)S(1)}, f32[2,32,256]{2,1,0:T(8,128)S(1)}, u32[]{:S(2)}, u32[]{:S(2)}) collective-permute-start(f32[2,32,256]{2,1,0:T(8,128)S(1)} %get-tuple-element.69), channel_id=1, source_target_pairs={{0,32},{32,0},{64,96},{96,64},{128,160},{160,128},{192,224},{224,1... | collective-permute-start | bytes 196616 | tf_op jit(solution)/shard_map/ppermute | solution.py:485
  73.1 3.2 %collective-permute-start.16 = (f32[2,32,256]{2,1,0:T(8,128)S(1)}, f32[2,32,256]{2,1,0:T(8,128)S(1)}, u32[]{:S(2)}, u32[]{:S(2)}) collective-permute-start(f32[2,32,256]{2,1,0:T(8,128)S(1)} %pair.3.refs_0_), channel_id=1, source_target_pairs={{0,192},{32,224},{64,0},{96,32},{128,64},{160,96},{192,128},{224,1... | collective-permute-start | bytes 196616 | tf_op jit(solution)/shard_map/ppermute | solution.py:489
  73.3 4.6 %collective-permute-start.15 = (f32[2,32,256]{2,1,0:T(8,128)S(1)}, f32[2,32,256]{2,1,0:T(8,128)S(1)}, u32[]{:S(2)}, u32[]{:S(2)}) collective-permute-start(f32[2,32,256]{2,1,0:T(8,128)S(1)} %pair.3.refs_0_), channel_id=1, source_target_pairs={{0,128},{32,160},{64,192},{96,224},{128,0},{160,32},{192,64},{224,... | collective-permute-start | bytes 196616 | tf_op jit(solution)/shard_map/ppermute | solution.py:489
  74.4 5.0 %collective-permute-start.14 = (f32[2,32,256]{2,1,0:T(8,128)S(1)}, f32[2,32,256]{2,1,0:T(8,128)S(1)}, u32[]{:S(2)}, u32[]{:S(2)}) collective-permute-start(f32[2,32,256]{2,1,0:T(8,128)S(1)} %pair.3.refs_0_), channel_id=1, source_target_pairs={{0,64},{32,96},{64,128},{96,160},{128,192},{160,224},{192,0},{224,... | collective-permute-start | bytes 196616 | tf_op jit(solution)/shard_map/ppermute | solution.py:489
  79.5 2.4 %collective-permute-start.17 = (f32[2,32,256]{2,1,0:T(8,128)S(1)}, f32[2,32,256]{2,1,0:T(8,128)S(1)}, u32[]{:S(2)}, u32[]{:S(2)}) collective-permute-start(f32[2,32,256]{2,1,0:T(8,128)S(1)} %get-tuple-element.71), channel_id=1, source_target_pairs={{0,32},{32,0},{64,96},{96,64},{128,160},{160,128},{192,224},{224,1... | collective-permute-start | bytes 196616 | tf_op jit(solution)/shard_map/ppermute | solution.py:485

commit v8 on v7

--- a/solution.py
+++ b/solution.py
@@ -20,7 +20,7 @@
 WELLS = 256
 TILES = 32
 GROUPS = 8
-PARTS = 4
+PARTS = 8
 F32 = jnp.float32
 VMEM = pl.BlockSpec(memory_space=pltpu.VMEM)
 SMEM = pl.BlockSpec(memory_space=pltpu.SMEM)
@@ -201,7 +201,9 @@
         ],
         sem,
     )
-    for copy in copies:
+    copies[2].wait()
+    send_y(partials, y_edge_v[0:8], y_edge_v[8:16])
+    for copy in copies[:2] + copies[3:]:
         copy.wait()
     at = gather_slots(split, column_s)
     at_slots[...] = at
@@ -216,7 +218,6 @@
         [totals_by_well(weighted_c, wells_c) + own_rates(rate_v), totals_by_well(total_c, wells_c)], axis=0
     )
     send_wells(partials, values)
-    send_y(partials, y_edge_v[0:8], y_edge_v[8:16])
 
 
 def wells_next_kernel(split, live, wells, rate, column, partials, at_slots, live_v, wells_v, rate_v, column_s, sem):

time: 83.2 us -> 83.1 us (level)
  no operation moved by 1% of the time
where the time goes in v8:
time: 83.1 us; the launch traced here: 82.8 us
  starting transfers between devices  41.3 us (50%)
  waiting for transfers between devices  19.6 us (24%)
  Pallas kernels  19 us (23%)
  between operations  1.56 us (2%)
  local copies, waits for them, and re-layouts  1.26 us (2%)
    all_to_all x2, starting transfers between devices, shards(): lax.all_to_all(partials, ('gx', 'gy'), split_axis=0, concat_axis=0, tiled...  16.4 us
    ppermute x9, waiting for transfers between devices, all_chips(): lax.ppermute(value, 'layer', around(GROUPS, 2 * d))  11.7 us
    ppermute x5, starting transfers between devices, swapped(): return lax.ppermute(value, 'layer', [(i, i ^ 1) for i in range(GROUPS)])  10.5 us
    ppermute x9, starting transfers between devices, all_chips(): lax.ppermute(value, 'layer', around(GROUPS, 2 * d))  9.17 us
    pallas_call x2, Pallas kernels, shards(): pl.pallas_call(functools.partial(solve_kernel, first, len(operands)), out...  7.29 us
    all_to_all x2, waiting for transfers between devices, shards(): lax.all_to_all(partials, ('gx', 'gy'), split_axis=0, concat_axis=0, tiled...  4.27 us
    pallas_call x2, Pallas kernels, shards(): pl.pallas_call(functools.partial(lateral_kernel, first), out_shape=shape(...  4.07 us
    ppermute x2, starting transfers between devices, from_sides(): lax.ppermute(xlo, 'gx', around(8, -1))  3.96 us
  transfers between devices with their start and end apart: 20, of which 12 were waited for; matrix products, arithmetic and copies ran while one was open for 0% of the time, Pallas kernels for 8%

profile of v8, /device:TPU:1, one launch (start us, length us, event | category | flops | bytes accessed | tf_op | source)
XLA Modules:
  0.0 82.8 jit_solution(617345150461291283)
XLA Ops:
  0.7 1.8 %first_edges.1 = (f32[16,256]{1,0:T(8,128)S(1)}, f32[16,256]{1,0:T(8,128)S(1)}, f32[16,128]{1,0:T(8,128)S(1)}, f32[3,32,256]{2,1,0:T(8,128)S(1)}, f32[3,32,256]{2,1,0:T(8,128)S(1)}) custom-call(f32[512,256]{1,0:T(8,128)} %bitcast.16, f32[8,64,256]{2,1,0:T(8,128)} %perm_x.1, f32[512,256]{1,0:T(8,128)} %bitcast.25, f32[8,8,64,256]{3,2,1,0:T(8,128)} %bitcast.22), custom_call_target="tpu_custom_call" | custom-call | tf_op jit(solution)/shard_map/first_edges/pallas_call | solution.py:528
  2.5 3.3 %collective-permute-start = (f32[3,32,256]{2,1,0:T(8,128)S(1)}, f32[3,32,256]{2,1,0:T(8,128)S(1)}, u32[]{:S(2)}, u32[]{:S(2)}) collective-permute-start(f32[3,32,256]{2,1,0:T(8,128)S(1)} %get-tuple-element.41), channel_id=1, source_target_pairs={{0,32},{32,0},{64,96},{96,64},{128,160},{160,128},{192,224},{224,1... | collective-permute-start | bytes 294920 | tf_op jit(solution)/shard_map/ppermute | solution.py:486
  6.6 2.2 %first_wells.1 = (f32[96,4,128]{2,1,0:T(4,128)}, f32[8,128]{1,0:T(8,128)S(1)}, f32[8,128]{1,0:T(8,128)S(1)}, f32[1,128]{1,0:T(1,128)S(1)}) custom-call(f32[16,128]{1,0:T(8,128)S(1)} %get-tuple-element.38.refs_0_.refs_5_, f32[512,256]{1,0:T(8,128)S(1)} %bitcast.17, f32[8,48]{1,0:T(8,128)S(1)} %bitcast.20, s32[1,48]{1,0:T(1,128)S(1)} %bitcast.21, ...), custom_call_target="tpu_custom_call" | custom-call | tf_op jit(solution)/shard_map/first_wells/pallas_call | solution.py:547
  8.8 9.5 %all-to-all-start = ((f32[96,4,128]{2,1,0:T(4,128)}), f32[96,4,128]{2,1,0:T(4,128)S(1)}, u32[]{:S(2)}, u32[]{:S(2)}) async-start(f32[96,4,128]{2,1,0:T(4,128)} %get-tuple-element.42), calls=%async_computation | async-start | bytes 393216 | tf_op jit(solution)/shard_map/all_to_all | solution.py:574
  18.3 2.6 %collective-permute-start.3 = (f32[3,32,256]{2,1,0:T(8,128)S(1)}, f32[3,32,256]{2,1,0:T(8,128)S(1)}, u32[]{:S(2)}, u32[]{:S(2)}) collective-permute-start(f32[3,32,256]{2,1,0:T(8,128)S(1)} %pair_fixed.1.refs_4_), channel_id=1, source_target_pairs={{0,192},{32,224},{64,0},{96,32},{128,64},{160,96},{192,128},{224,1... | collective-permute-start | bytes 294920 | tf_op jit(solution)/shard_map/ppermute | solution.py:490
  20.9 0.5 collective-permute-start.2
  21.4 0.6 collective-permute-start.1
  22.0 2.5 %collective-permute-start.5 = (f32[16,256]{1,0:T(8,128)S(1)}, f32[16,256]{1,0:T(8,128)S(1)}, u32[]{:S(2)}, u32[]{:S(2)}) collective-permute-start(f32[16,256]{1,0:T(8,128)S(1)} %get-tuple-element.47.refs_6_), channel_id=1, source_target_pairs={{0,28},{4,0},{8,4},{12,8},{16,12},{20,16},{24,20},{28,24},{1,29},{... | collective-permute-start | bytes 49160 | tf_op jit(solution)/shard_map/ppermute | solution.py:482
  24.5 2.0 %lateral.2.refs_10_ = f32[2,512,128]{2,1,0:T(8,128)S(1)} custom-call(f32[512,256]{1,0:T(8,128)S(1)} %bitcast.18, f32[512,256]{1,0:T(8,128)S(1)} %bitcast.14, f32[512,256]{1,0:T(8,128)} %bitcast.26, f32[512,256]{1,0:T(8,128)} %bitcast.28), custom_call_target="tpu_custom_call" | custom-call | flops 2228224 | bytes 2621440 | tf_op jit(solution)/shard_map/lateral/pallas_call | solution.py:578
  26.6 0.0 collective-permute-done.3.refs_7_
  26.6 2.5 %collective-permute-done.1.refs_5_ = f32[3,32,256]{2,1,0:T(8,128)S(1)} collective-permute-done((f32[3,32,256]{2,1,0:T(8,128)S(1)}, f32[3,32,256]{2,1,0:T(8,128)S(1)}, u32[]{:S(2)}, u32[]{:S(2)}) %collective-permute-start.1) | collective-permute-done | bytes 98336 | tf_op jit(solution)/shard_map/ppermute | solution.py:490
  29.1 0.0 all-to-all-done.refs_1_
  29.1 0.0 collective-permute-done.4.refs_8_.refs_10_
  29.1 3.9 %solve_lines.2 = (f32[512,256]{1,0:T(8,128)S(1)}, f32[2,32,256]{2,1,0:T(8,128)S(1)}, f32[2,32,256]{2,1,0:T(8,128)S(1)}, f32[2,128]{1,0:T(2,128)S(1)}, f32[8,128]...) custom-call(s32[1,48]{1,0:T(1,128)S(1)} %copy-done.5, f32[96,4,128]{2,1,0:T(4,128)S(1)} %all-to-all-done.refs_1_, ...), custom_call_target="tpu_custom_call" | custom-call | tf_op jit(solution)/shard_map/solve_lines/pallas_call | solution.py:594
  33.0 2.1 %collective-permute-start.6 = (f32[2,32,256]{2,1,0:T(8,128)S(1)}, f32[2,32,256]{2,1,0:T(8,128)S(1)}, u32[]{:S(2)}, u32[]{:S(2)}) collective-permute-start(f32[2,32,256]{2,1,0:T(8,128)S(1)} %get-tuple-element.50), channel_id=1, source_target_pairs={{0,32},{32,0},{64,96},{96,64},{128,160},{160,128},{192,224},{224,1... | collective-permute-start | bytes 196616 | tf_op jit(solution)/shard_map/ppermute | solution.py:486
  35.1 0.9 %collective-permute-done.6.other.refs_9_ = f32[2,32,256]{2,1,0:T(8,128)S(1)} collective-permute-done((f32[2,32,256]{2,1,0:T(8,128)S(1)}, f32[2,32,256]{2,1,0:T(8,128)S(1)}, u32[]{:S(2)}, u32[]{:S(2)}) %collective-permute-start.6) | collective-permute-done | bytes 65568 | tf_op jit(solution)/shard_map/ppermute | solution.py:486
  36.1 2.5 %collective-permute-start.9 = (f32[2,32,256]{2,1,0:T(8,128)S(1)}, f32[2,32,256]{2,1,0:T(8,128)S(1)}, u32[]{:S(2)}, u32[]{:S(2)}) collective-permute-start(f32[2,32,256]{2,1,0:T(8,128)S(1)} %pair.2.refs_0_), channel_id=1, source_target_pairs={{0,192},{32,224},{64,0},{96,32},{128,64},{160,96},{192,128},{224,1... | collective-permute-start | bytes 196616 | tf_op jit(solution)/shard_map/ppermute | solution.py:490
  38.5 0.9 %collective-permute-start.8 = (f32[2,32,256]{2,1,0:T(8,128)S(1)}, f32[2,32,256]{2,1,0:T(8,128)S(1)}, u32[]{:S(2)}, u32[]{:S(2)}) collective-permute-start(f32[2,32,256]{2,1,0:T(8,128)S(1)} %pair.2.refs_0_), channel_id=1, source_target_pairs={{0,128},{32,160},{64,192},{96,224},{128,0},{160,32},{192,64},{224,... | collective-permute-start | bytes 196616 | tf_op jit(solution)/shard_map/ppermute | solution.py:490
  39.4 0.2 collective-permute-start.7
  39.7 0.2 collective-permute-done.9.refs_3_
  39.9 3.3 %collective-permute-done.8.refs_2_ = f32[2,32,256]{2,1,0:T(8,128)S(1)} collective-permute-done((f32[2,32,256]{2,1,0:T(8,128)S(1)}, f32[2,32,256]{2,1,0:T(8,128)S(1)}, u32[]{:S(2)}, u32[]{:S(2)}) %collective-permute-start.8) | collective-permute-done | bytes 65568 | tf_op jit(solution)/shard_map/ppermute | solution.py:490
  43.2 1.3 %collective-permute-done.7.refs_1_ = f32[2,32,256]{2,1,0:T(8,128)S(1)} collective-permute-done((f32[2,32,256]{2,1,0:T(8,128)S(1)}, f32[2,32,256]{2,1,0:T(8,128)S(1)}, u32[]{:S(2)}, u32[]{:S(2)}) %collective-permute-start.7) | collective-permute-done | bytes 65568 | tf_op jit(solution)/shard_map/ppermute | solution.py:490
  44.4 0.1 chain.2
  44.5 1.6 %collective-permute-start.10 = (f32[2,32,256]{2,1,0:T(8,128)S(1)}, f32[2,32,256]{2,1,0:T(8,128)S(1)}, u32[]{:S(2)}, u32[]{:S(2)}) collective-permute-start(f32[2,32,256]{2,1,0:T(8,128)S(1)} %get-tuple-element.56), channel_id=1, source_target_pairs={{0,32},{32,0},{64,96},{96,64},{128,160},{160,128},{192,224},{224,1... | collective-permute-start | bytes 196616 | tf_op jit(solution)/shard_map/ppermute | solution.py:486
  46.1 0.9 %collective-permute-done.10.other = f32[2,32,256]{2,1,0:T(8,128)S(1)} collective-permute-done((f32[2,32,256]{2,1,0:T(8,128)S(1)}, f32[2,32,256]{2,1,0:T(8,128)S(1)}, u32[]{:S(2)}, u32[]{:S(2)}) %collective-permute-start.10) | collective-permute-done | bytes 65568 | tf_op jit(solution)/shard_map/ppermute | solution.py:486
  47.1 1.2 %copy-done.2 = f32[2,8,64,256]{3,2,1,0:T(8,128)S(1)} copy-done((f32[2,8,64,256]{3,2,1,0:T(8,128)S(1)}, f32[2,8,64,256]{3,2,1,0:T(8,128)}, u32[]{:S(2)}) %copy-start.2) | copy-done | bytes 1048600
  48.3 0.3 sweep_mid.1
  48.6 2.1 %next_wells.1 = (f32[96,2,128]{2,1,0:T(2,128)}, f32[8,128]{1,0:T(8,128)S(1)}) custom-call(f32[2,512,128]{2,1,0:T(8,128)S(1)} %get-tuple-element.59.split.field, f32[8,128]{1,0:T(8,128)S(1)} %get-tuple-element.44.refs_2_.live, f32[1,128]{1,0:T(1,128)S(1)} %get-tuple-element.45.refs_3_.wells, f32[1,8]{1,0:T(1,128)S(1)} %copy-done.7, s32[1,48]{1,0:T(1,128)S(1)} %copy-done.5), custom_call_target="tpu_custom_call" | custom-call | tf_op jit(solution)/shard_map/next_wells/pallas_call | solution.py:632
  50.7 6.9 %all-to-all-start.1 = ((f32[96,2,128]{2,1,0:T(2,128)}), f32[96,2,128]{2,1,0:T(2,128)S(1)}, u32[]{:S(2)}, u32[]{:S(2)}) async-start(f32[96,2,128]{2,1,0:T(2,128)} %get-tuple-element.60), calls=%async_computation.1 | async-start | bytes 196608 | tf_op jit(solution)/shard_map/all_to_all | solution.py:574
  57.6 1.3 %collective-permute-start.11 = (f32[8,256]{1,0:T(8,128)S(1)}, f32[8,256]{1,0:T(8,128)S(1)}, u32[]{:S(2)}, u32[]{:S(2)}) collective-permute-start(f32[8,256]{1,0:T(8,128)S(1)} %get-tuple-element.62), channel_id=1, source_target_pairs={{0,4},{4,8},{8,12},{12,16},{16,20},{20,24},{24,28},{28,0},{1,5},{5... | collective-permute-start | bytes 24584 | tf_op jit(solution)/shard_map/ppermute | solution.py:482
  58.9 1.4 %collective-permute-start.12 = (f32[8,256]{1,0:T(8,128)S(1)}, f32[8,256]{1,0:T(8,128)S(1)}, u32[]{:S(2)}, u32[]{:S(2)}) collective-permute-start(f32[8,256]{1,0:T(8,128)S(1)} %get-tuple-element.63), channel_id=1, source_target_pairs={{0,28},{4,0},{8,4},{12,8},{16,12},{20,16},{24,20},{28,24},{1,29},{... | collective-permute-start | bytes 24584 | tf_op jit(solution)/shard_map/ppermute | solution.py:482
  60.4 2.0 %lateral.3.refs_15_ = f32[2,512,128]{2,1,0:T(8,128)S(1)} custom-call(f32[2,512,128]{2,1,0:T(8,128)S(1)} %get-tuple-element.59.split.field, f32[512,256]{1,0:T(8,128)S(1)} %bitcast.15, f32[512,256]{1,0:T(8,128)} %bitcast.27, f32[512,256]{1,0:T(8,128)} %bitcast.29), custom_call_target="tpu_custom_call" | custom-call | flops 2228224 | bytes 2621440 | tf_op jit(solution)/shard_map/lateral/pallas_call | solution.py:578
  62.4 0.0 collective-permute-done.11.refs_8_
  62.4 0.0 collective-permute-done.12.refs_9_
  62.4 4.3 %all-to-all-done.1.refs_1_ = f32[96,2,128]{2,1,0:T(2,128)S(1)} async-done(((f32[96,2,128]{2,1,0:T(2,128)}), f32[96,2,128]{2,1,0:T(2,128)S(1)}, u32[]{:S(2)}, u32[]{:S(2)}) %all-to-all-start.1) | async-done | bytes 98336 | tf_op jit(solution)/shard_map/all_to_all | solution.py:574
  66.7 3.4 %solve_lines.3 = (f32[512,256]{1,0:T(8,128)S(1)}, f32[2,32,256]{2,1,0:T(8,128)S(1)}, f32[2,32,256]{2,1,0:T(8,128)S(1)}, f32[8,48]{1,0:T(8,128)}) custom-call(s32[1,48]{1,0:T(1,128)S(1)} %copy-done.5, f32[96,2,128]{2,1,0:T(2,128)S(1)} %all-to-all-done.1.refs_1_, f32[8,128]{1,0:T(8,128)S(1)} %get-tuple-element.44.refs_2_.live, ...), custom_call_target="tpu_custom_call" | custom-call | tf_op jit(solution)/shard_map/solve_lines/pallas_call | solution.py:594
  70.1 2.0 %collective-permute-start.13 = (f32[2,32,256]{2,1,0:T(8,128)S(1)}, f32[2,32,256]{2,1,0:T(8,128)S(1)}, u32[]{:S(2)}, u32[]{:S(2)}) collective-permute-start(f32[2,32,256]{2,1,0:T(8,128)S(1)} %get-tuple-element.69), channel_id=1, source_target_pairs={{0,32},{32,0},{64,96},{96,64},{128,160},{160,128},{192,224},{224,1... | collective-permute-start | bytes 196616 | tf_op jit(solution)/shard_map/ppermute | solution.py:486
  72.0 0.9 %collective-permute-done.13.other.refs_9_ = f32[2,32,256]{2,1,0:T(8,128)S(1)} collective-permute-done((f32[2,32,256]{2,1,0:T(8,128)S(1)}, f32[2,32,256]{2,1,0:T(8,128)S(1)}, u32[]{:S(2)}, u32[]{:S(2)}) %collective-permute-start.13) | collective-permute-done | bytes 65568 | tf_op jit(solution)/shard_map/ppermute | solution.py:486
  72.9 0.2 collective-permute-start.16
  73.1 1.1 %collective-permute-start.15 = (f32[2,32,256]{2,1,0:T(8,128)S(1)}, f32[2,32,256]{2,1,0:T(8,128)S(1)}, u32[]{:S(2)}, u32[]{:S(2)}) collective-permute-start(f32[2,32,256]{2,1,0:T(8,128)S(1)} %pair.3.refs_0_), channel_id=1, source_target_pairs={{0,128},{32,160},{64,192},{96,224},{128,0},{160,32},{192,64},{224,... | collective-permute-start | bytes 196616 | tf_op jit(solution)/shard_map/ppermute | solution.py:490
  74.3 0.6 collective-permute-start.14
  74.8 1.3 %collective-permute-done.16.refs_3_ = f32[2,32,256]{2,1,0:T(8,128)S(1)} collective-permute-done((f32[2,32,256]{2,1,0:T(8,128)S(1)}, f32[2,32,256]{2,1,0:T(8,128)S(1)}, u32[]{:S(2)}, u32[]{:S(2)}) %collective-permute-start.16) | collective-permute-done | bytes 65568 | tf_op jit(solution)/shard_map/ppermute | solution.py:490
  76.1 1.6 %collective-permute-done.15.refs_2_ = f32[2,32,256]{2,1,0:T(8,128)S(1)} collective-permute-done((f32[2,32,256]{2,1,0:T(8,128)S(1)}, f32[2,32,256]{2,1,0:T(8,128)S(1)}, u32[]{:S(2)}, u32[]{:S(2)}) %collective-permute-start.15) | collective-permute-done | bytes 65568 | tf_op jit(solution)/shard_map/ppermute | solution.py:490
  77.8 1.6 %collective-permute-done.14.refs_1_ = f32[2,32,256]{2,1,0:T(8,128)S(1)} collective-permute-done((f32[2,32,256]{2,1,0:T(8,128)S(1)}, f32[2,32,256]{2,1,0:T(8,128)S(1)}, u32[]{:S(2)}, u32[]{:S(2)}) %collective-permute-start.14) | collective-permute-done | bytes 65568 | tf_op jit(solution)/shard_map/ppermute | solution.py:490
  79.3 0.1 chain.3
  79.4 1.5 %collective-permute-start.17 = (f32[2,32,256]{2,1,0:T(8,128)S(1)}, f32[2,32,256]{2,1,0:T(8,128)S(1)}, u32[]{:S(2)}, u32[]{:S(2)}) collective-permute-start(f32[2,32,256]{2,1,0:T(8,128)S(1)} %get-tuple-element.71), channel_id=1, source_target_pairs={{0,32},{32,0},{64,96},{96,64},{128,160},{160,128},{192,224},{224,1... | collective-permute-start | bytes 196616 | tf_op jit(solution)/shard_map/ppermute | solution.py:486
  80.9 0.9 %collective-permute-done.17.other = f32[2,32,256]{2,1,0:T(8,128)S(1)} collective-permute-done((f32[2,32,256]{2,1,0:T(8,128)S(1)}, f32[2,32,256]{2,1,0:T(8,128)S(1)}, u32[]{:S(2)}, u32[]{:S(2)}) %collective-permute-start.17) | collective-permute-done | bytes 65568 | tf_op jit(solution)/shard_map/ppermute | solution.py:486
  81.8 0.9 %sweep_last.1 = f32[512,256]{1,0:T(8,128)} custom-call(f32[2,32,256]{2,1,0:T(8,128)S(1)} %get-tuple-element.70.mine, f32[2,32,256]{2,1,0:T(8,128)S(1)} %collective-permute-done.17.other, f32[512,256]{1,0:T(8,128)S(1)} %get-tuple-element.72.solved, f32[2,8,64,256]{3,2,1,0:T(8,128)S(1)} %copy-done.3), custom_call_target="tpu_custom_call" | custom-call | tf_op jit(solution)/shard_map/sweep_last/pallas_call | solution.py:494
  (26 shorter events, 0.1 us)
Async XLA Ops:
  0.6 23.9 %copy-start = (f32[8,64,256]{2,1,0:T(8,128)S(1)}, f32[8,64,256]{2,1,0:T(8,128)}, u32[]{:S(2)}) copy-start(f32[8,64,256]{2,1,0:T(8,128)} %perm_x.1) | copy-start | bytes 1572868
  0.6 5.9 %copy-start.1 = (f32[8,64,256]{2,1,0:T(8,128)S(1)}, f32[8,64,256]{2,1,0:T(8,128)}, u32[]{:S(2)}) copy-start(f32[8,64,256]{2,1,0:T(8,128)} %param.12) | copy-start | bytes 1572868
  0.7 5.9 %copy-start.5 = (s32[1,48]{1,0:T(1,128)S(1)}, s32[1,48]{1,0:T(1,128)}, u32[]{:S(2)}) copy-start(s32[1,48]{1,0:T(1,128)} %refs_0_.3) | copy-start | bytes 580
  0.7 5.9 %copy-start.7 = (f32[1,8]{1,0:T(1,128)S(1)}, f32[1,8]{1,0:T(1,128)}, u32[]{:S(2)}) copy-start(f32[1,8]{1,0:T(1,128)} %rate.1) | copy-start | bytes 100
  0.7 5.9 %copy-start.6 = (f32[1,48,8]{1,2,0:T(8,128)S(1)}, f32[1,48,8]{1,2,0:T(8,128)}, u32[]{:S(2)}) copy-start(f32[1,48,8]{1,2,0:T(8,128)} %param.22) | copy-start | bytes 4612
  0.7 5.9 %copy-start.9 = (s32[1,48]{1,0:T(1,128)S(1)}, s32[1,48]{1,0:T(1,128)}, u32[]{:S(2)}) copy-start(s32[1,48]{1,0:T(1,128)} %refs_4_.1) | copy-start | bytes 580
  0.7 5.9 %copy-start.8 = (s32[1,48,1]{1,2,0:T(1,128)S(1)}, s32[1,48,1]{1,2,0:T(1,128)}, u32[]{:S(2)}) copy-start(s32[1,48,1]{1,2,0:T(1,128)} %param.19) | copy-start | bytes 580
  0.7 28.4 %copy-start.4 = (f32[1,64,256]{2,1,0:T(8,128)S(1)}, f32[1,64,256]{2,1,0:T(8,128)}, u32[]{:S(2)}) copy-start(f32[1,64,256]{2,1,0:T(8,128)} %param.17) | copy-start | bytes 196612
  2.5 6.2 %collective-permute-start = (f32[3,32,256]{2,1,0:T(8,128)S(1)}, f32[3,32,256]{2,1,0:T(8,128)S(1)}, u32[]{:S(2)}, u32[]{:S(2)}) collective-permute-start(f32[3,32,256]{2,1,0:T(8,128)S(1)} %get-tuple-element.41), channel_id=1, source_target_pairs={{0,32},{32,0},{64,96},{96,64},{128,160},{160,128},{192,224},{224,1... | collective-permute-start | bytes 294920 | tf_op jit(solution)/shard_map/ppermute | solution.py:486
  8.8 20.3 %all-to-all-start = ((f32[96,4,128]{2,1,0:T(4,128)}), f32[96,4,128]{2,1,0:T(4,128)S(1)}, u32[]{:S(2)}, u32[]{:S(2)}) async-start(f32[96,4,128]{2,1,0:T(4,128)} %get-tuple-element.42), calls=%async_computation | async-start | bytes 393216 | tf_op jit(solution)/shard_map/all_to_all | solution.py:574
  18.3 8.2 %collective-permute-start.3 = (f32[3,32,256]{2,1,0:T(8,128)S(1)}, f32[3,32,256]{2,1,0:T(8,128)S(1)}, u32[]{:S(2)}, u32[]{:S(2)}) collective-permute-start(f32[3,32,256]{2,1,0:T(8,128)S(1)} %pair_fixed.1.refs_4_), channel_id=1, source_target_pairs={{0,192},{32,224},{64,0},{96,32},{128,64},{160,96},{192,128},{224,1... | collective-permute-start | bytes 294920 | tf_op jit(solution)/shard_map/ppermute | solution.py:490
  20.9 5.7 %collective-permute-start.2 = (f32[3,32,256]{2,1,0:T(8,128)S(1)}, f32[3,32,256]{2,1,0:T(8,128)S(1)}, u32[]{:S(2)}, u32[]{:S(2)}) collective-permute-start(f32[3,32,256]{2,1,0:T(8,128)S(1)} %pair_fixed.1.refs_4_), channel_id=1, source_target_pairs={{0,128},{32,160},{64,192},{96,224},{128,0},{160,32},{192,64},{224,... | collective-permute-start | bytes 294920 | tf_op jit(solution)/shard_map/ppermute | solution.py:490
  21.4 7.7 %collective-permute-start.1 = (f32[3,32,256]{2,1,0:T(8,128)S(1)}, f32[3,32,256]{2,1,0:T(8,128)S(1)}, u32[]{:S(2)}, u32[]{:S(2)}) collective-permute-start(f32[3,32,256]{2,1,0:T(8,128)S(1)} %pair_fixed.1.refs_4_), channel_id=1, source_target_pairs={{0,64},{32,96},{64,128},{96,160},{128,192},{160,224},{192,0},{224,... | collective-permute-start | bytes 294920 | tf_op jit(solution)/shard_map/ppermute | solution.py:490
  22.0 7.1 %collective-permute-start.5 = (f32[16,256]{1,0:T(8,128)S(1)}, f32[16,256]{1,0:T(8,128)S(1)}, u32[]{:S(2)}, u32[]{:S(2)}) collective-permute-start(f32[16,256]{1,0:T(8,128)S(1)} %get-tuple-element.47.refs_6_), channel_id=1, source_target_pairs={{0,28},{4,0},{8,4},{12,8},{16,12},{20,16},{24,20},{28,24},{1,29},{... | collective-permute-start | bytes 49160 | tf_op jit(solution)/shard_map/ppermute | solution.py:482
  24.5 4.6 %collective-permute-start.4 = (f32[16,256]{1,0:T(8,128)S(1)}, f32[16,256]{1,0:T(8,128)S(1)}, u32[]{:S(2)}, u32[]{:S(2)}) collective-permute-start(f32[16,256]{1,0:T(8,128)S(1)} %get-tuple-element.48.refs_7_), channel_id=1, source_target_pairs={{0,4},{4,8},{8,12},{12,16},{16,20},{20,24},{24,28},{28,0},{1,5},{5... | collective-permute-start | bytes 49160 | tf_op jit(solution)/shard_map/ppermute | solution.py:482
  33.0 3.0 %collective-permute-start.6 = (f32[2,32,256]{2,1,0:T(8,128)S(1)}, f32[2,32,256]{2,1,0:T(8,128)S(1)}, u32[]{:S(2)}, u32[]{:S(2)}) collective-permute-start(f32[2,32,256]{2,1,0:T(8,128)S(1)} %get-tuple-element.50), channel_id=1, source_target_pairs={{0,32},{32,0},{64,96},{96,64},{128,160},{160,128},{192,224},{224,1... | collective-permute-start | bytes 196616 | tf_op jit(solution)/shard_map/ppermute | solution.py:486
  36.1 3.8 %collective-permute-start.9 = (f32[2,32,256]{2,1,0:T(8,128)S(1)}, f32[2,32,256]{2,1,0:T(8,128)S(1)}, u32[]{:S(2)}, u32[]{:S(2)}) collective-permute-start(f32[2,32,256]{2,1,0:T(8,128)S(1)} %pair.2.refs_0_), channel_id=1, source_target_pairs={{0,192},{32,224},{64,0},{96,32},{128,64},{160,96},{192,128},{224,1... | collective-permute-start | bytes 196616 | tf_op jit(solution)/shard_map/ppermute | solution.py:490
  38.5 4.6 %collective-permute-start.8 = (f32[2,32,256]{2,1,0:T(8,128)S(1)}, f32[2,32,256]{2,1,0:T(8,128)S(1)}, u32[]{:S(2)}, u32[]{:S(2)}) collective-permute-start(f32[2,32,256]{2,1,0:T(8,128)S(1)} %pair.2.refs_0_), channel_id=1, source_target_pairs={{0,128},{32,160},{64,192},{96,224},{128,0},{160,32},{192,64},{224,... | collective-permute-start | bytes 196616 | tf_op jit(solution)/shard_map/ppermute | solution.py:490
  39.4 5.0 %collective-permute-start.7 = (f32[2,32,256]{2,1,0:T(8,128)S(1)}, f32[2,32,256]{2,1,0:T(8,128)S(1)}, u32[]{:S(2)}, u32[]{:S(2)}) collective-permute-start(f32[2,32,256]{2,1,0:T(8,128)S(1)} %pair.2.refs_0_), channel_id=1, source_target_pairs={{0,64},{32,96},{64,128},{96,160},{128,192},{160,224},{192,0},{224,... | collective-permute-start | bytes 196616 | tf_op jit(solution)/shard_map/ppermute | solution.py:490
  44.5 2.5 %collective-permute-start.10 = (f32[2,32,256]{2,1,0:T(8,128)S(1)}, f32[2,32,256]{2,1,0:T(8,128)S(1)}, u32[]{:S(2)}, u32[]{:S(2)}) collective-permute-start(f32[2,32,256]{2,1,0:T(8,128)S(1)} %get-tuple-element.56), channel_id=1, source_target_pairs={{0,32},{32,0},{64,96},{96,64},{128,160},{160,128},{192,224},{224,1... | collective-permute-start | bytes 196616 | tf_op jit(solution)/shard_map/ppermute | solution.py:486
  47.1 1.2 %copy-start.2 = (f32[2,8,64,256]{3,2,1,0:T(8,128)S(1)}, f32[2,8,64,256]{3,2,1,0:T(8,128)}, u32[]{:S(2)}) copy-start(f32[2,8,64,256]{3,2,1,0:T(8,128)} %get-tuple-element.58.rims) | copy-start | bytes 3145732
  50.7 16.0 %all-to-all-start.1 = ((f32[96,2,128]{2,1,0:T(2,128)}), f32[96,2,128]{2,1,0:T(2,128)S(1)}, u32[]{:S(2)}, u32[]{:S(2)}) async-start(f32[96,2,128]{2,1,0:T(2,128)} %get-tuple-element.60), calls=%async_computation.1 | async-start | bytes 196608 | tf_op jit(solution)/shard_map/all_to_all | solution.py:574
  57.6 4.8 %collective-permute-start.11 = (f32[8,256]{1,0:T(8,128)S(1)}, f32[8,256]{1,0:T(8,128)S(1)}, u32[]{:S(2)}, u32[]{:S(2)}) collective-permute-start(f32[8,256]{1,0:T(8,128)S(1)} %get-tuple-element.62), channel_id=1, source_target_pairs={{0,4},{4,8},{8,12},{12,16},{16,20},{20,24},{24,28},{28,0},{1,5},{5... | collective-permute-start | bytes 24584 | tf_op jit(solution)/shard_map/ppermute | solution.py:482
  58.9 22.9 %copy-start.3 = (f32[2,8,64,256]{3,2,1,0:T(8,128)S(1)}, f32[2,8,64,256]{3,2,1,0:T(8,128)}, u32[]{:S(2)}) copy-start(f32[2,8,64,256]{3,2,1,0:T(8,128)} %get-tuple-element.58.rims) | copy-start | bytes 3145732
  58.9 3.5 %collective-permute-start.12 = (f32[8,256]{1,0:T(8,128)S(1)}, f32[8,256]{1,0:T(8,128)S(1)}, u32[]{:S(2)}, u32[]{:S(2)}) collective-permute-start(f32[8,256]{1,0:T(8,128)S(1)} %get-tuple-element.63), channel_id=1, source_target_pairs={{0,28},{4,0},{8,4},{12,8},{16,12},{20,16},{24,20},{28,24},{1,29},{... | collective-permute-start | bytes 24584 | tf_op jit(solution)/shard_map/ppermute | solution.py:482
  70.1 2.9 %collective-permute-start.13 = (f32[2,32,256]{2,1,0:T(8,128)S(1)}, f32[2,32,256]{2,1,0:T(8,128)S(1)}, u32[]{:S(2)}, u32[]{:S(2)}) collective-permute-start(f32[2,32,256]{2,1,0:T(8,128)S(1)} %get-tuple-element.69), channel_id=1, source_target_pairs={{0,32},{32,0},{64,96},{96,64},{128,160},{160,128},{192,224},{224,1... | collective-permute-start | bytes 196616 | tf_op jit(solution)/shard_map/ppermute | solution.py:486
  72.9 3.2 %collective-permute-start.16 = (f32[2,32,256]{2,1,0:T(8,128)S(1)}, f32[2,32,256]{2,1,0:T(8,128)S(1)}, u32[]{:S(2)}, u32[]{:S(2)}) collective-permute-start(f32[2,32,256]{2,1,0:T(8,128)S(1)} %pair.3.refs_0_), channel_id=1, source_target_pairs={{0,192},{32,224},{64,0},{96,32},{128,64},{160,96},{192,128},{224,1... | collective-permute-start | bytes 196616 | tf_op jit(solution)/shard_map/ppermute | solution.py:490
  73.1 4.6 %collective-permute-start.15 = (f32[2,32,256]{2,1,0:T(8,128)S(1)}, f32[2,32,256]{2,1,0:T(8,128)S(1)}, u32[]{:S(2)}, u32[]{:S(2)}) collective-permute-start(f32[2,32,256]{2,1,0:T(8,128)S(1)} %pair.3.refs_0_), channel_id=1, source_target_pairs={{0,128},{32,160},{64,192},{96,224},{128,0},{160,32},{192,64},{224,... | collective-permute-start | bytes 196616 | tf_op jit(solution)/shard_map/ppermute | solution.py:490
  74.3 5.0 %collective-permute-start.14 = (f32[2,32,256]{2,1,0:T(8,128)S(1)}, f32[2,32,256]{2,1,0:T(8,128)S(1)}, u32[]{:S(2)}, u32[]{:S(2)}) collective-permute-start(f32[2,32,256]{2,1,0:T(8,128)S(1)} %pair.3.refs_0_), channel_id=1, source_target_pairs={{0,64},{32,96},{64,128},{96,160},{128,192},{160,224},{192,0},{224,... | collective-permute-start | bytes 196616 | tf_op jit(solution)/shard_map/ppermute | solution.py:490
  79.4 2.4 %collective-permute-start.17 = (f32[2,32,256]{2,1,0:T(8,128)S(1)}, f32[2,32,256]{2,1,0:T(8,128)S(1)}, u32[]{:S(2)}, u32[]{:S(2)}) collective-permute-start(f32[2,32,256]{2,1,0:T(8,128)S(1)} %get-tuple-element.71), channel_id=1, source_target_pairs={{0,32},{32,0},{64,96},{96,64},{128,160},{160,128},{192,224},{224,1... | collective-permute-start | bytes 196616 | tf_op jit(solution)/shard_map/ppermute | solution.py:486
